TPU v7x, 256 devices: a whole 4x4x8 slice. The times are simulated.
256 devices in a mesh: ctx: 32 (over y, x, core), tp: 8 (over z).
Axes of the slice: x: 4, y: 4, z: 8, core: 2. Of those that a mesh axis runs over, the one named last changes fastest.
Arguments:
- streams: bfloat16 [4096, 3, 4096], P(('ctx', 'tp')), may hold values from -6 to 6
- short_taps: float32 [3, 3, 4096], P(None, None, 'tp'), may hold values from -3.5 to 3.5
- residues: float32 [16, 4096], P(None, 'tp'), may hold values from -0.0546875 to 0.0546875
- rates: float32 [16, 4096], P(None, 'tp'), may hold values from 0.5 to 200
- bias: float32 [4096], P('tp'), may hold values from -1 to 1
Outputs:
- mixed: bfloat16 [4096, 4096], P('ctx', 'tp')
All inputs are finite; a program needn't handle non-finite values.
Results may differ from a plain program's by a relative error of at most 0.0015.
Values may be sent and summed in bfloat16 or wider, within the bound.
No kernel may reach another device: no remote copies, remote signals or barrier semaphores. Data moves between devices by JAX's collectives and lax.ppermute only.
A program may use at most 64 MiB of HBM per device.

v0:
```python
import jax
import jax.numpy as jnp
from jax import lax
from jax.experimental import pallas as pl
from jax.experimental.pallas import tpu as pltpu
from jax.sharding import PartitionSpec as P

LENGTH = 4096
SUB = 16
SHIFTS = (4, 3, 5, 2, 6, 1, 7)
LANES = 128
VMEM = pl.BlockSpec(memory_space=pltpu.VMEM)


def row_iota():
    return lax.broadcasted_iota(jnp.int32, (8, LANES), 0)


def spread(row):
    return jnp.broadcast_to(row, (8, LANES))


def fill_tokens(blocks, order, stream, scratch):
    me = lax.axis_index("tp")
    count = len(blocks)
    for block, shift in zip(blocks, order):
        source = lax.rem(me - shift + count, count)
        at = pl.multiple_of(source * SUB, SUB)
        for group in range(scratch.shape[0]):
            lanes = pl.ds(group * LANES, LANES)
            scratch[group, pl.ds(at, SUB), :] = block[stream, :, lanes].astype(jnp.float32)


def featurize(scratch, stream, lanes, taps_ref, halo_ref):
    group = lanes.start // LANES
    values = [scratch[group, pl.ds(i, 8, stride=SUB), :] for i in range(SUB)]
    first = row_iota() == 0
    back = []
    for far in (2, 1):
        halo = halo_ref[stream, 2 - far : 3 - far, lanes].astype(jnp.float32)
        back.append(jnp.where(first, spread(halo), pltpu.roll(values[SUB - far], 1, 0)))
    joined = back + values
    t0, t1, t2 = (spread(taps_ref[j, stream : stream + 1, lanes]) for j in range(3))
    return [t0 * joined[i + 2] + t1 * joined[i + 1] + t2 * joined[i] for i in range(SUB)]


def state_kernel(order, *refs):
    count = len(order)
    blocks = refs[:count]
    halo_ref, taps_ref, rates_ref, state_ref, ends_ref, signal_ref, one, two = refs[count:]
    modes, channels = rates_ref.shape
    fill_tokens(blocks, order, 1, one)
    fill_tokens(blocks, order, 2, two)
    step = row_iota().astype(jnp.float32)
    remaining = (7.0 - step) * (SUB / LENGTH)
    for start in range(0, channels, LANES):
        lanes = pl.ds(start, LANES)
        left = featurize(one, 1, lanes, taps_ref, halo_ref)
        right = featurize(two, 2, lanes, taps_ref, halo_ref)
        signal = [a * b for a, b in zip(left, right)]
        for i in range(SUB):
            signal_ref[i, :, lanes] = signal[i]
        for mode in range(modes):
            rate = spread(rates_ref[mode : mode + 1, lanes])
            decay = jnp.exp(rate * (-1.0 / LENGTH))
            state = signal[0]
            for i in range(1, SUB):
                state = state * decay + signal[i]
            ends_ref[mode, :, lanes] = state
            weight = jnp.exp(-rate * remaining)
            state_ref[mode : mode + 1, lanes] = jnp.sum(state * weight, axis=0, keepdims=True)


def local_kernel(order, *refs):
    count = len(order)
    blocks = refs[:count]
    (halo_ref, taps_ref, rates_ref, residues_ref, bias_ref, ends_ref, signal_ref, local_ref, front_ref, zero) = refs[count:]
    modes, channels = rates_ref.shape
    fill_tokens(blocks, order, 0, zero)
    rows = row_iota()
    step = rows.astype(jnp.float32)
    for start in range(0, channels, LANES):
        lanes = pl.ds(start, LANES)
        front = featurize(zero, 0, lanes, taps_ref, halo_ref)
        for i in range(SUB):
            front_ref[i, :, lanes] = front[i]
        signal = [signal_ref[i, :, lanes] for i in range(SUB)]
        taps = [jnp.zeros((8, LANES), jnp.float32) for _ in range(SUB // 8)]
        for mode in range(modes):
            rate = spread(rates_ref[mode : mode + 1, lanes])
            residue = spread(residues_ref[mode : mode + 1, lanes])
            for part in range(SUB // 8):
                taps[part] = taps[part] + residue * jnp.exp(-rate * ((step + 8.0 * part) * (1.0 / LENGTH)))
        bias = spread(bias_ref[0:1, lanes])
        total = [bias * signal[i] for i in range(SUB)]
        for lag in range(SUB):
            tap = spread(taps[lag // 8][lag % 8 : lag % 8 + 1])
            for i in range(lag, SUB):
                total[i] = total[i] + tap * signal[i - lag]
        for mode in range(modes):
            rate = spread(rates_ref[mode : mode + 1, lanes])
            residue = spread(residues_ref[mode : mode + 1, lanes])
            decay = jnp.exp(rate * (-1.0 / LENGTH))
            state = ends_ref[mode, :, lanes]
            for far in (1, 2, 4):
                power = jnp.exp(rate * (-far * SUB / LENGTH))
                state = state + jnp.where(rows >= far, power * pltpu.roll(state, far, 0), 0.0)
            carried = jnp.where(rows >= 1, pltpu.roll(state, 1, 0), 0.0) * residue
            for i in range(SUB):
                carried = carried * decay
                total[i] = total[i] + carried
        for i in range(SUB):
            local_ref[i, :, lanes] = total[i]


def final_kernel(carry_ref, rates_ref, residues_ref, local_ref, front_ref, out_ref, natural):
    modes, channels = rates_ref.shape
    step = row_iota().astype(jnp.float32)
    for start in range(0, channels, LANES):
        lanes = pl.ds(start, LANES)
        total = [local_ref[i, :, lanes] for i in range(SUB)]
        for mode in range(modes):
            rate = spread(rates_ref[mode : mode + 1, lanes])
            decay = jnp.exp(rate * (-1.0 / LENGTH))
            first = residues_ref[mode : mode + 1, lanes] * carry_ref[mode : mode + 1, lanes]
            carried = spread(first) * jnp.exp(-rate * ((step * SUB + 1.0) * (1.0 / LENGTH)))
            total[0] = total[0] + carried
            for i in range(1, SUB):
                carried = carried * decay
                total[i] = total[i] + carried
        for i in range(SUB):
            natural[start // LANES, pl.ds(i, 8, stride=SUB), :] = front_ref[i, :, lanes] * total[i]
        out_ref[:, lanes] = natural[start // LANES].astype(out_ref.dtype)


def scan_states(state, rates, mesh):
    index = lax.axis_index("ctx")
    core = index % 2
    column = (index // 2) % 4
    line = index // 8
    total_blocks = lax.axis_size("ctx")

    def power(blocks):
        return jnp.exp(rates * (-jnp.asarray(blocks, jnp.float32) / total_blocks))

    other = lax.ppermute(state, "ctx", [(i, i ^ 1) for i in range(total_blocks)])
    upper = core == 1
    pair = jnp.where(upper, state + power(1) * other, other + power(1) * state)
    inner = jnp.where(upper, other, 0.0)

    def across(value, weight, size, wrap):
        parts = {}
        for by in (2, 1, 3):
            route = []
            for i in range(total_blocks):
                place = (i // weight) % size
                if wrap or place + by < size:
                    route.append((i, i + ((place + by) % size - place) * weight))
            parts[by] = lax.ppermute(value, "ctx", route)
        return parts

    got = across(pair, 2, 4, True)
    before = jnp.zeros_like(pair)
    whole = power(2 * (3 - column)) * pair
    for by, part in got.items():
        before = before + jnp.where(column >= by, power(2 * (by - 1)) * part, 0.0)
        whole = whole + power(2 * (3 - (column - by) % 4)) * part
    got = across(whole, 8, 4, False)
    above = jnp.zeros_like(pair)
    for by, part in got.items():
        above = above + jnp.where(line >= by, power(8 * (by - 1)) * part, 0.0)
    return above * power(2 * column + core) + before * power(core) + inner


def body(streams, short_taps, residues, rates, bias):
    parts = lax.axis_size("tp")
    me = lax.axis_index("tp")
    channels = rates.shape[1]
    modes = rates.shape[0]
    by_stream = jnp.transpose(streams, (1, 0, 2))

    def block_for(shift):
        at = ((me + shift) % parts) * channels
        return lax.dynamic_slice(by_stream, (0, 0, at), (3, SUB, channels))

    order = SHIFTS + (0,)
    blocks = [
        lax.ppermute(block_for(shift), "tp", [(i, (i + shift) % parts) for i in range(parts)]) for shift in SHIFTS
    ] + [block_for(0)]
    tails = [block[:, SUB - 2 :] for block in blocks]
    tail = tails[0]
    for shift, piece in zip(order[1:], tails[1:]):
        tail = jnp.where((me - shift) % parts == parts - 1, piece, tail)
    ctx = lax.axis_size("ctx")
    halo = lax.ppermute(tail, "ctx", [(i, i + 1) for i in range(ctx - 1)])
    f32 = jnp.float32
    tokens = SUB * parts
    wide = jax.ShapeDtypeStruct((SUB, parts, channels), f32)
    limit = pltpu.CompilerParams(vmem_limit_bytes=24 << 20)
    state, ends, signal = pl.pallas_call(
        lambda *refs: state_kernel(order, *refs),
        out_shape=(
            jax.ShapeDtypeStruct((modes, channels), f32),
            jax.ShapeDtypeStruct((modes, parts, channels), f32),
            wide,
        ),
        in_specs=[VMEM] * 11,
        out_specs=(VMEM,) * 3,
        scratch_shapes=[pltpu.VMEM((channels // LANES, tokens, LANES), f32)] * 2,
        compiler_params=limit,
        name="state",
    )(*blocks, halo, short_taps, rates)
    carry = scan_states(state, rates, None)
    local, front = pl.pallas_call(
        lambda *refs: local_kernel(order, *refs),
        out_shape=(wide, wide),
        in_specs=[VMEM] * 15,
        out_specs=(VMEM,) * 2,
        scratch_shapes=[pltpu.VMEM((channels // LANES, tokens, LANES), f32)],
        compiler_params=limit,
        cost_estimate=pl.CostEstimate(flops=8 << 20, bytes_accessed=2 << 20, transcendentals=0),
        name="local",
    )(*blocks, halo, short_taps, rates, residues, bias[None], ends, signal)
    return pl.pallas_call(
        final_kernel,
        out_shape=jax.ShapeDtypeStruct((tokens, channels), jnp.bfloat16),
        in_specs=[VMEM] * 5,
        out_specs=VMEM,
        scratch_shapes=[pltpu.VMEM((channels // LANES, tokens, LANES), f32)],
        compiler_params=limit,
        name="final",
    )(carry, rates, residues, local, front)


def solution(mesh):
    in_specs = (
        P(("ctx", "tp"), None, None),
        P(None, None, "tp"),
        P(None, "tp"),
        P(None, "tp"),
        P("tp"),
    )
    out_specs = P("ctx", "tp")
    return jax.shard_map(body, mesh=mesh, in_specs=in_specs, out_specs=out_specs, check_vma=False)
```

profile of v0, /device:TPU:16, one launch (start us, length us, event | category | flops | bytes accessed | tf_op | source)
XLA Modules:
  0.0 52.3 jit_solution(14792092602534264593)
XLA Ops:
  0.0 1.0 %dynamic-slice_bitcast_fusion = (bf16[3,16,512]{2,1,0:T(8,128)(2,1)S(1)}, bf16[3,16,512]{2,1,0:T(8,128)(2,1)S(1)}, bf16[3,16,512]{2,1,0:T(8,128)(2,1)S(1)}, bf16...) fusion(bf16[16,3,4096]{2,0,1:T(8,128)(2,1)} %param.5, ...), kind=kLoop, calls=%fused_computation | loop fusion | bytes 786464 | tf_op jit(solution)/shard_map/dynamic_slice | solution.py:184
  1.0 7.3 %collective-permute-start = (bf16[3,16,512]{2,1,0:T(8,128)(2,1)S(1)}, bf16[3,16,512]{2,1,0:T(8,128)(2,1)S(1)}, u32[]{:S(2)}, u32[]{:S(2)}) collective-permute-start(bf16[3,16,512]{2,1,0:T(8,128)(2,1)S(1)} %get-tuple-element.21), channel_id=1, source_target_pairs={{0,4},{1,5},{2,6},{3,7},{4,0},{5,1},{6,2},{7,3},{8,12},{9,13},{10,... | collective-permute-start | bytes 147464 | tf_op jit(solution)/shard_map/ppermute | solution.py:188
  8.3 1.9 %collective-permute-start.1 = (bf16[3,16,512]{2,1,0:T(8,128)(2,1)S(1)}, bf16[3,16,512]{2,1,0:T(8,128)(2,1)S(1)}, u32[]{:S(2)}, u32[]{:S(2)}) collective-permute-start(bf16[3,16,512]{2,1,0:T(8,128)(2,1)S(1)} %get-tuple-element.20), channel_id=1, source_target_pairs={{0,3},{1,4},{2,5},{3,6},{4,7},{5,0},{6,1},{7,2},{8,11},{9,12},{10,... | collective-permute-start | bytes 147464 | tf_op jit(solution)/shard_map/ppermute | solution.py:188
  10.2 3.1 %collective-permute-start.2 = (bf16[3,16,512]{2,1,0:T(8,128)(2,1)S(1)}, bf16[3,16,512]{2,1,0:T(8,128)(2,1)S(1)}, u32[]{:S(2)}, u32[]{:S(2)}) collective-permute-start(bf16[3,16,512]{2,1,0:T(8,128)(2,1)S(1)} %get-tuple-element.19), channel_id=1, source_target_pairs={{0,5},{1,6},{2,7},{3,0},{4,1},{5,2},{6,3},{7,4},{8,13},{9,14},{10,... | collective-permute-start | bytes 147464 | tf_op jit(solution)/shard_map/ppermute | solution.py:188
  13.3 1.5 %collective-permute-start.3 = (bf16[3,16,512]{2,1,0:T(8,128)(2,1)S(1)}, bf16[3,16,512]{2,1,0:T(8,128)(2,1)S(1)}, u32[]{:S(2)}, u32[]{:S(2)}) collective-permute-start(bf16[3,16,512]{2,1,0:T(8,128)(2,1)S(1)} %get-tuple-element.18), channel_id=1, source_target_pairs={{0,2},{1,3},{2,4},{3,5},{4,6},{5,7},{6,0},{7,1},{8,10},{9,11},{10,... | collective-permute-start | bytes 147464 | tf_op jit(solution)/shard_map/ppermute | solution.py:188
  14.8 2.7 %collective-permute-start.4 = (bf16[3,16,512]{2,1,0:T(8,128)(2,1)S(1)}, bf16[3,16,512]{2,1,0:T(8,128)(2,1)S(1)}, u32[]{:S(2)}, u32[]{:S(2)}) collective-permute-start(bf16[3,16,512]{2,1,0:T(8,128)(2,1)S(1)} %get-tuple-element.17), channel_id=1, source_target_pairs={{0,6},{1,7},{2,0},{3,1},{4,2},{5,3},{6,4},{7,5},{8,14},{9,15},{10,... | collective-permute-start | bytes 147464 | tf_op jit(solution)/shard_map/ppermute | solution.py:188
  17.4 0.0 collective-permute-done.refs_0_
  17.4 1.0 %collective-permute-start.5 = (bf16[3,16,512]{2,1,0:T(8,128)(2,1)S(1)}, bf16[3,16,512]{2,1,0:T(8,128)(2,1)S(1)}, u32[]{:S(2)}, u32[]{:S(2)}) collective-permute-start(bf16[3,16,512]{2,1,0:T(8,128)(2,1)S(1)} %get-tuple-element.16), channel_id=1, source_target_pairs={{0,1},{1,2},{2,3},{3,4},{4,5},{5,6},{6,7},{7,0},{8,9},{9,10},{10,1... | collective-permute-start | bytes 147464 | tf_op jit(solution)/shard_map/ppermute | solution.py:188
  18.5 0.0 collective-permute-done.1.refs_1_
  18.5 2.2 %collective-permute-start.6 = (bf16[3,16,512]{2,1,0:T(8,128)(2,1)S(1)}, bf16[3,16,512]{2,1,0:T(8,128)(2,1)S(1)}, u32[]{:S(2)}, u32[]{:S(2)}) collective-permute-start(bf16[3,16,512]{2,1,0:T(8,128)(2,1)S(1)} %get-tuple-element.22), channel_id=1, source_target_pairs={{0,7},{1,0},{2,1},{3,2},{4,3},{5,4},{6,5},{7,6},{8,15},{9,8},{10,9... | collective-permute-start | bytes 147464 | tf_op jit(solution)/shard_map/ppermute | solution.py:188
  20.7 0.0 copy-start
  20.7 0.0 collective-permute-done.2.refs_2_
  20.7 0.0 collective-permute-done.3.refs_3_
  20.7 0.0 collective-permute-done.4.refs_4_
  20.7 2.0 %collective-permute-done.5.refs_5_ = bf16[3,16,512]{2,1,0:T(8,128)(2,1)S(1)} collective-permute-done((bf16[3,16,512]{2,1,0:T(8,128)(2,1)S(1)}, bf16[3,16,512]{2,1,0:T(8,128)(2,1)S(1)}, u32[]{:S(2)}, u32[]{:S(2)}) %collective-permute-start.5) | collective-permute-done | bytes 49184 | tf_op jit(solution)/shard_map/ppermute | solution.py:188
  22.8 0.0 collective-permute-done.6.refs_6_
  22.8 0.0 copy-start.2
  22.8 0.1 broadcast_select_fusion.6
  22.8 1.9 %collective-permute-start.7 = (bf16[3,2,512]{2,1,0:T(2,128)(2,1)S(1)}, bf16[3,2,512]{2,1,0:T(2,128)(2,1)S(1)}, u32[]{:S(2)}, u32[]{:S(2)}) collective-permute-start(bf16[3,2,512]{2,1,0:T(2,128)(2,1)S(1)} %broadcast_select_fusion.6), channel_id=1, source_target_pairs={{0,8},{8,16},{16,24},{24,32},{32,40},{40,48},{48,56},{56,64},{64,7... | collective-permute-start | bytes 18440 | tf_op jit(solution)/shard_map/ppermute | solution.py:195
  24.8 5.1 %collective-permute-done.7.refs_8_ = bf16[3,2,512]{2,1,0:T(2,128)(2,1)S(1)} collective-permute-done((bf16[3,2,512]{2,1,0:T(2,128)(2,1)S(1)}, bf16[3,2,512]{2,1,0:T(2,128)(2,1)S(1)}, u32[]{:S(2)}, u32[]{:S(2)}) %collective-permute-start.7) | collective-permute-done | bytes 6176 | tf_op jit(solution)/shard_map/ppermute | solution.py:195
  29.9 0.0 copy-done
  29.9 0.0 copy-done.2
  29.9 0.6 %state.1 = (f32[16,512]{1,0:T(8,128)S(1)}, f32[16,8,512]{2,1,0:T(8,128)S(1)}, f32[16,8,512]{2,1,0:T(8,128)S(1)}) custom-call(bf16[3,16,512]{2,1,0:T(8,128)(2,1)S(1)} %collective-permute-done.refs_0_, bf16[3,16,512]{2,1,0:T(8,128)(2,1)S(1)} %collective-permute-done.1.refs_1_, bf16[3,16,512]{2,1,0:T(8,128)(2,1)S(1)} %collective-permute-done.2.refs_2_, ...), custom_call_target="tpu_custom_call" | custom-call | tf_op jit(solution)/shard_map/state/pallas_call | solution.py:200
  30.5 0.1 collective-permute-start.8
  30.6 1.2 %collective-permute-done.8 = f32[16,512]{1,0:T(8,128)S(1)} collective-permute-done((f32[16,512]{1,0:T(8,128)S(1)}, f32[16,512]{1,0:T(8,128)S(1)}, u32[]{:S(2)}, u32[]{:S(2)}) %collective-permute-start.8) | collective-permute-done | bytes 32800 | tf_op jit(solution)/shard_map/ppermute | solution.py:146
  31.8 0.7 %collective-permute-start.11 = (f32[16,512]{1,0:T(8,128)S(1)}, f32[16,512]{1,0:T(8,128)S(1)}, u32[]{:S(2)}, u32[]{:S(2)}) collective-permute-start(f32[16,512]{1,0:T(8,128)S(1)} %add_select_fusion), channel_id=1, source_target_pairs={{0,48},{8,56},{16,0},{24,8},{32,16},{40,24},{48,32},{56,40},{64,11... | collective-permute-start | bytes 98312 | tf_op jit(solution)/shard_map/ppermute | solution.py:159
  32.5 1.4 %collective-permute-start.10 = (f32[16,512]{1,0:T(8,128)S(1)}, f32[16,512]{1,0:T(8,128)S(1)}, u32[]{:S(2)}, u32[]{:S(2)}) collective-permute-start(f32[16,512]{1,0:T(8,128)S(1)} %add_select_fusion), channel_id=1, source_target_pairs={{0,16},{8,24},{16,32},{24,40},{32,48},{40,56},{48,0},{56,8},{64,80... | collective-permute-start | bytes 98312 | tf_op jit(solution)/shard_map/ppermute | solution.py:159
  33.9 0.9 %collective-permute-start.9 = (f32[16,512]{1,0:T(8,128)S(1)}, f32[16,512]{1,0:T(8,128)S(1)}, u32[]{:S(2)}, u32[]{:S(2)}) collective-permute-start(f32[16,512]{1,0:T(8,128)S(1)} %add_select_fusion), channel_id=1, source_target_pairs={{0,32},{8,40},{16,48},{24,56},{32,0},{40,8},{48,16},{56,24},{64,96... | collective-permute-start | bytes 98312 | tf_op jit(solution)/shard_map/ppermute | solution.py:159
  34.8 1.0 %collective-permute-done.11 = f32[16,512]{1,0:T(8,128)S(1)} collective-permute-done((f32[16,512]{1,0:T(8,128)S(1)}, f32[16,512]{1,0:T(8,128)S(1)}, u32[]{:S(2)}, u32[]{:S(2)}) %collective-permute-start.11) | collective-permute-done | bytes 32800 | tf_op jit(solution)/shard_map/ppermute | solution.py:159
  35.8 1.9 %collective-permute-done.10 = f32[16,512]{1,0:T(8,128)S(1)} collective-permute-done((f32[16,512]{1,0:T(8,128)S(1)}, f32[16,512]{1,0:T(8,128)S(1)}, u32[]{:S(2)}, u32[]{:S(2)}) %collective-permute-start.10) | collective-permute-done | bytes 32800 | tf_op jit(solution)/shard_map/ppermute | solution.py:159
  37.7 1.7 %collective-permute-done.9 = f32[16,512]{1,0:T(8,128)S(1)} collective-permute-done((f32[16,512]{1,0:T(8,128)S(1)}, f32[16,512]{1,0:T(8,128)S(1)}, u32[]{:S(2)}, u32[]{:S(2)}) %collective-permute-start.9) | collective-permute-done | bytes 32800 | tf_op jit(solution)/shard_map/ppermute | solution.py:159
  39.4 0.0 copy-start.1
  39.4 0.7 %collective-permute-start.14 = (f32[16,512]{1,0:T(8,128)S(1)}, f32[16,512]{1,0:T(8,128)S(1)}, u32[]{:S(2)}, u32[]{:S(2)}) collective-permute-start(f32[16,512]{1,0:T(8,128)S(1)} %multiply_add_fusion), channel_id=1, source_target_pairs={{0,192},{8,200},{16,208},{24,216},{32,224},{40,232},{48,240},{56,2... | collective-permute-start | bytes 98312 | tf_op jit(solution)/shard_map/ppermute | solution.py:159
  40.0 3.8 %collective-permute-start.13 = (f32[16,512]{1,0:T(8,128)S(1)}, f32[16,512]{1,0:T(8,128)S(1)}, u32[]{:S(2)}, u32[]{:S(2)}) collective-permute-start(f32[16,512]{1,0:T(8,128)S(1)} %multiply_add_fusion), channel_id=1, source_target_pairs={{0,64},{8,72},{16,80},{24,88},{32,96},{40,104},{48,112},{56,120},{... | collective-permute-start | bytes 98312 | tf_op jit(solution)/shard_map/ppermute | solution.py:159
  43.9 1.3 %collective-permute-start.12 = (f32[16,512]{1,0:T(8,128)S(1)}, f32[16,512]{1,0:T(8,128)S(1)}, u32[]{:S(2)}, u32[]{:S(2)}) collective-permute-start(f32[16,512]{1,0:T(8,128)S(1)} %multiply_add_fusion), channel_id=1, source_target_pairs={{0,128},{8,136},{16,144},{24,152},{32,160},{40,168},{48,176},{56,1... | collective-permute-start | bytes 98312 | tf_op jit(solution)/shard_map/ppermute | solution.py:159
  45.2 0.0 copy-start.3
  45.2 0.0 copy-done.1
  45.2 0.7 %copy-done.3 = f32[512]{0:T(512)S(1)} copy-done((f32[512]{0:T(512)S(1)}, f32[512]{0:T(512)}, u32[]{:S(2)}) %copy-start.3) | copy-done | bytes 2072
  45.9 0.9 %local.1 = (f32[16,8,512]{2,1,0:T(8,128)S(1)}, f32[16,8,512]{2,1,0:T(8,128)S(1)}) custom-call(bf16[3,16,512]{2,1,0:T(8,128)(2,1)S(1)} %collective-permute-done.refs_0_, bf16[3,16,512]{2,1,0:T(8,128)(2,1)S(1)} %collective-permute-done.1.refs_1_, bf16[3,16,512]{2,1,0:T(8,128)(2,1)S(1)} %collective-permute-done.2.refs_2_, ...), custom_call_target="tpu_custom_call" | custom-call | flops 8388608 | bytes 2097152 | tf_op jit(solution)/shard_map/local/pallas_call | solution.py:214
  46.8 0.0 collective-permute-done.14
  46.8 0.0 collective-permute-done.13
  46.8 4.4 %collective-permute-done.12 = f32[16,512]{1,0:T(8,128)S(1)} collective-permute-done((f32[16,512]{1,0:T(8,128)S(1)}, f32[16,512]{1,0:T(8,128)S(1)}, u32[]{:S(2)}, u32[]{:S(2)}) %collective-permute-start.12) | collective-permute-done | bytes 32800 | tf_op jit(solution)/shard_map/ppermute | solution.py:159
  51.2 0.1 select_add_fusion.carry_ref
  51.2 1.1 %final.1 = bf16[128,512]{1,0:T(8,128)(2,1)} custom-call(f32[16,512]{1,0:T(8,128)S(1)} %select_add_fusion.carry_ref, f32[16,512]{1,0:T(8,128)S(1)} %copy-done, f32[16,512]{1,0:T(8,128)S(1)} %copy-done.1, f32[16,8,512]{2,1,0:T(8,128)S(1)} %get-tuple-element.13.local_ref, f32[16,8,512]{2,1,0:T(8,128)S(1)} %get-tuple-element.14.front_ref), custom_call_target="tpu_custom_call" | custom-call | tf_op jit(solution)/shard_map/final/pallas_call | solution.py:224
  (2 shorter events, 0.0 us)
Async XLA Ops:
  1.0 16.5 %collective-permute-start = (bf16[3,16,512]{2,1,0:T(8,128)(2,1)S(1)}, bf16[3,16,512]{2,1,0:T(8,128)(2,1)S(1)}, u32[]{:S(2)}, u32[]{:S(2)}) collective-permute-start(bf16[3,16,512]{2,1,0:T(8,128)(2,1)S(1)} %get-tuple-element.21), channel_id=1, source_target_pairs={{0,4},{1,5},{2,6},{3,7},{4,0},{5,1},{6,2},{7,3},{8,12},{9,13},{10,... | collective-permute-start | bytes 147464 | tf_op jit(solution)/shard_map/ppermute | solution.py:188
  8.3 10.2 %collective-permute-start.1 = (bf16[3,16,512]{2,1,0:T(8,128)(2,1)S(1)}, bf16[3,16,512]{2,1,0:T(8,128)(2,1)S(1)}, u32[]{:S(2)}, u32[]{:S(2)}) collective-permute-start(bf16[3,16,512]{2,1,0:T(8,128)(2,1)S(1)} %get-tuple-element.20), channel_id=1, source_target_pairs={{0,3},{1,4},{2,5},{3,6},{4,7},{5,0},{6,1},{7,2},{8,11},{9,12},{10,... | collective-permute-start | bytes 147464 | tf_op jit(solution)/shard_map/ppermute | solution.py:188
  10.2 10.5 %collective-permute-start.2 = (bf16[3,16,512]{2,1,0:T(8,128)(2,1)S(1)}, bf16[3,16,512]{2,1,0:T(8,128)(2,1)S(1)}, u32[]{:S(2)}, u32[]{:S(2)}) collective-permute-start(bf16[3,16,512]{2,1,0:T(8,128)(2,1)S(1)} %get-tuple-element.19), channel_id=1, source_target_pairs={{0,5},{1,6},{2,7},{3,0},{4,1},{5,2},{6,3},{7,4},{8,13},{9,14},{10,... | collective-permute-start | bytes 147464 | tf_op jit(solution)/shard_map/ppermute | solution.py:188
  13.3 7.4 %collective-permute-start.3 = (bf16[3,16,512]{2,1,0:T(8,128)(2,1)S(1)}, bf16[3,16,512]{2,1,0:T(8,128)(2,1)S(1)}, u32[]{:S(2)}, u32[]{:S(2)}) collective-permute-start(bf16[3,16,512]{2,1,0:T(8,128)(2,1)S(1)} %get-tuple-element.18), channel_id=1, source_target_pairs={{0,2},{1,3},{2,4},{3,5},{4,6},{5,7},{6,0},{7,1},{8,10},{9,11},{10,... | collective-permute-start | bytes 147464 | tf_op jit(solution)/shard_map/ppermute | solution.py:188
  14.8 5.9 %collective-permute-start.4 = (bf16[3,16,512]{2,1,0:T(8,128)(2,1)S(1)}, bf16[3,16,512]{2,1,0:T(8,128)(2,1)S(1)}, u32[]{:S(2)}, u32[]{:S(2)}) collective-permute-start(bf16[3,16,512]{2,1,0:T(8,128)(2,1)S(1)} %get-tuple-element.17), channel_id=1, source_target_pairs={{0,6},{1,7},{2,0},{3,1},{4,2},{5,3},{6,4},{7,5},{8,14},{9,15},{10,... | collective-permute-start | bytes 147464 | tf_op jit(solution)/shard_map/ppermute | solution.py:188
  17.4 5.3 %collective-permute-start.5 = (bf16[3,16,512]{2,1,0:T(8,128)(2,1)S(1)}, bf16[3,16,512]{2,1,0:T(8,128)(2,1)S(1)}, u32[]{:S(2)}, u32[]{:S(2)}) collective-permute-start(bf16[3,16,512]{2,1,0:T(8,128)(2,1)S(1)} %get-tuple-element.16), channel_id=1, source_target_pairs={{0,1},{1,2},{2,3},{3,4},{4,5},{5,6},{6,7},{7,0},{8,9},{9,10},{10,1... | collective-permute-start | bytes 147464 | tf_op jit(solution)/shard_map/ppermute | solution.py:188
  18.5 4.3 %collective-permute-start.6 = (bf16[3,16,512]{2,1,0:T(8,128)(2,1)S(1)}, bf16[3,16,512]{2,1,0:T(8,128)(2,1)S(1)}, u32[]{:S(2)}, u32[]{:S(2)}) collective-permute-start(bf16[3,16,512]{2,1,0:T(8,128)(2,1)S(1)} %get-tuple-element.22), channel_id=1, source_target_pairs={{0,7},{1,0},{2,1},{3,2},{4,3},{5,4},{6,5},{7,6},{8,15},{9,8},{10,9... | collective-permute-start | bytes 147464 | tf_op jit(solution)/shard_map/ppermute | solution.py:188
  20.7 9.2 %copy-start = (f32[16,512]{1,0:T(8,128)S(1)}, f32[16,512]{1,0:T(8,128)}, u32[]{:S(2)}) copy-start(f32[16,512]{1,0:T(8,128)} %rates_ref.1) | copy-start | bytes 98308
  22.8 7.1 %copy-start.2 = (f32[3,3,512]{2,1,0:T(4,128)S(1)}, f32[3,3,512]{2,1,0:T(4,128)}, u32[]{:S(2)}) copy-start(f32[3,3,512]{2,1,0:T(4,128)} %refs_9_.3) | copy-start | bytes 55300
  22.8 7.1 %collective-permute-start.7 = (bf16[3,2,512]{2,1,0:T(2,128)(2,1)S(1)}, bf16[3,2,512]{2,1,0:T(2,128)(2,1)S(1)}, u32[]{:S(2)}, u32[]{:S(2)}) collective-permute-start(bf16[3,2,512]{2,1,0:T(2,128)(2,1)S(1)} %broadcast_select_fusion.6), channel_id=1, source_target_pairs={{0,8},{8,16},{16,24},{24,32},{32,40},{40,48},{48,56},{56,64},{64,7... | collective-permute-start | bytes 18440 | tf_op jit(solution)/shard_map/ppermute | solution.py:195
  30.5 1.3 %collective-permute-start.8 = (f32[16,512]{1,0:T(8,128)S(1)}, f32[16,512]{1,0:T(8,128)S(1)}, u32[]{:S(2)}, u32[]{:S(2)}) collective-permute-start(f32[16,512]{1,0:T(8,128)S(1)} %get-tuple-element.10), channel_id=1, source_target_pairs={{0,8},{8,0},{16,24},{24,16},{32,40},{40,32},{48,56},{56,48},{64,72... | collective-permute-start | bytes 98312 | tf_op jit(solution)/shard_map/ppermute | solution.py:146
  31.8 4.0 %collective-permute-start.11 = (f32[16,512]{1,0:T(8,128)S(1)}, f32[16,512]{1,0:T(8,128)S(1)}, u32[]{:S(2)}, u32[]{:S(2)}) collective-permute-start(f32[16,512]{1,0:T(8,128)S(1)} %add_select_fusion), channel_id=1, source_target_pairs={{0,48},{8,56},{16,0},{24,8},{32,16},{40,24},{48,32},{56,40},{64,11... | collective-permute-start | bytes 98312 | tf_op jit(solution)/shard_map/ppermute | solution.py:159
  32.5 5.1 %collective-permute-start.10 = (f32[16,512]{1,0:T(8,128)S(1)}, f32[16,512]{1,0:T(8,128)S(1)}, u32[]{:S(2)}, u32[]{:S(2)}) collective-permute-start(f32[16,512]{1,0:T(8,128)S(1)} %add_select_fusion), channel_id=1, source_target_pairs={{0,16},{8,24},{16,32},{24,40},{32,48},{40,56},{48,0},{56,8},{64,80... | collective-permute-start | bytes 98312 | tf_op jit(solution)/shard_map/ppermute | solution.py:159
  33.9 5.4 %collective-permute-start.9 = (f32[16,512]{1,0:T(8,128)S(1)}, f32[16,512]{1,0:T(8,128)S(1)}, u32[]{:S(2)}, u32[]{:S(2)}) collective-permute-start(f32[16,512]{1,0:T(8,128)S(1)} %add_select_fusion), channel_id=1, source_target_pairs={{0,32},{8,40},{16,48},{24,56},{32,0},{40,8},{48,16},{56,24},{64,96... | collective-permute-start | bytes 98312 | tf_op jit(solution)/shard_map/ppermute | solution.py:159
  39.4 5.9 %copy-start.1 = (f32[16,512]{1,0:T(8,128)S(1)}, f32[16,512]{1,0:T(8,128)}, u32[]{:S(2)}) copy-start(f32[16,512]{1,0:T(8,128)} %residues_ref.1) | copy-start | bytes 98308
  39.4 7.4 %collective-permute-start.14 = (f32[16,512]{1,0:T(8,128)S(1)}, f32[16,512]{1,0:T(8,128)S(1)}, u32[]{:S(2)}, u32[]{:S(2)}) collective-permute-start(f32[16,512]{1,0:T(8,128)S(1)} %multiply_add_fusion), channel_id=1, source_target_pairs={{0,192},{8,200},{16,208},{24,216},{32,224},{40,232},{48,240},{56,2... | collective-permute-start | bytes 98312 | tf_op jit(solution)/shard_map/ppermute | solution.py:159
  40.0 6.7 %collective-permute-start.13 = (f32[16,512]{1,0:T(8,128)S(1)}, f32[16,512]{1,0:T(8,128)S(1)}, u32[]{:S(2)}, u32[]{:S(2)}) collective-permute-start(f32[16,512]{1,0:T(8,128)S(1)} %multiply_add_fusion), channel_id=1, source_target_pairs={{0,64},{8,72},{16,80},{24,88},{32,96},{40,104},{48,112},{56,120},{... | collective-permute-start | bytes 98312 | tf_op jit(solution)/shard_map/ppermute | solution.py:159
  43.9 7.3 %collective-permute-start.12 = (f32[16,512]{1,0:T(8,128)S(1)}, f32[16,512]{1,0:T(8,128)S(1)}, u32[]{:S(2)}, u32[]{:S(2)}) collective-permute-start(f32[16,512]{1,0:T(8,128)S(1)} %multiply_add_fusion), channel_id=1, source_target_pairs={{0,128},{8,136},{16,144},{24,152},{32,160},{40,168},{48,176},{56,1... | collective-permute-start | bytes 98312 | tf_op jit(solution)/shard_map/ppermute | solution.py:159
  45.2 0.7 %copy-start.3 = (f32[512]{0:T(512)S(1)}, f32[512]{0:T(512)}, u32[]{:S(2)}) copy-start(f32[512]{0:T(512)} %param.9) | copy-start | bytes 6148
where the time goes:
time: 52.7 us; the launch traced here: 52.3 us
  starting transfers between devices  30.5 us (58%)
  waiting for transfers between devices  17.3 us (33%)
  Pallas kernels  2.53 us (5%)
  local copies, waits for them, and re-layouts  1.67 us (3%)
    ppermute x7, starting transfers between devices, body(): lax.ppermute(block_for(shift), 'tp', [(i, (i + shift) % parts) for i in r...  19.7 us
    ppermute x6, waiting for transfers between devices, across(): parts[by] = lax.ppermute(value, 'ctx', route)  8.92 us
    ppermute x6, starting transfers between devices, across(): parts[by] = lax.ppermute(value, 'ctx', route)  8.79 us
    ppermute x1, waiting for transfers between devices, body(): halo = lax.ppermute(tail, 'ctx', [(i, i + 1) for i in range(ctx - 1)])  5.13 us
    ppermute x7, waiting for transfers between devices, body(): lax.ppermute(block_for(shift), 'tp', [(i, (i + shift) % parts) for i in r...  2.05 us
    ppermute x1, starting transfers between devices, body(): halo = lax.ppermute(tail, 'ctx', [(i, i + 1) for i in range(ctx - 1)])  1.92 us
    ppermute x1, waiting for transfers between devices, scan_states(): lax.ppermute(state, 'ctx', [(i, i ^ 1) for i in range(total_blocks)])  1.18 us
    pallas_call x1, Pallas kernels, body(): pl.pallas_call(final_kernel, out_shape=jax.ShapeDtypeStruct((tokens, chan...  1.08 us
  transfers between devices with their start and end apart: 15, of which 7 were waited for; matrix products, arithmetic and copies ran while one was open for 0% of the time, Pallas kernels for 2%

commit v1 on v0

--- a/solution.py
+++ b/solution.py
@@ -7,7 +7,7 @@
 
 LENGTH = 4096
 SUB = 16
-SHIFTS = (4, 3, 5, 2, 6, 1, 7)
+PIECES = 7
 LANES = 128
 VMEM = pl.BlockSpec(memory_space=pltpu.VMEM)
 
@@ -20,15 +20,21 @@
     return jnp.broadcast_to(row, (8, LANES))
 
 
-def fill_tokens(blocks, order, stream, scratch):
+def fill_tokens(blocks, stream, scratch):
     me = lax.axis_index("tp")
-    count = len(blocks)
-    for block, shift in zip(blocks, order):
-        source = lax.rem(me - shift + count, count)
+    turn = 2 * lax.rem(lax.axis_index("ctx"), 2) - 1
+    for block, shift in blocks:
+        source = lax.rem(me - turn * shift + 8, 8)
         at = pl.multiple_of(source * SUB, SUB)
         for group in range(scratch.shape[0]):
             lanes = pl.ds(group * LANES, LANES)
             scratch[group, pl.ds(at, SUB), :] = block[stream, :, lanes].astype(jnp.float32)
+
+
+def arrange(refs):
+    far, near, *single = refs
+    shifts = (-3, 2, -2, -1, 0)
+    return [(far.at[0], 3), (near.at[0], 1), (near.at[1], 4), *zip(single, shifts)]
 
 
 def featurize(scratch, stream, lanes, taps_ref, halo_ref):
@@ -44,13 +50,12 @@
     return [t0 * joined[i + 2] + t1 * joined[i + 1] + t2 * joined[i] for i in range(SUB)]
 
 
-def state_kernel(order, *refs):
-    count = len(order)
-    blocks = refs[:count]
-    halo_ref, taps_ref, rates_ref, state_ref, ends_ref, signal_ref, one, two = refs[count:]
+def state_kernel(*refs):
+    blocks = arrange(refs[:PIECES])
+    halo_ref, taps_ref, rates_ref, state_ref, ends_ref, signal_ref, one, two = refs[PIECES:]
     modes, channels = rates_ref.shape
-    fill_tokens(blocks, order, 1, one)
-    fill_tokens(blocks, order, 2, two)
+    fill_tokens(blocks, 1, one)
+    fill_tokens(blocks, 2, two)
     step = row_iota().astype(jnp.float32)
     remaining = (7.0 - step) * (SUB / LENGTH)
     for start in range(0, channels, LANES):
@@ -71,12 +76,11 @@
             state_ref[mode : mode + 1, lanes] = jnp.sum(state * weight, axis=0, keepdims=True)
 
 
-def local_kernel(order, *refs):
-    count = len(order)
-    blocks = refs[:count]
-    (halo_ref, taps_ref, rates_ref, residues_ref, bias_ref, ends_ref, signal_ref, local_ref, front_ref, zero) = refs[count:]
+def local_kernel(*refs):
+    blocks = arrange(refs[:PIECES])
+    halo_ref, taps_ref, rates_ref, residues_ref, bias_ref, ends_ref, signal_ref, local_ref, front_ref, zero = refs[PIECES:]
     modes, channels = rates_ref.shape
-    fill_tokens(blocks, order, 0, zero)
+    fill_tokens(blocks, 0, zero)
     rows = row_iota()
     step = rows.astype(jnp.float32)
     for start in range(0, channels, LANES):
@@ -133,94 +137,87 @@
         out_ref[:, lanes] = natural[start // LANES].astype(out_ref.dtype)
 
 
-def scan_states(state, rates, mesh):
+def scan_states(state, rates):
     index = lax.axis_index("ctx")
-    core = index % 2
-    column = (index // 2) % 4
-    line = index // 8
-    total_blocks = lax.axis_size("ctx")
-
-    def power(blocks):
-        return jnp.exp(rates * (-jnp.asarray(blocks, jnp.float32) / total_blocks))
-
-    other = lax.ppermute(state, "ctx", [(i, i ^ 1) for i in range(total_blocks)])
-    upper = core == 1
-    pair = jnp.where(upper, state + power(1) * other, other + power(1) * state)
-    inner = jnp.where(upper, other, 0.0)
-
-    def across(value, weight, size, wrap):
-        parts = {}
-        for by in (2, 1, 3):
-            route = []
-            for i in range(total_blocks):
-                place = (i // weight) % size
-                if wrap or place + by < size:
-                    route.append((i, i + ((place + by) % size - place) * weight))
-            parts[by] = lax.ppermute(value, "ctx", route)
-        return parts
-
-    got = across(pair, 2, 4, True)
-    before = jnp.zeros_like(pair)
-    whole = power(2 * (3 - column)) * pair
-    for by, part in got.items():
-        before = before + jnp.where(column >= by, power(2 * (by - 1)) * part, 0.0)
-        whole = whole + power(2 * (3 - (column - by) % 4)) * part
-    got = across(whole, 8, 4, False)
-    above = jnp.zeros_like(pair)
-    for by, part in got.items():
-        above = above + jnp.where(line >= by, power(8 * (by - 1)) * part, 0.0)
-    return above * power(2 * column + core) + before * power(core) + inner
+    blocks = lax.axis_size("ctx")
+    carry = jnp.zeros_like(state)
+
+    def power(count):
+        return jnp.exp(rates * (-jnp.asarray(count, jnp.float32) / blocks))
+
+    for level, flip in enumerate((1, 2, 6, 8, 24)):
+        size = 1 << level
+        last = 2 * size == blocks
+        route = [(i, i ^ flip) for i in range(blocks) if not (last and i & size)]
+        other = lax.ppermute(state, "ctx", route)
+        upper = (index & size) != 0
+        carry = carry + jnp.where(upper, power(index % size) * other, 0.0)
+        if not last:
+            state = jnp.where(upper, state + power(size) * other, other + power(size) * state)
+    return carry
 
 
 def body(streams, short_taps, residues, rates, bias):
     parts = lax.axis_size("tp")
+    ctx = lax.axis_size("ctx")
     me = lax.axis_index("tp")
-    channels = rates.shape[1]
-    modes = rates.shape[0]
+    turn = 2 * (lax.axis_index("ctx") % 2) - 1
+    modes, channels = rates.shape
+    tokens = SUB * parts
+    f32 = jnp.float32
     by_stream = jnp.transpose(streams, (1, 0, 2))
 
     def block_for(shift):
-        at = ((me + shift) % parts) * channels
+        at = ((me + turn * shift) % parts) * channels
         return lax.dynamic_slice(by_stream, (0, 0, at), (3, SUB, channels))
 
-    order = SHIFTS + (0,)
-    blocks = [
-        lax.ppermute(block_for(shift), "tp", [(i, (i + shift) % parts) for i in range(parts)]) for shift in SHIFTS
-    ] + [block_for(0)]
-    tails = [block[:, SUB - 2 :] for block in blocks]
-    tail = tails[0]
-    for shift, piece in zip(order[1:], tails[1:]):
-        tail = jnp.where((me - shift) % parts == parts - 1, piece, tail)
-    ctx = lax.axis_size("ctx")
+    def send(block, shift):
+        route = []
+        for c in range(ctx):
+            step = shift if c % 2 else -shift
+            route += [(c * parts + z, c * parts + (z + step) % parts) for z in range(parts)]
+        return lax.ppermute(block, ("ctx", "tp"), route)
+
+    far = send(jnp.stack([block_for(3), block_for(4)]), 3)
+    single = [send(block_for(shift), shift) for shift in (-3, 2, -2)]
+    own = block_for(1)
+    for later in single[:2]:
+        own = jnp.where(me < 0, later, own)
+    near = send(jnp.stack([own, far[1]]), 1)
+    single += [send(block_for(-1), -1), block_for(0)]
+    pieces = [far, near, *single]
+
+    ends = ((far[0], 3), (near[0], 1), (near[1], 4), *zip(single, (-3, 2, -2, -1, 0)))
+    tail = single[-1][:, SUB - 2 :]
+    for block, shift in ends[:-1]:
+        tail = jnp.where((me - turn * shift) % parts == parts - 1, block[:, SUB - 2 :], tail)
     halo = lax.ppermute(tail, "ctx", [(i, i + 1) for i in range(ctx - 1)])
-    f32 = jnp.float32
-    tokens = SUB * parts
     wide = jax.ShapeDtypeStruct((SUB, parts, channels), f32)
     limit = pltpu.CompilerParams(vmem_limit_bytes=24 << 20)
     state, ends, signal = pl.pallas_call(
-        lambda *refs: state_kernel(order, *refs),
+        state_kernel,
         out_shape=(
             jax.ShapeDtypeStruct((modes, channels), f32),
             jax.ShapeDtypeStruct((modes, parts, channels), f32),
             wide,
         ),
-        in_specs=[VMEM] * 11,
+        in_specs=[VMEM] * (PIECES + 3),
         out_specs=(VMEM,) * 3,
         scratch_shapes=[pltpu.VMEM((channels // LANES, tokens, LANES), f32)] * 2,
         compiler_params=limit,
         name="state",
-    )(*blocks, halo, short_taps, rates)
-    carry = scan_states(state, rates, None)
+    )(*pieces, halo, short_taps, rates)
+    carry = scan_states(state, rates)
     local, front = pl.pallas_call(
-        lambda *refs: local_kernel(order, *refs),
+        local_kernel,
         out_shape=(wide, wide),
-        in_specs=[VMEM] * 15,
+        in_specs=[VMEM] * (PIECES + 7),
         out_specs=(VMEM,) * 2,
         scratch_shapes=[pltpu.VMEM((channels // LANES, tokens, LANES), f32)],
         compiler_params=limit,
         cost_estimate=pl.CostEstimate(flops=8 << 20, bytes_accessed=2 << 20, transcendentals=0),
         name="local",
-    )(*blocks, halo, short_taps, rates, residues, bias[None], ends, signal)
+    )(*pieces, halo, short_taps, rates, residues, bias[None], ends, signal)
     return pl.pallas_call(
         final_kernel,
         out_shape=jax.ShapeDtypeStruct((tokens, channels), jnp.bfloat16),

time: 52.7 us -> 57.4 us (1.089)
  the two profiles are of different devices: /device:TPU:16 before, /device:TPU:24 now
where the time goes in v1:
time: 57.4 us; the launch traced here: 57.1 us
  waiting for transfers between devices  30.8 us (54%)
  starting transfers between devices  20.9 us (36%)
  Pallas kernels  2.54 us (4%)
  local copies, waits for them, and re-layouts  1.7 us (3%)
  other arithmetic  1.01 us (2%)
    ppermute x5, waiting for transfers between devices, scan_states(): other = lax.ppermute(state, 'ctx', route)  16.8 us
    ppermute x6, starting transfers between devices, send(): return lax.ppermute(block, ('ctx', 'tp'), route)  15.9 us
    ppermute x6, waiting for transfers between devices, send(): return lax.ppermute(block, ('ctx', 'tp'), route)  8.82 us
    ppermute x1, waiting for transfers between devices, body(): halo = lax.ppermute(tail, 'ctx', [(i, i + 1) for i in range(ctx - 1)])  5.13 us
    ppermute x5, starting transfers between devices, scan_states(): other = lax.ppermute(state, 'ctx', route)  3.04 us
    ppermute x1, starting transfers between devices, body(): halo = lax.ppermute(tail, 'ctx', [(i, i + 1) for i in range(ctx - 1)])  1.92 us
  transfers between devices with their start and end apart: 12, of which 10 were waited for; matrix products, arithmetic and copies ran while one was open for 1% of the time, Pallas kernels for 1%

profile of v1, /device:TPU:24, one launch (start us, length us, event | category | flops | bytes accessed | tf_op | source)
XLA Modules:
  0.0 57.1 jit_solution(17983376890837654975)
XLA Ops:
  0.0 1.0 %dynamic-slice_bitcast_fusion = (bf16[3,16,512]{2,1,0:T(8,128)(2,1)S(1)}, bf16[3,16,512]{2,1,0:T(8,128)(2,1)S(1)}, bf16[3,16,512]{2,1,0:T(8,128)(2,1)S(1)}, bf16...) fusion(bf16[16,3,4096]{2,0,1:T(8,128)(2,1)} %param.5, ...), kind=kLoop, calls=%fused_computation.8 | loop fusion | bytes 688156 | tf_op jit(solution)/shard_map/dynamic_slice | solution.py:172
  1.0 6.4 %collective-permute-start.1 = (bf16[3,16,512]{2,1,0:T(8,128)(2,1)S(1)}, bf16[3,16,512]{2,1,0:T(8,128)(2,1)S(1)}, u32[]{:S(2)}, u32[]{:S(2)}) collective-permute-start(bf16[3,16,512]{2,1,0:T(8,128)(2,1)S(1)} %get-tuple-element.18), channel_id=1, source_target_pairs={{0,6},{1,7},{2,0},{3,1},{4,2},{5,3},{6,4},{7,5},{8,10},{9,11},{10,... | collective-permute-start | bytes 147464 | tf_op jit(solution)/shard_map/ppermute | solution.py:179
  7.3 0.0 collective-permute-start.2
  7.4 5.1 %collective-permute-start = (bf16[2,3,16,512]{3,2,1,0:T(8,128)(2,1)S(1)}, bf16[2,3,16,512]{3,2,1,0:T(8,128)(2,1)S(1)}, u32[]{:S(2)}, u32[]{:S(2)}) collective-permute-start(bf16[2,3,16,512]{3,2,1,0:T(8,128)(2,1)S(1)} %pad_maximum_fusion), channel_id=1, source_target_pairs={{0,5},{1,6},{2,7},{3,0},{4,1},{5,2},{6,3},{7,4},{8,11},{9,12},{10,... | collective-permute-start | bytes 294920 | tf_op jit(solution)/shard_map/ppermute | solution.py:179
  12.5 0.0 collective-permute-done.1.refs_3_
  12.5 4.0 %collective-permute-done.2.refs_2_ = bf16[3,16,512]{2,1,0:T(8,128)(2,1)S(1)} collective-permute-done((bf16[3,16,512]{2,1,0:T(8,128)(2,1)S(1)}, bf16[3,16,512]{2,1,0:T(8,128)(2,1)S(1)}, u32[]{:S(2)}, u32[]{:S(2)}) %collective-permute-start.2) | collective-permute-done | bytes 49184 | tf_op jit(solution)/shard_map/ppermute | solution.py:179
  16.5 0.8 %fusion.1 = bf16[1,3,16,512]{3,2,1,0:T(8,128)(2,1)S(1)} fusion(bf16[3,16,512]{2,1,0:T(8,128)(2,1)S(1)} %collective-permute-done.1.refs_3_, bf16[3,16,512]{2,1,0:T(8,128)(2,1)S(1)} %collective-permute-done.2.refs_2_, bf16[16,3,4096]{2,0,1:T(8,128)(2,1)} %param.5, s32[]{:T(128)S(6)} %select_n.225, pred[]{:T(512)S(6)} %lt.115), kind=kLoop, calls=%fused_computation.7 | loop fusion | flops 49152 | bytes 196613 | tf_op jit(solution)/shard_map/stack | solution.py:186
  17.3 0.0 collective-permute-done.refs_0_
  17.3 0.1 collective-permute-start.3
  17.4 3.9 %collective-permute-start.4 = (bf16[3,16,512]{2,1,0:T(8,128)(2,1)S(1)}, bf16[3,16,512]{2,1,0:T(8,128)(2,1)S(1)}, u32[]{:S(2)}, u32[]{:S(2)}) collective-permute-start(bf16[3,16,512]{2,1,0:T(8,128)(2,1)S(1)} %get-tuple-element.16), channel_id=1, source_target_pairs={{0,2},{1,3},{2,4},{3,5},{4,6},{5,7},{6,0},{7,1},{8,14},{9,15},{10,... | collective-permute-start | bytes 147464 | tf_op jit(solution)/shard_map/ppermute | solution.py:179
  21.3 0.5 collective-permute-start.5
  21.8 1.7 %collective-permute-done.3.refs_1_ = bf16[2,3,16,512]{3,2,1,0:T(8,128)(2,1)S(1)} collective-permute-done((bf16[2,3,16,512]{3,2,1,0:T(8,128)(2,1)S(1)}, bf16[2,3,16,512]{3,2,1,0:T(8,128)(2,1)S(1)}, u32[]{:S(2)}, u32[]{:S(2)}) %collective-permute-start.3) | collective-permute-done | bytes 98336 | tf_op jit(solution)/shard_map/ppermute | solution.py:179
  23.5 0.4 collective-permute-done.4.refs_4_
  23.9 2.7 %collective-permute-done.5.refs_5_ = bf16[3,16,512]{2,1,0:T(8,128)(2,1)S(1)} collective-permute-done((bf16[3,16,512]{2,1,0:T(8,128)(2,1)S(1)}, bf16[3,16,512]{2,1,0:T(8,128)(2,1)S(1)}, u32[]{:S(2)}, u32[]{:S(2)}) %collective-permute-start.5) | collective-permute-done | bytes 49184 | tf_op jit(solution)/shard_map/ppermute | solution.py:179
  26.6 0.0 copy-start
  26.6 0.0 copy-start.2
  26.6 0.1 broadcast_select_fusion.6
  26.7 1.9 %collective-permute-start.6 = (bf16[3,2,512]{2,1,0:T(2,128)(2,1)S(1)}, bf16[3,2,512]{2,1,0:T(2,128)(2,1)S(1)}, u32[]{:S(2)}, u32[]{:S(2)}) collective-permute-start(bf16[3,2,512]{2,1,0:T(2,128)(2,1)S(1)} %broadcast_select_fusion.6), channel_id=1, source_target_pairs={{0,8},{8,16},{16,24},{24,32},{32,40},{40,48},{48,56},{56,64},{64,7... | collective-permute-start | bytes 18440 | tf_op jit(solution)/shard_map/ppermute | solution.py:194
  28.6 5.1 %collective-permute-done.6.refs_7_ = bf16[3,2,512]{2,1,0:T(2,128)(2,1)S(1)} collective-permute-done((bf16[3,2,512]{2,1,0:T(2,128)(2,1)S(1)}, bf16[3,2,512]{2,1,0:T(2,128)(2,1)S(1)}, u32[]{:S(2)}, u32[]{:S(2)}) %collective-permute-start.6) | collective-permute-done | bytes 6176 | tf_op jit(solution)/shard_map/ppermute | solution.py:194
  33.7 0.0 copy-done
  33.7 0.0 copy-done.2
  33.7 0.6 %state.1 = (f32[16,512]{1,0:T(8,128)S(1)}, f32[16,8,512]{2,1,0:T(8,128)S(1)}, f32[16,8,512]{2,1,0:T(8,128)S(1)}) custom-call(bf16[2,3,16,512]{3,2,1,0:T(8,128)(2,1)S(1)} %collective-permute-done.refs_0_, bf16[2,3,16,512]{3,2,1,0:T(8,128)(2,1)S(1)} %collective-permute-done.3.refs_1_, bf16[3,16,512]{2,1,0:T(8,128)(2,1)S(1)} %collective-permute-done.2.refs_2_, ...), custom_call_target="tpu_custom_call" | custom-call | tf_op jit(solution)/shard_map/state/pallas_call | solution.py:197
  34.4 0.1 collective-permute-start.7
  34.5 1.2 %collective-permute-done.7 = f32[16,512]{1,0:T(8,128)S(1)} collective-permute-done((f32[16,512]{1,0:T(8,128)S(1)}, f32[16,512]{1,0:T(8,128)S(1)}, u32[]{:S(2)}, u32[]{:S(2)}) %collective-permute-start.7) | collective-permute-done | bytes 32800 | tf_op jit(solution)/shard_map/ppermute | solution.py:152
  35.7 0.1 collective-permute-start.8
  35.8 3.9 %collective-permute-done.8 = f32[16,512]{1,0:T(8,128)S(1)} collective-permute-done((f32[16,512]{1,0:T(8,128)S(1)}, f32[16,512]{1,0:T(8,128)S(1)}, u32[]{:S(2)}, u32[]{:S(2)}) %collective-permute-start.8) | collective-permute-done | bytes 32800 | tf_op jit(solution)/shard_map/ppermute | solution.py:152
  39.7 0.7 %collective-permute-start.9 = (f32[16,512]{1,0:T(8,128)S(1)}, f32[16,512]{1,0:T(8,128)S(1)}, u32[]{:S(2)}, u32[]{:S(2)}) collective-permute-start(f32[16,512]{1,0:T(8,128)S(1)} %add_select_fusion.2), channel_id=1, source_target_pairs={{0,48},{8,56},{16,32},{24,40},{32,16},{40,24},{48,0},{56,8},{64,11... | collective-permute-start | bytes 98312 | tf_op jit(solution)/shard_map/ppermute | solution.py:152
  40.4 4.5 %collective-permute-done.9 = f32[16,512]{1,0:T(8,128)S(1)} collective-permute-done((f32[16,512]{1,0:T(8,128)S(1)}, f32[16,512]{1,0:T(8,128)S(1)}, u32[]{:S(2)}, u32[]{:S(2)}) %collective-permute-start.9) | collective-permute-done | bytes 32800 | tf_op jit(solution)/shard_map/ppermute | solution.py:152
  44.9 0.8 %collective-permute-start.10 = (f32[16,512]{1,0:T(8,128)S(1)}, f32[16,512]{1,0:T(8,128)S(1)}, u32[]{:S(2)}, u32[]{:S(2)}) collective-permute-start(f32[16,512]{1,0:T(8,128)S(1)} %add_select_fusion.1), channel_id=1, source_target_pairs={{0,64},{8,72},{16,80},{24,88},{32,96},{40,104},{48,112},{56,120},{... | collective-permute-start | bytes 98312 | tf_op jit(solution)/shard_map/ppermute | solution.py:152
  45.8 3.2 %collective-permute-done.10 = f32[16,512]{1,0:T(8,128)S(1)} collective-permute-done((f32[16,512]{1,0:T(8,128)S(1)}, f32[16,512]{1,0:T(8,128)S(1)}, u32[]{:S(2)}, u32[]{:S(2)}) %collective-permute-start.10) | collective-permute-done | bytes 32800 | tf_op jit(solution)/shard_map/ppermute | solution.py:152
  48.9 1.3 %collective-permute-start.11 = (f32[16,512]{1,0:T(8,128)S(1)}, f32[16,512]{1,0:T(8,128)S(1)}, u32[]{:S(2)}, u32[]{:S(2)}) collective-permute-start(f32[16,512]{1,0:T(8,128)S(1)} %add_select_fusion), channel_id=1, source_target_pairs={{0,192},{8,200},{16,208},{24,216},{32,224},{40,232},{48,240},{56,2... | collective-permute-start | bytes 98312 | tf_op jit(solution)/shard_map/ppermute | solution.py:152
  50.2 0.0 copy-start.1
  50.3 0.0 copy-start.3
  50.3 0.7 %copy-done.1 = f32[16,512]{1,0:T(8,128)S(1)} copy-done((f32[16,512]{1,0:T(8,128)S(1)}, f32[16,512]{1,0:T(8,128)}, u32[]{:S(2)}) %copy-start.1) | copy-done | bytes 32792
  51.0 0.0 copy-done.3
  51.0 0.9 %local.1 = (f32[16,8,512]{2,1,0:T(8,128)S(1)}, f32[16,8,512]{2,1,0:T(8,128)S(1)}) custom-call(bf16[2,3,16,512]{3,2,1,0:T(8,128)(2,1)S(1)} %collective-permute-done.refs_0_, bf16[2,3,16,512]{3,2,1,0:T(8,128)(2,1)S(1)} %collective-permute-done.3.refs_1_, bf16[3,16,512]{2,1,0:T(8,128)(2,1)S(1)} %collective-permute-done.2.refs_2_, ...), custom_call_target="tpu_custom_call" | custom-call | flops 8388608 | bytes 2097152 | tf_op jit(solution)/shard_map/local/pallas_call | solution.py:211
  51.9 4.1 %collective-permute-done.11 = f32[16,512]{1,0:T(8,128)S(1)} collective-permute-done((f32[16,512]{1,0:T(8,128)S(1)}, f32[16,512]{1,0:T(8,128)S(1)}, u32[]{:S(2)}, u32[]{:S(2)}) %collective-permute-start.11) | collective-permute-done | bytes 32800 | tf_op jit(solution)/shard_map/ppermute | solution.py:152
  56.0 1.1 %final.1 = bf16[128,512]{1,0:T(8,128)(2,1)} custom-call(f32[16,512]{1,0:T(8,128)S(1)} %select_add_fusion.carry_ref, f32[16,512]{1,0:T(8,128)S(1)} %copy-done, f32[16,512]{1,0:T(8,128)S(1)} %copy-done.1, f32[16,8,512]{2,1,0:T(8,128)S(1)} %get-tuple-element.13.local_ref, f32[16,8,512]{2,1,0:T(8,128)S(1)} %get-tuple-element.14.front_ref), custom_call_target="tpu_custom_call" | custom-call | tf_op jit(solution)/shard_map/final/pallas_call | solution.py:221
  (9 shorter events, 0.1 us)
Async XLA Ops:
  1.0 11.5 %collective-permute-start.1 = (bf16[3,16,512]{2,1,0:T(8,128)(2,1)S(1)}, bf16[3,16,512]{2,1,0:T(8,128)(2,1)S(1)}, u32[]{:S(2)}, u32[]{:S(2)}) collective-permute-start(bf16[3,16,512]{2,1,0:T(8,128)(2,1)S(1)} %get-tuple-element.18), channel_id=1, source_target_pairs={{0,6},{1,7},{2,0},{3,1},{4,2},{5,3},{6,4},{7,5},{8,10},{9,11},{10,... | collective-permute-start | bytes 147464 | tf_op jit(solution)/shard_map/ppermute | solution.py:179
  7.3 9.1 %collective-permute-start.2 = (bf16[3,16,512]{2,1,0:T(8,128)(2,1)S(1)}, bf16[3,16,512]{2,1,0:T(8,128)(2,1)S(1)}, u32[]{:S(2)}, u32[]{:S(2)}) collective-permute-start(bf16[3,16,512]{2,1,0:T(8,128)(2,1)S(1)} %get-tuple-element.17), channel_id=1, source_target_pairs={{0,3},{1,4},{2,5},{3,6},{4,7},{5,0},{6,1},{7,2},{8,13},{9,14},{10,... | collective-permute-start | bytes 147464 | tf_op jit(solution)/shard_map/ppermute | solution.py:179
  7.4 9.9 %collective-permute-start = (bf16[2,3,16,512]{3,2,1,0:T(8,128)(2,1)S(1)}, bf16[2,3,16,512]{3,2,1,0:T(8,128)(2,1)S(1)}, u32[]{:S(2)}, u32[]{:S(2)}) collective-permute-start(bf16[2,3,16,512]{3,2,1,0:T(8,128)(2,1)S(1)} %pad_maximum_fusion), channel_id=1, source_target_pairs={{0,5},{1,6},{2,7},{3,0},{4,1},{5,2},{6,3},{7,4},{8,11},{9,12},{10,... | collective-permute-start | bytes 294920 | tf_op jit(solution)/shard_map/ppermute | solution.py:179
  17.3 6.1 %collective-permute-start.3 = (bf16[2,3,16,512]{3,2,1,0:T(8,128)(2,1)S(1)}, bf16[2,3,16,512]{3,2,1,0:T(8,128)(2,1)S(1)}, u32[]{:S(2)}, u32[]{:S(2)}) collective-permute-start(bf16[2,3,16,512]{3,2,1,0:T(8,128)(2,1)S(1)} %pad_maximum_fusion.1), channel_id=1, source_target_pairs={{0,7},{1,0},{2,1},{3,2},{4,3},{5,4},{6,5},{7,6},{8,9},{9,10},{10,1... | collective-permute-start | bytes 294920 | tf_op jit(solution)/shard_map/ppermute | solution.py:179
  17.4 6.5 %collective-permute-start.4 = (bf16[3,16,512]{2,1,0:T(8,128)(2,1)S(1)}, bf16[3,16,512]{2,1,0:T(8,128)(2,1)S(1)}, u32[]{:S(2)}, u32[]{:S(2)}) collective-permute-start(bf16[3,16,512]{2,1,0:T(8,128)(2,1)S(1)} %get-tuple-element.16), channel_id=1, source_target_pairs={{0,2},{1,3},{2,4},{3,5},{4,6},{5,7},{6,0},{7,1},{8,14},{9,15},{10,... | collective-permute-start | bytes 147464 | tf_op jit(solution)/shard_map/ppermute | solution.py:179
  21.3 5.3 %collective-permute-start.5 = (bf16[3,16,512]{2,1,0:T(8,128)(2,1)S(1)}, bf16[3,16,512]{2,1,0:T(8,128)(2,1)S(1)}, u32[]{:S(2)}, u32[]{:S(2)}) collective-permute-start(bf16[3,16,512]{2,1,0:T(8,128)(2,1)S(1)} %get-tuple-element.21), channel_id=1, source_target_pairs={{0,1},{1,2},{2,3},{3,4},{4,5},{5,6},{6,7},{7,0},{8,15},{9,8},{10,9... | collective-permute-start | bytes 147464 | tf_op jit(solution)/shard_map/ppermute | solution.py:179
  26.6 7.1 %copy-start = (f32[16,512]{1,0:T(8,128)S(1)}, f32[16,512]{1,0:T(8,128)}, u32[]{:S(2)}) copy-start(f32[16,512]{1,0:T(8,128)} %rates_ref.1) | copy-start | bytes 98308
  26.6 7.1 %copy-start.2 = (f32[3,3,512]{2,1,0:T(4,128)S(1)}, f32[3,3,512]{2,1,0:T(4,128)}, u32[]{:S(2)}) copy-start(f32[3,3,512]{2,1,0:T(4,128)} %refs_8_.3) | copy-start | bytes 55300
  26.7 7.1 %collective-permute-start.6 = (bf16[3,2,512]{2,1,0:T(2,128)(2,1)S(1)}, bf16[3,2,512]{2,1,0:T(2,128)(2,1)S(1)}, u32[]{:S(2)}, u32[]{:S(2)}) collective-permute-start(bf16[3,2,512]{2,1,0:T(2,128)(2,1)S(1)} %broadcast_select_fusion.6), channel_id=1, source_target_pairs={{0,8},{8,16},{16,24},{24,32},{32,40},{40,48},{48,56},{56,64},{64,7... | collective-permute-start | bytes 18440 | tf_op jit(solution)/shard_map/ppermute | solution.py:194
  34.4 1.3 %collective-permute-start.7 = (f32[16,512]{1,0:T(8,128)S(1)}, f32[16,512]{1,0:T(8,128)S(1)}, u32[]{:S(2)}, u32[]{:S(2)}) collective-permute-start(f32[16,512]{1,0:T(8,128)S(1)} %get-tuple-element.10), channel_id=1, source_target_pairs={{0,8},{8,0},{16,24},{24,16},{32,40},{40,32},{48,56},{56,48},{64,72... | collective-permute-start | bytes 98312 | tf_op jit(solution)/shard_map/ppermute | solution.py:152
  35.7 4.0 %collective-permute-start.8 = (f32[16,512]{1,0:T(8,128)S(1)}, f32[16,512]{1,0:T(8,128)S(1)}, u32[]{:S(2)}, u32[]{:S(2)}) collective-permute-start(f32[16,512]{1,0:T(8,128)S(1)} %add_select_fusion.3), channel_id=1, source_target_pairs={{0,16},{8,24},{16,0},{24,8},{32,48},{40,56},{48,32},{56,40},{64,80... | collective-permute-start | bytes 98312 | tf_op jit(solution)/shard_map/ppermute | solution.py:152
  39.7 5.2 %collective-permute-start.9 = (f32[16,512]{1,0:T(8,128)S(1)}, f32[16,512]{1,0:T(8,128)S(1)}, u32[]{:S(2)}, u32[]{:S(2)}) collective-permute-start(f32[16,512]{1,0:T(8,128)S(1)} %add_select_fusion.2), channel_id=1, source_target_pairs={{0,48},{8,56},{16,32},{24,40},{32,16},{40,24},{48,0},{56,8},{64,11... | collective-permute-start | bytes 98312 | tf_op jit(solution)/shard_map/ppermute | solution.py:152
  44.9 4.0 %collective-permute-start.10 = (f32[16,512]{1,0:T(8,128)S(1)}, f32[16,512]{1,0:T(8,128)S(1)}, u32[]{:S(2)}, u32[]{:S(2)}) collective-permute-start(f32[16,512]{1,0:T(8,128)S(1)} %add_select_fusion.1), channel_id=1, source_target_pairs={{0,64},{8,72},{16,80},{24,88},{32,96},{40,104},{48,112},{56,120},{... | collective-permute-start | bytes 98312 | tf_op jit(solution)/shard_map/ppermute | solution.py:152
  48.9 7.0 %collective-permute-start.11 = (f32[16,512]{1,0:T(8,128)S(1)}, f32[16,512]{1,0:T(8,128)S(1)}, u32[]{:S(2)}, u32[]{:S(2)}) collective-permute-start(f32[16,512]{1,0:T(8,128)S(1)} %add_select_fusion), channel_id=1, source_target_pairs={{0,192},{8,200},{16,208},{24,216},{32,224},{40,232},{48,240},{56,2... | collective-permute-start | bytes 98312 | tf_op jit(solution)/shard_map/ppermute | solution.py:152
  50.2 0.8 %copy-start.1 = (f32[16,512]{1,0:T(8,128)S(1)}, f32[16,512]{1,0:T(8,128)}, u32[]{:S(2)}) copy-start(f32[16,512]{1,0:T(8,128)} %residues_ref.1) | copy-start | bytes 98308
  50.3 0.7 %copy-start.3 = (f32[512]{0:T(512)S(1)}, f32[512]{0:T(512)}, u32[]{:S(2)}) copy-start(f32[512]{0:T(512)} %param.9) | copy-start | bytes 6148

commit v2 on v1

v2 whole, which is shorter than its diff:
```python
import jax
import jax.numpy as jnp
from jax import lax
from jax.experimental import pallas as pl
from jax.experimental.pallas import tpu as pltpu
from jax.sharding import PartitionSpec as P

LENGTH = 4096
SUB = 16
SHIFTS = (4, 3, 5, 2, 6, 1, 7)
LANES = 128
VMEM = pl.BlockSpec(memory_space=pltpu.VMEM)


def row_iota():
    return lax.broadcasted_iota(jnp.int32, (8, LANES), 0)


def spread(row):
    return jnp.broadcast_to(row, (8, LANES))


def gather_kernel(streams_ref, out_ref, sems):
    count, _, channels = out_ref.shape
    copies = [
        pltpu.make_async_copy(
            streams_ref.at[s, :, pl.ds(d * channels, channels)],
            out_ref.at[d, pl.ds(s * SUB, SUB), :],
            sems.at[d * 3 + s],
        )
        for d in range(count)
        for s in range(3)
    ]
    for copy in copies:
        copy.start()
    for copy in copies:
        copy.wait()


def fill_tokens(blocks_ref, stream, scratch):
    for source in range(blocks_ref.shape[0]):
        for group in range(scratch.shape[0]):
            lanes = pl.ds(group * LANES, LANES)
            rows = blocks_ref[source, pl.ds(stream * SUB, SUB), lanes]
            scratch[group, pl.ds(source * SUB, SUB), :] = rows.astype(jnp.float32)


def featurize(scratch, stream, lanes, taps_ref, halo_ref):
    group = lanes.start // LANES
    values = [scratch[group, pl.ds(i, 8, stride=SUB), :] for i in range(SUB)]
    first = row_iota() == 0
    back = []
    for far in (2, 1):
        moved = pltpu.roll(values[SUB - far], 1, 0)
        if halo_ref is not None:
            halo = halo_ref[stream, 2 - far : 3 - far, lanes].astype(jnp.float32)
            moved = jnp.where(first, spread(halo), moved)
        back.append(moved)
    joined = back + values
    t0, t1, t2 = (spread(taps_ref[j, stream : stream + 1, lanes]) for j in range(3))
    return [t0 * joined[i + 2] + t1 * joined[i + 1] + t2 * joined[i] for i in range(SUB)]


def state_kernel(blocks_ref, taps_ref, rates_ref, residues_ref, bias_ref, state_ref, ends_ref, signal_ref, one, two):
    del residues_ref, bias_ref
    modes, channels = rates_ref.shape
    fill_tokens(blocks_ref, 1, one)
    fill_tokens(blocks_ref, 2, two)
    rows = row_iota()
    step = rows.astype(jnp.float32)
    remaining = (7.0 - step) * (SUB / LENGTH)
    for start in range(0, channels, LANES):
        lanes = pl.ds(start, LANES)
        left = featurize(one, 1, lanes, taps_ref, None)
        right = featurize(two, 2, lanes, taps_ref, None)
        signal = [a * b for a, b in zip(left, right)]
        for i in range(2):
            signal[i] = jnp.where(rows == 0, 0.0, signal[i])
        for i in range(SUB):
            signal_ref[i, :, lanes] = signal[i]
        for mode in range(modes):
            rate = spread(rates_ref[mode : mode + 1, lanes])
            decay = jnp.exp(rate * (-1.0 / LENGTH))
            state = signal[0]
            for i in range(1, SUB):
                state = state * decay + signal[i]
            ends_ref[mode, :, lanes] = state
            weight = jnp.exp(-rate * remaining)
            state_ref[mode : mode + 1, lanes] = jnp.sum(state * weight, axis=0, keepdims=True)


def local_kernel(
    blocks_ref, halo_ref, edge_ref, taps_ref, rates_ref, residues_ref, bias_ref, ends_ref, signal_ref, local_ref, front_ref, zero
):
    modes, channels = rates_ref.shape
    fill_tokens(blocks_ref, 0, zero)
    rows = row_iota()
    step = rows.astype(jnp.float32)
    for start in range(0, channels, LANES):
        lanes = pl.ds(start, LANES)
        front = featurize(zero, 0, lanes, taps_ref, halo_ref)
        for i in range(SUB):
            front_ref[i, :, lanes] = front[i]
        signal = [signal_ref[i, :, lanes] for i in range(SUB)]
        edge = [jnp.where(rows == 0, spread(edge_ref[i : i + 1, lanes]), 0.0) for i in range(2)]
        for i in range(2):
            signal[i] = signal[i] + edge[i]
        taps = [jnp.zeros((8, LANES), jnp.float32) for _ in range(SUB // 8)]
        for mode in range(modes):
            rate = spread(rates_ref[mode : mode + 1, lanes])
            residue = spread(residues_ref[mode : mode + 1, lanes])
            for part in range(SUB // 8):
                taps[part] = taps[part] + residue * jnp.exp(-rate * ((step + 8.0 * part) * (1.0 / LENGTH)))
        bias = spread(bias_ref[0:1, lanes])
        total = [bias * signal[i] for i in range(SUB)]
        for lag in range(SUB):
            tap = spread(taps[lag // 8][lag % 8 : lag % 8 + 1])
            for i in range(lag, SUB):
                total[i] = total[i] + tap * signal[i - lag]
        for mode in range(modes):
            rate = spread(rates_ref[mode : mode + 1, lanes])
            residue = spread(residues_ref[mode : mode + 1, lanes])
            decay = jnp.exp(rate * (-1.0 / LENGTH))
            state = ends_ref[mode, :, lanes] + jnp.exp(rate * (-14.0 / LENGTH)) * (decay * edge[0] + edge[1])
            for far in (1, 2, 4):
                power = jnp.exp(rate * (-far * SUB / LENGTH))
                state = state + jnp.where(rows >= far, power * pltpu.roll(state, far, 0), 0.0)
            carried = jnp.where(rows >= 1, pltpu.roll(state, 1, 0), 0.0) * residue
            for i in range(SUB):
                carried = carried * decay
                total[i] = total[i] + carried
        for i in range(SUB):
            local_ref[i, :, lanes] = total[i]


def final_kernel(mine_ref, other_ref, rates_ref, residues_ref, local_ref, front_ref, out_ref, natural):
    modes, channels = rates_ref.shape
    step = row_iota().astype(jnp.float32)
    core = lax.rem(lax.axis_index("ctx"), 2)
    half = channels // 2
    for start in range(0, channels, LANES):
        lanes = pl.ds(start, LANES)
        within = pl.ds(start % half, LANES)
        own = core == start // half
        total = [local_ref[i, :, lanes] for i in range(SUB)]
        for mode in range(modes):
            rate = spread(rates_ref[mode : mode + 1, lanes])
            decay = jnp.exp(rate * (-1.0 / LENGTH))
            carry = jnp.where(own, mine_ref[mode : mode + 1, within], other_ref[mode : mode + 1, within])
            first = residues_ref[mode : mode + 1, lanes] * carry
            carried = spread(first) * jnp.exp(-rate * ((step * SUB + 1.0) * (1.0 / LENGTH)))
            total[0] = total[0] + carried
            for i in range(1, SUB):
                carried = carried * decay
                total[i] = total[i] + carried
        for i in range(SUB):
            natural[start // LANES, pl.ds(i, 8, stride=SUB), :] = front_ref[i, :, lanes] * total[i]
        out_ref[:, lanes] = natural[start // LANES].astype(out_ref.dtype)


def scan_states(state, rates):
    index = lax.axis_index("ctx")
    blocks = lax.axis_size("ctx")
    chips = blocks // 2
    chip, core = index // 2, index % 2
    modes, channels = state.shape
    half = channels // 2
    swap = [(i, i ^ 1) for i in range(blocks)]

    def power(rate, count):
        return jnp.exp(rate * (-jnp.asarray(count, jnp.float32) / blocks))

    def pick(value, which):
        return jnp.where(which == 0, value[:, :half], value[:, half:])

    rate = pick(rates, core)
    got = lax.ppermute(pick(state, 1 - core), "ctx", swap)
    kept = pick(state, core)
    lower = jnp.where(core == 0, kept, got)
    upper = jnp.where(core == 0, got, kept)
    pair = upper + power(rate, 1) * lower
    groups = [[2 * k + c for k in range(chips)] for c in range(2)]
    every = lax.all_to_all(
        jnp.broadcast_to(pair[None], (chips, modes, half)), "ctx", 0, 0, axis_index_groups=groups, tiled=True
    )
    before = jnp.zeros_like(pair)
    for k in range(chips - 1):
        ahead = jnp.maximum(chip - 1 - k, 0)
        before = before + jnp.where(k < chip, power(rate, 2 * ahead), 0.0) * every[k]
    after = power(rate, 1) * before + lower
    mine = jnp.where(core == 0, before, after)
    return mine, lax.ppermute(jnp.where(core == 0, after, before), "ctx", swap)


def body(streams, short_taps, residues, rates, bias):
    parts = lax.axis_size("tp")
    ctx = lax.axis_size("ctx")
    modes, channels = rates.shape
    tokens = SUB * parts
    f32 = jnp.float32
    limit = pltpu.CompilerParams(vmem_limit_bytes=24 << 20)
    outgoing = pl.pallas_call(
        gather_kernel,
        out_shape=jax.ShapeDtypeStruct((parts, 3 * SUB, channels), streams.dtype),
        in_specs=[pl.BlockSpec(memory_space=pl.ANY)],
        out_specs=VMEM,
        scratch_shapes=[pltpu.SemaphoreType.DMA((3 * parts,))],
        compiler_params=limit,
        name="gather",
    )(jnp.transpose(streams, (1, 0, 2)))
    blocks = lax.all_to_all(outgoing, "tp", 0, 0, tiled=True)
    ends_of = [slice(s * SUB + SUB - 2, s * SUB + SUB) for s in range(3)]
    tail = jnp.stack([blocks[parts - 1, rows] for rows in ends_of])
    halo = lax.ppermute(tail, "ctx", [(i, i + 1) for i in range(ctx - 1)])
    wide = jax.ShapeDtypeStruct((SUB, parts, channels), f32)
    state, ends, signal = pl.pallas_call(
        state_kernel,
        out_shape=(
            jax.ShapeDtypeStruct((modes, channels), f32),
            jax.ShapeDtypeStruct((modes, parts, channels), f32),
            wide,
        ),
        in_specs=[VMEM] * 5,
        out_specs=(VMEM,) * 3,
        scratch_shapes=[pltpu.VMEM((channels // LANES, tokens, LANES), f32)] * 2,
        compiler_params=limit,
        cost_estimate=pl.CostEstimate(flops=8 << 20, bytes_accessed=2 << 20, transcendentals=0),
        name="state",
    )(blocks, short_taps, rates, residues, bias[None])
    edge = None
    for s in (1, 2):
        x = [blocks[0, s * SUB + i].astype(f32) for i in range(2)]
        h = [halo[s, i].astype(f32) for i in range(2)]
        t0, t1, t2 = (short_taps[j, s] for j in range(3))
        feat = jnp.stack([t0 * x[0] + t1 * h[1] + t2 * h[0], t0 * x[1] + t1 * x[0] + t2 * h[1]])
        edge = feat if edge is None else edge * feat
    state = state + jnp.exp(rates * (-(tokens - 2.0) / LENGTH)) * (jnp.exp(rates * (-1.0 / LENGTH)) * edge[0] + edge[1])
    mine, other = scan_states(state, rates)
    local, front = pl.pallas_call(
        local_kernel,
        out_shape=(wide, wide),
        in_specs=[VMEM] * 9,
        out_specs=(VMEM,) * 2,
        scratch_shapes=[pltpu.VMEM((channels // LANES, tokens, LANES), f32)],
        compiler_params=limit,
        cost_estimate=pl.CostEstimate(flops=8 << 20, bytes_accessed=2 << 20, transcendentals=0),
        name="local",
    )(blocks, halo, edge, short_taps, rates, residues, bias[None], ends, signal)
    return pl.pallas_call(
        final_kernel,
        out_shape=jax.ShapeDtypeStruct((tokens, channels), jnp.bfloat16),
        in_specs=[VMEM] * 6,
        out_specs=VMEM,
        scratch_shapes=[pltpu.VMEM((channels // LANES, tokens, LANES), f32)],
        compiler_params=limit,
        name="final",
    )(mine, other, rates, residues, local, front)


def solution(mesh):
    in_specs = (
        P(("ctx", "tp"), None, None),
        P(None, None, "tp"),
        P(None, "tp"),
        P(None, "tp"),
        P("tp"),
    )
    out_specs = P("ctx", "tp")
    return jax.shard_map(body, mesh=mesh, in_specs=in_specs, out_specs=out_specs, check_vma=False)
```

time: 57.4 us -> 51.6 us (0.90)
  the two profiles are of different devices: /device:TPU:24 before, /device:TPU:1 now
where the time goes in v2:
time: 51.6 us; the launch traced here: 51.3 us
  blocking collectives  22.3 us (43%)
  starting transfers between devices  14.4 us (28%)
  waiting for transfers between devices  9.16 us (18%)
  Pallas kernels  3.11 us (6%)
  local copies, waits for them, and re-layouts  1.76 us (3%)
    all_to_all x1, blocking collectives, body(): blocks = lax.all_to_all(outgoing, 'tp', 0, 0, tiled=True)  22.3 us
    all_to_all x1, starting transfers between devices, scan_states(): lax.all_to_all(jnp.broadcast_to(pair[None], (chips, modes, half)), 'ctx',...  7.59 us
    all_to_all x1, waiting for transfers between devices, scan_states(): lax.all_to_all(jnp.broadcast_to(pair[None], (chips, modes, half)), 'ctx',...  7.08 us
    ppermute x1, starting transfers between devices, body(): halo = lax.ppermute(tail, 'ctx', [(i, i + 1) for i in range(ctx - 1)])  5.13 us
    ppermute x1, starting transfers between devices, scan_states(): lax.ppermute(jnp.where(core == 0, after, before), 'ctx', swap)  1.58 us
    ppermute x1, waiting for transfers between devices, scan_states(): got = lax.ppermute(pick(state, 1 - core), 'ctx', swap)  1.17 us
    pallas_call x1, Pallas kernels, body(): pl.pallas_call(final_kernel, out_shape=jax.ShapeDtypeStruct((tokens, chan...  1.08 us
  transfers between devices with their start and end apart: 4, of which 4 were waited for; matrix products, arithmetic and copies ran while one was open for 0% of the time, Pallas kernels for 3%

profile of v2, /device:TPU:1, one launch (start us, length us, event | category | flops | bytes accessed | tf_op | source)
XLA Modules:
  0.0 51.3 jit_solution(13457448639491687470)
XLA Ops:
  0.0 0.0 copy-start.1
  0.0 1.0 %copy-done.1 = bf16[16,3,4096]{2,0,1:T(8,128)(2,1)S(1)} copy-done((bf16[16,3,4096]{2,0,1:T(8,128)(2,1)S(1)}, bf16[16,3,4096]{2,0,1:T(8,128)(2,1)}, u32[]{:S(2)}) %copy-start.1) | copy-done | bytes 393240
  1.0 0.5 gather.1
  1.5 0.0 copy-start.3
  1.5 0.0 copy-start.4
  1.5 22.3 %all_to_all.10.blocks_ref = bf16[8,48,512]{2,1,0:T(8,128)(2,1)S(1)} all-to-all(bf16[8,48,512]{2,1,0:T(8,128)(2,1)S(1)} %gather.1), channel_id=1, replica_groups=mesh['ctx'=32,'tp'=8] {'tp'}, dimensions={0} | all-to-all | bytes 786432 | tf_op jit(solution)/shard_map/all_to_all | solution.py:211
  23.9 0.0 copy-start
  23.9 0.0 copy-start.2
  23.9 5.1 %collective-permute-start = (bf16[3,2,512]{2,1,0:T(2,128)(2,1)S(1)}, bf16[3,2,512]{2,1,0:T(2,128)(2,1)S(1)}, u32[]{:S(2)}, u32[]{:S(2)}) collective-permute-start(bf16[3,2,512]{2,1,0:T(2,128)(2,1)S(1)} %pad_maximum_fusion), channel_id=1, source_target_pairs={{0,8},{8,16},{16,24},{24,32},{32,40},{40,48},{48,56},{56,64},{64,7... | collective-permute-start | bytes 18440 | tf_op jit(solution)/shard_map/ppermute | solution.py:214
  29.0 0.0 copy-done.3
  29.1 0.0 copy-done.4
  29.1 0.0 copy-done
  29.1 0.0 copy-done.2
  29.1 0.6 %state.1 = (f32[16,512]{1,0:T(8,128)S(1)}, f32[16,8,512]{2,1,0:T(8,128)S(1)}, f32[16,8,512]{2,1,0:T(8,128)S(1)}) custom-call(bf16[8,48,512]{2,1,0:T(8,128)(2,1)S(1)} %all_to_all.10.blocks_ref, f32[3,3,512]{2,1,0:T(4,128)S(1)} %copy-done.3, f32[16,512]{1,0:T(8,128)S(1)} %copy-done, f32[16,512]{1,0:T(8,128)S(1)} %copy-done.2, f32[1,512]{1,0:T(1,128)S(1)} %bitcast.144), custom_call_target="tpu_custom_call" | custom-call | flops 8388608 | bytes 2097152 | tf_op jit(solution)/shard_map/state/pallas_call | solution.py:216
  29.7 0.1 collective-permute-done.halo_ref
  29.9 0.1 collective-permute-start.1
  30.0 1.2 %collective-permute-done.1 = f32[16,256]{1,0:T(8,128)S(1)} collective-permute-done((f32[16,256]{1,0:T(8,128)S(1)}, f32[16,256]{1,0:T(8,128)S(1)}, u32[]{:S(2)}, u32[]{:S(2)}) %collective-permute-start.1) | collective-permute-done | bytes 16416 | tf_op jit(solution)/shard_map/ppermute | solution.py:177
  31.2 0.7 %broadcast_in_dim.30 = f32[16,16,256]{2,1,0:T(8,128)} broadcast(f32[16,256]{1,0:T(8,128)S(1)} %get-tuple-element.17), dimensions={1,2} | broadcast | bytes 278528 | tf_op jit(solution)/shard_map/broadcast_in_dim | solution.py:184
  31.9 7.6 %all-to-all-start.1 = ((f32[16,16,256]{2,1,0:T(8,128)}), f32[16,16,256]{2,1,0:T(8,128)S(1)}, u32[]{:S(2)}, u32[]{:S(2)}) async-start(f32[16,16,256]{2,1,0:T(8,128)} %broadcast_in_dim.30), calls=%async_computation.1 | async-start | bytes 524288 | tf_op jit(solution)/shard_map/all_to_all | solution.py:183
  39.7 0.9 %local.1 = (f32[16,8,512]{2,1,0:T(8,128)S(1)}, f32[16,8,512]{2,1,0:T(8,128)S(1)}) custom-call(bf16[8,48,512]{2,1,0:T(8,128)(2,1)S(1)} %all_to_all.10.blocks_ref, bf16[3,2,512]{2,1,0:T(2,128)(2,1)S(1)} %collective-permute-done.halo_ref, f32[2,512]{1,0:T(2,128)S(1)} %maximum_multiply_fusion.edge_ref, f32[3,3,512]{2,1,0:T(4,128)S(1)} %copy-done.3, ...), custom_call_target="tpu_custom_call" | custom-call | flops 8388608 | bytes 2097152 | tf_op jit(solution)/shard_map/local/pallas_call | solution.py:239
  40.6 7.1 %all-to-all-done.1 = f32[16,16,256]{2,1,0:T(8,128)S(1)} async-done(((f32[16,16,256]{2,1,0:T(8,128)}), f32[16,16,256]{2,1,0:T(8,128)S(1)}, u32[]{:S(2)}, u32[]{:S(2)}) %all-to-all-start.1) | async-done | bytes 262176 | tf_op jit(solution)/shard_map/all_to_all | solution.py:183
  47.7 0.1 fusion.29
  47.8 1.6 %collective-permute-start.2 = (f32[16,256]{1,0:T(8,128)S(1)}, f32[16,256]{1,0:T(8,128)S(1)}, u32[]{:S(2)}, u32[]{:S(2)}) collective-permute-start(f32[16,256]{1,0:T(8,128)S(1)} %get-tuple-element.15), channel_id=1, source_target_pairs={{0,8},{8,0},{16,24},{24,16},{32,40},{40,32},{48,56},{56,48},{64,72... | collective-permute-start | bytes 49160 | tf_op jit(solution)/shard_map/ppermute | solution.py:192
  49.3 0.8 %collective-permute-done.2.other_ref = f32[16,256]{1,0:T(8,128)S(1)} collective-permute-done((f32[16,256]{1,0:T(8,128)S(1)}, f32[16,256]{1,0:T(8,128)S(1)}, u32[]{:S(2)}, u32[]{:S(2)}) %collective-permute-start.2) | collective-permute-done | bytes 16416 | tf_op jit(solution)/shard_map/ppermute | solution.py:192
  50.2 1.1 %final.1 = bf16[128,512]{1,0:T(8,128)(2,1)} custom-call(f32[16,256]{1,0:T(8,128)S(1)} %fusion.30.mine_ref, f32[16,256]{1,0:T(8,128)S(1)} %collective-permute-done.2.other_ref, f32[16,512]{1,0:T(8,128)S(1)} %copy-done, f32[16,512]{1,0:T(8,128)S(1)} %copy-done.2, f32[16,8,512]{2,1,0:T(8,128)S(1)} %get-tuple-element.13.local_ref, ...), custom_call_target="tpu_custom_call" | custom-call | tf_op jit(solution)/shard_map/final/pallas_call | solution.py:249
  (10 shorter events, 0.1 us)
Async XLA Ops:
  0.0 1.0 %copy-start.1 = (bf16[16,3,4096]{2,0,1:T(8,128)(2,1)S(1)}, bf16[16,3,4096]{2,0,1:T(8,128)(2,1)}, u32[]{:S(2)}) copy-start(bf16[16,3,4096]{2,0,1:T(8,128)(2,1)} %param.5) | copy-start | bytes 1179652
  1.5 27.5 %copy-start.3 = (f32[3,3,512]{2,1,0:T(4,128)S(1)}, f32[3,3,512]{2,1,0:T(4,128)}, u32[]{:S(2)}) copy-start(f32[3,3,512]{2,1,0:T(4,128)} %taps_ref.3) | copy-start | bytes 55300
  1.5 27.5 %copy-start.4 = (f32[512]{0:T(512)S(1)}, f32[512]{0:T(512)}, u32[]{:S(2)}) copy-start(f32[512]{0:T(512)} %param.9) | copy-start | bytes 6148
  23.9 5.2 %copy-start = (f32[16,512]{1,0:T(8,128)S(1)}, f32[16,512]{1,0:T(8,128)}, u32[]{:S(2)}) copy-start(f32[16,512]{1,0:T(8,128)} %rates_ref.5) | copy-start | bytes 98308
  23.9 5.2 %copy-start.2 = (f32[16,512]{1,0:T(8,128)S(1)}, f32[16,512]{1,0:T(8,128)}, u32[]{:S(2)}) copy-start(f32[16,512]{1,0:T(8,128)} %residues_ref.5) | copy-start | bytes 98308
  23.9 5.9 %collective-permute-start = (bf16[3,2,512]{2,1,0:T(2,128)(2,1)S(1)}, bf16[3,2,512]{2,1,0:T(2,128)(2,1)S(1)}, u32[]{:S(2)}, u32[]{:S(2)}) collective-permute-start(bf16[3,2,512]{2,1,0:T(2,128)(2,1)S(1)} %pad_maximum_fusion), channel_id=1, source_target_pairs={{0,8},{8,16},{16,24},{24,32},{32,40},{40,48},{48,56},{56,64},{64,7... | collective-permute-start | bytes 18440 | tf_op jit(solution)/shard_map/ppermute | solution.py:214
  29.9 1.3 %collective-permute-start.1 = (f32[16,256]{1,0:T(8,128)S(1)}, f32[16,256]{1,0:T(8,128)S(1)}, u32[]{:S(2)}, u32[]{:S(2)}) collective-permute-start(f32[16,256]{1,0:T(8,128)S(1)} %slice_select_fusion.2), channel_id=1, source_target_pairs={{0,8},{8,0},{16,24},{24,16},{32,40},{40,32},{48,56},{56,48},{64,72... | collective-permute-start | bytes 49160 | tf_op jit(solution)/shard_map/ppermute | solution.py:177
  31.9 15.7 %all-to-all-start.1 = ((f32[16,16,256]{2,1,0:T(8,128)}), f32[16,16,256]{2,1,0:T(8,128)S(1)}, u32[]{:S(2)}, u32[]{:S(2)}) async-start(f32[16,16,256]{2,1,0:T(8,128)} %broadcast_in_dim.30), calls=%async_computation.1 | async-start | bytes 524288 | tf_op jit(solution)/shard_map/all_to_all | solution.py:183
  47.8 2.4 %collective-permute-start.2 = (f32[16,256]{1,0:T(8,128)S(1)}, f32[16,256]{1,0:T(8,128)S(1)}, u32[]{:S(2)}, u32[]{:S(2)}) collective-permute-start(f32[16,256]{1,0:T(8,128)S(1)} %get-tuple-element.15), channel_id=1, source_target_pairs={{0,8},{8,0},{16,24},{24,16},{32,40},{40,32},{48,56},{56,48},{64,72... | collective-permute-start | bytes 49160 | tf_op jit(solution)/shard_map/ppermute | solution.py:192

commit v3 on v2

v3 whole, which is shorter than its diff:
```python
import jax
import jax.numpy as jnp
from jax import lax
from jax.experimental import pallas as pl
from jax.experimental.pallas import tpu as pltpu
from jax.sharding import PartitionSpec as P

LENGTH = 4096
SUB = 16
SHIFTS = (4, 3, 5, 2, 6, 1, 7)
LANES = 128
BLOCK = 128
CHIPS = 16
VMEM = pl.BlockSpec(memory_space=pltpu.VMEM)


def row_iota():
    return lax.broadcasted_iota(jnp.int32, (8, LANES), 0)


def spread(row):
    return jnp.broadcast_to(row, (8, LANES))


def gather_kernel(streams_ref, out_ref, sems):
    count, _, channels = out_ref.shape
    copies = [
        pltpu.make_async_copy(
            streams_ref.at[s, :, pl.ds(d * channels, channels)],
            out_ref.at[d, pl.ds(s * SUB, SUB), :],
            sems.at[d * 3 + s],
        )
        for d in range(count)
        for s in range(3)
    ]
    for copy in copies:
        copy.start()
    for copy in copies:
        copy.wait()


def fill_tokens(blocks_ref, stream, scratch):
    for source in range(blocks_ref.shape[0]):
        for group in range(scratch.shape[0]):
            lanes = pl.ds(group * LANES, LANES)
            rows = blocks_ref[source, pl.ds(stream * SUB, SUB), lanes]
            scratch[group, pl.ds(source * SUB, SUB), :] = rows.astype(jnp.float32)


def featurize(scratch, stream, lanes, taps_ref):
    group = lanes.start // LANES
    values = [scratch[group, pl.ds(i, 8, stride=SUB), :] for i in range(SUB)]
    first = row_iota() == 0
    joined = [jnp.where(first, 0.0, pltpu.roll(values[SUB - far], 1, 0)) for far in (2, 1)] + values
    t0, t1, t2 = (spread(taps_ref[j, stream : stream + 1, lanes]) for j in range(3))
    return [t0 * joined[i + 2] + t1 * joined[i + 1] + t2 * joined[i] for i in range(SUB)]


def power(rate, tokens):
    return jnp.exp(rate * (-float(tokens) / LENGTH))


def core_index():
    return lax.rem(lax.axis_index("ctx"), 2)


def half_of(value, which):
    half = value.shape[-1] // 2
    return jnp.where(which == 0, value[:, :half], value[:, half:])


TAIL = 4


def edge_signal(tail, head, taps):
    result = None
    for n, (t0, t1, t2) in enumerate(taps):
        x0, x1 = (head[2 * n + i : 2 * n + i + 1] for i in range(2))
        h0, h1 = (tail[2 * n + i : 2 * n + i + 1] for i in range(2))
        feats = (t0 * x0 + t1 * h1 + t2 * h0, t0 * x1 + t1 * x0 + t2 * h1)
        result = feats if result is None else tuple(a * b for a, b in zip(result, feats))
    return result


def half_taps(taps_ref, core):
    return [[half_of(taps_ref[j, s : s + 1, :], core) for j in range(3)] for s in (1, 2)]


def state_kernel(
    blocks_ref, taps_ref, rates_ref, residues_ref, bias_ref, kept_ref, sent_ref, ends_ref, signal_ref, one, two, full
):
    del residues_ref, bias_ref
    modes, channels = rates_ref.shape
    fill_tokens(blocks_ref, 1, one)
    fill_tokens(blocks_ref, 2, two)
    rows = row_iota()
    step = rows.astype(jnp.float32)
    remaining = (7.0 - step) * (SUB / LENGTH)
    full[modes:, :] = jnp.zeros((SUB, channels), jnp.float32)
    for n, s in enumerate((1, 2)):
        full[modes + 2 * n : modes + 2 * n + 2, :] = blocks_ref[0, s * SUB : (s + 1) * SUB, :].astype(jnp.float32)[:2]
    for n, s in enumerate((1, 2, 0)):
        at = modes + TAIL + 2 * n
        full[at : at + 2, :] = blocks_ref[7, s * SUB : (s + 1) * SUB, :].astype(jnp.float32)[SUB - 2 :]
    for start in range(0, channels, LANES):
        lanes = pl.ds(start, LANES)
        left = featurize(one, 1, lanes, taps_ref)
        right = featurize(two, 2, lanes, taps_ref)
        signal = [a * b for a, b in zip(left, right)]
        for i in range(2):
            signal[i] = jnp.where(rows == 0, 0.0, signal[i])
        for i in range(SUB):
            signal_ref[i, :, lanes] = signal[i]
        for mode in range(modes):
            rate = spread(rates_ref[mode : mode + 1, lanes])
            decay = jnp.exp(rate * (-1.0 / LENGTH))
            state = signal[0]
            for i in range(1, SUB):
                state = state * decay + signal[i]
            ends_ref[mode, :, lanes] = state
            weight = jnp.exp(-rate * remaining)
            full[mode : mode + 1, lanes] = jnp.sum(state * weight, axis=0, keepdims=True)
    core = core_index()
    kept_ref[...] = half_of(full[...], core)
    sent_ref[...] = half_of(full[...], 1 - core)


def pair_kernel(kept_ref, got_ref, rates_ref, taps_ref, out_ref, lower_ref):
    modes = rates_ref.shape[0]
    core = core_index()
    rate = half_of(rates_ref[...], core)
    kept, got = kept_ref[...], got_ref[...]
    lower = jnp.where(core == 0, kept, got)
    upper = jnp.where(core == 0, got, kept)
    low_edge, high_edge = lower[modes:], upper[modes:]
    s0, s1 = edge_signal(low_edge[TAIL:], high_edge, half_taps(taps_ref, core))
    inner = power(rate, BLOCK - 2) * (power(rate, 1) * s0 + s1)
    state = upper[:modes] + inner + power(rate, BLOCK) * lower[:modes]
    rows = lax.broadcasted_iota(jnp.int32, low_edge.shape, 0)
    edge = jnp.where(rows < TAIL, low_edge, high_edge).astype(jnp.bfloat16)
    high = state.astype(jnp.bfloat16)
    rest = (state - high.astype(jnp.float32)).astype(jnp.bfloat16)
    for chip in range(CHIPS):
        out_ref[chip, 0:SUB, :] = high
        out_ref[chip, SUB : 2 * SUB, :] = rest
        out_ref[chip, 2 * SUB : 3 * SUB, :] = edge
    lower_ref[...] = lower


def merge_kernel(every_ref, lower_ref, rates_ref, taps_ref, mine_ref, other_ref):
    modes = rates_ref.shape[0]
    core = core_index()
    chip = lax.div(lax.axis_index("ctx"), 2)
    rate = half_of(rates_ref[...], core)
    taps = half_taps(taps_ref, core)
    single, pair = power(rate, 1), power(rate, 2 * BLOCK)
    last = power(rate, 2 * BLOCK - 2)
    carry = jnp.zeros_like(rate)
    before = jnp.zeros_like(rate)
    halo = jnp.zeros_like(rate)
    first = [jnp.zeros_like(rate[:1])] * 2
    for k in range(CHIPS):
        edge = every_ref[k, 2 * SUB : 3 * SUB, :].astype(jnp.float32)
        pieces = edge_signal(before[TAIL:], edge, taps)
        first = [jnp.where(chip == k, new, old) for new, old in zip(pieces, first)]
        halo = jnp.where(chip == k, before, halo)
        if k < CHIPS - 1:
            state = every_ref[k, 0:SUB, :].astype(jnp.float32) + every_ref[k, SUB : 2 * SUB, :].astype(jnp.float32)
            state = state + last * (single * pieces[0] + pieces[1])
            carry = jnp.where(k < chip, carry * pair + state, carry)
        before = edge
    lower = lower_ref[...]
    inner = power(rate, BLOCK - 2) * (single * first[0] + first[1])
    carries = carry, power(rate, BLOCK) * carry + lower[:modes] + inner
    halos = halo[TAIL : TAIL + 8], lower[modes + TAIL : modes + TAIL + 8]
    for ref, which in ((mine_ref, core), (other_ref, 1 - core)):
        ref[0:modes, :] = jnp.where(which == 0, *carries)
        ref[modes:, :] = jnp.where(which == 0, *halos)


def local_kernel(blocks_ref, taps_ref, rates_ref, residues_ref, bias_ref, ends_ref, signal_ref, local_ref, front_ref, zero):
    modes, channels = rates_ref.shape
    fill_tokens(blocks_ref, 0, zero)
    rows = row_iota()
    step = rows.astype(jnp.float32)
    for start in range(0, channels, LANES):
        lanes = pl.ds(start, LANES)
        front = featurize(zero, 0, lanes, taps_ref)
        for i in range(SUB):
            front_ref[i, :, lanes] = front[i]
        signal = [signal_ref[i, :, lanes] for i in range(SUB)]
        taps = [jnp.zeros((8, LANES), jnp.float32) for _ in range(SUB // 8)]
        for mode in range(modes):
            rate = spread(rates_ref[mode : mode + 1, lanes])
            residue = spread(residues_ref[mode : mode + 1, lanes])
            for part in range(SUB // 8):
                taps[part] = taps[part] + residue * jnp.exp(-rate * ((step + 8.0 * part) * (1.0 / LENGTH)))
        bias = spread(bias_ref[0:1, lanes])
        total = [bias * signal[i] for i in range(SUB)]
        for lag in range(SUB):
            tap = spread(taps[lag // 8][lag % 8 : lag % 8 + 1])
            for i in range(lag, SUB):
                total[i] = total[i] + tap * signal[i - lag]
        for mode in range(modes):
            rate = spread(rates_ref[mode : mode + 1, lanes])
            residue = spread(residues_ref[mode : mode + 1, lanes])
            decay = jnp.exp(rate * (-1.0 / LENGTH))
            state = ends_ref[mode, :, lanes]
            for far in (1, 2, 4):
                state = state + jnp.where(rows >= far, power(rate, far * SUB) * pltpu.roll(state, far, 0), 0.0)
            carried = jnp.where(rows >= 1, pltpu.roll(state, 1, 0), 0.0) * residue
            for i in range(SUB):
                carried = carried * decay
                total[i] = total[i] + carried
        for i in range(SUB):
            local_ref[i, :, lanes] = total[i]


def final_kernel(
    mine_ref, other_ref, blocks_ref, taps_ref, rates_ref, residues_ref, bias_ref, local_ref, front_ref, out_ref, natural
):
    modes, channels = rates_ref.shape
    rows = row_iota()
    step = rows.astype(jnp.float32)
    core = core_index()
    half = channels // 2

    def at_first(row):
        return jnp.where(rows == 0, spread(row), 0.0)

    for start in range(0, channels, LANES):
        lanes = pl.ds(start, LANES)
        within = pl.ds(start % half, LANES)
        got = jnp.where(core == start // half, mine_ref[:, within], other_ref[:, within])
        halo = got[modes:]
        head = [blocks_ref[0, s * SUB : (s + 1) * SUB, lanes].astype(jnp.float32)[:2] for s in (1, 2)]
        taps = [[taps_ref[j, s : s + 1, lanes] for j in range(3)] for s in (1, 2, 0)]
        s0, s1 = edge_signal(halo, jnp.concatenate(head, axis=0), taps[:2])
        _, t1, t2 = taps[2]
        bias = bias_ref[0:1, lanes]
        total = [local_ref[i, :, lanes] for i in range(SUB)]
        front = [front_ref[i, :, lanes] for i in range(SUB)]
        total[0] = total[0] + at_first(bias * s0)
        total[1] = total[1] + at_first(bias * s1)
        front[0] = front[0] + at_first(t1 * halo[5:6] + t2 * halo[4:5])
        front[1] = front[1] + at_first(t2 * halo[5:6])
        for mode in range(modes):
            row = rates_ref[mode : mode + 1, lanes]
            residue = residues_ref[mode : mode + 1, lanes]
            grow = jnp.exp(row * (1.0 / LENGTH))
            rate = spread(row)
            decay = jnp.exp(rate * (-1.0 / LENGTH))
            start_row = spread(residue * (got[mode : mode + 1] + grow * s0))
            later = jnp.where(rows >= 1, spread(residue * (grow * (grow * s1))), 0.0)
            carried = (start_row + later) * jnp.exp(-rate * ((step * SUB + 1.0) * (1.0 / LENGTH)))
            total[0] = total[0] + carried
            carried = carried * decay + at_first(residue * s1)
            total[1] = total[1] + carried
            for i in range(2, SUB):
                carried = carried * decay
                total[i] = total[i] + carried
        for i in range(SUB):
            natural[start // LANES, pl.ds(i, 8, stride=SUB), :] = front[i] * total[i]
        out_ref[:, lanes] = natural[start // LANES].astype(out_ref.dtype)


def body(streams, short_taps, residues, rates, bias):
    parts = lax.axis_size("tp")
    ctx = lax.axis_size("ctx")
    modes, channels = rates.shape
    half = channels // 2
    tokens = SUB * parts
    f32 = jnp.float32
    wide = jax.ShapeDtypeStruct((SUB, parts, channels), f32)
    packed = jax.ShapeDtypeStruct((modes + SUB, half), f32)
    carried = jax.ShapeDtypeStruct((modes + 8, half), f32)
    plane = pltpu.VMEM((channels // LANES, tokens, LANES), f32)
    bias = bias[None]

    def kernel(function, out_shape, operands, scratch=(), cost=None, in_specs=None, limit=24):
        several = isinstance(out_shape, tuple)
        return pl.pallas_call(
            function,
            out_shape=out_shape,
            in_specs=in_specs or [VMEM] * len(operands),
            out_specs=(VMEM,) * len(out_shape) if several else VMEM,
            scratch_shapes=list(scratch),
            compiler_params=pltpu.CompilerParams(vmem_limit_bytes=limit << 20),
            cost_estimate=cost,
            name=function.__name__,
        )(*operands)

    outgoing = kernel(
        gather_kernel,
        jax.ShapeDtypeStruct((parts, 3 * SUB, channels), streams.dtype),
        (jnp.transpose(streams, (1, 0, 2)),),
        [pltpu.SemaphoreType.DMA((3 * parts,))],
        in_specs=[pl.BlockSpec(memory_space=pl.ANY)],
        limit=60,
    )
    blocks = lax.all_to_all(outgoing, "tp", 0, 0, tiled=True)
    kept, sent, ends, signal = kernel(
        state_kernel,
        (packed, packed, jax.ShapeDtypeStruct((modes, parts, channels), f32), wide),
        (blocks, short_taps, rates, residues, bias),
        [plane, plane, pltpu.VMEM((modes + SUB, channels), f32)],
    )
    swap = [(i, i ^ 1) for i in range(ctx)]
    got = lax.ppermute(sent, "ctx", swap)
    every, lower = kernel(
        pair_kernel,
        (jax.ShapeDtypeStruct((CHIPS, 3 * SUB, half), jnp.bfloat16), packed),
        (kept, got, rates, short_taps),
    )
    groups = [[2 * k + c for k in range(CHIPS)] for c in range(2)]
    every = lax.all_to_all(every, "ctx", 0, 0, axis_index_groups=groups, tiled=True)
    mine, other = kernel(merge_kernel, (carried, carried), (every, lower, rates, short_taps))
    other = lax.ppermute(other, "ctx", swap)
    local, front = kernel(
        local_kernel,
        (wide, wide),
        (blocks, short_taps, rates, residues, bias, ends, signal),
        [plane],
        cost=pl.CostEstimate(flops=8 << 20, bytes_accessed=2 << 20, transcendentals=0),
    )
    return kernel(
        final_kernel,
        jax.ShapeDtypeStruct((tokens, channels), jnp.bfloat16),
        (mine, other, blocks, short_taps, rates, residues, bias, local, front),
        [plane],
    )


def solution(mesh):
    in_specs = (
        P(("ctx", "tp"), None, None),
        P(None, None, "tp"),
        P(None, "tp"),
        P(None, "tp"),
        P("tp"),
    )
    out_specs = P("ctx", "tp")
    return jax.shard_map(body, mesh=mesh, in_specs=in_specs, out_specs=out_specs, check_vma=False)
```

time: 51.6 us -> 48.8 us (0.946)
  blocking collectives: 22.3 us -> 38.8 us
  starting transfers between devices: 14.4 us -> 3.79 us
  waiting for transfers between devices: 9.16 us -> 0.86 us
  Pallas kernels: 3.11 us -> 4.92 us
  local copies, waits for them, and re-layouts: 1.76 us -> 0.03 us
    all_to_all x0 -> x1, blocking collectives: none -> 16.1 us  [body(): lax.all_to_all(every, 'ctx', 0, 0, axis_index_groups=groups, tiled=True)]
    all_to_all x1 -> x0, starting transfers between devices: 7.59 us -> none  [scan_states(): lax.all_to_all(jnp.broadcast_to(pair[None], (chips, modes, half)), 'ctx',...]
    all_to_all x1 -> x0, waiting for transfers between devices: 7.08 us -> none  [scan_states(): lax.all_to_all(jnp.broadcast_to(pair[None], (chips, modes, half)), 'ctx',...]
    ppermute x3 -> x2, starting transfers between devices: 6.8 us -> 3.79 us  [the longest x1 2.21 us: body(): got = lax.ppermute(sent, 'ctx', swap)]
    pallas_call x4 -> x6, Pallas kernels: 3.11 us -> 4.92 us  [kernel(): pl.pallas_call(function, out_shape=out_shape, in_specs=in_specs or [VMEM]...]
    ppermute x3 -> x2, waiting for transfers between devices: 2.08 us -> 0.86 us  [the longest x1 0.86 us: body(): got = lax.ppermute(sent, 'ctx', swap)]
    unnamed x10 -> x8, local copies, waits for them, and re-layouts: 1.02 us -> 0.03 us
    broadcast_in_dim x1 -> x0, local copies, waits for them, and re-layouts: 0.72 us -> none  [scan_states(): jnp.broadcast_to(pair[None], (chips, modes, half))]
  transfers between devices with their start and end apart: 4 -> 2, of which waited for: 4 -> 1; matrix products, arithmetic and copies ran while one was open for 0% -> 0% of each run, Pallas kernels for 3% -> 2%
where the time goes in v3:
time: 48.8 us; the launch traced here: 48.4 us
  blocking collectives  38.8 us (80%)
  Pallas kernels  4.92 us (10%)
  starting transfers between devices  3.79 us (8%)
  waiting for transfers between devices  0.86 us (2%)
    all_to_all x1, blocking collectives, body(): blocks = lax.all_to_all(outgoing, 'tp', 0, 0, tiled=True)  22.7 us
    all_to_all x1, blocking collectives, body(): lax.all_to_all(every, 'ctx', 0, 0, axis_index_groups=groups, tiled=True)  16.1 us
    pallas_call x6, Pallas kernels, kernel(): pl.pallas_call(function, out_shape=out_shape, in_specs=in_specs or [VMEM]...  4.92 us
    ppermute x1, starting transfers between devices, body(): got = lax.ppermute(sent, 'ctx', swap)  2.21 us
    ppermute x1, starting transfers between devices, body(): other = lax.ppermute(other, 'ctx', swap)  1.58 us
  transfers between devices with their start and end apart: 2, of which 1 were waited for; matrix products, arithmetic and copies ran while one was open for 0% of the time, Pallas kernels for 2%

profile of v3, /device:TPU:1, one launch (start us, length us, event | category | flops | bytes accessed | tf_op | source)
XLA Modules:
  0.0 48.4 jit_solution(5656284335364250184)
XLA Ops:
  0.0 1.9 %gather_kernel.1 = bf16[8,48,512]{2,1,0:T(8,128)(2,1)} custom-call(bf16[3,16,4096]{2,1,0:T(8,128)(2,1)} %bitcast.5), custom_call_target="tpu_custom_call" | custom-call | tf_op jit(solution)/shard_map/gather_kernel/pallas_call | solution.py:282
  1.9 0.0 copy-start
  1.9 0.0 copy-start.1
  1.9 0.0 copy-start.2
  1.9 0.0 copy-start.3
  1.9 22.7 %all_to_all.10.blocks_ref = bf16[8,48,512]{2,1,0:T(8,128)(2,1)S(1)} all-to-all(bf16[8,48,512]{2,1,0:T(8,128)(2,1)} %gather_kernel.1), channel_id=1, replica_groups=mesh['ctx'=32,'tp'=8] {'tp'}, dimensions={0} | all-to-all | bytes 786432 | tf_op jit(solution)/shard_map/all_to_all | solution.py:301
  24.6 0.0 copy-done
  24.6 0.0 copy-done.1
  24.6 0.0 copy-done.2
  24.6 0.0 copy-done.3
  24.6 0.6 %state_kernel.1 = (f32[32,256]{1,0:T(8,128)S(1)}, f32[32,256]{1,0:T(8,128)S(1)}, f32[16,8,512]{2,1,0:T(8,128)S(1)}, f32[16,8,512]{2,1,0:T(8,128)S(1)}) custom-call(bf16[8,48,512]{2,1,0:T(8,128)(2,1)S(1)} %all_to_all.10.blocks_ref, f32[3,3,512]{2,1,0:T(4,128)S(1)} %copy-done.1, f32[16,512]{1,0:T(8,128)S(1)} %copy-done, f32[16,512]{1,0:T(8,128)S(1)} %copy-done.2, ...), custom_call_target="tpu_custom_call" | custom-call | tf_op jit(solution)/shard_map/state_kernel/pallas_call | solution.py:282
  25.3 2.2 %collective-permute-start = (f32[32,256]{1,0:T(8,128)S(1)}, f32[32,256]{1,0:T(8,128)S(1)}, u32[]{:S(2)}, u32[]{:S(2)}) collective-permute-start(f32[32,256]{1,0:T(8,128)S(1)} %get-tuple-element.16), channel_id=1, source_target_pairs={{0,8},{8,0},{16,24},{24,16},{32,40},{40,32},{48,56},{56,48},{64,72... | collective-permute-start | bytes 98312 | tf_op jit(solution)/shard_map/ppermute | solution.py:309
  27.5 0.9 %collective-permute-done.got_ref = f32[32,256]{1,0:T(8,128)S(1)} collective-permute-done((f32[32,256]{1,0:T(8,128)S(1)}, f32[32,256]{1,0:T(8,128)S(1)}, u32[]{:S(2)}, u32[]{:S(2)}) %collective-permute-start) | collective-permute-done | bytes 32800 | tf_op jit(solution)/shard_map/ppermute | solution.py:309
  28.4 16.1 %all_to_all.11.every_ref = bf16[16,48,256]{2,1,0:T(8,128)(2,1)S(1)} all-to-all(bf16[16,48,256]{2,1,0:T(8,128)(2,1)S(1)} %get-tuple-element.17), channel_id=1, replica_groups={{0,16,32,48,64,80,96,112,128,144,160,176,192,208,224,240},{8,24,40,56,7..., dimensions={0} | all-to-all | bytes 786432 | tf_op jit(solution)/shard_map/all_to_all | solution.py:316
  44.5 0.2 merge_kernel.1
  44.7 1.6 %collective-permute-start.1 = (f32[24,256]{1,0:T(8,128)S(1)}, f32[24,256]{1,0:T(8,128)S(1)}, u32[]{:S(2)}, u32[]{:S(2)}) collective-permute-start(f32[24,256]{1,0:T(8,128)S(1)} %get-tuple-element.20), channel_id=1, source_target_pairs={{0,8},{8,0},{16,24},{24,16},{32,40},{40,32},{48,56},{56,48},{64,72... | collective-permute-start | bytes 73736 | tf_op jit(solution)/shard_map/ppermute | solution.py:318
  46.3 0.9 %local_kernel.1 = (f32[16,8,512]{2,1,0:T(8,128)S(1)}, f32[16,8,512]{2,1,0:T(8,128)S(1)}) custom-call(bf16[8,48,512]{2,1,0:T(8,128)(2,1)S(1)} %all_to_all.10.blocks_ref, f32[3,3,512]{2,1,0:T(4,128)S(1)} %copy-done.1, f32[16,512]{1,0:T(8,128)S(1)} %copy-done, f32[16,512]{1,0:T(8,128)S(1)} %copy-done.2, f32[1,512]{1,0:T(1,128)S(1)} %bitcast.3, ...), custom_call_target="tpu_custom_call" | custom-call | flops 8388608 | bytes 2097152 | tf_op jit(solution)/shard_map/local_kernel/pallas_call | solution.py:282
  47.2 0.0 collective-permute-done.1.other_ref
  47.2 1.3 %final_kernel.1 = bf16[128,512]{1,0:T(8,128)(2,1)} custom-call(f32[24,256]{1,0:T(8,128)S(1)} %get-tuple-element.19.mine_ref, f32[24,256]{1,0:T(8,128)S(1)} %collective-permute-done.1.other_ref, bf16[8,48,512]{2,1,0:T(8,128)(2,1)S(1)} %all_to_all.10.blocks_ref, f32[3,3,512]{2,1,0:T(4,128)S(1)} %copy-done.1, f32[16,512]{1,0:T(8,128)S(1)} %copy-done, ...), custom_call_target="tpu_custom_call" | custom-call | tf_op jit(solution)/shard_map/final_kernel/pallas_call | solution.py:282
  (1 shorter events, 0.0 us)
Async XLA Ops:
  1.9 22.7 %copy-start = (f32[16,512]{1,0:T(8,128)S(1)}, f32[16,512]{1,0:T(8,128)}, u32[]{:S(2)}) copy-start(f32[16,512]{1,0:T(8,128)} %rates_ref.9) | copy-start | bytes 98308
  1.9 22.7 %copy-start.1 = (f32[3,3,512]{2,1,0:T(4,128)S(1)}, f32[3,3,512]{2,1,0:T(4,128)}, u32[]{:S(2)}) copy-start(f32[3,3,512]{2,1,0:T(4,128)} %taps_ref.9) | copy-start | bytes 55300
  1.9 22.7 %copy-start.2 = (f32[16,512]{1,0:T(8,128)S(1)}, f32[16,512]{1,0:T(8,128)}, u32[]{:S(2)}) copy-start(f32[16,512]{1,0:T(8,128)} %residues_ref.5) | copy-start | bytes 98308
  1.9 22.7 %copy-start.3 = (f32[512]{0:T(512)S(1)}, f32[512]{0:T(512)}, u32[]{:S(2)}) copy-start(f32[512]{0:T(512)} %param.9) | copy-start | bytes 6148
  25.3 3.1 %collective-permute-start = (f32[32,256]{1,0:T(8,128)S(1)}, f32[32,256]{1,0:T(8,128)S(1)}, u32[]{:S(2)}, u32[]{:S(2)}) collective-permute-start(f32[32,256]{1,0:T(8,128)S(1)} %get-tuple-element.16), channel_id=1, source_target_pairs={{0,8},{8,0},{16,24},{24,16},{32,40},{40,32},{48,56},{56,48},{64,72... | collective-permute-start | bytes 98312 | tf_op jit(solution)/shard_map/ppermute | solution.py:309
  44.7 2.5 %collective-permute-start.1 = (f32[24,256]{1,0:T(8,128)S(1)}, f32[24,256]{1,0:T(8,128)S(1)}, u32[]{:S(2)}, u32[]{:S(2)}) collective-permute-start(f32[24,256]{1,0:T(8,128)S(1)} %get-tuple-element.20), channel_id=1, source_target_pairs={{0,8},{8,0},{16,24},{24,16},{32,40},{40,32},{48,56},{56,48},{64,72... | collective-permute-start | bytes 73736 | tf_op jit(solution)/shard_map/ppermute | solution.py:318

commit v4 on v3

--- a/solution.py
+++ b/solution.py
@@ -7,10 +7,9 @@
 
 LENGTH = 4096
 SUB = 16
-SHIFTS = (4, 3, 5, 2, 6, 1, 7)
+SHIFTS = (4, 1, 3, 5, 2, 6, 7, 0)
 LANES = 128
 BLOCK = 128
-CHIPS = 16
 VMEM = pl.BlockSpec(memory_space=pltpu.VMEM)
 
 
@@ -22,29 +21,17 @@
     return jnp.broadcast_to(row, (8, LANES))
 
 
-def gather_kernel(streams_ref, out_ref, sems):
-    count, _, channels = out_ref.shape
-    copies = [
-        pltpu.make_async_copy(
-            streams_ref.at[s, :, pl.ds(d * channels, channels)],
-            out_ref.at[d, pl.ds(s * SUB, SUB), :],
-            sems.at[d * 3 + s],
-        )
-        for d in range(count)
-        for s in range(3)
-    ]
-    for copy in copies:
-        copy.start()
-    for copy in copies:
-        copy.wait()
-
-
-def fill_tokens(blocks_ref, stream, scratch):
-    for source in range(blocks_ref.shape[0]):
+def fill_tokens(blocks, stream, scratch):
+    for block, source in blocks:
+        at = pl.multiple_of(source * SUB, SUB)
         for group in range(scratch.shape[0]):
             lanes = pl.ds(group * LANES, LANES)
-            rows = blocks_ref[source, pl.ds(stream * SUB, SUB), lanes]
-            scratch[group, pl.ds(source * SUB, SUB), :] = rows.astype(jnp.float32)
+            scratch[group, pl.ds(at, SUB), :] = block[stream, :, lanes].astype(jnp.float32)
+
+
+def with_sources(refs):
+    me = lax.axis_index("tp")
+    return [(ref, lax.rem(me - shift + 8, 8)) for ref, shift in zip(refs, SHIFTS)]
 
 
 def featurize(scratch, stream, lanes, taps_ref):
@@ -86,22 +73,27 @@
     return [[half_of(taps_ref[j, s : s + 1, :], core) for j in range(3)] for s in (1, 2)]
 
 
-def state_kernel(
-    blocks_ref, taps_ref, rates_ref, residues_ref, bias_ref, kept_ref, sent_ref, ends_ref, signal_ref, one, two, full
-):
-    del residues_ref, bias_ref
+def state_kernel(*refs):
+    blocks = with_sources(refs[: len(SHIFTS)])
+    taps_ref, rates_ref, _, _, kept_ref, sent_ref, edge_ref, ends_ref, signal_ref, one, two, full = refs[len(SHIFTS) :]
     modes, channels = rates_ref.shape
-    fill_tokens(blocks_ref, 1, one)
-    fill_tokens(blocks_ref, 2, two)
+    fill_tokens(blocks, 1, one)
+    fill_tokens(blocks, 2, two)
     rows = row_iota()
     step = rows.astype(jnp.float32)
     remaining = (7.0 - step) * (SUB / LENGTH)
     full[modes:, :] = jnp.zeros((SUB, channels), jnp.float32)
-    for n, s in enumerate((1, 2)):
-        full[modes + 2 * n : modes + 2 * n + 2, :] = blocks_ref[0, s * SUB : (s + 1) * SUB, :].astype(jnp.float32)[:2]
-    for n, s in enumerate((1, 2, 0)):
-        at = modes + TAIL + 2 * n
-        full[at : at + 2, :] = blocks_ref[7, s * SUB : (s + 1) * SUB, :].astype(jnp.float32)[SUB - 2 :]
+    for group in range(channels // LANES):
+        lanes = pl.ds(group * LANES, LANES)
+        for n, scratch in enumerate((one, two)):
+            full[modes + 2 * n : modes + 2 * n + 2, lanes] = scratch[group, 0:2, :]
+            full[modes + TAIL + 2 * n : modes + TAIL + 2 * n + 2, lanes] = scratch[group, BLOCK - 2 : BLOCK, :]
+    for block, source in blocks:
+
+        @pl.when(source == 7)
+        def _(block=block):
+            full[modes + TAIL + 4 : modes + TAIL + 6, :] = block[0].astype(jnp.float32)[SUB - 2 :]
+
     for start in range(0, channels, LANES):
         lanes = pl.ds(start, LANES)
         left = featurize(one, 1, lanes, taps_ref)
@@ -120,9 +112,22 @@
             ends_ref[mode, :, lanes] = state
             weight = jnp.exp(-rate * remaining)
             full[mode : mode + 1, lanes] = jnp.sum(state * weight, axis=0, keepdims=True)
+    edge_ref[...] = full[modes:, :]
     core = core_index()
     kept_ref[...] = half_of(full[...], core)
     sent_ref[...] = half_of(full[...], 1 - core)
+
+
+def pack(state, edge, out_ref):
+    high = state.astype(jnp.bfloat16)
+    out_ref[0:SUB, :] = high
+    out_ref[SUB : 2 * SUB, :] = (state - high.astype(jnp.float32)).astype(jnp.bfloat16)
+    out_ref[2 * SUB : 3 * SUB, :] = edge.astype(jnp.bfloat16)
+
+
+def join_edges(first, last):
+    rows = lax.broadcasted_iota(jnp.int32, first.shape, 0)
+    return jnp.where(rows < TAIL, first, last)
 
 
 def pair_kernel(kept_ref, got_ref, rates_ref, taps_ref, out_ref, lower_ref):
@@ -132,43 +137,75 @@
     kept, got = kept_ref[...], got_ref[...]
     lower = jnp.where(core == 0, kept, got)
     upper = jnp.where(core == 0, got, kept)
-    low_edge, high_edge = lower[modes:], upper[modes:]
-    s0, s1 = edge_signal(low_edge[TAIL:], high_edge, half_taps(taps_ref, core))
+    s0, s1 = edge_signal(lower[modes + TAIL :], upper[modes:], half_taps(taps_ref, core))
     inner = power(rate, BLOCK - 2) * (power(rate, 1) * s0 + s1)
     state = upper[:modes] + inner + power(rate, BLOCK) * lower[:modes]
-    rows = lax.broadcasted_iota(jnp.int32, low_edge.shape, 0)
-    edge = jnp.where(rows < TAIL, low_edge, high_edge).astype(jnp.bfloat16)
-    high = state.astype(jnp.bfloat16)
-    rest = (state - high.astype(jnp.float32)).astype(jnp.bfloat16)
-    for chip in range(CHIPS):
-        out_ref[chip, 0:SUB, :] = high
-        out_ref[chip, SUB : 2 * SUB, :] = rest
-        out_ref[chip, 2 * SUB : 3 * SUB, :] = edge
+    pack(state, join_edges(lower[modes:], upper[modes:]), out_ref)
     lower_ref[...] = lower
 
 
-def merge_kernel(every_ref, lower_ref, rates_ref, taps_ref, mine_ref, other_ref):
+def chain(refs, place, tokens, rate, taps, opened):
+    single, whole, last = power(rate, 1), power(rate, tokens), power(rate, tokens - 2)
+    size = len(refs)
+    carry = halo = before = total = jnp.zeros_like(rate)
+    first = (jnp.zeros_like(rate[:1]),) * 2
+    head = None
+    for k in range(size):
+        piece = refs[0][...]
+        for by in range(1, size):
+            piece = jnp.where(lax.rem(place - k + size, size) == by, refs[by][...], piece)
+        state = piece[0:SUB].astype(jnp.float32) + piece[SUB : 2 * SUB].astype(jnp.float32)
+        edge = piece[2 * SUB :].astype(jnp.float32)
+        pieces = edge_signal(before[TAIL:], edge, taps)
+        carry = jnp.where(place == k, total, carry)
+        halo = jnp.where(place == k, before, halo)
+        first = [jnp.where(place == k, new, old) for new, old in zip(pieces, first)]
+        inner = last * (single * pieces[0] + pieces[1])
+        if k == 0:
+            head = edge
+            total = state + inner if opened else state
+        else:
+            total = total * whole + state + inner
+        before = edge
+    return carry, first, halo, total, join_edges(head, before)
+
+
+def place_of(stride):
+    return lax.rem(lax.div(lax.axis_index("ctx"), stride), 4)
+
+
+def row_kernel(own_ref, one_ref, three_ref, two_ref, rates_ref, taps_ref, out_ref, inside_ref):
     modes = rates_ref.shape[0]
     core = core_index()
-    chip = lax.div(lax.axis_index("ctx"), 2)
     rate = half_of(rates_ref[...], core)
+    refs = (own_ref, one_ref, two_ref, three_ref)
+    carry, first, halo, total, edges = chain(refs, place_of(2), 2 * BLOCK, rate, half_taps(taps_ref, core), False)
+    pack(total, edges, out_ref)
+    inside_ref[0:modes, :] = carry
+    inside_ref[modes : 2 * modes, :] = halo
+    for i in range(2):
+        inside_ref[2 * modes + i : 2 * modes + i + 1, :] = first[i]
+
+
+def merge_kernel(
+    own_ref, one_ref, three_ref, two_ref, inside_ref, lower_ref, rates_ref, taps_ref, mine_ref, other_ref
+):
+    modes = rates_ref.shape[0]
+    core = core_index()
+    column, line = place_of(2), place_of(8)
+    rate = half_of(rates_ref[...], core)
+    refs = (own_ref, one_ref, two_ref, three_ref)
     taps = half_taps(taps_ref, core)
-    single, pair = power(rate, 1), power(rate, 2 * BLOCK)
-    last = power(rate, 2 * BLOCK - 2)
-    carry = jnp.zeros_like(rate)
-    before = jnp.zeros_like(rate)
-    halo = jnp.zeros_like(rate)
-    first = [jnp.zeros_like(rate[:1])] * 2
-    for k in range(CHIPS):
-        edge = every_ref[k, 2 * SUB : 3 * SUB, :].astype(jnp.float32)
-        pieces = edge_signal(before[TAIL:], edge, taps)
-        first = [jnp.where(chip == k, new, old) for new, old in zip(pieces, first)]
-        halo = jnp.where(chip == k, before, halo)
-        if k < CHIPS - 1:
-            state = every_ref[k, 0:SUB, :].astype(jnp.float32) + every_ref[k, SUB : 2 * SUB, :].astype(jnp.float32)
-            state = state + last * (single * pieces[0] + pieces[1])
-            carry = jnp.where(k < chip, carry * pair + state, carry)
-        before = edge
+    single = power(rate, 1)
+    above, first, halo, _, _ = chain(refs, line, 8 * BLOCK, rate, taps, True)
+    steps = (column * (2 * BLOCK)).astype(jnp.float32) * (-1.0 / LENGTH)
+    behind = (column * (2 * BLOCK) - 2).astype(jnp.float32) * (-1.0 / LENGTH)
+    inside = inside_ref[0:modes, :]
+    opened = inside + jnp.exp(rate * behind) * (single * first[0] + first[1])
+    carry = jnp.exp(rate * steps) * above + jnp.where(column > 0, opened, inside)
+    within = [inside_ref[2 * modes + i : 2 * modes + i + 1, :] for i in range(2)]
+    first = [jnp.where(column > 0, a, b) for a, b in zip(within, first)]
+    halo = jnp.where(column > 0, inside_ref[modes : 2 * modes, :], halo)
     lower = lower_ref[...]
     inner = power(rate, BLOCK - 2) * (single * first[0] + first[1])
     carries = carry, power(rate, BLOCK) * carry + lower[:modes] + inner
@@ -178,9 +215,11 @@
         ref[modes:, :] = jnp.where(which == 0, *halos)
 
 
-def local_kernel(blocks_ref, taps_ref, rates_ref, residues_ref, bias_ref, ends_ref, signal_ref, local_ref, front_ref, zero):
+def local_kernel(*refs):
+    blocks = with_sources(refs[: len(SHIFTS)])
+    taps_ref, rates_ref, residues_ref, bias_ref, ends_ref, signal_ref, local_ref, front_ref, zero = refs[len(SHIFTS) :]
     modes, channels = rates_ref.shape
-    fill_tokens(blocks_ref, 0, zero)
+    fill_tokens(blocks, 0, zero)
     rows = row_iota()
     step = rows.astype(jnp.float32)
     for start in range(0, channels, LANES):
@@ -217,7 +256,7 @@
 
 
 def final_kernel(
-    mine_ref, other_ref, blocks_ref, taps_ref, rates_ref, residues_ref, bias_ref, local_ref, front_ref, out_ref, natural
+    mine_ref, other_ref, edge_ref, taps_ref, rates_ref, residues_ref, bias_ref, local_ref, front_ref, out_ref, natural
 ):
     modes, channels = rates_ref.shape
     rows = row_iota()
@@ -233,9 +272,8 @@
         within = pl.ds(start % half, LANES)
         got = jnp.where(core == start // half, mine_ref[:, within], other_ref[:, within])
         halo = got[modes:]
-        head = [blocks_ref[0, s * SUB : (s + 1) * SUB, lanes].astype(jnp.float32)[:2] for s in (1, 2)]
         taps = [[taps_ref[j, s : s + 1, lanes] for j in range(3)] for s in (1, 2, 0)]
-        s0, s1 = edge_signal(halo, jnp.concatenate(head, axis=0), taps[:2])
+        s0, s1 = edge_signal(halo, edge_ref[:, lanes], taps[:2])
         _, t1, t2 = taps[2]
         bias = bias_ref[0:1, lanes]
         total = [local_ref[i, :, lanes] for i in range(SUB)]
@@ -290,43 +328,56 @@
             name=function.__name__,
         )(*operands)
 
-    outgoing = kernel(
-        gather_kernel,
-        jax.ShapeDtypeStruct((parts, 3 * SUB, channels), streams.dtype),
-        (jnp.transpose(streams, (1, 0, 2)),),
-        [pltpu.SemaphoreType.DMA((3 * parts,))],
-        in_specs=[pl.BlockSpec(memory_space=pl.ANY)],
-        limit=60,
-    )
-    blocks = lax.all_to_all(outgoing, "tp", 0, 0, tiled=True)
-    kept, sent, ends, signal = kernel(
+    by_stream = jnp.transpose(streams, (1, 0, 2))
+    blocks = []
+    for shift in SHIFTS:
+        at = ((lax.axis_index("tp") + shift) % parts) * channels
+        block = lax.dynamic_slice(by_stream, (0, 0, at), (3, SUB, channels))
+        blocks.append(lax.ppermute(block, "tp", [(i, (i + shift) % parts) for i in range(parts)]) if shift else block)
+    kept, sent, edges, ends, signal = kernel(
         state_kernel,
-        (packed, packed, jax.ShapeDtypeStruct((modes, parts, channels), f32), wide),
-        (blocks, short_taps, rates, residues, bias),
+        (
+            packed,
+            packed,
+            jax.ShapeDtypeStruct((SUB, channels), f32),
+            jax.ShapeDtypeStruct((modes, parts, channels), f32),
+            wide,
+        ),
+        (*blocks, short_taps, rates, residues, bias),
         [plane, plane, pltpu.VMEM((modes + SUB, channels), f32)],
     )
     swap = [(i, i ^ 1) for i in range(ctx)]
     got = lax.ppermute(sent, "ctx", swap)
-    every, lower = kernel(
-        pair_kernel,
-        (jax.ShapeDtypeStruct((CHIPS, 3 * SUB, half), jnp.bfloat16), packed),
-        (kept, got, rates, short_taps),
-    )
-    groups = [[2 * k + c for k in range(CHIPS)] for c in range(2)]
-    every = lax.all_to_all(every, "ctx", 0, 0, axis_index_groups=groups, tiled=True)
-    mine, other = kernel(merge_kernel, (carried, carried), (every, lower, rates, short_taps))
+    group = jax.ShapeDtypeStruct((3 * SUB, half), jnp.bfloat16)
+
+    def around(value, stride):
+        parts = {}
+        for by in (3, 1, 2):
+            route = [(i, i + ((i // stride + by) % 4 - i // stride % 4) * stride) for i in range(ctx)]
+            parts[by] = lax.ppermute(value, "ctx", route)
+        return parts[1], parts[3], parts[2]
+
+    pair, lower = kernel(pair_kernel, (group, packed), (kept, got, rates, short_taps))
+    row, inside = kernel(
+        row_kernel,
+        (group, jax.ShapeDtypeStruct((2 * modes + 8, half), f32)),
+        (pair, *around(pair, 2), rates, short_taps),
+    )
+    mine, other = kernel(
+        merge_kernel, (carried, carried), (row, *around(row, 8), inside, lower, rates, short_taps)
+    )
     other = lax.ppermute(other, "ctx", swap)
     local, front = kernel(
         local_kernel,
         (wide, wide),
-        (blocks, short_taps, rates, residues, bias, ends, signal),
+        (*blocks, short_taps, rates, residues, bias, ends, signal),
         [plane],
         cost=pl.CostEstimate(flops=8 << 20, bytes_accessed=2 << 20, transcendentals=0),
     )
     return kernel(
         final_kernel,
         jax.ShapeDtypeStruct((tokens, channels), jnp.bfloat16),
-        (mine, other, blocks, short_taps, rates, residues, bias, local, front),
+        (mine, other, edges, short_taps, rates, residues, bias, local, front),
         [plane],
     )
 

time: 48.8 us -> 47.3 us (0.969)
  blocking collectives: 38.8 us -> 0 us
  starting transfers between devices: 3.79 us -> 31.2 us
  waiting for transfers between devices: 0.86 us -> 11.8 us
  Pallas kernels: 4.92 us -> 3.01 us
  local copies, waits for them, and re-layouts: 0.03 us -> 1.04 us
    all_to_all x2 -> x0, blocking collectives: 38.8 us -> none  [the longest x1 22.7 us: body(): blocks = lax.all_to_all(outgoing, 'tp', 0, 0, tiled=True)]
    ppermute x0 -> x13, starting transfers between devices: none -> 24.9 us  [the longest x7 16.1 us: body(): lax.ppermute(block, 'tp', [(i, (i + shift) % parts) for i in range(parts)])]
    ppermute x0 -> x13, waiting for transfers between devices: none -> 10.9 us  [the longest x6 6.48 us: around(): parts[by] = lax.ppermute(value, 'ctx', route)]
    ppermute x1, starting transfers between devices: 1.58 us -> 3.85 us  [body(): other = lax.ppermute(other, 'ctx', swap)]
    pallas_call x6, Pallas kernels: 4.92 us -> 3.01 us  [kernel(): pl.pallas_call(function, out_shape=out_shape, in_specs=in_specs or [VMEM]...]
    dynamic_slice x0 -> x1, local copies, waits for them, and re-layouts: none -> 1.03 us  [body(): block = lax.dynamic_slice(by_stream, (0, 0, at), (3, SUB, channels))]
  transfers between devices with their start and end apart: 2 -> 15, of which waited for: 1 -> 7; matrix products, arithmetic and copies ran while one was open for 0% -> 0% of each run, Pallas kernels for 2% -> 2%
where the time goes in v4:
time: 47.3 us; the launch traced here: 47.1 us
  starting transfers between devices  31.2 us (66%)
  waiting for transfers between devices  11.8 us (25%)
  Pallas kernels  3.01 us (6%)
  local copies, waits for them, and re-layouts  1.04 us (2%)
    ppermute x7, starting transfers between devices, body(): lax.ppermute(block, 'tp', [(i, (i + shift) % parts) for i in range(parts)])  16.1 us
    ppermute x6, starting transfers between devices, around(): parts[by] = lax.ppermute(value, 'ctx', route)  8.76 us
    ppermute x6, waiting for transfers between devices, around(): parts[by] = lax.ppermute(value, 'ctx', route)  6.48 us
    ppermute x7, waiting for transfers between devices, body(): lax.ppermute(block, 'tp', [(i, (i + shift) % parts) for i in range(parts)])  4.43 us
    ppermute x1, starting transfers between devices, body(): other = lax.ppermute(other, 'ctx', swap)  3.85 us
    pallas_call x6, Pallas kernels, kernel(): pl.pallas_call(function, out_shape=out_shape, in_specs=in_specs or [VMEM]...  3.01 us
    ppermute x1, starting transfers between devices, body(): got = lax.ppermute(sent, 'ctx', swap)  2.51 us
    dynamic_slice x1, local copies, waits for them, and re-layouts, body(): block = lax.dynamic_slice(by_stream, (0, 0, at), (3, SUB, channels))  1.03 us
  transfers between devices with their start and end apart: 15, of which 7 were waited for; matrix products, arithmetic and copies ran while one was open for 0% of the time, Pallas kernels for 2%

profile of v4, /device:TPU:1, one launch (start us, length us, event | category | flops | bytes accessed | tf_op | source)
XLA Modules:
  0.0 47.1 jit_solution(1309419087103315429)
XLA Ops:
  0.0 0.0 copy-start
  0.0 0.0 copy-start.1
  0.0 0.0 copy-start.2
  0.0 1.0 %dynamic-slice_bitcast_fusion = (bf16[3,16,512]{2,1,0:T(8,128)(2,1)S(1)}, bf16[3,16,512]{2,1,0:T(8,128)(2,1)S(1)}, bf16[3,16,512]{2,1,0:T(8,128)(2,1)S(1)}, bf16...) fusion(bf16[16,3,4096]{2,0,1:T(8,128)(2,1)} %param.5, ...), kind=kLoop, calls=%fused_computation | loop fusion | bytes 786464 | tf_op jit(solution)/shard_map/dynamic_slice | solution.py:335
  1.0 6.9 %collective-permute-start.5 = (bf16[3,16,512]{2,1,0:T(8,128)(2,1)S(1)}, bf16[3,16,512]{2,1,0:T(8,128)(2,1)S(1)}, u32[]{:S(2)}, u32[]{:S(2)}) collective-permute-start(bf16[3,16,512]{2,1,0:T(8,128)(2,1)S(1)} %get-tuple-element.32), channel_id=1, source_target_pairs={{0,6},{1,7},{2,0},{3,1},{4,2},{5,3},{6,4},{7,5},{8,14},{9,15},{10,... | collective-permute-start | bytes 147464 | tf_op jit(solution)/shard_map/ppermute | solution.py:336
  8.0 0.0 collective-permute-start.4
  8.0 2.8 %collective-permute-start.3 = (bf16[3,16,512]{2,1,0:T(8,128)(2,1)S(1)}, bf16[3,16,512]{2,1,0:T(8,128)(2,1)S(1)}, u32[]{:S(2)}, u32[]{:S(2)}) collective-permute-start(bf16[3,16,512]{2,1,0:T(8,128)(2,1)S(1)} %get-tuple-element.34), channel_id=1, source_target_pairs={{0,5},{1,6},{2,7},{3,0},{4,1},{5,2},{6,3},{7,4},{8,13},{9,14},{10,... | collective-permute-start | bytes 147464 | tf_op jit(solution)/shard_map/ppermute | solution.py:336
  10.8 0.5 collective-permute-start.2
  11.2 1.9 %collective-permute-start.1 = (bf16[3,16,512]{2,1,0:T(8,128)(2,1)S(1)}, bf16[3,16,512]{2,1,0:T(8,128)(2,1)S(1)}, u32[]{:S(2)}, u32[]{:S(2)}) collective-permute-start(bf16[3,16,512]{2,1,0:T(8,128)(2,1)S(1)} %get-tuple-element.36), channel_id=1, source_target_pairs={{0,1},{1,2},{2,3},{3,4},{4,5},{5,6},{6,7},{7,0},{8,9},{9,10},{10,1... | collective-permute-start | bytes 147464 | tf_op jit(solution)/shard_map/ppermute | solution.py:336
  13.2 0.0 collective-permute-done.5.refs_5_
  13.2 3.3 %collective-permute-start = (bf16[3,16,512]{2,1,0:T(8,128)(2,1)S(1)}, bf16[3,16,512]{2,1,0:T(8,128)(2,1)S(1)}, u32[]{:S(2)}, u32[]{:S(2)}) collective-permute-start(bf16[3,16,512]{2,1,0:T(8,128)(2,1)S(1)} %get-tuple-element.37), channel_id=1, source_target_pairs={{0,4},{1,5},{2,6},{3,7},{4,0},{5,1},{6,2},{7,3},{8,12},{9,13},{10,... | collective-permute-start | bytes 147464 | tf_op jit(solution)/shard_map/ppermute | solution.py:336
  16.4 0.0 collective-permute-done.4.refs_4_
  16.4 0.0 copy-start.3
  16.4 0.7 %collective-permute-start.6 = (bf16[3,16,512]{2,1,0:T(8,128)(2,1)S(1)}, bf16[3,16,512]{2,1,0:T(8,128)(2,1)S(1)}, u32[]{:S(2)}, u32[]{:S(2)}) collective-permute-start(bf16[3,16,512]{2,1,0:T(8,128)(2,1)S(1)} %get-tuple-element.38), channel_id=1, source_target_pairs={{0,7},{1,0},{2,1},{3,2},{4,3},{5,4},{6,5},{7,6},{8,15},{9,8},{10,9... | collective-permute-start | bytes 147464 | tf_op jit(solution)/shard_map/ppermute | solution.py:336
  17.2 0.0 collective-permute-done.3.refs_3_
  17.2 0.0 collective-permute-done.2.refs_2_
  17.2 1.5 %collective-permute-done.1.refs_1_ = bf16[3,16,512]{2,1,0:T(8,128)(2,1)S(1)} collective-permute-done((bf16[3,16,512]{2,1,0:T(8,128)(2,1)S(1)}, bf16[3,16,512]{2,1,0:T(8,128)(2,1)S(1)}, u32[]{:S(2)}, u32[]{:S(2)}) %collective-permute-start.1) | collective-permute-done | bytes 49184 | tf_op jit(solution)/shard_map/ppermute | solution.py:336
  18.6 3.0 %collective-permute-done.refs_0_ = bf16[3,16,512]{2,1,0:T(8,128)(2,1)S(1)} collective-permute-done((bf16[3,16,512]{2,1,0:T(8,128)(2,1)S(1)}, bf16[3,16,512]{2,1,0:T(8,128)(2,1)S(1)}, u32[]{:S(2)}, u32[]{:S(2)}) %collective-permute-start) | collective-permute-done | bytes 49184 | tf_op jit(solution)/shard_map/ppermute | solution.py:336
  21.6 0.0 collective-permute-done.6.refs_6_
  21.6 0.0 copy-done
  21.6 0.0 copy-done.1
  21.6 0.0 copy-done.2
  21.6 0.0 copy-done.3
  21.6 0.7 %state_kernel.1 = (f32[32,256]{1,0:T(8,128)S(1)}, f32[32,256]{1,0:T(8,128)S(1)}, f32[16,512]{1,0:T(8,128)S(1)}, f32[16,8,512]{2,1,0:T(8,128)S(1)}, f32[16,8,512]{2,1,0:T(8,128)S(1)}) custom-call(bf16[3,16,512]{2,1,0:T(8,128)(2,1)S(1)} %collective-permute-done.refs_0_, bf16[3,16,512]{2,1,0:T(8,128)(2,1)S(1)} %collective-permute-done.1.refs_1_, ...), custom_call_target="tpu_custom_call" | custom-call | tf_op jit(solution)/shard_map/state_kernel/pallas_call | solution.py:320
  22.3 2.5 %collective-permute-start.7 = (f32[32,256]{1,0:T(8,128)S(1)}, f32[32,256]{1,0:T(8,128)S(1)}, u32[]{:S(2)}, u32[]{:S(2)}) collective-permute-start(f32[32,256]{1,0:T(8,128)S(1)} %get-tuple-element.19), channel_id=1, source_target_pairs={{0,8},{8,0},{16,24},{24,16},{32,40},{40,32},{48,56},{56,48},{64,72... | collective-permute-start | bytes 98312 | tf_op jit(solution)/shard_map/ppermute | solution.py:350
  24.8 0.9 %collective-permute-done.7.got_ref = f32[32,256]{1,0:T(8,128)S(1)} collective-permute-done((f32[32,256]{1,0:T(8,128)S(1)}, f32[32,256]{1,0:T(8,128)S(1)}, u32[]{:S(2)}, u32[]{:S(2)}) %collective-permute-start.7) | collective-permute-done | bytes 32800 | tf_op jit(solution)/shard_map/ppermute | solution.py:350
  25.7 2.8 %collective-permute-start.10 = (bf16[48,256]{1,0:T(8,128)(2,1)S(1)}, bf16[48,256]{1,0:T(8,128)(2,1)S(1)}, u32[]{:S(2)}, u32[]{:S(2)}) collective-permute-start(bf16[48,256]{1,0:T(8,128)(2,1)S(1)} %get-tuple-element.20.own_ref), channel_id=1, source_target_pairs={{0,32},{8,40},{16,48},{24,56},{32,0},{40,8},{48,16},{56,24},{64,96... | collective-permute-start | bytes 73736 | tf_op jit(solution)/shard_map/ppermute | solution.py:357
  28.6 0.9 %collective-permute-start.9 = (bf16[48,256]{1,0:T(8,128)(2,1)S(1)}, bf16[48,256]{1,0:T(8,128)(2,1)S(1)}, u32[]{:S(2)}, u32[]{:S(2)}) collective-permute-start(bf16[48,256]{1,0:T(8,128)(2,1)S(1)} %get-tuple-element.20.own_ref), channel_id=1, source_target_pairs={{0,48},{8,56},{16,0},{24,8},{32,16},{40,24},{48,32},{56,40},{64,11... | collective-permute-start | bytes 73736 | tf_op jit(solution)/shard_map/ppermute | solution.py:357
  29.4 0.6 %collective-permute-start.8 = (bf16[48,256]{1,0:T(8,128)(2,1)S(1)}, bf16[48,256]{1,0:T(8,128)(2,1)S(1)}, u32[]{:S(2)}, u32[]{:S(2)}) collective-permute-start(bf16[48,256]{1,0:T(8,128)(2,1)S(1)} %get-tuple-element.20.own_ref), channel_id=1, source_target_pairs={{0,16},{8,24},{16,32},{24,40},{32,48},{40,56},{48,0},{56,8},{64,80... | collective-permute-start | bytes 73736 | tf_op jit(solution)/shard_map/ppermute | solution.py:357
  30.0 0.0 collective-permute-done.10.two_ref
  30.0 1.2 %collective-permute-done.9.three_ref = bf16[48,256]{1,0:T(8,128)(2,1)S(1)} collective-permute-done((bf16[48,256]{1,0:T(8,128)(2,1)S(1)}, bf16[48,256]{1,0:T(8,128)(2,1)S(1)}, u32[]{:S(2)}, u32[]{:S(2)}) %collective-permute-start.9) | collective-permute-done | bytes 24608 | tf_op jit(solution)/shard_map/ppermute | solution.py:357
  31.2 2.1 %collective-permute-done.8.one_ref = bf16[48,256]{1,0:T(8,128)(2,1)S(1)} collective-permute-done((bf16[48,256]{1,0:T(8,128)(2,1)S(1)}, bf16[48,256]{1,0:T(8,128)(2,1)S(1)}, u32[]{:S(2)}, u32[]{:S(2)}) %collective-permute-start.8) | collective-permute-done | bytes 24608 | tf_op jit(solution)/shard_map/ppermute | solution.py:357
  33.3 0.1 row_kernel.1
  33.4 3.0 %collective-permute-start.13 = (bf16[48,256]{1,0:T(8,128)(2,1)S(1)}, bf16[48,256]{1,0:T(8,128)(2,1)S(1)}, u32[]{:S(2)}, u32[]{:S(2)}) collective-permute-start(bf16[48,256]{1,0:T(8,128)(2,1)S(1)} %get-tuple-element.21.own_ref), channel_id=1, source_target_pairs={{0,128},{8,136},{16,144},{24,152},{32,160},{40,168},{48,176},{56,1... | collective-permute-start | bytes 73736 | tf_op jit(solution)/shard_map/ppermute | solution.py:357
  36.4 0.8 %collective-permute-start.12 = (bf16[48,256]{1,0:T(8,128)(2,1)S(1)}, bf16[48,256]{1,0:T(8,128)(2,1)S(1)}, u32[]{:S(2)}, u32[]{:S(2)}) collective-permute-start(bf16[48,256]{1,0:T(8,128)(2,1)S(1)} %get-tuple-element.21.own_ref), channel_id=1, source_target_pairs={{0,192},{8,200},{16,208},{24,216},{32,224},{40,232},{48,240},{56,2... | collective-permute-start | bytes 73736 | tf_op jit(solution)/shard_map/ppermute | solution.py:357
  37.2 0.7 %collective-permute-start.11 = (bf16[48,256]{1,0:T(8,128)(2,1)S(1)}, bf16[48,256]{1,0:T(8,128)(2,1)S(1)}, u32[]{:S(2)}, u32[]{:S(2)}) collective-permute-start(bf16[48,256]{1,0:T(8,128)(2,1)S(1)} %get-tuple-element.21.own_ref), channel_id=1, source_target_pairs={{0,64},{8,72},{16,80},{24,88},{32,96},{40,104},{48,112},{56,120},{... | collective-permute-start | bytes 73736 | tf_op jit(solution)/shard_map/ppermute | solution.py:357
  37.9 0.0 collective-permute-done.13.two_ref
  37.9 1.2 %collective-permute-done.12.three_ref = bf16[48,256]{1,0:T(8,128)(2,1)S(1)} collective-permute-done((bf16[48,256]{1,0:T(8,128)(2,1)S(1)}, bf16[48,256]{1,0:T(8,128)(2,1)S(1)}, u32[]{:S(2)}, u32[]{:S(2)}) %collective-permute-start.12) | collective-permute-done | bytes 24608 | tf_op jit(solution)/shard_map/ppermute | solution.py:357
  39.1 2.0 %collective-permute-done.11.one_ref = bf16[48,256]{1,0:T(8,128)(2,1)S(1)} collective-permute-done((bf16[48,256]{1,0:T(8,128)(2,1)S(1)}, bf16[48,256]{1,0:T(8,128)(2,1)S(1)}, u32[]{:S(2)}, u32[]{:S(2)}) %collective-permute-start.11) | collective-permute-done | bytes 24608 | tf_op jit(solution)/shard_map/ppermute | solution.py:357
  41.1 0.1 merge_kernel.1
  41.2 3.9 %collective-permute-start.14 = (f32[24,256]{1,0:T(8,128)S(1)}, f32[24,256]{1,0:T(8,128)S(1)}, u32[]{:S(2)}, u32[]{:S(2)}) collective-permute-start(f32[24,256]{1,0:T(8,128)S(1)} %get-tuple-element.25), channel_id=1, source_target_pairs={{0,8},{8,0},{16,24},{24,16},{32,40},{40,32},{48,56},{56,48},{64,72... | collective-permute-start | bytes 73736 | tf_op jit(solution)/shard_map/ppermute | solution.py:369
  45.0 0.9 %local_kernel.1 = (f32[16,8,512]{2,1,0:T(8,128)S(1)}, f32[16,8,512]{2,1,0:T(8,128)S(1)}) custom-call(bf16[3,16,512]{2,1,0:T(8,128)(2,1)S(1)} %collective-permute-done.refs_0_, bf16[3,16,512]{2,1,0:T(8,128)(2,1)S(1)} %collective-permute-done.1.refs_1_, bf16[3,16,512]{2,1,0:T(8,128)(2,1)S(1)} %collective-permute-done.2.refs_2_, ...), custom_call_target="tpu_custom_call" | custom-call | flops 8388608 | bytes 2097152 | tf_op jit(solution)/shard_map/local_kernel/pallas_call | solution.py:320
  45.9 0.0 collective-permute-done.14.other_ref
  45.9 1.2 %final_kernel.1 = bf16[128,512]{1,0:T(8,128)(2,1)} custom-call(f32[24,256]{1,0:T(8,128)S(1)} %get-tuple-element.24.mine_ref, f32[24,256]{1,0:T(8,128)S(1)} %collective-permute-done.14.other_ref, f32[16,512]{1,0:T(8,128)S(1)} %get-tuple-element.26.edge_ref, f32[3,3,512]{2,1,0:T(4,128)S(1)} %copy-done.1, f32[16,512]{1,0:T(8,128)S(1)} %copy-done, ...), custom_call_target="tpu_custom_call" | custom-call | tf_op jit(solution)/shard_map/final_kernel/pallas_call | solution.py:320
  (1 shorter events, 0.0 us)
Async XLA Ops:
  0.0 21.6 %copy-start = (f32[16,512]{1,0:T(8,128)S(1)}, f32[16,512]{1,0:T(8,128)}, u32[]{:S(2)}) copy-start(f32[16,512]{1,0:T(8,128)} %rates_ref.7) | copy-start | bytes 98308
  0.0 21.6 %copy-start.1 = (f32[3,3,512]{2,1,0:T(4,128)S(1)}, f32[3,3,512]{2,1,0:T(4,128)}, u32[]{:S(2)}) copy-start(f32[3,3,512]{2,1,0:T(4,128)} %taps_ref.7) | copy-start | bytes 55300
  0.0 21.6 %copy-start.2 = (f32[16,512]{1,0:T(8,128)S(1)}, f32[16,512]{1,0:T(8,128)}, u32[]{:S(2)}) copy-start(f32[16,512]{1,0:T(8,128)} %residues_ref.1) | copy-start | bytes 98308
  1.0 12.1 %collective-permute-start.5 = (bf16[3,16,512]{2,1,0:T(8,128)(2,1)S(1)}, bf16[3,16,512]{2,1,0:T(8,128)(2,1)S(1)}, u32[]{:S(2)}, u32[]{:S(2)}) collective-permute-start(bf16[3,16,512]{2,1,0:T(8,128)(2,1)S(1)} %get-tuple-element.32), channel_id=1, source_target_pairs={{0,6},{1,7},{2,0},{3,1},{4,2},{5,3},{6,4},{7,5},{8,14},{9,15},{10,... | collective-permute-start | bytes 147464 | tf_op jit(solution)/shard_map/ppermute | solution.py:336
  8.0 8.5 %collective-permute-start.4 = (bf16[3,16,512]{2,1,0:T(8,128)(2,1)S(1)}, bf16[3,16,512]{2,1,0:T(8,128)(2,1)S(1)}, u32[]{:S(2)}, u32[]{:S(2)}) collective-permute-start(bf16[3,16,512]{2,1,0:T(8,128)(2,1)S(1)} %get-tuple-element.33), channel_id=1, source_target_pairs={{0,2},{1,3},{2,4},{3,5},{4,6},{5,7},{6,0},{7,1},{8,10},{9,11},{10,... | collective-permute-start | bytes 147464 | tf_op jit(solution)/shard_map/ppermute | solution.py:336
  8.0 9.2 %collective-permute-start.3 = (bf16[3,16,512]{2,1,0:T(8,128)(2,1)S(1)}, bf16[3,16,512]{2,1,0:T(8,128)(2,1)S(1)}, u32[]{:S(2)}, u32[]{:S(2)}) collective-permute-start(bf16[3,16,512]{2,1,0:T(8,128)(2,1)S(1)} %get-tuple-element.34), channel_id=1, source_target_pairs={{0,5},{1,6},{2,7},{3,0},{4,1},{5,2},{6,3},{7,4},{8,13},{9,14},{10,... | collective-permute-start | bytes 147464 | tf_op jit(solution)/shard_map/ppermute | solution.py:336
  10.8 6.4 %collective-permute-start.2 = (bf16[3,16,512]{2,1,0:T(8,128)(2,1)S(1)}, bf16[3,16,512]{2,1,0:T(8,128)(2,1)S(1)}, u32[]{:S(2)}, u32[]{:S(2)}) collective-permute-start(bf16[3,16,512]{2,1,0:T(8,128)(2,1)S(1)} %get-tuple-element.35), channel_id=1, source_target_pairs={{0,3},{1,4},{2,5},{3,6},{4,7},{5,0},{6,1},{7,2},{8,11},{9,12},{10,... | collective-permute-start | bytes 147464 | tf_op jit(solution)/shard_map/ppermute | solution.py:336
  11.2 7.4 %collective-permute-start.1 = (bf16[3,16,512]{2,1,0:T(8,128)(2,1)S(1)}, bf16[3,16,512]{2,1,0:T(8,128)(2,1)S(1)}, u32[]{:S(2)}, u32[]{:S(2)}) collective-permute-start(bf16[3,16,512]{2,1,0:T(8,128)(2,1)S(1)} %get-tuple-element.36), channel_id=1, source_target_pairs={{0,1},{1,2},{2,3},{3,4},{4,5},{5,6},{6,7},{7,0},{8,9},{9,10},{10,1... | collective-permute-start | bytes 147464 | tf_op jit(solution)/shard_map/ppermute | solution.py:336
  13.2 8.4 %collective-permute-start = (bf16[3,16,512]{2,1,0:T(8,128)(2,1)S(1)}, bf16[3,16,512]{2,1,0:T(8,128)(2,1)S(1)}, u32[]{:S(2)}, u32[]{:S(2)}) collective-permute-start(bf16[3,16,512]{2,1,0:T(8,128)(2,1)S(1)} %get-tuple-element.37), channel_id=1, source_target_pairs={{0,4},{1,5},{2,6},{3,7},{4,0},{5,1},{6,2},{7,3},{8,12},{9,13},{10,... | collective-permute-start | bytes 147464 | tf_op jit(solution)/shard_map/ppermute | solution.py:336
  16.4 5.2 %copy-start.3 = (f32[512]{0:T(512)S(1)}, f32[512]{0:T(512)}, u32[]{:S(2)}) copy-start(f32[512]{0:T(512)} %param.9) | copy-start | bytes 6148
  16.4 5.2 %collective-permute-start.6 = (bf16[3,16,512]{2,1,0:T(8,128)(2,1)S(1)}, bf16[3,16,512]{2,1,0:T(8,128)(2,1)S(1)}, u32[]{:S(2)}, u32[]{:S(2)}) collective-permute-start(bf16[3,16,512]{2,1,0:T(8,128)(2,1)S(1)} %get-tuple-element.38), channel_id=1, source_target_pairs={{0,7},{1,0},{2,1},{3,2},{4,3},{5,4},{6,5},{7,6},{8,15},{9,8},{10,9... | collective-permute-start | bytes 147464 | tf_op jit(solution)/shard_map/ppermute | solution.py:336
  22.3 3.4 %collective-permute-start.7 = (f32[32,256]{1,0:T(8,128)S(1)}, f32[32,256]{1,0:T(8,128)S(1)}, u32[]{:S(2)}, u32[]{:S(2)}) collective-permute-start(f32[32,256]{1,0:T(8,128)S(1)} %get-tuple-element.19), channel_id=1, source_target_pairs={{0,8},{8,0},{16,24},{24,16},{32,40},{40,32},{48,56},{56,48},{64,72... | collective-permute-start | bytes 98312 | tf_op jit(solution)/shard_map/ppermute | solution.py:350
  25.7 4.3 %collective-permute-start.10 = (bf16[48,256]{1,0:T(8,128)(2,1)S(1)}, bf16[48,256]{1,0:T(8,128)(2,1)S(1)}, u32[]{:S(2)}, u32[]{:S(2)}) collective-permute-start(bf16[48,256]{1,0:T(8,128)(2,1)S(1)} %get-tuple-element.20.own_ref), channel_id=1, source_target_pairs={{0,32},{8,40},{16,48},{24,56},{32,0},{40,8},{48,16},{56,24},{64,96... | collective-permute-start | bytes 73736 | tf_op jit(solution)/shard_map/ppermute | solution.py:357
  28.6 2.7 %collective-permute-start.9 = (bf16[48,256]{1,0:T(8,128)(2,1)S(1)}, bf16[48,256]{1,0:T(8,128)(2,1)S(1)}, u32[]{:S(2)}, u32[]{:S(2)}) collective-permute-start(bf16[48,256]{1,0:T(8,128)(2,1)S(1)} %get-tuple-element.20.own_ref), channel_id=1, source_target_pairs={{0,48},{8,56},{16,0},{24,8},{32,16},{40,24},{48,32},{56,40},{64,11... | collective-permute-start | bytes 73736 | tf_op jit(solution)/shard_map/ppermute | solution.py:357
  29.4 3.9 %collective-permute-start.8 = (bf16[48,256]{1,0:T(8,128)(2,1)S(1)}, bf16[48,256]{1,0:T(8,128)(2,1)S(1)}, u32[]{:S(2)}, u32[]{:S(2)}) collective-permute-start(bf16[48,256]{1,0:T(8,128)(2,1)S(1)} %get-tuple-element.20.own_ref), channel_id=1, source_target_pairs={{0,16},{8,24},{16,32},{24,40},{32,48},{40,56},{48,0},{56,8},{64,80... | collective-permute-start | bytes 73736 | tf_op jit(solution)/shard_map/ppermute | solution.py:357
  33.4 4.5 %collective-permute-start.13 = (bf16[48,256]{1,0:T(8,128)(2,1)S(1)}, bf16[48,256]{1,0:T(8,128)(2,1)S(1)}, u32[]{:S(2)}, u32[]{:S(2)}) collective-permute-start(bf16[48,256]{1,0:T(8,128)(2,1)S(1)} %get-tuple-element.21.own_ref), channel_id=1, source_target_pairs={{0,128},{8,136},{16,144},{24,152},{32,160},{40,168},{48,176},{56,1... | collective-permute-start | bytes 73736 | tf_op jit(solution)/shard_map/ppermute | solution.py:357
  36.4 2.7 %collective-permute-start.12 = (bf16[48,256]{1,0:T(8,128)(2,1)S(1)}, bf16[48,256]{1,0:T(8,128)(2,1)S(1)}, u32[]{:S(2)}, u32[]{:S(2)}) collective-permute-start(bf16[48,256]{1,0:T(8,128)(2,1)S(1)} %get-tuple-element.21.own_ref), channel_id=1, source_target_pairs={{0,192},{8,200},{16,208},{24,216},{32,224},{40,232},{48,240},{56,2... | collective-permute-start | bytes 73736 | tf_op jit(solution)/shard_map/ppermute | solution.py:357
  37.2 3.9 %collective-permute-start.11 = (bf16[48,256]{1,0:T(8,128)(2,1)S(1)}, bf16[48,256]{1,0:T(8,128)(2,1)S(1)}, u32[]{:S(2)}, u32[]{:S(2)}) collective-permute-start(bf16[48,256]{1,0:T(8,128)(2,1)S(1)} %get-tuple-element.21.own_ref), channel_id=1, source_target_pairs={{0,64},{8,72},{16,80},{24,88},{32,96},{40,104},{48,112},{56,120},{... | collective-permute-start | bytes 73736 | tf_op jit(solution)/shard_map/ppermute | solution.py:357
  41.2 4.7 %collective-permute-start.14 = (f32[24,256]{1,0:T(8,128)S(1)}, f32[24,256]{1,0:T(8,128)S(1)}, u32[]{:S(2)}, u32[]{:S(2)}) collective-permute-start(f32[24,256]{1,0:T(8,128)S(1)} %get-tuple-element.25), channel_id=1, source_target_pairs={{0,8},{8,0},{16,24},{24,16},{32,40},{40,32},{48,56},{56,48},{64,72... | collective-permute-start | bytes 73736 | tf_op jit(solution)/shard_map/ppermute | solution.py:369

commit v5 on v4

--- a/solution.py
+++ b/solution.py
@@ -7,7 +7,7 @@
 
 LENGTH = 4096
 SUB = 16
-SHIFTS = (4, 1, 3, 5, 2, 6, 7, 0)
+SHIFTS = (1, 6, 2, 5, 3, 4, 7, 0)
 LANES = 128
 BLOCK = 128
 VMEM = pl.BlockSpec(memory_space=pltpu.VMEM)
@@ -49,11 +49,6 @@
 
 def core_index():
     return lax.rem(lax.axis_index("ctx"), 2)
-
-
-def half_of(value, which):
-    half = value.shape[-1] // 2
-    return jnp.where(which == 0, value[:, :half], value[:, half:])
 
 
 TAIL = 4
@@ -69,13 +64,13 @@
     return result
 
 
-def half_taps(taps_ref, core):
-    return [[half_of(taps_ref[j, s : s + 1, :], core) for j in range(3)] for s in (1, 2)]
+def edge_taps(taps_ref):
+    return [[taps_ref[j, s : s + 1, :] for j in range(3)] for s in (1, 2)]
 
 
 def state_kernel(*refs):
     blocks = with_sources(refs[: len(SHIFTS)])
-    taps_ref, rates_ref, _, _, kept_ref, sent_ref, edge_ref, ends_ref, signal_ref, one, two, full = refs[len(SHIFTS) :]
+    taps_ref, rates_ref, _, _, full, ends_ref, signal_ref, one, two = refs[len(SHIFTS) :]
     modes, channels = rates_ref.shape
     fill_tokens(blocks, 1, one)
     fill_tokens(blocks, 2, two)
@@ -112,10 +107,6 @@
             ends_ref[mode, :, lanes] = state
             weight = jnp.exp(-rate * remaining)
             full[mode : mode + 1, lanes] = jnp.sum(state * weight, axis=0, keepdims=True)
-    edge_ref[...] = full[modes:, :]
-    core = core_index()
-    kept_ref[...] = half_of(full[...], core)
-    sent_ref[...] = half_of(full[...], 1 - core)
 
 
 def pack(state, edge, out_ref):
@@ -133,11 +124,11 @@
 def pair_kernel(kept_ref, got_ref, rates_ref, taps_ref, out_ref, lower_ref):
     modes = rates_ref.shape[0]
     core = core_index()
-    rate = half_of(rates_ref[...], core)
+    rate = rates_ref[...]
     kept, got = kept_ref[...], got_ref[...]
     lower = jnp.where(core == 0, kept, got)
     upper = jnp.where(core == 0, got, kept)
-    s0, s1 = edge_signal(lower[modes + TAIL :], upper[modes:], half_taps(taps_ref, core))
+    s0, s1 = edge_signal(lower[modes + TAIL :], upper[modes:], edge_taps(taps_ref))
     inner = power(rate, BLOCK - 2) * (power(rate, 1) * s0 + s1)
     state = upper[:modes] + inner + power(rate, BLOCK) * lower[:modes]
     pack(state, join_edges(lower[modes:], upper[modes:]), out_ref)
@@ -176,10 +167,9 @@
 
 def row_kernel(own_ref, one_ref, three_ref, two_ref, rates_ref, taps_ref, out_ref, inside_ref):
     modes = rates_ref.shape[0]
-    core = core_index()
-    rate = half_of(rates_ref[...], core)
+    rate = rates_ref[...]
     refs = (own_ref, one_ref, two_ref, three_ref)
-    carry, first, halo, total, edges = chain(refs, place_of(2), 2 * BLOCK, rate, half_taps(taps_ref, core), False)
+    carry, first, halo, total, edges = chain(refs, place_of(2), 2 * BLOCK, rate, edge_taps(taps_ref), False)
     pack(total, edges, out_ref)
     inside_ref[0:modes, :] = carry
     inside_ref[modes : 2 * modes, :] = halo
@@ -188,14 +178,14 @@
 
 
 def merge_kernel(
-    own_ref, one_ref, three_ref, two_ref, inside_ref, lower_ref, rates_ref, taps_ref, mine_ref, other_ref
+    own_ref, one_ref, three_ref, two_ref, inside_ref, lower_ref, rates_ref, taps_ref, out_ref
 ):
     modes = rates_ref.shape[0]
     core = core_index()
     column, line = place_of(2), place_of(8)
-    rate = half_of(rates_ref[...], core)
+    rate = rates_ref[...]
     refs = (own_ref, one_ref, two_ref, three_ref)
-    taps = half_taps(taps_ref, core)
+    taps = edge_taps(taps_ref)
     single = power(rate, 1)
     above, first, halo, _, _ = chain(refs, line, 8 * BLOCK, rate, taps, True)
     steps = (column * (2 * BLOCK)).astype(jnp.float32) * (-1.0 / LENGTH)
@@ -210,9 +200,8 @@
     inner = power(rate, BLOCK - 2) * (single * first[0] + first[1])
     carries = carry, power(rate, BLOCK) * carry + lower[:modes] + inner
     halos = halo[TAIL : TAIL + 8], lower[modes + TAIL : modes + TAIL + 8]
-    for ref, which in ((mine_ref, core), (other_ref, 1 - core)):
-        ref[0:modes, :] = jnp.where(which == 0, *carries)
-        ref[modes:, :] = jnp.where(which == 0, *halos)
+    out_ref[0:modes, :] = jnp.where(core == 0, *carries)
+    out_ref[modes:, :] = jnp.where(core == 0, *halos)
 
 
 def local_kernel(*refs):
@@ -256,24 +245,21 @@
 
 
 def final_kernel(
-    mine_ref, other_ref, edge_ref, taps_ref, rates_ref, residues_ref, bias_ref, local_ref, front_ref, out_ref, natural
+    carry_ref, summary_ref, taps_ref, rates_ref, residues_ref, bias_ref, local_ref, front_ref, out_ref, natural
 ):
     modes, channels = rates_ref.shape
     rows = row_iota()
     step = rows.astype(jnp.float32)
-    core = core_index()
-    half = channels // 2
 
     def at_first(row):
         return jnp.where(rows == 0, spread(row), 0.0)
 
     for start in range(0, channels, LANES):
         lanes = pl.ds(start, LANES)
-        within = pl.ds(start % half, LANES)
-        got = jnp.where(core == start // half, mine_ref[:, within], other_ref[:, within])
+        got = carry_ref[:, lanes]
         halo = got[modes:]
         taps = [[taps_ref[j, s : s + 1, lanes] for j in range(3)] for s in (1, 2, 0)]
-        s0, s1 = edge_signal(halo, edge_ref[:, lanes], taps[:2])
+        s0, s1 = edge_signal(halo, summary_ref[modes:, lanes], taps[:2])
         _, t1, t2 = taps[2]
         bias = bias_ref[0:1, lanes]
         total = [local_ref[i, :, lanes] for i in range(SUB)]
@@ -306,12 +292,11 @@
     parts = lax.axis_size("tp")
     ctx = lax.axis_size("ctx")
     modes, channels = rates.shape
-    half = channels // 2
     tokens = SUB * parts
     f32 = jnp.float32
     wide = jax.ShapeDtypeStruct((SUB, parts, channels), f32)
-    packed = jax.ShapeDtypeStruct((modes + SUB, half), f32)
-    carried = jax.ShapeDtypeStruct((modes + 8, half), f32)
+    packed = jax.ShapeDtypeStruct((modes + SUB, channels), f32)
+    carried = jax.ShapeDtypeStruct((modes + 8, channels), f32)
     plane = pltpu.VMEM((channels // LANES, tokens, LANES), f32)
     bias = bias[None]
 
@@ -334,21 +319,14 @@
         at = ((lax.axis_index("tp") + shift) % parts) * channels
         block = lax.dynamic_slice(by_stream, (0, 0, at), (3, SUB, channels))
         blocks.append(lax.ppermute(block, "tp", [(i, (i + shift) % parts) for i in range(parts)]) if shift else block)
-    kept, sent, edges, ends, signal = kernel(
+    summary, ends, signal = kernel(
         state_kernel,
-        (
-            packed,
-            packed,
-            jax.ShapeDtypeStruct((SUB, channels), f32),
-            jax.ShapeDtypeStruct((modes, parts, channels), f32),
-            wide,
-        ),
+        (packed, jax.ShapeDtypeStruct((modes, parts, channels), f32), wide),
         (*blocks, short_taps, rates, residues, bias),
-        [plane, plane, pltpu.VMEM((modes + SUB, channels), f32)],
-    )
-    swap = [(i, i ^ 1) for i in range(ctx)]
-    got = lax.ppermute(sent, "ctx", swap)
-    group = jax.ShapeDtypeStruct((3 * SUB, half), jnp.bfloat16)
+        [plane, plane],
+    )
+    got = lax.ppermute(summary, "ctx", [(i, i ^ 1) for i in range(ctx)])
+    group = jax.ShapeDtypeStruct((3 * SUB, channels), jnp.bfloat16)
 
     def around(value, stride):
         parts = {}
@@ -357,16 +335,13 @@
             parts[by] = lax.ppermute(value, "ctx", route)
         return parts[1], parts[3], parts[2]
 
-    pair, lower = kernel(pair_kernel, (group, packed), (kept, got, rates, short_taps))
+    pair, lower = kernel(pair_kernel, (group, packed), (summary, got, rates, short_taps))
     row, inside = kernel(
         row_kernel,
-        (group, jax.ShapeDtypeStruct((2 * modes + 8, half), f32)),
+        (group, jax.ShapeDtypeStruct((2 * modes + 8, channels), f32)),
         (pair, *around(pair, 2), rates, short_taps),
     )
-    mine, other = kernel(
-        merge_kernel, (carried, carried), (row, *around(row, 8), inside, lower, rates, short_taps)
-    )
-    other = lax.ppermute(other, "ctx", swap)
+    carry = kernel(merge_kernel, carried, (row, *around(row, 8), inside, lower, rates, short_taps))
     local, front = kernel(
         local_kernel,
         (wide, wide),
@@ -377,7 +352,7 @@
     return kernel(
         final_kernel,
         jax.ShapeDtypeStruct((tokens, channels), jnp.bfloat16),
-        (mine, other, edges, short_taps, rates, residues, bias, local, front),
+        (carry, summary, short_taps, rates, residues, bias, local, front),
         [plane],
     )
 

time: 47.3 us -> 44 us (0.930)
  the two profiles are of different devices: /device:TPU:1 before, /device:TPU:32 now
where the time goes in v5:
time: 44 us; the launch traced here: 43.6 us
  starting transfers between devices  28.1 us (64%)
  waiting for transfers between devices  11.3 us (26%)
  Pallas kernels  3.08 us (7%)
  local copies, waits for them, and re-layouts  1.05 us (2%)
    ppermute x7, starting transfers between devices, body(): lax.ppermute(block, 'tp', [(i, (i + shift) % parts) for i in range(parts)])  17.6 us
    ppermute x6, starting transfers between devices, around(): parts[by] = lax.ppermute(value, 'ctx', route)  10.4 us
    ppermute x6, waiting for transfers between devices, around(): parts[by] = lax.ppermute(value, 'ctx', route)  7.87 us
    pallas_call x6, Pallas kernels, kernel(): pl.pallas_call(function, out_shape=out_shape, in_specs=in_specs or [VMEM]...  3.08 us
    ppermute x7, waiting for transfers between devices, body(): lax.ppermute(block, 'tp', [(i, (i + shift) % parts) for i in range(parts)])  2.16 us
    ppermute x1, waiting for transfers between devices, body(): got = lax.ppermute(summary, 'ctx', [(i, i ^ 1) for i in range(ctx)])  1.24 us
    dynamic_slice x1, local copies, waits for them, and re-layouts, body(): block = lax.dynamic_slice(by_stream, (0, 0, at), (3, SUB, channels))  1.03 us
  transfers between devices with their start and end apart: 14, of which 9 were waited for; matrix products, arithmetic and copies ran while one was open for 0% of the time, Pallas kernels for 2%

profile of v5, /device:TPU:32, one launch (start us, length us, event | category | flops | bytes accessed | tf_op | source)
XLA Modules:
  0.0 43.6 jit_solution(7671226134881135771)
XLA Ops:
  0.0 0.0 copy-start
  0.0 0.0 copy-start.1
  0.0 0.0 copy-start.2
  0.0 1.0 %dynamic-slice_bitcast_fusion = (bf16[3,16,512]{2,1,0:T(8,128)(2,1)S(1)}, bf16[3,16,512]{2,1,0:T(8,128)(2,1)S(1)}, bf16[3,16,512]{2,1,0:T(8,128)(2,1)S(1)}, bf16...) fusion(bf16[16,3,4096]{2,0,1:T(8,128)(2,1)} %param.5, ...), kind=kLoop, calls=%fused_computation | loop fusion | bytes 786464 | tf_op jit(solution)/shard_map/dynamic_slice | solution.py:320
  1.0 6.4 %collective-permute-start.5 = (bf16[3,16,512]{2,1,0:T(8,128)(2,1)S(1)}, bf16[3,16,512]{2,1,0:T(8,128)(2,1)S(1)}, u32[]{:S(2)}, u32[]{:S(2)}) collective-permute-start(bf16[3,16,512]{2,1,0:T(8,128)(2,1)S(1)} %get-tuple-element.24), channel_id=1, source_target_pairs={{0,4},{1,5},{2,6},{3,7},{4,0},{5,1},{6,2},{7,3},{8,12},{9,13},{10,... | collective-permute-start | bytes 147464 | tf_op jit(solution)/shard_map/ppermute | solution.py:321
  7.4 0.0 collective-permute-start.4
  7.4 5.0 %collective-permute-start.3 = (bf16[3,16,512]{2,1,0:T(8,128)(2,1)S(1)}, bf16[3,16,512]{2,1,0:T(8,128)(2,1)S(1)}, u32[]{:S(2)}, u32[]{:S(2)}) collective-permute-start(bf16[3,16,512]{2,1,0:T(8,128)(2,1)S(1)} %get-tuple-element.26), channel_id=1, source_target_pairs={{0,5},{1,6},{2,7},{3,0},{4,1},{5,2},{6,3},{7,4},{8,13},{9,14},{10,... | collective-permute-start | bytes 147464 | tf_op jit(solution)/shard_map/ppermute | solution.py:321
  12.5 0.3 collective-permute-start.2
  12.7 3.9 %collective-permute-start.1 = (bf16[3,16,512]{2,1,0:T(8,128)(2,1)S(1)}, bf16[3,16,512]{2,1,0:T(8,128)(2,1)S(1)}, u32[]{:S(2)}, u32[]{:S(2)}) collective-permute-start(bf16[3,16,512]{2,1,0:T(8,128)(2,1)S(1)} %get-tuple-element.28), channel_id=1, source_target_pairs={{0,6},{1,7},{2,0},{3,1},{4,2},{5,3},{6,4},{7,5},{8,14},{9,15},{10,... | collective-permute-start | bytes 147464 | tf_op jit(solution)/shard_map/ppermute | solution.py:321
  16.6 0.0 collective-permute-done.5.refs_5_
  16.6 0.0 collective-permute-start
  16.6 0.0 collective-permute-done.4.refs_4_
  16.6 0.0 copy-start.3
  16.6 2.0 %collective-permute-start.6 = (bf16[3,16,512]{2,1,0:T(8,128)(2,1)S(1)}, bf16[3,16,512]{2,1,0:T(8,128)(2,1)S(1)}, u32[]{:S(2)}, u32[]{:S(2)}) collective-permute-start(bf16[3,16,512]{2,1,0:T(8,128)(2,1)S(1)} %get-tuple-element.30), channel_id=1, source_target_pairs={{0,7},{1,0},{2,1},{3,2},{4,3},{5,4},{6,5},{7,6},{8,15},{9,8},{10,9... | collective-permute-start | bytes 147464 | tf_op jit(solution)/shard_map/ppermute | solution.py:321
  18.6 0.0 collective-permute-done.3.refs_3_
  18.6 0.6 %collective-permute-done.2.refs_2_ = bf16[3,16,512]{2,1,0:T(8,128)(2,1)S(1)} collective-permute-done((bf16[3,16,512]{2,1,0:T(8,128)(2,1)S(1)}, bf16[3,16,512]{2,1,0:T(8,128)(2,1)S(1)}, u32[]{:S(2)}, u32[]{:S(2)}) %collective-permute-start.2) | collective-permute-done | bytes 49184 | tf_op jit(solution)/shard_map/ppermute | solution.py:321
  19.2 0.0 collective-permute-done.1.refs_1_
  19.2 1.5 %collective-permute-done.refs_0_ = bf16[3,16,512]{2,1,0:T(8,128)(2,1)S(1)} collective-permute-done((bf16[3,16,512]{2,1,0:T(8,128)(2,1)S(1)}, bf16[3,16,512]{2,1,0:T(8,128)(2,1)S(1)}, u32[]{:S(2)}, u32[]{:S(2)}) %collective-permute-start) | collective-permute-done | bytes 49184 | tf_op jit(solution)/shard_map/ppermute | solution.py:321
  20.7 0.1 collective-permute-done.6.refs_6_
  20.8 0.0 copy-done
  20.8 0.0 copy-done.1
  20.8 0.0 copy-done.2
  20.8 0.0 copy-done.3
  20.8 0.7 %state_kernel.1 = (f32[32,512]{1,0:T(8,128)S(1)}, f32[16,8,512]{2,1,0:T(8,128)S(1)}, f32[16,8,512]{2,1,0:T(8,128)S(1)}) custom-call(bf16[3,16,512]{2,1,0:T(8,128)(2,1)S(1)} %collective-permute-done.refs_0_, bf16[3,16,512]{2,1,0:T(8,128)(2,1)S(1)} %collective-permute-done.1.refs_1_, bf16[3,16,512]{2,1,0:T(8,128)(2,1)S(1)} %collective-permute-done.2.refs_2_, ...), custom_call_target="tpu_custom_call" | custom-call | tf_op jit(solution)/shard_map/state_kernel/pallas_call | solution.py:305
  21.5 0.1 collective-permute-start.7
  21.6 1.2 %collective-permute-done.7.got_ref = f32[32,512]{1,0:T(8,128)S(1)} collective-permute-done((f32[32,512]{1,0:T(8,128)S(1)}, f32[32,512]{1,0:T(8,128)S(1)}, u32[]{:S(2)}, u32[]{:S(2)}) %collective-permute-start.7) | collective-permute-done | bytes 65568 | tf_op jit(solution)/shard_map/ppermute | solution.py:328
  22.9 3.1 %collective-permute-start.10 = (bf16[48,512]{1,0:T(8,128)(2,1)S(1)}, bf16[48,512]{1,0:T(8,128)(2,1)S(1)}, u32[]{:S(2)}, u32[]{:S(2)}) collective-permute-start(bf16[48,512]{1,0:T(8,128)(2,1)S(1)} %get-tuple-element.15.own_ref), channel_id=1, source_target_pairs={{0,32},{8,40},{16,48},{24,56},{32,0},{40,8},{48,16},{56,24},{64,96... | collective-permute-start | bytes 147464 | tf_op jit(solution)/shard_map/ppermute | solution.py:335
  26.0 1.1 %collective-permute-start.9 = (bf16[48,512]{1,0:T(8,128)(2,1)S(1)}, bf16[48,512]{1,0:T(8,128)(2,1)S(1)}, u32[]{:S(2)}, u32[]{:S(2)}) collective-permute-start(bf16[48,512]{1,0:T(8,128)(2,1)S(1)} %get-tuple-element.15.own_ref), channel_id=1, source_target_pairs={{0,48},{8,56},{16,0},{24,8},{32,16},{40,24},{48,32},{56,40},{64,11... | collective-permute-start | bytes 147464 | tf_op jit(solution)/shard_map/ppermute | solution.py:335
  27.1 0.9 %collective-permute-start.8 = (bf16[48,512]{1,0:T(8,128)(2,1)S(1)}, bf16[48,512]{1,0:T(8,128)(2,1)S(1)}, u32[]{:S(2)}, u32[]{:S(2)}) collective-permute-start(bf16[48,512]{1,0:T(8,128)(2,1)S(1)} %get-tuple-element.15.own_ref), channel_id=1, source_target_pairs={{0,16},{8,24},{16,32},{24,40},{32,48},{40,56},{48,0},{56,8},{64,80... | collective-permute-start | bytes 147464 | tf_op jit(solution)/shard_map/ppermute | solution.py:335
  28.0 0.5 %collective-permute-done.10.two_ref = bf16[48,512]{1,0:T(8,128)(2,1)S(1)} collective-permute-done((bf16[48,512]{1,0:T(8,128)(2,1)S(1)}, bf16[48,512]{1,0:T(8,128)(2,1)S(1)}, u32[]{:S(2)}, u32[]{:S(2)}) %collective-permute-start.10) | collective-permute-done | bytes 49184 | tf_op jit(solution)/shard_map/ppermute | solution.py:335
  28.5 1.5 %collective-permute-done.9.three_ref = bf16[48,512]{1,0:T(8,128)(2,1)S(1)} collective-permute-done((bf16[48,512]{1,0:T(8,128)(2,1)S(1)}, bf16[48,512]{1,0:T(8,128)(2,1)S(1)}, u32[]{:S(2)}, u32[]{:S(2)}) %collective-permute-start.9) | collective-permute-done | bytes 49184 | tf_op jit(solution)/shard_map/ppermute | solution.py:335
  30.1 2.4 %collective-permute-done.8.one_ref = bf16[48,512]{1,0:T(8,128)(2,1)S(1)} collective-permute-done((bf16[48,512]{1,0:T(8,128)(2,1)S(1)}, bf16[48,512]{1,0:T(8,128)(2,1)S(1)}, u32[]{:S(2)}, u32[]{:S(2)}) %collective-permute-start.8) | collective-permute-done | bytes 49184 | tf_op jit(solution)/shard_map/ppermute | solution.py:335
  32.4 0.1 row_kernel.1
  32.5 3.3 %collective-permute-start.13 = (bf16[48,512]{1,0:T(8,128)(2,1)S(1)}, bf16[48,512]{1,0:T(8,128)(2,1)S(1)}, u32[]{:S(2)}, u32[]{:S(2)}) collective-permute-start(bf16[48,512]{1,0:T(8,128)(2,1)S(1)} %get-tuple-element.16.own_ref), channel_id=1, source_target_pairs={{0,128},{8,136},{16,144},{24,152},{32,160},{40,168},{48,176},{56,1... | collective-permute-start | bytes 147464 | tf_op jit(solution)/shard_map/ppermute | solution.py:335
  35.8 1.1 %collective-permute-start.12 = (bf16[48,512]{1,0:T(8,128)(2,1)S(1)}, bf16[48,512]{1,0:T(8,128)(2,1)S(1)}, u32[]{:S(2)}, u32[]{:S(2)}) collective-permute-start(bf16[48,512]{1,0:T(8,128)(2,1)S(1)} %get-tuple-element.16.own_ref), channel_id=1, source_target_pairs={{0,192},{8,200},{16,208},{24,216},{32,224},{40,232},{48,240},{56,2... | collective-permute-start | bytes 147464 | tf_op jit(solution)/shard_map/ppermute | solution.py:335
  36.9 1.0 %collective-permute-start.11 = (bf16[48,512]{1,0:T(8,128)(2,1)S(1)}, bf16[48,512]{1,0:T(8,128)(2,1)S(1)}, u32[]{:S(2)}, u32[]{:S(2)}) collective-permute-start(bf16[48,512]{1,0:T(8,128)(2,1)S(1)} %get-tuple-element.16.own_ref), channel_id=1, source_target_pairs={{0,64},{8,72},{16,80},{24,88},{32,96},{40,104},{48,112},{56,120},{... | collective-permute-start | bytes 147464 | tf_op jit(solution)/shard_map/ppermute | solution.py:335
  37.8 0.9 %local_kernel.1 = (f32[16,8,512]{2,1,0:T(8,128)S(1)}, f32[16,8,512]{2,1,0:T(8,128)S(1)}) custom-call(bf16[3,16,512]{2,1,0:T(8,128)(2,1)S(1)} %collective-permute-done.refs_0_, bf16[3,16,512]{2,1,0:T(8,128)(2,1)S(1)} %collective-permute-done.1.refs_1_, bf16[3,16,512]{2,1,0:T(8,128)(2,1)S(1)} %collective-permute-done.2.refs_2_, ...), custom_call_target="tpu_custom_call" | custom-call | flops 8388608 | bytes 2097152 | tf_op jit(solution)/shard_map/local_kernel/pallas_call | solution.py:305
  38.7 0.0 collective-permute-done.13.two_ref
  38.7 1.2 %collective-permute-done.12.three_ref = bf16[48,512]{1,0:T(8,128)(2,1)S(1)} collective-permute-done((bf16[48,512]{1,0:T(8,128)(2,1)S(1)}, bf16[48,512]{1,0:T(8,128)(2,1)S(1)}, u32[]{:S(2)}, u32[]{:S(2)}) %collective-permute-start.12) | collective-permute-done | bytes 49184 | tf_op jit(solution)/shard_map/ppermute | solution.py:335
  39.9 2.3 %collective-permute-done.11.one_ref = bf16[48,512]{1,0:T(8,128)(2,1)S(1)} collective-permute-done((bf16[48,512]{1,0:T(8,128)(2,1)S(1)}, bf16[48,512]{1,0:T(8,128)(2,1)S(1)}, u32[]{:S(2)}, u32[]{:S(2)}) %collective-permute-start.11) | collective-permute-done | bytes 49184 | tf_op jit(solution)/shard_map/ppermute | solution.py:335
  42.2 0.1 merge_kernel.1.carry_ref
  42.3 1.2 %final_kernel.1 = bf16[128,512]{1,0:T(8,128)(2,1)} custom-call(f32[24,512]{1,0:T(8,128)S(1)} %merge_kernel.1.carry_ref, f32[32,512]{1,0:T(8,128)S(1)} %get-tuple-element.14.kept_ref.summary_ref, f32[3,3,512]{2,1,0:T(4,128)S(1)} %copy-done.1, f32[16,512]{1,0:T(8,128)S(1)} %copy-done, f32[16,512]{1,0:T(8,128)S(1)} %copy-done.2, f32[1,512]{1,0:T(1,128)S(1)} %bitcast.19, ...), custom_call_target="tpu_custom_call" | custom-call | tf_op jit(solution)/shard_map/final_kernel/pallas_call | solution.py:305
  (1 shorter events, 0.0 us)
Async XLA Ops:
  0.0 20.8 %copy-start = (f32[16,512]{1,0:T(8,128)S(1)}, f32[16,512]{1,0:T(8,128)}, u32[]{:S(2)}) copy-start(f32[16,512]{1,0:T(8,128)} %rates_ref.7) | copy-start | bytes 98308
  0.0 20.8 %copy-start.1 = (f32[3,3,512]{2,1,0:T(4,128)S(1)}, f32[3,3,512]{2,1,0:T(4,128)}, u32[]{:S(2)}) copy-start(f32[3,3,512]{2,1,0:T(4,128)} %taps_ref.7) | copy-start | bytes 55300
  0.0 20.8 %copy-start.2 = (f32[16,512]{1,0:T(8,128)S(1)}, f32[16,512]{1,0:T(8,128)}, u32[]{:S(2)}) copy-start(f32[16,512]{1,0:T(8,128)} %residues_ref.1) | copy-start | bytes 98308
  1.0 15.6 %collective-permute-start.5 = (bf16[3,16,512]{2,1,0:T(8,128)(2,1)S(1)}, bf16[3,16,512]{2,1,0:T(8,128)(2,1)S(1)}, u32[]{:S(2)}, u32[]{:S(2)}) collective-permute-start(bf16[3,16,512]{2,1,0:T(8,128)(2,1)S(1)} %get-tuple-element.24), channel_id=1, source_target_pairs={{0,4},{1,5},{2,6},{3,7},{4,0},{5,1},{6,2},{7,3},{8,12},{9,13},{10,... | collective-permute-start | bytes 147464 | tf_op jit(solution)/shard_map/ppermute | solution.py:321
  7.4 9.2 %collective-permute-start.4 = (bf16[3,16,512]{2,1,0:T(8,128)(2,1)S(1)}, bf16[3,16,512]{2,1,0:T(8,128)(2,1)S(1)}, u32[]{:S(2)}, u32[]{:S(2)}) collective-permute-start(bf16[3,16,512]{2,1,0:T(8,128)(2,1)S(1)} %get-tuple-element.25), channel_id=1, source_target_pairs={{0,3},{1,4},{2,5},{3,6},{4,7},{5,0},{6,1},{7,2},{8,11},{9,12},{10,... | collective-permute-start | bytes 147464 | tf_op jit(solution)/shard_map/ppermute | solution.py:321
  7.4 11.2 %collective-permute-start.3 = (bf16[3,16,512]{2,1,0:T(8,128)(2,1)S(1)}, bf16[3,16,512]{2,1,0:T(8,128)(2,1)S(1)}, u32[]{:S(2)}, u32[]{:S(2)}) collective-permute-start(bf16[3,16,512]{2,1,0:T(8,128)(2,1)S(1)} %get-tuple-element.26), channel_id=1, source_target_pairs={{0,5},{1,6},{2,7},{3,0},{4,1},{5,2},{6,3},{7,4},{8,13},{9,14},{10,... | collective-permute-start | bytes 147464 | tf_op jit(solution)/shard_map/ppermute | solution.py:321
  12.5 6.7 %collective-permute-start.2 = (bf16[3,16,512]{2,1,0:T(8,128)(2,1)S(1)}, bf16[3,16,512]{2,1,0:T(8,128)(2,1)S(1)}, u32[]{:S(2)}, u32[]{:S(2)}) collective-permute-start(bf16[3,16,512]{2,1,0:T(8,128)(2,1)S(1)} %get-tuple-element.27), channel_id=1, source_target_pairs={{0,2},{1,3},{2,4},{3,5},{4,6},{5,7},{6,0},{7,1},{8,10},{9,11},{10,... | collective-permute-start | bytes 147464 | tf_op jit(solution)/shard_map/ppermute | solution.py:321
  12.7 6.5 %collective-permute-start.1 = (bf16[3,16,512]{2,1,0:T(8,128)(2,1)S(1)}, bf16[3,16,512]{2,1,0:T(8,128)(2,1)S(1)}, u32[]{:S(2)}, u32[]{:S(2)}) collective-permute-start(bf16[3,16,512]{2,1,0:T(8,128)(2,1)S(1)} %get-tuple-element.28), channel_id=1, source_target_pairs={{0,6},{1,7},{2,0},{3,1},{4,2},{5,3},{6,4},{7,5},{8,14},{9,15},{10,... | collective-permute-start | bytes 147464 | tf_op jit(solution)/shard_map/ppermute | solution.py:321
  16.6 4.1 %collective-permute-start = (bf16[3,16,512]{2,1,0:T(8,128)(2,1)S(1)}, bf16[3,16,512]{2,1,0:T(8,128)(2,1)S(1)}, u32[]{:S(2)}, u32[]{:S(2)}) collective-permute-start(bf16[3,16,512]{2,1,0:T(8,128)(2,1)S(1)} %get-tuple-element.29), channel_id=1, source_target_pairs={{0,1},{1,2},{2,3},{3,4},{4,5},{5,6},{6,7},{7,0},{8,9},{9,10},{10,1... | collective-permute-start | bytes 147464 | tf_op jit(solution)/shard_map/ppermute | solution.py:321
  16.6 4.2 %copy-start.3 = (f32[512]{0:T(512)S(1)}, f32[512]{0:T(512)}, u32[]{:S(2)}) copy-start(f32[512]{0:T(512)} %param.9) | copy-start | bytes 6148
  16.6 4.2 %collective-permute-start.6 = (bf16[3,16,512]{2,1,0:T(8,128)(2,1)S(1)}, bf16[3,16,512]{2,1,0:T(8,128)(2,1)S(1)}, u32[]{:S(2)}, u32[]{:S(2)}) collective-permute-start(bf16[3,16,512]{2,1,0:T(8,128)(2,1)S(1)} %get-tuple-element.30), channel_id=1, source_target_pairs={{0,7},{1,0},{2,1},{3,2},{4,3},{5,4},{6,5},{7,6},{8,15},{9,8},{10,9... | collective-permute-start | bytes 147464 | tf_op jit(solution)/shard_map/ppermute | solution.py:321
  21.5 1.3 %collective-permute-start.7 = (f32[32,512]{1,0:T(8,128)S(1)}, f32[32,512]{1,0:T(8,128)S(1)}, u32[]{:S(2)}, u32[]{:S(2)}) collective-permute-start(f32[32,512]{1,0:T(8,128)S(1)} %get-tuple-element.14.kept_ref.summary_ref), channel_id=1, source_target_pairs={{0,8},{8,0},{16,24},{24,16},{32,40},{40,32},{48,56},{56,48},{64,72... | collective-permute-start | bytes 196616 | tf_op jit(solution)/shard_map/ppermute | solution.py:328
  22.9 5.7 %collective-permute-start.10 = (bf16[48,512]{1,0:T(8,128)(2,1)S(1)}, bf16[48,512]{1,0:T(8,128)(2,1)S(1)}, u32[]{:S(2)}, u32[]{:S(2)}) collective-permute-start(bf16[48,512]{1,0:T(8,128)(2,1)S(1)} %get-tuple-element.15.own_ref), channel_id=1, source_target_pairs={{0,32},{8,40},{16,48},{24,56},{32,0},{40,8},{48,16},{56,24},{64,96... | collective-permute-start | bytes 147464 | tf_op jit(solution)/shard_map/ppermute | solution.py:335
  26.0 4.1 %collective-permute-start.9 = (bf16[48,512]{1,0:T(8,128)(2,1)S(1)}, bf16[48,512]{1,0:T(8,128)(2,1)S(1)}, u32[]{:S(2)}, u32[]{:S(2)}) collective-permute-start(bf16[48,512]{1,0:T(8,128)(2,1)S(1)} %get-tuple-element.15.own_ref), channel_id=1, source_target_pairs={{0,48},{8,56},{16,0},{24,8},{32,16},{40,24},{48,32},{56,40},{64,11... | collective-permute-start | bytes 147464 | tf_op jit(solution)/shard_map/ppermute | solution.py:335
  27.1 5.3 %collective-permute-start.8 = (bf16[48,512]{1,0:T(8,128)(2,1)S(1)}, bf16[48,512]{1,0:T(8,128)(2,1)S(1)}, u32[]{:S(2)}, u32[]{:S(2)}) collective-permute-start(bf16[48,512]{1,0:T(8,128)(2,1)S(1)} %get-tuple-element.15.own_ref), channel_id=1, source_target_pairs={{0,16},{8,24},{16,32},{24,40},{32,48},{40,56},{48,0},{56,8},{64,80... | collective-permute-start | bytes 147464 | tf_op jit(solution)/shard_map/ppermute | solution.py:335
  32.5 6.2 %collective-permute-start.13 = (bf16[48,512]{1,0:T(8,128)(2,1)S(1)}, bf16[48,512]{1,0:T(8,128)(2,1)S(1)}, u32[]{:S(2)}, u32[]{:S(2)}) collective-permute-start(bf16[48,512]{1,0:T(8,128)(2,1)S(1)} %get-tuple-element.16.own_ref), channel_id=1, source_target_pairs={{0,128},{8,136},{16,144},{24,152},{32,160},{40,168},{48,176},{56,1... | collective-permute-start | bytes 147464 | tf_op jit(solution)/shard_map/ppermute | solution.py:335
  35.8 4.1 %collective-permute-start.12 = (bf16[48,512]{1,0:T(8,128)(2,1)S(1)}, bf16[48,512]{1,0:T(8,128)(2,1)S(1)}, u32[]{:S(2)}, u32[]{:S(2)}) collective-permute-start(bf16[48,512]{1,0:T(8,128)(2,1)S(1)} %get-tuple-element.16.own_ref), channel_id=1, source_target_pairs={{0,192},{8,200},{16,208},{24,216},{32,224},{40,232},{48,240},{56,2... | collective-permute-start | bytes 147464 | tf_op jit(solution)/shard_map/ppermute | solution.py:335
  36.9 5.3 %collective-permute-start.11 = (bf16[48,512]{1,0:T(8,128)(2,1)S(1)}, bf16[48,512]{1,0:T(8,128)(2,1)S(1)}, u32[]{:S(2)}, u32[]{:S(2)}) collective-permute-start(bf16[48,512]{1,0:T(8,128)(2,1)S(1)} %get-tuple-element.16.own_ref), channel_id=1, source_target_pairs={{0,64},{8,72},{16,80},{24,88},{32,96},{40,104},{48,112},{56,120},{... | collective-permute-start | bytes 147464 | tf_op jit(solution)/shard_map/ppermute | solution.py:335

commit v6 on v5

--- a/solution.py
+++ b/solution.py
@@ -1,3 +1,5 @@
+import functools
+
 import jax
 import jax.numpy as jnp
 from jax import lax
@@ -7,7 +9,7 @@
 
 LENGTH = 4096
 SUB = 16
-SHIFTS = (1, 6, 2, 5, 3, 4, 7, 0)
+PIECES = 6
 LANES = 128
 BLOCK = 128
 VMEM = pl.BlockSpec(memory_space=pltpu.VMEM)
@@ -29,9 +31,24 @@
             scratch[group, pl.ds(at, SUB), :] = block[stream, :, lanes].astype(jnp.float32)
 
 
+def join_kernel(at, own_ref, passed_ref, *refs):
+    out_ref = refs[-1]
+    out_ref[0] = own_ref[...]
+    out_ref[1] = passed_ref[at]
+
+
+def back_kernel(third_ref, second_ref, first_ref, out_ref):
+    for at, ref in enumerate((first_ref, second_ref, third_ref)):
+        out_ref[at] = ref[1]
+
+
 def with_sources(refs):
+    far, third, second, first, back, own = refs
     me = lax.axis_index("tp")
-    return [(ref, lax.rem(me - shift + 8, 8)) for ref, shift in zip(refs, SHIFTS)]
+    turn = 1 - 2 * core_index()
+    places = [(own, 0), (far, 4), (first.at[0], 1), (second.at[0], 2), (third.at[0], 3)]
+    places += [(back.at[k - 1], -k) for k in (1, 2, 3)]
+    return [(ref, lax.rem(me - turn * shift + 8, 8)) for ref, shift in places]
 
 
 def featurize(scratch, stream, lanes, taps_ref):
@@ -69,8 +86,8 @@
 
 
 def state_kernel(*refs):
-    blocks = with_sources(refs[: len(SHIFTS)])
-    taps_ref, rates_ref, _, _, full, ends_ref, signal_ref, one, two = refs[len(SHIFTS) :]
+    blocks = with_sources(refs[: PIECES])
+    taps_ref, rates_ref, _, _, full, ends_ref, signal_ref, one, two = refs[PIECES :]
     modes, channels = rates_ref.shape
     fill_tokens(blocks, 1, one)
     fill_tokens(blocks, 2, two)
@@ -205,8 +222,8 @@
 
 
 def local_kernel(*refs):
-    blocks = with_sources(refs[: len(SHIFTS)])
-    taps_ref, rates_ref, residues_ref, bias_ref, ends_ref, signal_ref, local_ref, front_ref, zero = refs[len(SHIFTS) :]
+    blocks = with_sources(refs[: PIECES])
+    taps_ref, rates_ref, residues_ref, bias_ref, ends_ref, signal_ref, local_ref, front_ref, zero = refs[PIECES :]
     modes, channels = rates_ref.shape
     fill_tokens(blocks, 0, zero)
     rows = row_iota()
@@ -300,32 +317,53 @@
     plane = pltpu.VMEM((channels // LANES, tokens, LANES), f32)
     bias = bias[None]
 
-    def kernel(function, out_shape, operands, scratch=(), cost=None, in_specs=None, limit=24):
+    def kernel(function, out_shape, operands, scratch=(), cost=None, name=None):
         several = isinstance(out_shape, tuple)
         return pl.pallas_call(
             function,
             out_shape=out_shape,
-            in_specs=in_specs or [VMEM] * len(operands),
+            in_specs=[VMEM] * len(operands),
             out_specs=(VMEM,) * len(out_shape) if several else VMEM,
             scratch_shapes=list(scratch),
-            compiler_params=pltpu.CompilerParams(vmem_limit_bytes=limit << 20),
+            compiler_params=pltpu.CompilerParams(vmem_limit_bytes=24 << 20),
             cost_estimate=cost,
-            name=function.__name__,
+            name=name or function.__name__,
         )(*operands)
 
     by_stream = jnp.transpose(streams, (1, 0, 2))
-    blocks = []
-    for shift in SHIFTS:
-        at = ((lax.axis_index("tp") + shift) % parts) * channels
-        block = lax.dynamic_slice(by_stream, (0, 0, at), (3, SUB, channels))
-        blocks.append(lax.ppermute(block, "tp", [(i, (i + shift) % parts) for i in range(parts)]) if shift else block)
+    turn = 1 - 2 * core_index()
+    swap = [(i, i ^ 1) for i in range(ctx)]
+
+    def block_for(shift):
+        at = ((lax.axis_index("tp") + turn * shift) % parts) * channels
+        return lax.dynamic_slice(by_stream, (0, 0, at), (3, SUB, channels))
+
+    def along(value, shift):
+        route = []
+        for c in range(ctx):
+            step = -shift if c % 2 else shift
+            route += [(c * parts + z, c * parts + (z + step) % parts) for z in range(parts)]
+        return lax.ppermute(value, ("ctx", "tp"), route)
+
+    passed = lax.ppermute(jnp.stack([block_for(-k) for k in (1, 2, 3)]), "ctx", swap)
+    far = along(block_for(4), 4)
+    two = jax.ShapeDtypeStruct((2, 3, SUB, channels), streams.dtype)
+    three = jax.ShapeDtypeStruct((3, 3, SUB, channels), streams.dtype)
+
+    def both(shift, *after):
+        return kernel(functools.partial(join_kernel, shift - 1), two, (block_for(shift), passed, *after), name="join")
+
+    third, second = (along(both(k), k) for k in (3, 2))
+    first = along(both(1, far), 1)
+    back = lax.ppermute(kernel(back_kernel, three, (third, second, first)), "ctx", swap)
+    blocks = [far, third, second, first, back, block_for(0)]
     summary, ends, signal = kernel(
         state_kernel,
         (packed, jax.ShapeDtypeStruct((modes, parts, channels), f32), wide),
         (*blocks, short_taps, rates, residues, bias),
         [plane, plane],
     )
-    got = lax.ppermute(summary, "ctx", [(i, i ^ 1) for i in range(ctx)])
+    got = lax.ppermute(summary, "ctx", swap)
     group = jax.ShapeDtypeStruct((3 * SUB, channels), jnp.bfloat16)
 
     def around(value, stride):

time: 44 us -> 43.4 us (0.986)
  starting transfers between devices: 28.1 us -> 19.7 us
  waiting for transfers between devices: 11.3 us -> 19.2 us
    ppermute x8 -> x7, starting transfers between devices: 17.7 us -> 9.31 us  [the longest x4 8.89 us: along(): return lax.ppermute(value, ('ctx', 'tp'), route)]
    ppermute x8 -> x7, waiting for transfers between devices: 3.4 us -> 11.4 us  [the longest x4 8.9 us: along(): return lax.ppermute(value, ('ctx', 'tp'), route)]
    pallas_call x6 -> x10, Pallas kernels: 3.08 us -> 3.11 us  [kernel(): pl.pallas_call(function, out_shape=out_shape, in_specs=[VMEM] * len(opera...]
  transfers between devices with their start and end apart: 14 -> 13, of which waited for: 9 -> 10; matrix products, arithmetic and copies ran while one was open for 0% -> 0% of each run, Pallas kernels for 2% -> 2%
where the time goes in v6:
time: 43.4 us; the launch traced here: 43.3 us
  starting transfers between devices  19.7 us (45%)
  waiting for transfers between devices  19.2 us (44%)
  Pallas kernels  3.11 us (7%)
  local copies, waits for them, and re-layouts  1.02 us (2%)
    ppermute x6, starting transfers between devices, around(): parts[by] = lax.ppermute(value, 'ctx', route)  10.4 us
    ppermute x4, waiting for transfers between devices, along(): return lax.ppermute(value, ('ctx', 'tp'), route)  8.9 us
    ppermute x4, starting transfers between devices, along(): return lax.ppermute(value, ('ctx', 'tp'), route)  8.89 us
    ppermute x6, waiting for transfers between devices, around(): parts[by] = lax.ppermute(value, 'ctx', route)  7.87 us
    pallas_call x10, Pallas kernels, kernel(): pl.pallas_call(function, out_shape=out_shape, in_specs=[VMEM] * len(opera...  3.11 us
    ppermute x1, waiting for transfers between devices, body(): lax.ppermute(kernel(back_kernel, three, (third, second, first)), 'ctx', s...  1.36 us
    ppermute x1, waiting for transfers between devices, body(): got = lax.ppermute(summary, 'ctx', swap)  1.12 us
    dynamic_slice x1, local copies, waits for them, and re-layouts, block_for(): return lax.dynamic_slice(by_stream, (0, 0, at), (3, SUB, channels))  0.99 us
  transfers between devices with their start and end apart: 13, of which 10 were waited for; matrix products, arithmetic and copies ran while one was open for 0% of the time, Pallas kernels for 2%

profile of v6, /device:TPU:32, one launch (start us, length us, event | category | flops | bytes accessed | tf_op | source)
XLA Modules:
  0.0 43.3 jit_solution(3413466095184164210)
XLA Ops:
  0.0 1.0 %dynamic-slice_bitcast_fusion = (bf16[3,16,512]{2,1,0:T(8,128)(2,1)S(1)}, bf16[3,16,512]{2,1,0:T(8,128)(2,1)S(1)}, bf16[1,3,16,512]{3,2,1,0:T(8,128)(2,1)S(1)}, ...) fusion(bf16[16,3,4096]{2,0,1:T(8,128)(2,1)} %param.5, ...), kind=kLoop, calls=%fused_computation.1 | loop fusion | bytes 786464 | tf_op jit(solution)/shard_map/dynamic_slice | solution.py:339
  1.0 0.1 collective-permute-start.1
  1.1 6.4 %collective-permute-start = (bf16[3,16,512]{2,1,0:T(8,128)(2,1)S(1)}, bf16[3,16,512]{2,1,0:T(8,128)(2,1)S(1)}, u32[]{:S(2)}, u32[]{:S(2)}) collective-permute-start(bf16[3,16,512]{2,1,0:T(8,128)(2,1)S(1)} %get-tuple-element.29), channel_id=1, source_target_pairs={{0,4},{1,5},{2,6},{3,7},{4,0},{5,1},{6,2},{7,3},{8,12},{9,13},{10,... | collective-permute-start | bytes 147464 | tf_op jit(solution)/shard_map/ppermute | solution.py:346
  7.5 0.0 collective-permute-done.1.passed_ref
  7.5 0.9 %collective-permute-start.2 = (bf16[2,3,16,512]{3,2,1,0:T(8,128)(2,1)S(1)}, bf16[2,3,16,512]{3,2,1,0:T(8,128)(2,1)S(1)}, u32[]{:S(2)}, u32[]{:S(2)}) collective-permute-start(bf16[2,3,16,512]{3,2,1,0:T(8,128)(2,1)S(1)} %join.3), channel_id=1, source_target_pairs={{0,3},{1,4},{2,5},{3,6},{4,7},{5,0},{6,1},{7,2},{8,13},{9,14},{10,... | collective-permute-start | bytes 294920 | tf_op jit(solution)/shard_map/ppermute | solution.py:346
  8.4 1.5 %collective-permute-start.3 = (bf16[2,3,16,512]{3,2,1,0:T(8,128)(2,1)S(1)}, bf16[2,3,16,512]{3,2,1,0:T(8,128)(2,1)S(1)}, u32[]{:S(2)}, u32[]{:S(2)}) collective-permute-start(bf16[2,3,16,512]{3,2,1,0:T(8,128)(2,1)S(1)} %join.4), channel_id=1, source_target_pairs={{0,2},{1,3},{2,4},{3,5},{4,6},{5,7},{6,0},{7,1},{8,14},{9,15},{10,... | collective-permute-start | bytes 294920 | tf_op jit(solution)/shard_map/ppermute | solution.py:346
  10.0 2.3 %collective-permute-done.refs_0_ = bf16[3,16,512]{2,1,0:T(8,128)(2,1)S(1)} collective-permute-done((bf16[3,16,512]{2,1,0:T(8,128)(2,1)S(1)}, bf16[3,16,512]{2,1,0:T(8,128)(2,1)S(1)}, u32[]{:S(2)}, u32[]{:S(2)}) %collective-permute-start) | collective-permute-done | bytes 49184 | tf_op jit(solution)/shard_map/ppermute | solution.py:346
  12.3 0.0 copy-start
  12.3 0.0 copy-start.1
  12.3 0.0 copy-start.2
  12.3 0.1 collective-permute-start.4
  12.4 5.0 %collective-permute-done.2.third_ref.refs_1_ = bf16[2,3,16,512]{3,2,1,0:T(8,128)(2,1)S(1)} collective-permute-done((bf16[2,3,16,512]{3,2,1,0:T(8,128)(2,1)S(1)}, bf16[2,3,16,512]{3,2,1,0:T(8,128)(2,1)S(1)}, u32[]{:S(2)}, u32[]{:S(2)}) %collective-permute-start.2) | collective-permute-done | bytes 98336 | tf_op jit(solution)/shard_map/ppermute | solution.py:346
  17.5 1.5 %collective-permute-done.3.second_ref.refs_2_ = bf16[2,3,16,512]{3,2,1,0:T(8,128)(2,1)S(1)} collective-permute-done((bf16[2,3,16,512]{3,2,1,0:T(8,128)(2,1)S(1)}, bf16[2,3,16,512]{3,2,1,0:T(8,128)(2,1)S(1)}, u32[]{:S(2)}, u32[]{:S(2)}) %collective-permute-start.3) | collective-permute-done | bytes 98336 | tf_op jit(solution)/shard_map/ppermute | solution.py:346
  19.0 0.0 collective-permute-done.4.first_ref.refs_3_
  19.0 0.0 copy-start.3
  19.0 0.1 collective-permute-start.5
  19.1 1.4 %collective-permute-done.5.refs_4_ = bf16[3,3,16,512]{3,2,1,0:T(8,128)(2,1)S(1)} collective-permute-done((bf16[3,3,16,512]{3,2,1,0:T(8,128)(2,1)S(1)}, bf16[3,3,16,512]{3,2,1,0:T(8,128)(2,1)S(1)}, u32[]{:S(2)}, u32[]{:S(2)}) %collective-permute-start.5) | collective-permute-done | bytes 147488 | tf_op jit(solution)/shard_map/ppermute | solution.py:358
  20.5 0.0 copy-done
  20.5 0.0 copy-done.1
  20.5 0.0 copy-done.2
  20.5 0.0 copy-done.3
  20.5 0.7 %state_kernel.1 = (f32[32,512]{1,0:T(8,128)S(1)}, f32[16,8,512]{2,1,0:T(8,128)S(1)}, f32[16,8,512]{2,1,0:T(8,128)S(1)}) custom-call(bf16[3,16,512]{2,1,0:T(8,128)(2,1)S(1)} %collective-permute-done.refs_0_, bf16[2,3,16,512]{3,2,1,0:T(8,128)(2,1)S(1)} %collective-permute-done.2.third_ref.refs_1_, ...), custom_call_target="tpu_custom_call" | custom-call | tf_op jit(solution)/shard_map/state_kernel/pallas_call | solution.py:322
  21.2 0.2 collective-permute-start.6
  21.4 1.1 %collective-permute-done.6.got_ref = f32[32,512]{1,0:T(8,128)S(1)} collective-permute-done((f32[32,512]{1,0:T(8,128)S(1)}, f32[32,512]{1,0:T(8,128)S(1)}, u32[]{:S(2)}, u32[]{:S(2)}) %collective-permute-start.6) | collective-permute-done | bytes 65568 | tf_op jit(solution)/shard_map/ppermute | solution.py:366
  22.6 3.1 %collective-permute-start.9 = (bf16[48,512]{1,0:T(8,128)(2,1)S(1)}, bf16[48,512]{1,0:T(8,128)(2,1)S(1)}, u32[]{:S(2)}, u32[]{:S(2)}) collective-permute-start(bf16[48,512]{1,0:T(8,128)(2,1)S(1)} %get-tuple-element.15.own_ref), channel_id=1, source_target_pairs={{0,32},{8,40},{16,48},{24,56},{32,0},{40,8},{48,16},{56,24},{64,96... | collective-permute-start | bytes 147464 | tf_op jit(solution)/shard_map/ppermute | solution.py:373
  25.7 1.1 %collective-permute-start.8 = (bf16[48,512]{1,0:T(8,128)(2,1)S(1)}, bf16[48,512]{1,0:T(8,128)(2,1)S(1)}, u32[]{:S(2)}, u32[]{:S(2)}) collective-permute-start(bf16[48,512]{1,0:T(8,128)(2,1)S(1)} %get-tuple-element.15.own_ref), channel_id=1, source_target_pairs={{0,48},{8,56},{16,0},{24,8},{32,16},{40,24},{48,32},{56,40},{64,11... | collective-permute-start | bytes 147464 | tf_op jit(solution)/shard_map/ppermute | solution.py:373
  26.8 0.9 %collective-permute-start.7 = (bf16[48,512]{1,0:T(8,128)(2,1)S(1)}, bf16[48,512]{1,0:T(8,128)(2,1)S(1)}, u32[]{:S(2)}, u32[]{:S(2)}) collective-permute-start(bf16[48,512]{1,0:T(8,128)(2,1)S(1)} %get-tuple-element.15.own_ref), channel_id=1, source_target_pairs={{0,16},{8,24},{16,32},{24,40},{32,48},{40,56},{48,0},{56,8},{64,80... | collective-permute-start | bytes 147464 | tf_op jit(solution)/shard_map/ppermute | solution.py:373
  27.7 0.5 %collective-permute-done.9.two_ref = bf16[48,512]{1,0:T(8,128)(2,1)S(1)} collective-permute-done((bf16[48,512]{1,0:T(8,128)(2,1)S(1)}, bf16[48,512]{1,0:T(8,128)(2,1)S(1)}, u32[]{:S(2)}, u32[]{:S(2)}) %collective-permute-start.9) | collective-permute-done | bytes 49184 | tf_op jit(solution)/shard_map/ppermute | solution.py:373
  28.2 1.5 %collective-permute-done.8.three_ref = bf16[48,512]{1,0:T(8,128)(2,1)S(1)} collective-permute-done((bf16[48,512]{1,0:T(8,128)(2,1)S(1)}, bf16[48,512]{1,0:T(8,128)(2,1)S(1)}, u32[]{:S(2)}, u32[]{:S(2)}) %collective-permute-start.8) | collective-permute-done | bytes 49184 | tf_op jit(solution)/shard_map/ppermute | solution.py:373
  29.8 2.4 %collective-permute-done.7.one_ref = bf16[48,512]{1,0:T(8,128)(2,1)S(1)} collective-permute-done((bf16[48,512]{1,0:T(8,128)(2,1)S(1)}, bf16[48,512]{1,0:T(8,128)(2,1)S(1)}, u32[]{:S(2)}, u32[]{:S(2)}) %collective-permute-start.7) | collective-permute-done | bytes 49184 | tf_op jit(solution)/shard_map/ppermute | solution.py:373
  32.1 0.1 row_kernel.1
  32.2 3.3 %collective-permute-start.12 = (bf16[48,512]{1,0:T(8,128)(2,1)S(1)}, bf16[48,512]{1,0:T(8,128)(2,1)S(1)}, u32[]{:S(2)}, u32[]{:S(2)}) collective-permute-start(bf16[48,512]{1,0:T(8,128)(2,1)S(1)} %get-tuple-element.16.own_ref), channel_id=1, source_target_pairs={{0,128},{8,136},{16,144},{24,152},{32,160},{40,168},{48,176},{56,1... | collective-permute-start | bytes 147464 | tf_op jit(solution)/shard_map/ppermute | solution.py:373
  35.5 1.1 %collective-permute-start.11 = (bf16[48,512]{1,0:T(8,128)(2,1)S(1)}, bf16[48,512]{1,0:T(8,128)(2,1)S(1)}, u32[]{:S(2)}, u32[]{:S(2)}) collective-permute-start(bf16[48,512]{1,0:T(8,128)(2,1)S(1)} %get-tuple-element.16.own_ref), channel_id=1, source_target_pairs={{0,192},{8,200},{16,208},{24,216},{32,224},{40,232},{48,240},{56,2... | collective-permute-start | bytes 147464 | tf_op jit(solution)/shard_map/ppermute | solution.py:373
  36.6 1.0 %collective-permute-start.10 = (bf16[48,512]{1,0:T(8,128)(2,1)S(1)}, bf16[48,512]{1,0:T(8,128)(2,1)S(1)}, u32[]{:S(2)}, u32[]{:S(2)}) collective-permute-start(bf16[48,512]{1,0:T(8,128)(2,1)S(1)} %get-tuple-element.16.own_ref), channel_id=1, source_target_pairs={{0,64},{8,72},{16,80},{24,88},{32,96},{40,104},{48,112},{56,120},{... | collective-permute-start | bytes 147464 | tf_op jit(solution)/shard_map/ppermute | solution.py:373
  37.5 0.9 %local_kernel.1 = (f32[16,8,512]{2,1,0:T(8,128)S(1)}, f32[16,8,512]{2,1,0:T(8,128)S(1)}) custom-call(bf16[3,16,512]{2,1,0:T(8,128)(2,1)S(1)} %collective-permute-done.refs_0_, bf16[2,3,16,512]{3,2,1,0:T(8,128)(2,1)S(1)} %collective-permute-done.2.third_ref.refs_1_, bf16[2,3,16,512]{3,2,1,0:T(8,128)(2,1)S(1)} %collective-permute-done.3.second_ref.refs_2_, ...), custom_call_target="tpu_custom_call" | custom-call | flops 8388608 | bytes 2097152 | tf_op jit(solution)/shard_map/local_kernel/pallas_call | solution.py:322
  38.4 0.0 collective-permute-done.12.two_ref
  38.4 1.2 %collective-permute-done.11.three_ref = bf16[48,512]{1,0:T(8,128)(2,1)S(1)} collective-permute-done((bf16[48,512]{1,0:T(8,128)(2,1)S(1)}, bf16[48,512]{1,0:T(8,128)(2,1)S(1)}, u32[]{:S(2)}, u32[]{:S(2)}) %collective-permute-start.11) | collective-permute-done | bytes 49184 | tf_op jit(solution)/shard_map/ppermute | solution.py:373
  39.6 2.3 %collective-permute-done.10.one_ref = bf16[48,512]{1,0:T(8,128)(2,1)S(1)} collective-permute-done((bf16[48,512]{1,0:T(8,128)(2,1)S(1)}, bf16[48,512]{1,0:T(8,128)(2,1)S(1)}, u32[]{:S(2)}, u32[]{:S(2)}) %collective-permute-start.10) | collective-permute-done | bytes 49184 | tf_op jit(solution)/shard_map/ppermute | solution.py:373
  41.9 0.1 merge_kernel.1.carry_ref
  42.0 1.2 %final_kernel.1 = bf16[128,512]{1,0:T(8,128)(2,1)} custom-call(f32[24,512]{1,0:T(8,128)S(1)} %merge_kernel.1.carry_ref, f32[32,512]{1,0:T(8,128)S(1)} %get-tuple-element.14.kept_ref.summary_ref, f32[3,3,512]{2,1,0:T(4,128)S(1)} %copy-done.1, f32[16,512]{1,0:T(8,128)S(1)} %copy-done, f32[16,512]{1,0:T(8,128)S(1)} %copy-done.2, f32[1,512]{1,0:T(1,128)S(1)} %bitcast.25, ...), custom_call_target="tpu_custom_call" | custom-call | tf_op jit(solution)/shard_map/final_kernel/pallas_call | solution.py:322
  (6 shorter events, 0.1 us)
Async XLA Ops:
  1.0 6.5 %collective-permute-start.1 = (bf16[3,3,16,512]{3,2,1,0:T(8,128)(2,1)S(1)}, bf16[3,3,16,512]{3,2,1,0:T(8,128)(2,1)S(1)}, u32[]{:S(2)}, u32[]{:S(2)}) collective-permute-start(bf16[3,3,16,512]{3,2,1,0:T(8,128)(2,1)S(1)} %pad_maximum_fusion), channel_id=1, source_target_pairs={{0,8},{8,0},{16,24},{24,16},{32,40},{40,32},{48,56},{56,48},{64,72... | collective-permute-start | bytes 442376 | tf_op jit(solution)/shard_map/ppermute | solution.py:348
  1.1 11.2 %collective-permute-start = (bf16[3,16,512]{2,1,0:T(8,128)(2,1)S(1)}, bf16[3,16,512]{2,1,0:T(8,128)(2,1)S(1)}, u32[]{:S(2)}, u32[]{:S(2)}) collective-permute-start(bf16[3,16,512]{2,1,0:T(8,128)(2,1)S(1)} %get-tuple-element.29), channel_id=1, source_target_pairs={{0,4},{1,5},{2,6},{3,7},{4,0},{5,1},{6,2},{7,3},{8,12},{9,13},{10,... | collective-permute-start | bytes 147464 | tf_op jit(solution)/shard_map/ppermute | solution.py:346
  7.5 9.9 %collective-permute-start.2 = (bf16[2,3,16,512]{3,2,1,0:T(8,128)(2,1)S(1)}, bf16[2,3,16,512]{3,2,1,0:T(8,128)(2,1)S(1)}, u32[]{:S(2)}, u32[]{:S(2)}) collective-permute-start(bf16[2,3,16,512]{3,2,1,0:T(8,128)(2,1)S(1)} %join.3), channel_id=1, source_target_pairs={{0,3},{1,4},{2,5},{3,6},{4,7},{5,0},{6,1},{7,2},{8,13},{9,14},{10,... | collective-permute-start | bytes 294920 | tf_op jit(solution)/shard_map/ppermute | solution.py:346
  8.4 10.6 %collective-permute-start.3 = (bf16[2,3,16,512]{3,2,1,0:T(8,128)(2,1)S(1)}, bf16[2,3,16,512]{3,2,1,0:T(8,128)(2,1)S(1)}, u32[]{:S(2)}, u32[]{:S(2)}) collective-permute-start(bf16[2,3,16,512]{3,2,1,0:T(8,128)(2,1)S(1)} %join.4), channel_id=1, source_target_pairs={{0,2},{1,3},{2,4},{3,5},{4,6},{5,7},{6,0},{7,1},{8,14},{9,15},{10,... | collective-permute-start | bytes 294920 | tf_op jit(solution)/shard_map/ppermute | solution.py:346
  12.3 8.2 %copy-start = (f32[16,512]{1,0:T(8,128)S(1)}, f32[16,512]{1,0:T(8,128)}, u32[]{:S(2)}) copy-start(f32[16,512]{1,0:T(8,128)} %rates_ref.7) | copy-start | bytes 98308
  12.3 8.2 %copy-start.1 = (f32[3,3,512]{2,1,0:T(4,128)S(1)}, f32[3,3,512]{2,1,0:T(4,128)}, u32[]{:S(2)}) copy-start(f32[3,3,512]{2,1,0:T(4,128)} %taps_ref.7) | copy-start | bytes 55300
  12.3 8.2 %copy-start.2 = (f32[16,512]{1,0:T(8,128)S(1)}, f32[16,512]{1,0:T(8,128)}, u32[]{:S(2)}) copy-start(f32[16,512]{1,0:T(8,128)} %residues_ref.1) | copy-start | bytes 98308
  12.3 6.7 %collective-permute-start.4 = (bf16[2,3,16,512]{3,2,1,0:T(8,128)(2,1)S(1)}, bf16[2,3,16,512]{3,2,1,0:T(8,128)(2,1)S(1)}, u32[]{:S(2)}, u32[]{:S(2)}) collective-permute-start(bf16[2,3,16,512]{3,2,1,0:T(8,128)(2,1)S(1)} %join.5), channel_id=1, source_target_pairs={{0,1},{1,2},{2,3},{3,4},{4,5},{5,6},{6,7},{7,0},{8,15},{9,8},{10,9... | collective-permute-start | bytes 294920 | tf_op jit(solution)/shard_map/ppermute | solution.py:346
  19.0 1.5 %copy-start.3 = (f32[512]{0:T(512)S(1)}, f32[512]{0:T(512)}, u32[]{:S(2)}) copy-start(f32[512]{0:T(512)} %param.9) | copy-start | bytes 6148
  19.0 1.5 %collective-permute-start.5 = (bf16[3,3,16,512]{3,2,1,0:T(8,128)(2,1)S(1)}, bf16[3,3,16,512]{3,2,1,0:T(8,128)(2,1)S(1)}, u32[]{:S(2)}, u32[]{:S(2)}) collective-permute-start(bf16[3,3,16,512]{3,2,1,0:T(8,128)(2,1)S(1)} %back_kernel.1), channel_id=1, source_target_pairs={{0,8},{8,0},{16,24},{24,16},{32,40},{40,32},{48,56},{56,48},{64,72... | collective-permute-start | bytes 442376 | tf_op jit(solution)/shard_map/ppermute | solution.py:358
  21.2 1.3 %collective-permute-start.6 = (f32[32,512]{1,0:T(8,128)S(1)}, f32[32,512]{1,0:T(8,128)S(1)}, u32[]{:S(2)}, u32[]{:S(2)}) collective-permute-start(f32[32,512]{1,0:T(8,128)S(1)} %get-tuple-element.14.kept_ref.summary_ref), channel_id=1, source_target_pairs={{0,8},{8,0},{16,24},{24,16},{32,40},{40,32},{48,56},{56,48},{64,72... | collective-permute-start | bytes 196616 | tf_op jit(solution)/shard_map/ppermute | solution.py:366
  22.6 5.7 %collective-permute-start.9 = (bf16[48,512]{1,0:T(8,128)(2,1)S(1)}, bf16[48,512]{1,0:T(8,128)(2,1)S(1)}, u32[]{:S(2)}, u32[]{:S(2)}) collective-permute-start(bf16[48,512]{1,0:T(8,128)(2,1)S(1)} %get-tuple-element.15.own_ref), channel_id=1, source_target_pairs={{0,32},{8,40},{16,48},{24,56},{32,0},{40,8},{48,16},{56,24},{64,96... | collective-permute-start | bytes 147464 | tf_op jit(solution)/shard_map/ppermute | solution.py:373
  25.7 4.1 %collective-permute-start.8 = (bf16[48,512]{1,0:T(8,128)(2,1)S(1)}, bf16[48,512]{1,0:T(8,128)(2,1)S(1)}, u32[]{:S(2)}, u32[]{:S(2)}) collective-permute-start(bf16[48,512]{1,0:T(8,128)(2,1)S(1)} %get-tuple-element.15.own_ref), channel_id=1, source_target_pairs={{0,48},{8,56},{16,0},{24,8},{32,16},{40,24},{48,32},{56,40},{64,11... | collective-permute-start | bytes 147464 | tf_op jit(solution)/shard_map/ppermute | solution.py:373
  26.8 5.3 %collective-permute-start.7 = (bf16[48,512]{1,0:T(8,128)(2,1)S(1)}, bf16[48,512]{1,0:T(8,128)(2,1)S(1)}, u32[]{:S(2)}, u32[]{:S(2)}) collective-permute-start(bf16[48,512]{1,0:T(8,128)(2,1)S(1)} %get-tuple-element.15.own_ref), channel_id=1, source_target_pairs={{0,16},{8,24},{16,32},{24,40},{32,48},{40,56},{48,0},{56,8},{64,80... | collective-permute-start | bytes 147464 | tf_op jit(solution)/shard_map/ppermute | solution.py:373
  32.2 6.2 %collective-permute-start.12 = (bf16[48,512]{1,0:T(8,128)(2,1)S(1)}, bf16[48,512]{1,0:T(8,128)(2,1)S(1)}, u32[]{:S(2)}, u32[]{:S(2)}) collective-permute-start(bf16[48,512]{1,0:T(8,128)(2,1)S(1)} %get-tuple-element.16.own_ref), channel_id=1, source_target_pairs={{0,128},{8,136},{16,144},{24,152},{32,160},{40,168},{48,176},{56,1... | collective-permute-start | bytes 147464 | tf_op jit(solution)/shard_map/ppermute | solution.py:373
  35.5 4.1 %collective-permute-start.11 = (bf16[48,512]{1,0:T(8,128)(2,1)S(1)}, bf16[48,512]{1,0:T(8,128)(2,1)S(1)}, u32[]{:S(2)}, u32[]{:S(2)}) collective-permute-start(bf16[48,512]{1,0:T(8,128)(2,1)S(1)} %get-tuple-element.16.own_ref), channel_id=1, source_target_pairs={{0,192},{8,200},{16,208},{24,216},{32,224},{40,232},{48,240},{56,2... | collective-permute-start | bytes 147464 | tf_op jit(solution)/shard_map/ppermute | solution.py:373
  36.6 5.3 %collective-permute-start.10 = (bf16[48,512]{1,0:T(8,128)(2,1)S(1)}, bf16[48,512]{1,0:T(8,128)(2,1)S(1)}, u32[]{:S(2)}, u32[]{:S(2)}) collective-permute-start(bf16[48,512]{1,0:T(8,128)(2,1)S(1)} %get-tuple-element.16.own_ref), channel_id=1, source_target_pairs={{0,64},{8,72},{16,80},{24,88},{32,96},{40,104},{48,112},{56,120},{... | collective-permute-start | bytes 147464 | tf_op jit(solution)/shard_map/ppermute | solution.py:373

commit v7 on v6

--- a/solution.py
+++ b/solution.py
@@ -85,15 +85,27 @@
     return [[taps_ref[j, s : s + 1, :] for j in range(3)] for s in (1, 2)]
 
 
+def weights_kernel(rates_ref, residues_ref, _, decay_ref, ends_ref, carry_ref):
+    modes, channels = rates_ref.shape
+    step = row_iota().astype(jnp.float32)
+    remaining = (7.0 - step) * (SUB / LENGTH)
+    elapsed = (step * SUB + 1.0) * (1.0 / LENGTH)
+    decay_ref[...] = power(rates_ref[...], 1)
+    for start in range(0, channels, LANES):
+        lanes = pl.ds(start, LANES)
+        for mode in range(modes):
+            rate = spread(rates_ref[mode : mode + 1, lanes])
+            ends_ref[mode, :, lanes] = jnp.exp(-rate * remaining)
+            carry_ref[mode, :, lanes] = spread(residues_ref[mode : mode + 1, lanes]) * jnp.exp(-rate * elapsed)
+
+
 def state_kernel(*refs):
     blocks = with_sources(refs[: PIECES])
-    taps_ref, rates_ref, _, _, full, ends_ref, signal_ref, one, two = refs[PIECES :]
-    modes, channels = rates_ref.shape
+    taps_ref, decay_ref, weight_ref, full, ends_ref, signal_ref, one, two = refs[PIECES :]
+    modes, channels = decay_ref.shape
     fill_tokens(blocks, 1, one)
     fill_tokens(blocks, 2, two)
     rows = row_iota()
-    step = rows.astype(jnp.float32)
-    remaining = (7.0 - step) * (SUB / LENGTH)
     full[modes:, :] = jnp.zeros((SUB, channels), jnp.float32)
     for group in range(channels // LANES):
         lanes = pl.ds(group * LANES, LANES)
@@ -116,14 +128,12 @@
         for i in range(SUB):
             signal_ref[i, :, lanes] = signal[i]
         for mode in range(modes):
-            rate = spread(rates_ref[mode : mode + 1, lanes])
-            decay = jnp.exp(rate * (-1.0 / LENGTH))
+            decay = spread(decay_ref[mode : mode + 1, lanes])
             state = signal[0]
             for i in range(1, SUB):
                 state = state * decay + signal[i]
             ends_ref[mode, :, lanes] = state
-            weight = jnp.exp(-rate * remaining)
-            full[mode : mode + 1, lanes] = jnp.sum(state * weight, axis=0, keepdims=True)
+            full[mode : mode + 1, lanes] = jnp.sum(state * weight_ref[mode, :, lanes], axis=0, keepdims=True)
 
 
 def pack(state, edge, out_ref):
@@ -262,42 +272,35 @@
 
 
 def final_kernel(
-    carry_ref, summary_ref, taps_ref, rates_ref, residues_ref, bias_ref, local_ref, front_ref, out_ref, natural
+    carry_ref, summary_ref, taps_ref, rates_ref, residues_ref, bias_ref, decay_ref, weight_ref, local_ref, front_ref, out_ref, natural
 ):
     modes, channels = rates_ref.shape
     rows = row_iota()
-    step = rows.astype(jnp.float32)
 
     def at_first(row):
         return jnp.where(rows == 0, spread(row), 0.0)
 
     for start in range(0, channels, LANES):
         lanes = pl.ds(start, LANES)
-        got = carry_ref[:, lanes]
-        halo = got[modes:]
+        halo = carry_ref[modes:, lanes]
         taps = [[taps_ref[j, s : s + 1, lanes] for j in range(3)] for s in (1, 2, 0)]
         s0, s1 = edge_signal(halo, summary_ref[modes:, lanes], taps[:2])
         _, t1, t2 = taps[2]
         bias = bias_ref[0:1, lanes]
+        grow = power(rates_ref[:, lanes], -1)
+        carry = carry_ref[:modes, lanes] + grow * (s0 + grow * s1)
+        excess = jnp.sum(residues_ref[:, lanes] * grow, axis=0, keepdims=True) * s1
         total = [local_ref[i, :, lanes] for i in range(SUB)]
         front = [front_ref[i, :, lanes] for i in range(SUB)]
-        total[0] = total[0] + at_first(bias * s0)
+        total[0] = total[0] + at_first(bias * s0 - excess)
         total[1] = total[1] + at_first(bias * s1)
         front[0] = front[0] + at_first(t1 * halo[5:6] + t2 * halo[4:5])
         front[1] = front[1] + at_first(t2 * halo[5:6])
         for mode in range(modes):
-            row = rates_ref[mode : mode + 1, lanes]
-            residue = residues_ref[mode : mode + 1, lanes]
-            grow = jnp.exp(row * (1.0 / LENGTH))
-            rate = spread(row)
-            decay = jnp.exp(rate * (-1.0 / LENGTH))
-            start_row = spread(residue * (got[mode : mode + 1] + grow * s0))
-            later = jnp.where(rows >= 1, spread(residue * (grow * (grow * s1))), 0.0)
-            carried = (start_row + later) * jnp.exp(-rate * ((step * SUB + 1.0) * (1.0 / LENGTH)))
+            decay = spread(decay_ref[mode : mode + 1, lanes])
+            carried = spread(carry[mode : mode + 1]) * weight_ref[mode, :, lanes]
             total[0] = total[0] + carried
-            carried = carried * decay + at_first(residue * s1)
-            total[1] = total[1] + carried
-            for i in range(2, SUB):
+            for i in range(1, SUB):
                 carried = carried * decay
                 total[i] = total[i] + carried
         for i in range(SUB):
@@ -330,6 +333,11 @@
             name=name or function.__name__,
         )(*operands)
 
+    spans = jax.ShapeDtypeStruct((modes, parts, channels), f32)
+    small = pl.CostEstimate(flops=8 << 20, bytes_accessed=2 << 20, transcendentals=0)
+    decay, ends_weight, carry_weight = kernel(
+        weights_kernel, (jax.ShapeDtypeStruct(rates.shape, f32), spans, spans), (rates, residues, bias), cost=small
+    )
     by_stream = jnp.transpose(streams, (1, 0, 2))
     turn = 1 - 2 * core_index()
     swap = [(i, i ^ 1) for i in range(ctx)]
@@ -359,8 +367,8 @@
     blocks = [far, third, second, first, back, block_for(0)]
     summary, ends, signal = kernel(
         state_kernel,
-        (packed, jax.ShapeDtypeStruct((modes, parts, channels), f32), wide),
-        (*blocks, short_taps, rates, residues, bias),
+        (packed, spans, wide),
+        (*blocks, short_taps, decay, ends_weight),
         [plane, plane],
     )
     got = lax.ppermute(summary, "ctx", swap)
@@ -385,12 +393,12 @@
         (wide, wide),
         (*blocks, short_taps, rates, residues, bias, ends, signal),
         [plane],
-        cost=pl.CostEstimate(flops=8 << 20, bytes_accessed=2 << 20, transcendentals=0),
+        cost=small,
     )
     return kernel(
         final_kernel,
         jax.ShapeDtypeStruct((tokens, channels), jnp.bfloat16),
-        (carry, summary, short_taps, rates, residues, bias, local, front),
+        (carry, summary, short_taps, rates, residues, bias, decay, carry_weight, local, front),
         [plane],
     )
 

time: 43.4 us -> 43.2 us (level)
  waiting for transfers between devices: 19.2 us -> 18.6 us
  local copies, waits for them, and re-layouts: 1.02 us -> 1.55 us
    ppermute x1, waiting for transfers between devices: 1.36 us -> 0.7 us  [body(): lax.ppermute(kernel(back_kernel, three, (third, second, first)), 'ctx', s...]
    unnamed x8, local copies, waits for them, and re-layouts: 0.02 us -> 0.56 us
    pallas_call x10 -> x11, Pallas kernels: 3.11 us -> 2.96 us  [kernel(): pl.pallas_call(function, out_shape=out_shape, in_specs=[VMEM] * len(opera...]
where the time goes in v7:
time: 43.2 us; the launch traced here: 43 us
  starting transfers between devices  19.8 us (46%)
  waiting for transfers between devices  18.6 us (43%)
  Pallas kernels  2.96 us (7%)
  local copies, waits for them, and re-layouts  1.55 us (4%)
    ppermute x6, starting transfers between devices, around(): parts[by] = lax.ppermute(value, 'ctx', route)  10.4 us
    ppermute x4, waiting for transfers between devices, along(): return lax.ppermute(value, ('ctx', 'tp'), route)  8.91 us
    ppermute x4, starting transfers between devices, along(): return lax.ppermute(value, ('ctx', 'tp'), route)  8.89 us
    ppermute x6, waiting for transfers between devices, around(): parts[by] = lax.ppermute(value, 'ctx', route)  7.87 us
    pallas_call x11, Pallas kernels, kernel(): pl.pallas_call(function, out_shape=out_shape, in_specs=[VMEM] * len(opera...  2.96 us
    ppermute x1, waiting for transfers between devices, body(): got = lax.ppermute(summary, 'ctx', swap)  1.11 us
    dynamic_slice x1, local copies, waits for them, and re-layouts, block_for(): return lax.dynamic_slice(by_stream, (0, 0, at), (3, SUB, channels))  0.99 us
  transfers between devices with their start and end apart: 13, of which 10 were waited for; matrix products, arithmetic and copies ran while one was open for 0% of the time, Pallas kernels for 2%

profile of v7, /device:TPU:32, one launch (start us, length us, event | category | flops | bytes accessed | tf_op | source)
XLA Modules:
  0.0 43.0 jit_solution(14375777333733456529)
XLA Ops:
  0.0 1.0 %dynamic-slice_bitcast_fusion = (bf16[3,16,512]{2,1,0:T(8,128)(2,1)S(1)}, bf16[3,16,512]{2,1,0:T(8,128)(2,1)S(1)}, bf16[1,3,16,512]{3,2,1,0:T(8,128)(2,1)S(1)}, ...) fusion(bf16[16,3,4096]{2,0,1:T(8,128)(2,1)} %param.5, ...), kind=kLoop, calls=%fused_computation.1 | loop fusion | bytes 786464 | tf_op jit(solution)/shard_map/dynamic_slice | solution.py:347
  1.0 0.1 collective-permute-start.1
  1.1 6.4 %collective-permute-start = (bf16[3,16,512]{2,1,0:T(8,128)(2,1)S(1)}, bf16[3,16,512]{2,1,0:T(8,128)(2,1)S(1)}, u32[]{:S(2)}, u32[]{:S(2)}) collective-permute-start(bf16[3,16,512]{2,1,0:T(8,128)(2,1)S(1)} %get-tuple-element.35), channel_id=1, source_target_pairs={{0,4},{1,5},{2,6},{3,7},{4,0},{5,1},{6,2},{7,3},{8,12},{9,13},{10,... | collective-permute-start | bytes 147464 | tf_op jit(solution)/shard_map/ppermute | solution.py:354
  7.5 0.0 collective-permute-done.1.passed_ref
  7.5 0.9 %collective-permute-start.2 = (bf16[2,3,16,512]{3,2,1,0:T(8,128)(2,1)S(1)}, bf16[2,3,16,512]{3,2,1,0:T(8,128)(2,1)S(1)}, u32[]{:S(2)}, u32[]{:S(2)}) collective-permute-start(bf16[2,3,16,512]{3,2,1,0:T(8,128)(2,1)S(1)} %join.3), channel_id=1, source_target_pairs={{0,3},{1,4},{2,5},{3,6},{4,7},{5,0},{6,1},{7,2},{8,13},{9,14},{10,... | collective-permute-start | bytes 294920 | tf_op jit(solution)/shard_map/ppermute | solution.py:354
  8.4 1.5 %collective-permute-start.3 = (bf16[2,3,16,512]{3,2,1,0:T(8,128)(2,1)S(1)}, bf16[2,3,16,512]{3,2,1,0:T(8,128)(2,1)S(1)}, u32[]{:S(2)}, u32[]{:S(2)}) collective-permute-start(bf16[2,3,16,512]{3,2,1,0:T(8,128)(2,1)S(1)} %join.4), channel_id=1, source_target_pairs={{0,2},{1,3},{2,4},{3,5},{4,6},{5,7},{6,0},{7,1},{8,14},{9,15},{10,... | collective-permute-start | bytes 294920 | tf_op jit(solution)/shard_map/ppermute | solution.py:354
  10.0 2.3 %collective-permute-done.refs_0_ = bf16[3,16,512]{2,1,0:T(8,128)(2,1)S(1)} collective-permute-done((bf16[3,16,512]{2,1,0:T(8,128)(2,1)S(1)}, bf16[3,16,512]{2,1,0:T(8,128)(2,1)S(1)}, u32[]{:S(2)}, u32[]{:S(2)}) %collective-permute-start) | collective-permute-done | bytes 49184 | tf_op jit(solution)/shard_map/ppermute | solution.py:354
  12.3 0.0 copy-start
  12.3 0.0 copy-start.2
  12.3 0.1 collective-permute-start.4
  12.4 5.0 %collective-permute-done.2.third_ref.refs_1_ = bf16[2,3,16,512]{3,2,1,0:T(8,128)(2,1)S(1)} collective-permute-done((bf16[2,3,16,512]{3,2,1,0:T(8,128)(2,1)S(1)}, bf16[2,3,16,512]{3,2,1,0:T(8,128)(2,1)S(1)}, u32[]{:S(2)}, u32[]{:S(2)}) %collective-permute-start.2) | collective-permute-done | bytes 98336 | tf_op jit(solution)/shard_map/ppermute | solution.py:354
  17.5 1.5 %collective-permute-done.3.second_ref.refs_2_ = bf16[2,3,16,512]{3,2,1,0:T(8,128)(2,1)S(1)} collective-permute-done((bf16[2,3,16,512]{3,2,1,0:T(8,128)(2,1)S(1)}, bf16[2,3,16,512]{3,2,1,0:T(8,128)(2,1)S(1)}, u32[]{:S(2)}, u32[]{:S(2)}) %collective-permute-start.3) | collective-permute-done | bytes 98336 | tf_op jit(solution)/shard_map/ppermute | solution.py:354
  19.0 0.0 collective-permute-done.4.first_ref.refs_3_
  19.0 0.0 copy-start.3
  19.0 0.1 collective-permute-start.5
  19.1 0.0 copy-done
  19.1 0.0 copy-done.2
  19.1 0.5 %copy-done.3 = f32[512]{0:T(512)S(1)} copy-done((f32[512]{0:T(512)S(1)}, f32[512]{0:T(512)}, u32[]{:S(2)}) %copy-start.3) | copy-done | bytes 2072
  19.7 0.0 copy-start.1
  19.7 0.1 weights_kernel.1
  19.8 0.7 %collective-permute-done.5.refs_4_ = bf16[3,3,16,512]{3,2,1,0:T(8,128)(2,1)S(1)} collective-permute-done((bf16[3,3,16,512]{3,2,1,0:T(8,128)(2,1)S(1)}, bf16[3,3,16,512]{3,2,1,0:T(8,128)(2,1)S(1)}, u32[]{:S(2)}, u32[]{:S(2)}) %collective-permute-start.5) | collective-permute-done | bytes 147488 | tf_op jit(solution)/shard_map/ppermute | solution.py:366
  20.5 0.0 copy-done.1
  20.5 0.6 %state_kernel.1 = (f32[32,512]{1,0:T(8,128)S(1)}, f32[16,8,512]{2,1,0:T(8,128)S(1)}, f32[16,8,512]{2,1,0:T(8,128)S(1)}) custom-call(bf16[3,16,512]{2,1,0:T(8,128)(2,1)S(1)} %collective-permute-done.refs_0_, bf16[2,3,16,512]{3,2,1,0:T(8,128)(2,1)S(1)} %collective-permute-done.2.third_ref.refs_1_, ...), custom_call_target="tpu_custom_call" | custom-call | tf_op jit(solution)/shard_map/state_kernel/pallas_call | solution.py:325
  21.1 0.2 collective-permute-start.6
  21.3 1.1 %collective-permute-done.6.got_ref = f32[32,512]{1,0:T(8,128)S(1)} collective-permute-done((f32[32,512]{1,0:T(8,128)S(1)}, f32[32,512]{1,0:T(8,128)S(1)}, u32[]{:S(2)}, u32[]{:S(2)}) %collective-permute-start.6) | collective-permute-done | bytes 65568 | tf_op jit(solution)/shard_map/ppermute | solution.py:374
  22.5 3.1 %collective-permute-start.9 = (bf16[48,512]{1,0:T(8,128)(2,1)S(1)}, bf16[48,512]{1,0:T(8,128)(2,1)S(1)}, u32[]{:S(2)}, u32[]{:S(2)}) collective-permute-start(bf16[48,512]{1,0:T(8,128)(2,1)S(1)} %get-tuple-element.20.own_ref), channel_id=1, source_target_pairs={{0,32},{8,40},{16,48},{24,56},{32,0},{40,8},{48,16},{56,24},{64,96... | collective-permute-start | bytes 147464 | tf_op jit(solution)/shard_map/ppermute | solution.py:381
  25.6 1.1 %collective-permute-start.8 = (bf16[48,512]{1,0:T(8,128)(2,1)S(1)}, bf16[48,512]{1,0:T(8,128)(2,1)S(1)}, u32[]{:S(2)}, u32[]{:S(2)}) collective-permute-start(bf16[48,512]{1,0:T(8,128)(2,1)S(1)} %get-tuple-element.20.own_ref), channel_id=1, source_target_pairs={{0,48},{8,56},{16,0},{24,8},{32,16},{40,24},{48,32},{56,40},{64,11... | collective-permute-start | bytes 147464 | tf_op jit(solution)/shard_map/ppermute | solution.py:381
  26.7 0.9 %collective-permute-start.7 = (bf16[48,512]{1,0:T(8,128)(2,1)S(1)}, bf16[48,512]{1,0:T(8,128)(2,1)S(1)}, u32[]{:S(2)}, u32[]{:S(2)}) collective-permute-start(bf16[48,512]{1,0:T(8,128)(2,1)S(1)} %get-tuple-element.20.own_ref), channel_id=1, source_target_pairs={{0,16},{8,24},{16,32},{24,40},{32,48},{40,56},{48,0},{56,8},{64,80... | collective-permute-start | bytes 147464 | tf_op jit(solution)/shard_map/ppermute | solution.py:381
  27.6 0.5 %collective-permute-done.9.two_ref = bf16[48,512]{1,0:T(8,128)(2,1)S(1)} collective-permute-done((bf16[48,512]{1,0:T(8,128)(2,1)S(1)}, bf16[48,512]{1,0:T(8,128)(2,1)S(1)}, u32[]{:S(2)}, u32[]{:S(2)}) %collective-permute-start.9) | collective-permute-done | bytes 49184 | tf_op jit(solution)/shard_map/ppermute | solution.py:381
  28.1 1.5 %collective-permute-done.8.three_ref = bf16[48,512]{1,0:T(8,128)(2,1)S(1)} collective-permute-done((bf16[48,512]{1,0:T(8,128)(2,1)S(1)}, bf16[48,512]{1,0:T(8,128)(2,1)S(1)}, u32[]{:S(2)}, u32[]{:S(2)}) %collective-permute-start.8) | collective-permute-done | bytes 49184 | tf_op jit(solution)/shard_map/ppermute | solution.py:381
  29.7 2.4 %collective-permute-done.7.one_ref = bf16[48,512]{1,0:T(8,128)(2,1)S(1)} collective-permute-done((bf16[48,512]{1,0:T(8,128)(2,1)S(1)}, bf16[48,512]{1,0:T(8,128)(2,1)S(1)}, u32[]{:S(2)}, u32[]{:S(2)}) %collective-permute-start.7) | collective-permute-done | bytes 49184 | tf_op jit(solution)/shard_map/ppermute | solution.py:381
  32.0 0.1 row_kernel.1
  32.1 3.3 %collective-permute-start.12 = (bf16[48,512]{1,0:T(8,128)(2,1)S(1)}, bf16[48,512]{1,0:T(8,128)(2,1)S(1)}, u32[]{:S(2)}, u32[]{:S(2)}) collective-permute-start(bf16[48,512]{1,0:T(8,128)(2,1)S(1)} %get-tuple-element.21.own_ref), channel_id=1, source_target_pairs={{0,128},{8,136},{16,144},{24,152},{32,160},{40,168},{48,176},{56,1... | collective-permute-start | bytes 147464 | tf_op jit(solution)/shard_map/ppermute | solution.py:381
  35.4 1.1 %collective-permute-start.11 = (bf16[48,512]{1,0:T(8,128)(2,1)S(1)}, bf16[48,512]{1,0:T(8,128)(2,1)S(1)}, u32[]{:S(2)}, u32[]{:S(2)}) collective-permute-start(bf16[48,512]{1,0:T(8,128)(2,1)S(1)} %get-tuple-element.21.own_ref), channel_id=1, source_target_pairs={{0,192},{8,200},{16,208},{24,216},{32,224},{40,232},{48,240},{56,2... | collective-permute-start | bytes 147464 | tf_op jit(solution)/shard_map/ppermute | solution.py:381
  36.5 1.0 %collective-permute-start.10 = (bf16[48,512]{1,0:T(8,128)(2,1)S(1)}, bf16[48,512]{1,0:T(8,128)(2,1)S(1)}, u32[]{:S(2)}, u32[]{:S(2)}) collective-permute-start(bf16[48,512]{1,0:T(8,128)(2,1)S(1)} %get-tuple-element.21.own_ref), channel_id=1, source_target_pairs={{0,64},{8,72},{16,80},{24,88},{32,96},{40,104},{48,112},{56,120},{... | collective-permute-start | bytes 147464 | tf_op jit(solution)/shard_map/ppermute | solution.py:381
  37.5 0.9 %local_kernel.1 = (f32[16,8,512]{2,1,0:T(8,128)S(1)}, f32[16,8,512]{2,1,0:T(8,128)S(1)}) custom-call(bf16[3,16,512]{2,1,0:T(8,128)(2,1)S(1)} %collective-permute-done.refs_0_, bf16[2,3,16,512]{3,2,1,0:T(8,128)(2,1)S(1)} %collective-permute-done.2.third_ref.refs_1_, bf16[2,3,16,512]{3,2,1,0:T(8,128)(2,1)S(1)} %collective-permute-done.3.second_ref.refs_2_, ...), custom_call_target="tpu_custom_call" | custom-call | flops 8388608 | bytes 2097152 | tf_op jit(solution)/shard_map/local_kernel/pallas_call | solution.py:325
  38.3 0.0 collective-permute-done.12.two_ref
  38.3 1.2 %collective-permute-done.11.three_ref = bf16[48,512]{1,0:T(8,128)(2,1)S(1)} collective-permute-done((bf16[48,512]{1,0:T(8,128)(2,1)S(1)}, bf16[48,512]{1,0:T(8,128)(2,1)S(1)}, u32[]{:S(2)}, u32[]{:S(2)}) %collective-permute-start.11) | collective-permute-done | bytes 49184 | tf_op jit(solution)/shard_map/ppermute | solution.py:381
  39.5 2.3 %collective-permute-done.10.one_ref = bf16[48,512]{1,0:T(8,128)(2,1)S(1)} collective-permute-done((bf16[48,512]{1,0:T(8,128)(2,1)S(1)}, bf16[48,512]{1,0:T(8,128)(2,1)S(1)}, u32[]{:S(2)}, u32[]{:S(2)}) %collective-permute-start.10) | collective-permute-done | bytes 49184 | tf_op jit(solution)/shard_map/ppermute | solution.py:381
  41.8 0.1 merge_kernel.1.carry_ref
  41.9 1.1 %final_kernel.1 = bf16[128,512]{1,0:T(8,128)(2,1)} custom-call(f32[24,512]{1,0:T(8,128)S(1)} %merge_kernel.1.carry_ref, f32[32,512]{1,0:T(8,128)S(1)} %get-tuple-element.19.kept_ref.summary_ref, f32[3,3,512]{2,1,0:T(4,128)S(1)} %copy-done.1, f32[16,512]{1,0:T(8,128)S(1)} %copy-done, f32[16,512]{1,0:T(8,128)S(1)} %copy-done.2, f32[1,512]{1,0:T(1,128)S(1)} %bitcast.25, ...), custom_call_target="tpu_custom_call" | custom-call | tf_op jit(solution)/shard_map/final_kernel/pallas_call | solution.py:325
  (6 shorter events, 0.1 us)
Async XLA Ops:
  1.0 6.5 %collective-permute-start.1 = (bf16[3,3,16,512]{3,2,1,0:T(8,128)(2,1)S(1)}, bf16[3,3,16,512]{3,2,1,0:T(8,128)(2,1)S(1)}, u32[]{:S(2)}, u32[]{:S(2)}) collective-permute-start(bf16[3,3,16,512]{3,2,1,0:T(8,128)(2,1)S(1)} %pad_maximum_fusion), channel_id=1, source_target_pairs={{0,8},{8,0},{16,24},{24,16},{32,40},{40,32},{48,56},{56,48},{64,72... | collective-permute-start | bytes 442376 | tf_op jit(solution)/shard_map/ppermute | solution.py:356
  1.1 11.2 %collective-permute-start = (bf16[3,16,512]{2,1,0:T(8,128)(2,1)S(1)}, bf16[3,16,512]{2,1,0:T(8,128)(2,1)S(1)}, u32[]{:S(2)}, u32[]{:S(2)}) collective-permute-start(bf16[3,16,512]{2,1,0:T(8,128)(2,1)S(1)} %get-tuple-element.35), channel_id=1, source_target_pairs={{0,4},{1,5},{2,6},{3,7},{4,0},{5,1},{6,2},{7,3},{8,12},{9,13},{10,... | collective-permute-start | bytes 147464 | tf_op jit(solution)/shard_map/ppermute | solution.py:354
  7.5 9.9 %collective-permute-start.2 = (bf16[2,3,16,512]{3,2,1,0:T(8,128)(2,1)S(1)}, bf16[2,3,16,512]{3,2,1,0:T(8,128)(2,1)S(1)}, u32[]{:S(2)}, u32[]{:S(2)}) collective-permute-start(bf16[2,3,16,512]{3,2,1,0:T(8,128)(2,1)S(1)} %join.3), channel_id=1, source_target_pairs={{0,3},{1,4},{2,5},{3,6},{4,7},{5,0},{6,1},{7,2},{8,13},{9,14},{10,... | collective-permute-start | bytes 294920 | tf_op jit(solution)/shard_map/ppermute | solution.py:354
  8.4 10.6 %collective-permute-start.3 = (bf16[2,3,16,512]{3,2,1,0:T(8,128)(2,1)S(1)}, bf16[2,3,16,512]{3,2,1,0:T(8,128)(2,1)S(1)}, u32[]{:S(2)}, u32[]{:S(2)}) collective-permute-start(bf16[2,3,16,512]{3,2,1,0:T(8,128)(2,1)S(1)} %join.4), channel_id=1, source_target_pairs={{0,2},{1,3},{2,4},{3,5},{4,6},{5,7},{6,0},{7,1},{8,14},{9,15},{10,... | collective-permute-start | bytes 294920 | tf_op jit(solution)/shard_map/ppermute | solution.py:354
  12.3 6.8 %copy-start = (f32[16,512]{1,0:T(8,128)S(1)}, f32[16,512]{1,0:T(8,128)}, u32[]{:S(2)}) copy-start(f32[16,512]{1,0:T(8,128)} %rates_ref.9) | copy-start | bytes 98308
  12.3 6.8 %copy-start.2 = (f32[16,512]{1,0:T(8,128)S(1)}, f32[16,512]{1,0:T(8,128)}, u32[]{:S(2)}) copy-start(f32[16,512]{1,0:T(8,128)} %residues_ref.3) | copy-start | bytes 98308
  12.3 6.7 %collective-permute-start.4 = (bf16[2,3,16,512]{3,2,1,0:T(8,128)(2,1)S(1)}, bf16[2,3,16,512]{3,2,1,0:T(8,128)(2,1)S(1)}, u32[]{:S(2)}, u32[]{:S(2)}) collective-permute-start(bf16[2,3,16,512]{3,2,1,0:T(8,128)(2,1)S(1)} %join.5), channel_id=1, source_target_pairs={{0,1},{1,2},{2,3},{3,4},{4,5},{5,6},{6,7},{7,0},{8,15},{9,8},{10,9... | collective-permute-start | bytes 294920 | tf_op jit(solution)/shard_map/ppermute | solution.py:354
  19.0 0.7 %copy-start.3 = (f32[512]{0:T(512)S(1)}, f32[512]{0:T(512)}, u32[]{:S(2)}) copy-start(f32[512]{0:T(512)} %param.9) | copy-start | bytes 6148
  19.0 1.5 %collective-permute-start.5 = (bf16[3,3,16,512]{3,2,1,0:T(8,128)(2,1)S(1)}, bf16[3,3,16,512]{3,2,1,0:T(8,128)(2,1)S(1)}, u32[]{:S(2)}, u32[]{:S(2)}) collective-permute-start(bf16[3,3,16,512]{3,2,1,0:T(8,128)(2,1)S(1)} %back_kernel.1), channel_id=1, source_target_pairs={{0,8},{8,0},{16,24},{24,16},{32,40},{40,32},{48,56},{56,48},{64,72... | collective-permute-start | bytes 442376 | tf_op jit(solution)/shard_map/ppermute | solution.py:366
  19.7 0.8 %copy-start.1 = (f32[3,3,512]{2,1,0:T(4,128)S(1)}, f32[3,3,512]{2,1,0:T(4,128)}, u32[]{:S(2)}) copy-start(f32[3,3,512]{2,1,0:T(4,128)} %taps_ref.7) | copy-start | bytes 55300
  21.1 1.3 %collective-permute-start.6 = (f32[32,512]{1,0:T(8,128)S(1)}, f32[32,512]{1,0:T(8,128)S(1)}, u32[]{:S(2)}, u32[]{:S(2)}) collective-permute-start(f32[32,512]{1,0:T(8,128)S(1)} %get-tuple-element.19.kept_ref.summary_ref), channel_id=1, source_target_pairs={{0,8},{8,0},{16,24},{24,16},{32,40},{40,32},{48,56},{56,48},{64,72... | collective-permute-start | bytes 196616 | tf_op jit(solution)/shard_map/ppermute | solution.py:374
  22.5 5.7 %collective-permute-start.9 = (bf16[48,512]{1,0:T(8,128)(2,1)S(1)}, bf16[48,512]{1,0:T(8,128)(2,1)S(1)}, u32[]{:S(2)}, u32[]{:S(2)}) collective-permute-start(bf16[48,512]{1,0:T(8,128)(2,1)S(1)} %get-tuple-element.20.own_ref), channel_id=1, source_target_pairs={{0,32},{8,40},{16,48},{24,56},{32,0},{40,8},{48,16},{56,24},{64,96... | collective-permute-start | bytes 147464 | tf_op jit(solution)/shard_map/ppermute | solution.py:381
  25.6 4.1 %collective-permute-start.8 = (bf16[48,512]{1,0:T(8,128)(2,1)S(1)}, bf16[48,512]{1,0:T(8,128)(2,1)S(1)}, u32[]{:S(2)}, u32[]{:S(2)}) collective-permute-start(bf16[48,512]{1,0:T(8,128)(2,1)S(1)} %get-tuple-element.20.own_ref), channel_id=1, source_target_pairs={{0,48},{8,56},{16,0},{24,8},{32,16},{40,24},{48,32},{56,40},{64,11... | collective-permute-start | bytes 147464 | tf_op jit(solution)/shard_map/ppermute | solution.py:381
  26.7 5.3 %collective-permute-start.7 = (bf16[48,512]{1,0:T(8,128)(2,1)S(1)}, bf16[48,512]{1,0:T(8,128)(2,1)S(1)}, u32[]{:S(2)}, u32[]{:S(2)}) collective-permute-start(bf16[48,512]{1,0:T(8,128)(2,1)S(1)} %get-tuple-element.20.own_ref), channel_id=1, source_target_pairs={{0,16},{8,24},{16,32},{24,40},{32,48},{40,56},{48,0},{56,8},{64,80... | collective-permute-start | bytes 147464 | tf_op jit(solution)/shard_map/ppermute | solution.py:381
  32.1 6.2 %collective-permute-start.12 = (bf16[48,512]{1,0:T(8,128)(2,1)S(1)}, bf16[48,512]{1,0:T(8,128)(2,1)S(1)}, u32[]{:S(2)}, u32[]{:S(2)}) collective-permute-start(bf16[48,512]{1,0:T(8,128)(2,1)S(1)} %get-tuple-element.21.own_ref), channel_id=1, source_target_pairs={{0,128},{8,136},{16,144},{24,152},{32,160},{40,168},{48,176},{56,1... | collective-permute-start | bytes 147464 | tf_op jit(solution)/shard_map/ppermute | solution.py:381
  35.4 4.1 %collective-permute-start.11 = (bf16[48,512]{1,0:T(8,128)(2,1)S(1)}, bf16[48,512]{1,0:T(8,128)(2,1)S(1)}, u32[]{:S(2)}, u32[]{:S(2)}) collective-permute-start(bf16[48,512]{1,0:T(8,128)(2,1)S(1)} %get-tuple-element.21.own_ref), channel_id=1, source_target_pairs={{0,192},{8,200},{16,208},{24,216},{32,224},{40,232},{48,240},{56,2... | collective-permute-start | bytes 147464 | tf_op jit(solution)/shard_map/ppermute | solution.py:381
  36.5 5.3 %collective-permute-start.10 = (bf16[48,512]{1,0:T(8,128)(2,1)S(1)}, bf16[48,512]{1,0:T(8,128)(2,1)S(1)}, u32[]{:S(2)}, u32[]{:S(2)}) collective-permute-start(bf16[48,512]{1,0:T(8,128)(2,1)S(1)} %get-tuple-element.21.own_ref), channel_id=1, source_target_pairs={{0,64},{8,72},{16,80},{24,88},{32,96},{40,104},{48,112},{56,120},{... | collective-permute-start | bytes 147464 | tf_op jit(solution)/shard_map/ppermute | solution.py:381

commit v8 on v7

--- a/solution.py
+++ b/solution.py
@@ -1,5 +1,3 @@
-import functools
-
 import jax
 import jax.numpy as jnp
 from jax import lax
@@ -9,7 +7,7 @@
 
 LENGTH = 4096
 SUB = 16
-PIECES = 6
+PIECES = 8
 LANES = 128
 BLOCK = 128
 VMEM = pl.BlockSpec(memory_space=pltpu.VMEM)
@@ -31,23 +29,20 @@
             scratch[group, pl.ds(at, SUB), :] = block[stream, :, lanes].astype(jnp.float32)
 
 
-def join_kernel(at, own_ref, passed_ref, *refs):
-    out_ref = refs[-1]
+def join_kernel(own_ref, passed_ref, out_ref):
     out_ref[0] = own_ref[...]
-    out_ref[1] = passed_ref[at]
-
-
-def back_kernel(third_ref, second_ref, first_ref, out_ref):
-    for at, ref in enumerate((first_ref, second_ref, third_ref)):
-        out_ref[at] = ref[1]
+    out_ref[1] = passed_ref[...]
+
+
+def back_kernel(third_ref, _far, _near, out_ref):
+    out_ref[...] = third_ref[1]
 
 
 def with_sources(refs):
-    far, third, second, first, back, own = refs
+    *near, third, far, back, own = refs
     me = lax.axis_index("tp")
     turn = 1 - 2 * core_index()
-    places = [(own, 0), (far, 4), (first.at[0], 1), (second.at[0], 2), (third.at[0], 3)]
-    places += [(back.at[k - 1], -k) for k in (1, 2, 3)]
+    places = [(own, 0), (far, 4), (third.at[0], 3), (back, -3), *zip(near, (1, -1, 2, -2))]
     return [(ref, lax.rem(me - turn * shift + 8, 8)) for ref, shift in places]
 
 
@@ -353,18 +348,14 @@
             route += [(c * parts + z, c * parts + (z + step) % parts) for z in range(parts)]
         return lax.ppermute(value, ("ctx", "tp"), route)
 
-    passed = lax.ppermute(jnp.stack([block_for(-k) for k in (1, 2, 3)]), "ctx", swap)
+    passed = lax.ppermute(block_for(-3), "ctx", swap)
     far = along(block_for(4), 4)
+    one = jax.ShapeDtypeStruct((3, SUB, channels), streams.dtype)
     two = jax.ShapeDtypeStruct((2, 3, SUB, channels), streams.dtype)
-    three = jax.ShapeDtypeStruct((3, 3, SUB, channels), streams.dtype)
-
-    def both(shift, *after):
-        return kernel(functools.partial(join_kernel, shift - 1), two, (block_for(shift), passed, *after), name="join")
-
-    third, second = (along(both(k), k) for k in (3, 2))
-    first = along(both(1, far), 1)
-    back = lax.ppermute(kernel(back_kernel, three, (third, second, first)), "ctx", swap)
-    blocks = [far, third, second, first, back, block_for(0)]
+    third = along(kernel(join_kernel, two, (block_for(3), passed)), 3)
+    near = {k: along(block_for(k), k) for k in (2, -2, 1, -1)}
+    back = lax.ppermute(kernel(back_kernel, one, (third, far, near[-1])), "ctx", swap)
+    blocks = [near[1], near[-1], near[2], near[-2], third, far, back, block_for(0)]
     summary, ends, signal = kernel(
         state_kernel,
         (packed, spans, wide),

time: 43.2 us -> 43.3 us (level)
  starting transfers between devices: 19.8 us -> 23.8 us
  waiting for transfers between devices: 18.6 us -> 14.7 us
    ppermute x4 -> x6, waiting for transfers between devices: 8.91 us -> 4.32 us  [along(): return lax.ppermute(value, ('ctx', 'tp'), route)]
    ppermute x4 -> x6, starting transfers between devices: 8.89 us -> 13.1 us  [along(): return lax.ppermute(value, ('ctx', 'tp'), route)]
    ppermute x2, waiting for transfers between devices: 0.71 us -> 1.22 us  [the longest x1 1.22 us: body(): passed = lax.ppermute(block_for(-3), 'ctx', swap)]
    pallas_call x11 -> x9, Pallas kernels: 2.96 us -> 2.94 us  [kernel(): pl.pallas_call(function, out_shape=out_shape, in_specs=[VMEM] * len(opera...]
  transfers between devices with their start and end apart: 13 -> 15, of which waited for: 10 -> 10; matrix products, arithmetic and copies ran while one was open for 0% -> 0% of each run, Pallas kernels for 2% -> 2%
where the time goes in v8:
time: 43.3 us; the launch traced here: 43.1 us
  starting transfers between devices  23.8 us (55%)
  waiting for transfers between devices  14.7 us (34%)
  Pallas kernels  2.94 us (7%)
  local copies, waits for them, and re-layouts  1.56 us (4%)
    ppermute x6, starting transfers between devices, along(): return lax.ppermute(value, ('ctx', 'tp'), route)  13.1 us
    ppermute x6, starting transfers between devices, around(): parts[by] = lax.ppermute(value, 'ctx', route)  10.4 us
    ppermute x6, waiting for transfers between devices, around(): parts[by] = lax.ppermute(value, 'ctx', route)  7.87 us
    ppermute x6, waiting for transfers between devices, along(): return lax.ppermute(value, ('ctx', 'tp'), route)  4.32 us
    pallas_call x9, Pallas kernels, kernel(): pl.pallas_call(function, out_shape=out_shape, in_specs=[VMEM] * len(opera...  2.94 us
    ppermute x1, waiting for transfers between devices, body(): got = lax.ppermute(summary, 'ctx', swap)  1.24 us
    ppermute x1, waiting for transfers between devices, body(): passed = lax.ppermute(block_for(-3), 'ctx', swap)  1.22 us
    dynamic_slice x1, local copies, waits for them, and re-layouts, block_for(): return lax.dynamic_slice(by_stream, (0, 0, at), (3, SUB, channels))  0.99 us
  transfers between devices with their start and end apart: 15, of which 10 were waited for; matrix products, arithmetic and copies ran while one was open for 0% of the time, Pallas kernels for 2%

profile of v8, /device:TPU:32, one launch (start us, length us, event | category | flops | bytes accessed | tf_op | source)
XLA Modules:
  0.0 43.1 jit_solution(548552923806717541)
XLA Ops:
  0.0 1.0 %dynamic-slice_bitcast_fusion = (bf16[3,16,512]{2,1,0:T(8,128)(2,1)S(1)}, bf16[3,16,512]{2,1,0:T(8,128)(2,1)S(1)}, bf16[3,16,512]{2,1,0:T(8,128)(2,1)S(1)}, bf16...) fusion(bf16[16,3,4096]{2,0,1:T(8,128)(2,1)} %param.5, ...), kind=kLoop, calls=%fused_computation | loop fusion | bytes 786464 | tf_op jit(solution)/shard_map/dynamic_slice | solution.py:342
  1.0 0.1 collective-permute-start.4
  1.1 1.2 %collective-permute-done.4.passed_ref = bf16[3,16,512]{2,1,0:T(8,128)(2,1)S(1)} collective-permute-done((bf16[3,16,512]{2,1,0:T(8,128)(2,1)S(1)}, bf16[3,16,512]{2,1,0:T(8,128)(2,1)S(1)}, u32[]{:S(2)}, u32[]{:S(2)}) %collective-permute-start.4) | collective-permute-done | bytes 49184 | tf_op jit(solution)/shard_map/ppermute | solution.py:351
  2.3 5.9 %collective-permute-start.5 = (bf16[2,3,16,512]{3,2,1,0:T(8,128)(2,1)S(1)}, bf16[2,3,16,512]{3,2,1,0:T(8,128)(2,1)S(1)}, u32[]{:S(2)}, u32[]{:S(2)}) collective-permute-start(bf16[2,3,16,512]{3,2,1,0:T(8,128)(2,1)S(1)} %join_kernel.1), channel_id=1, source_target_pairs={{0,3},{1,4},{2,5},{3,6},{4,7},{5,0},{6,1},{7,2},{8,13},{9,14},{10,... | collective-permute-start | bytes 294920 | tf_op jit(solution)/shard_map/ppermute | solution.py:349
  8.2 0.0 collective-permute-start.1
  8.2 3.4 %collective-permute-start.6 = (bf16[3,16,512]{2,1,0:T(8,128)(2,1)S(1)}, bf16[3,16,512]{2,1,0:T(8,128)(2,1)S(1)}, u32[]{:S(2)}, u32[]{:S(2)}) collective-permute-start(bf16[3,16,512]{2,1,0:T(8,128)(2,1)S(1)} %get-tuple-element.36), channel_id=1, source_target_pairs={{0,4},{1,5},{2,6},{3,7},{4,0},{5,1},{6,2},{7,3},{8,12},{9,13},{10,... | collective-permute-start | bytes 147464 | tf_op jit(solution)/shard_map/ppermute | solution.py:349
  11.6 2.7 %collective-permute-start.3 = (bf16[3,16,512]{2,1,0:T(8,128)(2,1)S(1)}, bf16[3,16,512]{2,1,0:T(8,128)(2,1)S(1)}, u32[]{:S(2)}, u32[]{:S(2)}) collective-permute-start(bf16[3,16,512]{2,1,0:T(8,128)(2,1)S(1)} %get-tuple-element.32), channel_id=1, source_target_pairs={{0,6},{1,7},{2,0},{3,1},{4,2},{5,3},{6,4},{7,5},{8,10},{9,11},{10,... | collective-permute-start | bytes 147464 | tf_op jit(solution)/shard_map/ppermute | solution.py:349
  14.3 0.3 collective-permute-start.2
  14.6 0.0 collective-permute-done.1._near.refs_1_
  14.6 0.0 copy-start
  14.6 0.0 copy-start.2
  14.6 0.8 %collective-permute-start = (bf16[3,16,512]{2,1,0:T(8,128)(2,1)S(1)}, bf16[3,16,512]{2,1,0:T(8,128)(2,1)S(1)}, u32[]{:S(2)}, u32[]{:S(2)}) collective-permute-start(bf16[3,16,512]{2,1,0:T(8,128)(2,1)S(1)} %get-tuple-element.35), channel_id=1, source_target_pairs={{0,1},{1,2},{2,3},{3,4},{4,5},{5,6},{6,7},{7,0},{8,15},{9,8},{10,9... | collective-permute-start | bytes 147464 | tf_op jit(solution)/shard_map/ppermute | solution.py:349
  15.4 1.3 %collective-permute-done.6._far.refs_5_ = bf16[3,16,512]{2,1,0:T(8,128)(2,1)S(1)} collective-permute-done((bf16[3,16,512]{2,1,0:T(8,128)(2,1)S(1)}, bf16[3,16,512]{2,1,0:T(8,128)(2,1)S(1)}, u32[]{:S(2)}, u32[]{:S(2)}) %collective-permute-start.6) | collective-permute-done | bytes 49184 | tf_op jit(solution)/shard_map/ppermute | solution.py:349
  16.7 0.0 collective-permute-done.5.third_ref.refs_4_
  16.7 0.0 copy-start.3
  16.7 0.1 collective-permute-start.7
  16.8 0.0 copy-done
  16.8 0.0 copy-done.2
  16.8 0.6 %copy-done.3 = f32[512]{0:T(512)S(1)} copy-done((f32[512]{0:T(512)S(1)}, f32[512]{0:T(512)}, u32[]{:S(2)}) %copy-start.3) | copy-done | bytes 2072
  17.4 0.0 copy-start.1
  17.4 0.1 weights_kernel.1
  17.5 0.5 %collective-permute-done.3.refs_3_ = bf16[3,16,512]{2,1,0:T(8,128)(2,1)S(1)} collective-permute-done((bf16[3,16,512]{2,1,0:T(8,128)(2,1)S(1)}, bf16[3,16,512]{2,1,0:T(8,128)(2,1)S(1)}, u32[]{:S(2)}, u32[]{:S(2)}) %collective-permute-start.3) | collective-permute-done | bytes 49184 | tf_op jit(solution)/shard_map/ppermute | solution.py:349
  18.0 2.5 %collective-permute-done.2.refs_2_ = bf16[3,16,512]{2,1,0:T(8,128)(2,1)S(1)} collective-permute-done((bf16[3,16,512]{2,1,0:T(8,128)(2,1)S(1)}, bf16[3,16,512]{2,1,0:T(8,128)(2,1)S(1)}, u32[]{:S(2)}, u32[]{:S(2)}) %collective-permute-start.2) | collective-permute-done | bytes 49184 | tf_op jit(solution)/shard_map/ppermute | solution.py:349
  20.5 0.0 collective-permute-done.refs_0_
  20.5 0.0 collective-permute-done.7.refs_6_
  20.5 0.0 copy-done.1
  20.5 0.6 %state_kernel.1 = (f32[32,512]{1,0:T(8,128)S(1)}, f32[16,8,512]{2,1,0:T(8,128)S(1)}, f32[16,8,512]{2,1,0:T(8,128)S(1)}) custom-call(bf16[3,16,512]{2,1,0:T(8,128)(2,1)S(1)} %collective-permute-done.refs_0_, bf16[3,16,512]{2,1,0:T(8,128)(2,1)S(1)} %collective-permute-done.1._near.refs_1_, bf16[3,16,512]{2,1,0:T(8,128)(2,1)S(1)} %collective-permute-done.2.refs_2_, ...), custom_call_target="tpu_custom_call" | custom-call | tf_op jit(solution)/shard_map/state_kernel/pallas_call | solution.py:320
  21.1 0.1 collective-permute-start.8
  21.2 1.2 %collective-permute-done.8.got_ref = f32[32,512]{1,0:T(8,128)S(1)} collective-permute-done((f32[32,512]{1,0:T(8,128)S(1)}, f32[32,512]{1,0:T(8,128)S(1)}, u32[]{:S(2)}, u32[]{:S(2)}) %collective-permute-start.8) | collective-permute-done | bytes 65568 | tf_op jit(solution)/shard_map/ppermute | solution.py:365
  22.5 3.1 %collective-permute-start.11 = (bf16[48,512]{1,0:T(8,128)(2,1)S(1)}, bf16[48,512]{1,0:T(8,128)(2,1)S(1)}, u32[]{:S(2)}, u32[]{:S(2)}) collective-permute-start(bf16[48,512]{1,0:T(8,128)(2,1)S(1)} %get-tuple-element.20.own_ref), channel_id=1, source_target_pairs={{0,32},{8,40},{16,48},{24,56},{32,0},{40,8},{48,16},{56,24},{64,96... | collective-permute-start | bytes 147464 | tf_op jit(solution)/shard_map/ppermute | solution.py:372
  25.6 1.1 %collective-permute-start.10 = (bf16[48,512]{1,0:T(8,128)(2,1)S(1)}, bf16[48,512]{1,0:T(8,128)(2,1)S(1)}, u32[]{:S(2)}, u32[]{:S(2)}) collective-permute-start(bf16[48,512]{1,0:T(8,128)(2,1)S(1)} %get-tuple-element.20.own_ref), channel_id=1, source_target_pairs={{0,48},{8,56},{16,0},{24,8},{32,16},{40,24},{48,32},{56,40},{64,11... | collective-permute-start | bytes 147464 | tf_op jit(solution)/shard_map/ppermute | solution.py:372
  26.8 0.9 %collective-permute-start.9 = (bf16[48,512]{1,0:T(8,128)(2,1)S(1)}, bf16[48,512]{1,0:T(8,128)(2,1)S(1)}, u32[]{:S(2)}, u32[]{:S(2)}) collective-permute-start(bf16[48,512]{1,0:T(8,128)(2,1)S(1)} %get-tuple-element.20.own_ref), channel_id=1, source_target_pairs={{0,16},{8,24},{16,32},{24,40},{32,48},{40,56},{48,0},{56,8},{64,80... | collective-permute-start | bytes 147464 | tf_op jit(solution)/shard_map/ppermute | solution.py:372
  27.6 0.5 %collective-permute-done.11.two_ref = bf16[48,512]{1,0:T(8,128)(2,1)S(1)} collective-permute-done((bf16[48,512]{1,0:T(8,128)(2,1)S(1)}, bf16[48,512]{1,0:T(8,128)(2,1)S(1)}, u32[]{:S(2)}, u32[]{:S(2)}) %collective-permute-start.11) | collective-permute-done | bytes 49184 | tf_op jit(solution)/shard_map/ppermute | solution.py:372
  28.2 1.5 %collective-permute-done.10.three_ref = bf16[48,512]{1,0:T(8,128)(2,1)S(1)} collective-permute-done((bf16[48,512]{1,0:T(8,128)(2,1)S(1)}, bf16[48,512]{1,0:T(8,128)(2,1)S(1)}, u32[]{:S(2)}, u32[]{:S(2)}) %collective-permute-start.10) | collective-permute-done | bytes 49184 | tf_op jit(solution)/shard_map/ppermute | solution.py:372
  29.7 2.4 %collective-permute-done.9.one_ref = bf16[48,512]{1,0:T(8,128)(2,1)S(1)} collective-permute-done((bf16[48,512]{1,0:T(8,128)(2,1)S(1)}, bf16[48,512]{1,0:T(8,128)(2,1)S(1)}, u32[]{:S(2)}, u32[]{:S(2)}) %collective-permute-start.9) | collective-permute-done | bytes 49184 | tf_op jit(solution)/shard_map/ppermute | solution.py:372
  32.1 0.1 row_kernel.1
  32.2 3.3 %collective-permute-start.14 = (bf16[48,512]{1,0:T(8,128)(2,1)S(1)}, bf16[48,512]{1,0:T(8,128)(2,1)S(1)}, u32[]{:S(2)}, u32[]{:S(2)}) collective-permute-start(bf16[48,512]{1,0:T(8,128)(2,1)S(1)} %get-tuple-element.21.own_ref), channel_id=1, source_target_pairs={{0,128},{8,136},{16,144},{24,152},{32,160},{40,168},{48,176},{56,1... | collective-permute-start | bytes 147464 | tf_op jit(solution)/shard_map/ppermute | solution.py:372
  35.5 1.1 %collective-permute-start.13 = (bf16[48,512]{1,0:T(8,128)(2,1)S(1)}, bf16[48,512]{1,0:T(8,128)(2,1)S(1)}, u32[]{:S(2)}, u32[]{:S(2)}) collective-permute-start(bf16[48,512]{1,0:T(8,128)(2,1)S(1)} %get-tuple-element.21.own_ref), channel_id=1, source_target_pairs={{0,192},{8,200},{16,208},{24,216},{32,224},{40,232},{48,240},{56,2... | collective-permute-start | bytes 147464 | tf_op jit(solution)/shard_map/ppermute | solution.py:372
  36.5 1.0 %collective-permute-start.12 = (bf16[48,512]{1,0:T(8,128)(2,1)S(1)}, bf16[48,512]{1,0:T(8,128)(2,1)S(1)}, u32[]{:S(2)}, u32[]{:S(2)}) collective-permute-start(bf16[48,512]{1,0:T(8,128)(2,1)S(1)} %get-tuple-element.21.own_ref), channel_id=1, source_target_pairs={{0,64},{8,72},{16,80},{24,88},{32,96},{40,104},{48,112},{56,120},{... | collective-permute-start | bytes 147464 | tf_op jit(solution)/shard_map/ppermute | solution.py:372
  37.5 0.9 %local_kernel.1 = (f32[16,8,512]{2,1,0:T(8,128)S(1)}, f32[16,8,512]{2,1,0:T(8,128)S(1)}) custom-call(bf16[3,16,512]{2,1,0:T(8,128)(2,1)S(1)} %collective-permute-done.refs_0_, bf16[3,16,512]{2,1,0:T(8,128)(2,1)S(1)} %collective-permute-done.1._near.refs_1_, bf16[3,16,512]{2,1,0:T(8,128)(2,1)S(1)} %collective-permute-done.2.refs_2_, ...), custom_call_target="tpu_custom_call" | custom-call | flops 8388608 | bytes 2097152 | tf_op jit(solution)/shard_map/local_kernel/pallas_call | solution.py:320
  38.4 0.0 collective-permute-done.14.two_ref
  38.4 1.2 %collective-permute-done.13.three_ref = bf16[48,512]{1,0:T(8,128)(2,1)S(1)} collective-permute-done((bf16[48,512]{1,0:T(8,128)(2,1)S(1)}, bf16[48,512]{1,0:T(8,128)(2,1)S(1)}, u32[]{:S(2)}, u32[]{:S(2)}) %collective-permute-start.13) | collective-permute-done | bytes 49184 | tf_op jit(solution)/shard_map/ppermute | solution.py:372
  39.6 2.3 %collective-permute-done.12.one_ref = bf16[48,512]{1,0:T(8,128)(2,1)S(1)} collective-permute-done((bf16[48,512]{1,0:T(8,128)(2,1)S(1)}, bf16[48,512]{1,0:T(8,128)(2,1)S(1)}, u32[]{:S(2)}, u32[]{:S(2)}) %collective-permute-start.12) | collective-permute-done | bytes 49184 | tf_op jit(solution)/shard_map/ppermute | solution.py:372
  41.8 0.1 merge_kernel.1.carry_ref
  42.0 1.1 %final_kernel.1 = bf16[128,512]{1,0:T(8,128)(2,1)} custom-call(f32[24,512]{1,0:T(8,128)S(1)} %merge_kernel.1.carry_ref, f32[32,512]{1,0:T(8,128)S(1)} %get-tuple-element.19.kept_ref.summary_ref, f32[3,3,512]{2,1,0:T(4,128)S(1)} %copy-done.1, f32[16,512]{1,0:T(8,128)S(1)} %copy-done, f32[16,512]{1,0:T(8,128)S(1)} %copy-done.2, f32[1,512]{1,0:T(1,128)S(1)} %bitcast.19, ...), custom_call_target="tpu_custom_call" | custom-call | tf_op jit(solution)/shard_map/final_kernel/pallas_call | solution.py:320
  (3 shorter events, 0.1 us)
Async XLA Ops:
  1.0 1.3 %collective-permute-start.4 = (bf16[3,16,512]{2,1,0:T(8,128)(2,1)S(1)}, bf16[3,16,512]{2,1,0:T(8,128)(2,1)S(1)}, u32[]{:S(2)}, u32[]{:S(2)}) collective-permute-start(bf16[3,16,512]{2,1,0:T(8,128)(2,1)S(1)} %get-tuple-element.30), channel_id=1, source_target_pairs={{0,8},{8,0},{16,24},{24,16},{32,40},{40,32},{48,56},{56,48},{64,72... | collective-permute-start | bytes 147464 | tf_op jit(solution)/shard_map/ppermute | solution.py:351
  2.3 14.4 %collective-permute-start.5 = (bf16[2,3,16,512]{3,2,1,0:T(8,128)(2,1)S(1)}, bf16[2,3,16,512]{3,2,1,0:T(8,128)(2,1)S(1)}, u32[]{:S(2)}, u32[]{:S(2)}) collective-permute-start(bf16[2,3,16,512]{3,2,1,0:T(8,128)(2,1)S(1)} %join_kernel.1), channel_id=1, source_target_pairs={{0,3},{1,4},{2,5},{3,6},{4,7},{5,0},{6,1},{7,2},{8,13},{9,14},{10,... | collective-permute-start | bytes 294920 | tf_op jit(solution)/shard_map/ppermute | solution.py:349
  8.2 6.3 %collective-permute-start.1 = (bf16[3,16,512]{2,1,0:T(8,128)(2,1)S(1)}, bf16[3,16,512]{2,1,0:T(8,128)(2,1)S(1)}, u32[]{:S(2)}, u32[]{:S(2)}) collective-permute-start(bf16[3,16,512]{2,1,0:T(8,128)(2,1)S(1)} %get-tuple-element.34), channel_id=1, source_target_pairs={{0,7},{1,0},{2,1},{3,2},{4,3},{5,4},{6,5},{7,6},{8,9},{9,10},{10,1... | collective-permute-start | bytes 147464 | tf_op jit(solution)/shard_map/ppermute | solution.py:349
  8.2 8.4 %collective-permute-start.6 = (bf16[3,16,512]{2,1,0:T(8,128)(2,1)S(1)}, bf16[3,16,512]{2,1,0:T(8,128)(2,1)S(1)}, u32[]{:S(2)}, u32[]{:S(2)}) collective-permute-start(bf16[3,16,512]{2,1,0:T(8,128)(2,1)S(1)} %get-tuple-element.36), channel_id=1, source_target_pairs={{0,4},{1,5},{2,6},{3,7},{4,0},{5,1},{6,2},{7,3},{8,12},{9,13},{10,... | collective-permute-start | bytes 147464 | tf_op jit(solution)/shard_map/ppermute | solution.py:349
  11.6 6.3 %collective-permute-start.3 = (bf16[3,16,512]{2,1,0:T(8,128)(2,1)S(1)}, bf16[3,16,512]{2,1,0:T(8,128)(2,1)S(1)}, u32[]{:S(2)}, u32[]{:S(2)}) collective-permute-start(bf16[3,16,512]{2,1,0:T(8,128)(2,1)S(1)} %get-tuple-element.32), channel_id=1, source_target_pairs={{0,6},{1,7},{2,0},{3,1},{4,2},{5,3},{6,4},{7,5},{8,10},{9,11},{10,... | collective-permute-start | bytes 147464 | tf_op jit(solution)/shard_map/ppermute | solution.py:349
  14.3 6.2 %collective-permute-start.2 = (bf16[3,16,512]{2,1,0:T(8,128)(2,1)S(1)}, bf16[3,16,512]{2,1,0:T(8,128)(2,1)S(1)}, u32[]{:S(2)}, u32[]{:S(2)}) collective-permute-start(bf16[3,16,512]{2,1,0:T(8,128)(2,1)S(1)} %get-tuple-element.33), channel_id=1, source_target_pairs={{0,2},{1,3},{2,4},{3,5},{4,6},{5,7},{6,0},{7,1},{8,14},{9,15},{10,... | collective-permute-start | bytes 147464 | tf_op jit(solution)/shard_map/ppermute | solution.py:349
  14.6 2.2 %copy-start = (f32[16,512]{1,0:T(8,128)S(1)}, f32[16,512]{1,0:T(8,128)}, u32[]{:S(2)}) copy-start(f32[16,512]{1,0:T(8,128)} %rates_ref.9) | copy-start | bytes 98308
  14.6 2.2 %copy-start.2 = (f32[16,512]{1,0:T(8,128)S(1)}, f32[16,512]{1,0:T(8,128)}, u32[]{:S(2)}) copy-start(f32[16,512]{1,0:T(8,128)} %residues_ref.3) | copy-start | bytes 98308
  14.6 5.9 %collective-permute-start = (bf16[3,16,512]{2,1,0:T(8,128)(2,1)S(1)}, bf16[3,16,512]{2,1,0:T(8,128)(2,1)S(1)}, u32[]{:S(2)}, u32[]{:S(2)}) collective-permute-start(bf16[3,16,512]{2,1,0:T(8,128)(2,1)S(1)} %get-tuple-element.35), channel_id=1, source_target_pairs={{0,1},{1,2},{2,3},{3,4},{4,5},{5,6},{6,7},{7,0},{8,15},{9,8},{10,9... | collective-permute-start | bytes 147464 | tf_op jit(solution)/shard_map/ppermute | solution.py:349
  16.7 0.7 %copy-start.3 = (f32[512]{0:T(512)S(1)}, f32[512]{0:T(512)}, u32[]{:S(2)}) copy-start(f32[512]{0:T(512)} %param.9) | copy-start | bytes 6148
  16.7 3.8 %collective-permute-start.7 = (bf16[3,16,512]{2,1,0:T(8,128)(2,1)S(1)}, bf16[3,16,512]{2,1,0:T(8,128)(2,1)S(1)}, u32[]{:S(2)}, u32[]{:S(2)}) collective-permute-start(bf16[3,16,512]{2,1,0:T(8,128)(2,1)S(1)} %back_kernel.1), channel_id=1, source_target_pairs={{0,8},{8,0},{16,24},{24,16},{32,40},{40,32},{48,56},{56,48},{64,72... | collective-permute-start | bytes 147464 | tf_op jit(solution)/shard_map/ppermute | solution.py:357
  17.4 3.1 %copy-start.1 = (f32[3,3,512]{2,1,0:T(4,128)S(1)}, f32[3,3,512]{2,1,0:T(4,128)}, u32[]{:S(2)}) copy-start(f32[3,3,512]{2,1,0:T(4,128)} %taps_ref.7) | copy-start | bytes 55300
  21.1 1.3 %collective-permute-start.8 = (f32[32,512]{1,0:T(8,128)S(1)}, f32[32,512]{1,0:T(8,128)S(1)}, u32[]{:S(2)}, u32[]{:S(2)}) collective-permute-start(f32[32,512]{1,0:T(8,128)S(1)} %get-tuple-element.19.kept_ref.summary_ref), channel_id=1, source_target_pairs={{0,8},{8,0},{16,24},{24,16},{32,40},{40,32},{48,56},{56,48},{64,72... | collective-permute-start | bytes 196616 | tf_op jit(solution)/shard_map/ppermute | solution.py:365
  22.5 5.7 %collective-permute-start.11 = (bf16[48,512]{1,0:T(8,128)(2,1)S(1)}, bf16[48,512]{1,0:T(8,128)(2,1)S(1)}, u32[]{:S(2)}, u32[]{:S(2)}) collective-permute-start(bf16[48,512]{1,0:T(8,128)(2,1)S(1)} %get-tuple-element.20.own_ref), channel_id=1, source_target_pairs={{0,32},{8,40},{16,48},{24,56},{32,0},{40,8},{48,16},{56,24},{64,96... | collective-permute-start | bytes 147464 | tf_op jit(solution)/shard_map/ppermute | solution.py:372
  25.6 4.1 %collective-permute-start.10 = (bf16[48,512]{1,0:T(8,128)(2,1)S(1)}, bf16[48,512]{1,0:T(8,128)(2,1)S(1)}, u32[]{:S(2)}, u32[]{:S(2)}) collective-permute-start(bf16[48,512]{1,0:T(8,128)(2,1)S(1)} %get-tuple-element.20.own_ref), channel_id=1, source_target_pairs={{0,48},{8,56},{16,0},{24,8},{32,16},{40,24},{48,32},{56,40},{64,11... | collective-permute-start | bytes 147464 | tf_op jit(solution)/shard_map/ppermute | solution.py:372
  26.8 5.3 %collective-permute-start.9 = (bf16[48,512]{1,0:T(8,128)(2,1)S(1)}, bf16[48,512]{1,0:T(8,128)(2,1)S(1)}, u32[]{:S(2)}, u32[]{:S(2)}) collective-permute-start(bf16[48,512]{1,0:T(8,128)(2,1)S(1)} %get-tuple-element.20.own_ref), channel_id=1, source_target_pairs={{0,16},{8,24},{16,32},{24,40},{32,48},{40,56},{48,0},{56,8},{64,80... | collective-permute-start | bytes 147464 | tf_op jit(solution)/shard_map/ppermute | solution.py:372
  32.2 6.2 %collective-permute-start.14 = (bf16[48,512]{1,0:T(8,128)(2,1)S(1)}, bf16[48,512]{1,0:T(8,128)(2,1)S(1)}, u32[]{:S(2)}, u32[]{:S(2)}) collective-permute-start(bf16[48,512]{1,0:T(8,128)(2,1)S(1)} %get-tuple-element.21.own_ref), channel_id=1, source_target_pairs={{0,128},{8,136},{16,144},{24,152},{32,160},{40,168},{48,176},{56,1... | collective-permute-start | bytes 147464 | tf_op jit(solution)/shard_map/ppermute | solution.py:372
  35.5 4.1 %collective-permute-start.13 = (bf16[48,512]{1,0:T(8,128)(2,1)S(1)}, bf16[48,512]{1,0:T(8,128)(2,1)S(1)}, u32[]{:S(2)}, u32[]{:S(2)}) collective-permute-start(bf16[48,512]{1,0:T(8,128)(2,1)S(1)} %get-tuple-element.21.own_ref), channel_id=1, source_target_pairs={{0,192},{8,200},{16,208},{24,216},{32,224},{40,232},{48,240},{56,2... | collective-permute-start | bytes 147464 | tf_op jit(solution)/shard_map/ppermute | solution.py:372
  36.5 5.3 %collective-permute-start.12 = (bf16[48,512]{1,0:T(8,128)(2,1)S(1)}, bf16[48,512]{1,0:T(8,128)(2,1)S(1)}, u32[]{:S(2)}, u32[]{:S(2)}) collective-permute-start(bf16[48,512]{1,0:T(8,128)(2,1)S(1)} %get-tuple-element.21.own_ref), channel_id=1, source_target_pairs={{0,64},{8,72},{16,80},{24,88},{32,96},{40,104},{48,112},{56,120},{... | collective-permute-start | bytes 147464 | tf_op jit(solution)/shard_map/ppermute | solution.py:372

commit v9 on v8

--- a/solution.py
+++ b/solution.py
@@ -34,7 +34,11 @@
     out_ref[1] = passed_ref[...]
 
 
-def back_kernel(third_ref, _far, _near, out_ref):
+def hold_kernel(own_ref, _, out_ref):
+    out_ref[...] = own_ref[...]
+
+
+def back_kernel(third_ref, _, out_ref):
     out_ref[...] = third_ref[1]
 
 
@@ -353,8 +357,9 @@
     one = jax.ShapeDtypeStruct((3, SUB, channels), streams.dtype)
     two = jax.ShapeDtypeStruct((2, 3, SUB, channels), streams.dtype)
     third = along(kernel(join_kernel, two, (block_for(3), passed)), 3)
-    near = {k: along(block_for(k), k) for k in (2, -2, 1, -1)}
-    back = lax.ppermute(kernel(back_kernel, one, (third, far, near[-1])), "ctx", swap)
+    near = {k: along(block_for(k), k) for k in (2, -2)}
+    near |= {k: along(kernel(hold_kernel, one, (block_for(k), far)), k) for k in (1, -1)}
+    back = lax.ppermute(kernel(back_kernel, one, (third, near[1])), "ctx", swap)
     blocks = [near[1], near[-1], near[2], near[-2], third, far, back, block_for(0)]
     summary, ends, signal = kernel(
         state_kernel,

time: 43.3 us -> 45.3 us (1.046)
  waiting for transfers between devices: 14.7 us -> 17.5 us
  starting transfers between devices: 23.8 us -> 22.9 us
    ppermute x6, waiting for transfers between devices: 4.32 us -> 8.42 us  [along(): return lax.ppermute(value, ('ctx', 'tp'), route)]
    ppermute x1, waiting for transfers between devices: 1.22 us -> 0.01 us  [body(): passed = lax.ppermute(block_for(-3), 'ctx', swap)]
    ppermute x6, starting transfers between devices: 13.1 us -> 12.2 us  [along(): return lax.ppermute(value, ('ctx', 'tp'), route)]
    pallas_call x9 -> x11, Pallas kernels: 2.94 us -> 2.94 us  [kernel(): pl.pallas_call(function, out_shape=out_shape, in_specs=[VMEM] * len(opera...]
where the time goes in v9:
time: 45.3 us; the launch traced here: 45 us
  starting transfers between devices  22.9 us (51%)
  waiting for transfers between devices  17.5 us (39%)
  Pallas kernels  2.94 us (6%)
  local copies, waits for them, and re-layouts  1.56 us (3%)
    ppermute x6, starting transfers between devices, along(): return lax.ppermute(value, ('ctx', 'tp'), route)  12.2 us
    ppermute x6, starting transfers between devices, around(): parts[by] = lax.ppermute(value, 'ctx', route)  10.4 us
    ppermute x6, waiting for transfers between devices, along(): return lax.ppermute(value, ('ctx', 'tp'), route)  8.42 us
    ppermute x6, waiting for transfers between devices, around(): parts[by] = lax.ppermute(value, 'ctx', route)  7.87 us
    pallas_call x11, Pallas kernels, kernel(): pl.pallas_call(function, out_shape=out_shape, in_specs=[VMEM] * len(opera...  2.94 us
    ppermute x1, waiting for transfers between devices, body(): got = lax.ppermute(summary, 'ctx', swap)  1.24 us
    dynamic_slice x1, local copies, waits for them, and re-layouts, block_for(): return lax.dynamic_slice(by_stream, (0, 0, at), (3, SUB, channels))  0.99 us
  transfers between devices with their start and end apart: 15, of which 10 were waited for; matrix products, arithmetic and copies ran while one was open for 0% of the time, Pallas kernels for 2%

profile of v9, /device:TPU:32, one launch (start us, length us, event | category | flops | bytes accessed | tf_op | source)
XLA Modules:
  0.0 45.0 jit_solution(5406257329069323620)
XLA Ops:
  0.0 1.0 %dynamic-slice_bitcast_fusion = (bf16[3,16,512]{2,1,0:T(8,128)(2,1)S(1)}, bf16[3,16,512]{2,1,0:T(8,128)(2,1)S(1)}, bf16[3,16,512]{2,1,0:T(8,128)(2,1)S(1)}, bf16...) fusion(bf16[16,3,4096]{2,0,1:T(8,128)(2,1)} %param.5, ...), kind=kLoop, calls=%fused_computation | loop fusion | bytes 786464 | tf_op jit(solution)/shard_map/dynamic_slice | solution.py:346
  1.0 0.1 collective-permute-start.5
  1.1 6.4 %collective-permute-start = (bf16[3,16,512]{2,1,0:T(8,128)(2,1)S(1)}, bf16[3,16,512]{2,1,0:T(8,128)(2,1)S(1)}, u32[]{:S(2)}, u32[]{:S(2)}) collective-permute-start(bf16[3,16,512]{2,1,0:T(8,128)(2,1)S(1)} %get-tuple-element.34), channel_id=1, source_target_pairs={{0,4},{1,5},{2,6},{3,7},{4,0},{5,1},{6,2},{7,3},{8,12},{9,13},{10,... | collective-permute-start | bytes 147464 | tf_op jit(solution)/shard_map/ppermute | solution.py:353
  7.5 0.0 collective-permute-done.5.passed_ref
  7.5 0.8 %collective-permute-start.6 = (bf16[2,3,16,512]{3,2,1,0:T(8,128)(2,1)S(1)}, bf16[2,3,16,512]{3,2,1,0:T(8,128)(2,1)S(1)}, u32[]{:S(2)}, u32[]{:S(2)}) collective-permute-start(bf16[2,3,16,512]{3,2,1,0:T(8,128)(2,1)S(1)} %join_kernel.1), channel_id=1, source_target_pairs={{0,3},{1,4},{2,5},{3,6},{4,7},{5,0},{6,1},{7,2},{8,13},{9,14},{10,... | collective-permute-start | bytes 294920 | tf_op jit(solution)/shard_map/ppermute | solution.py:353
  8.2 4.4 %collective-permute-done._.refs_5_ = bf16[3,16,512]{2,1,0:T(8,128)(2,1)S(1)} collective-permute-done((bf16[3,16,512]{2,1,0:T(8,128)(2,1)S(1)}, bf16[3,16,512]{2,1,0:T(8,128)(2,1)S(1)}, u32[]{:S(2)}, u32[]{:S(2)}) %collective-permute-start) | collective-permute-done | bytes 49184 | tf_op jit(solution)/shard_map/ppermute | solution.py:353
  12.6 0.0 collective-permute-start.1
  12.6 2.3 %collective-permute-start.4 = (bf16[3,16,512]{2,1,0:T(8,128)(2,1)S(1)}, bf16[3,16,512]{2,1,0:T(8,128)(2,1)S(1)}, u32[]{:S(2)}, u32[]{:S(2)}) collective-permute-start(bf16[3,16,512]{2,1,0:T(8,128)(2,1)S(1)} %get-tuple-element.31), channel_id=1, source_target_pairs={{0,6},{1,7},{2,0},{3,1},{4,2},{5,3},{6,4},{7,5},{8,10},{9,11},{10,... | collective-permute-start | bytes 147464 | tf_op jit(solution)/shard_map/ppermute | solution.py:353
  14.9 0.9 %collective-permute-start.3 = (bf16[3,16,512]{2,1,0:T(8,128)(2,1)S(1)}, bf16[3,16,512]{2,1,0:T(8,128)(2,1)S(1)}, u32[]{:S(2)}, u32[]{:S(2)}) collective-permute-start(bf16[3,16,512]{2,1,0:T(8,128)(2,1)S(1)} %get-tuple-element.32), channel_id=1, source_target_pairs={{0,2},{1,3},{2,4},{3,5},{4,6},{5,7},{6,0},{7,1},{8,14},{9,15},{10,... | collective-permute-start | bytes 147464 | tf_op jit(solution)/shard_map/ppermute | solution.py:353
  15.8 0.0 copy-start
  15.8 0.0 copy-start.2
  15.8 1.8 %collective-permute-start.2 = (bf16[3,16,512]{2,1,0:T(8,128)(2,1)S(1)}, bf16[3,16,512]{2,1,0:T(8,128)(2,1)S(1)}, u32[]{:S(2)}, u32[]{:S(2)}) collective-permute-start(bf16[3,16,512]{2,1,0:T(8,128)(2,1)S(1)} %hold_kernel.3), channel_id=1, source_target_pairs={{0,7},{1,0},{2,1},{3,2},{4,3},{5,4},{6,5},{7,6},{8,9},{9,10},{10,1... | collective-permute-start | bytes 147464 | tf_op jit(solution)/shard_map/ppermute | solution.py:353
  17.6 0.2 collective-permute-done.1._.refs_0_
  17.9 0.0 collective-permute-done.6.third_ref.refs_4_
  17.9 0.0 copy-start.3
  17.9 0.1 collective-permute-start.7
  18.0 0.0 copy-done
  18.0 0.0 copy-done.2
  18.0 0.6 %copy-done.3 = f32[512]{0:T(512)S(1)} copy-done((f32[512]{0:T(512)S(1)}, f32[512]{0:T(512)}, u32[]{:S(2)}) %copy-start.3) | copy-done | bytes 2072
  18.6 0.0 copy-start.1
  18.6 0.1 weights_kernel.1
  18.7 0.0 collective-permute-done.4.refs_3_
  18.7 3.6 %collective-permute-done.3.refs_2_ = bf16[3,16,512]{2,1,0:T(8,128)(2,1)S(1)} collective-permute-done((bf16[3,16,512]{2,1,0:T(8,128)(2,1)S(1)}, bf16[3,16,512]{2,1,0:T(8,128)(2,1)S(1)}, u32[]{:S(2)}, u32[]{:S(2)}) %collective-permute-start.3) | collective-permute-done | bytes 49184 | tf_op jit(solution)/shard_map/ppermute | solution.py:353
  22.3 0.2 collective-permute-done.2.refs_1_
  22.5 0.0 collective-permute-done.7.refs_6_
  22.5 0.0 copy-done.1
  22.5 0.6 %state_kernel.1 = (f32[32,512]{1,0:T(8,128)S(1)}, f32[16,8,512]{2,1,0:T(8,128)S(1)}, f32[16,8,512]{2,1,0:T(8,128)S(1)}) custom-call(bf16[3,16,512]{2,1,0:T(8,128)(2,1)S(1)} %collective-permute-done.1._.refs_0_, bf16[3,16,512]{2,1,0:T(8,128)(2,1)S(1)} %collective-permute-done.2.refs_1_, bf16[3,16,512]{2,1,0:T(8,128)(2,1)S(1)} %collective-permute-done.3.refs_2_, ...), custom_call_target="tpu_custom_call" | custom-call | tf_op jit(solution)/shard_map/state_kernel/pallas_call | solution.py:324
  23.1 0.1 collective-permute-start.8
  23.2 1.2 %collective-permute-done.8.got_ref = f32[32,512]{1,0:T(8,128)S(1)} collective-permute-done((f32[32,512]{1,0:T(8,128)S(1)}, f32[32,512]{1,0:T(8,128)S(1)}, u32[]{:S(2)}, u32[]{:S(2)}) %collective-permute-start.8) | collective-permute-done | bytes 65568 | tf_op jit(solution)/shard_map/ppermute | solution.py:370
  24.5 3.1 %collective-permute-start.11 = (bf16[48,512]{1,0:T(8,128)(2,1)S(1)}, bf16[48,512]{1,0:T(8,128)(2,1)S(1)}, u32[]{:S(2)}, u32[]{:S(2)}) collective-permute-start(bf16[48,512]{1,0:T(8,128)(2,1)S(1)} %get-tuple-element.20.own_ref), channel_id=1, source_target_pairs={{0,32},{8,40},{16,48},{24,56},{32,0},{40,8},{48,16},{56,24},{64,96... | collective-permute-start | bytes 147464 | tf_op jit(solution)/shard_map/ppermute | solution.py:377
  27.6 1.1 %collective-permute-start.10 = (bf16[48,512]{1,0:T(8,128)(2,1)S(1)}, bf16[48,512]{1,0:T(8,128)(2,1)S(1)}, u32[]{:S(2)}, u32[]{:S(2)}) collective-permute-start(bf16[48,512]{1,0:T(8,128)(2,1)S(1)} %get-tuple-element.20.own_ref), channel_id=1, source_target_pairs={{0,48},{8,56},{16,0},{24,8},{32,16},{40,24},{48,32},{56,40},{64,11... | collective-permute-start | bytes 147464 | tf_op jit(solution)/shard_map/ppermute | solution.py:377
  28.7 0.9 %collective-permute-start.9 = (bf16[48,512]{1,0:T(8,128)(2,1)S(1)}, bf16[48,512]{1,0:T(8,128)(2,1)S(1)}, u32[]{:S(2)}, u32[]{:S(2)}) collective-permute-start(bf16[48,512]{1,0:T(8,128)(2,1)S(1)} %get-tuple-element.20.own_ref), channel_id=1, source_target_pairs={{0,16},{8,24},{16,32},{24,40},{32,48},{40,56},{48,0},{56,8},{64,80... | collective-permute-start | bytes 147464 | tf_op jit(solution)/shard_map/ppermute | solution.py:377
  29.6 0.6 %collective-permute-done.11.two_ref = bf16[48,512]{1,0:T(8,128)(2,1)S(1)} collective-permute-done((bf16[48,512]{1,0:T(8,128)(2,1)S(1)}, bf16[48,512]{1,0:T(8,128)(2,1)S(1)}, u32[]{:S(2)}, u32[]{:S(2)}) %collective-permute-start.11) | collective-permute-done | bytes 49184 | tf_op jit(solution)/shard_map/ppermute | solution.py:377
  30.2 1.5 %collective-permute-done.10.three_ref = bf16[48,512]{1,0:T(8,128)(2,1)S(1)} collective-permute-done((bf16[48,512]{1,0:T(8,128)(2,1)S(1)}, bf16[48,512]{1,0:T(8,128)(2,1)S(1)}, u32[]{:S(2)}, u32[]{:S(2)}) %collective-permute-start.10) | collective-permute-done | bytes 49184 | tf_op jit(solution)/shard_map/ppermute | solution.py:377
  31.7 2.4 %collective-permute-done.9.one_ref = bf16[48,512]{1,0:T(8,128)(2,1)S(1)} collective-permute-done((bf16[48,512]{1,0:T(8,128)(2,1)S(1)}, bf16[48,512]{1,0:T(8,128)(2,1)S(1)}, u32[]{:S(2)}, u32[]{:S(2)}) %collective-permute-start.9) | collective-permute-done | bytes 49184 | tf_op jit(solution)/shard_map/ppermute | solution.py:377
  34.0 0.1 row_kernel.1
  34.2 3.3 %collective-permute-start.14 = (bf16[48,512]{1,0:T(8,128)(2,1)S(1)}, bf16[48,512]{1,0:T(8,128)(2,1)S(1)}, u32[]{:S(2)}, u32[]{:S(2)}) collective-permute-start(bf16[48,512]{1,0:T(8,128)(2,1)S(1)} %get-tuple-element.21.own_ref), channel_id=1, source_target_pairs={{0,128},{8,136},{16,144},{24,152},{32,160},{40,168},{48,176},{56,1... | collective-permute-start | bytes 147464 | tf_op jit(solution)/shard_map/ppermute | solution.py:377
  37.4 1.1 %collective-permute-start.13 = (bf16[48,512]{1,0:T(8,128)(2,1)S(1)}, bf16[48,512]{1,0:T(8,128)(2,1)S(1)}, u32[]{:S(2)}, u32[]{:S(2)}) collective-permute-start(bf16[48,512]{1,0:T(8,128)(2,1)S(1)} %get-tuple-element.21.own_ref), channel_id=1, source_target_pairs={{0,192},{8,200},{16,208},{24,216},{32,224},{40,232},{48,240},{56,2... | collective-permute-start | bytes 147464 | tf_op jit(solution)/shard_map/ppermute | solution.py:377
  38.5 1.0 %collective-permute-start.12 = (bf16[48,512]{1,0:T(8,128)(2,1)S(1)}, bf16[48,512]{1,0:T(8,128)(2,1)S(1)}, u32[]{:S(2)}, u32[]{:S(2)}) collective-permute-start(bf16[48,512]{1,0:T(8,128)(2,1)S(1)} %get-tuple-element.21.own_ref), channel_id=1, source_target_pairs={{0,64},{8,72},{16,80},{24,88},{32,96},{40,104},{48,112},{56,120},{... | collective-permute-start | bytes 147464 | tf_op jit(solution)/shard_map/ppermute | solution.py:377
  39.5 0.9 %local_kernel.1 = (f32[16,8,512]{2,1,0:T(8,128)S(1)}, f32[16,8,512]{2,1,0:T(8,128)S(1)}) custom-call(bf16[3,16,512]{2,1,0:T(8,128)(2,1)S(1)} %collective-permute-done.1._.refs_0_, bf16[3,16,512]{2,1,0:T(8,128)(2,1)S(1)} %collective-permute-done.2.refs_1_, bf16[3,16,512]{2,1,0:T(8,128)(2,1)S(1)} %collective-permute-done.3.refs_2_, ...), custom_call_target="tpu_custom_call" | custom-call | flops 8388608 | bytes 2097152 | tf_op jit(solution)/shard_map/local_kernel/pallas_call | solution.py:324
  40.3 0.0 collective-permute-done.14.two_ref
  40.3 1.2 %collective-permute-done.13.three_ref = bf16[48,512]{1,0:T(8,128)(2,1)S(1)} collective-permute-done((bf16[48,512]{1,0:T(8,128)(2,1)S(1)}, bf16[48,512]{1,0:T(8,128)(2,1)S(1)}, u32[]{:S(2)}, u32[]{:S(2)}) %collective-permute-start.13) | collective-permute-done | bytes 49184 | tf_op jit(solution)/shard_map/ppermute | solution.py:377
  41.5 2.3 %collective-permute-done.12.one_ref = bf16[48,512]{1,0:T(8,128)(2,1)S(1)} collective-permute-done((bf16[48,512]{1,0:T(8,128)(2,1)S(1)}, bf16[48,512]{1,0:T(8,128)(2,1)S(1)}, u32[]{:S(2)}, u32[]{:S(2)}) %collective-permute-start.12) | collective-permute-done | bytes 49184 | tf_op jit(solution)/shard_map/ppermute | solution.py:377
  43.8 0.1 merge_kernel.1.carry_ref
  43.9 1.1 %final_kernel.1 = bf16[128,512]{1,0:T(8,128)(2,1)} custom-call(f32[24,512]{1,0:T(8,128)S(1)} %merge_kernel.1.carry_ref, f32[32,512]{1,0:T(8,128)S(1)} %get-tuple-element.19.kept_ref.summary_ref, f32[3,3,512]{2,1,0:T(4,128)S(1)} %copy-done.1, f32[16,512]{1,0:T(8,128)S(1)} %copy-done, f32[16,512]{1,0:T(8,128)S(1)} %copy-done.2, f32[1,512]{1,0:T(1,128)S(1)} %bitcast.19, ...), custom_call_target="tpu_custom_call" | custom-call | tf_op jit(solution)/shard_map/final_kernel/pallas_call | solution.py:324
  (5 shorter events, 0.1 us)
Async XLA Ops:
  1.0 6.5 %collective-permute-start.5 = (bf16[3,16,512]{2,1,0:T(8,128)(2,1)S(1)}, bf16[3,16,512]{2,1,0:T(8,128)(2,1)S(1)}, u32[]{:S(2)}, u32[]{:S(2)}) collective-permute-start(bf16[3,16,512]{2,1,0:T(8,128)(2,1)S(1)} %get-tuple-element.36), channel_id=1, source_target_pairs={{0,8},{8,0},{16,24},{24,16},{32,40},{40,32},{48,56},{56,48},{64,72... | collective-permute-start | bytes 147464 | tf_op jit(solution)/shard_map/ppermute | solution.py:355
  1.1 11.5 %collective-permute-start = (bf16[3,16,512]{2,1,0:T(8,128)(2,1)S(1)}, bf16[3,16,512]{2,1,0:T(8,128)(2,1)S(1)}, u32[]{:S(2)}, u32[]{:S(2)}) collective-permute-start(bf16[3,16,512]{2,1,0:T(8,128)(2,1)S(1)} %get-tuple-element.34), channel_id=1, source_target_pairs={{0,4},{1,5},{2,6},{3,7},{4,0},{5,1},{6,2},{7,3},{8,12},{9,13},{10,... | collective-permute-start | bytes 147464 | tf_op jit(solution)/shard_map/ppermute | solution.py:353
  7.5 10.4 %collective-permute-start.6 = (bf16[2,3,16,512]{3,2,1,0:T(8,128)(2,1)S(1)}, bf16[2,3,16,512]{3,2,1,0:T(8,128)(2,1)S(1)}, u32[]{:S(2)}, u32[]{:S(2)}) collective-permute-start(bf16[2,3,16,512]{3,2,1,0:T(8,128)(2,1)S(1)} %join_kernel.1), channel_id=1, source_target_pairs={{0,3},{1,4},{2,5},{3,6},{4,7},{5,0},{6,1},{7,2},{8,13},{9,14},{10,... | collective-permute-start | bytes 294920 | tf_op jit(solution)/shard_map/ppermute | solution.py:353
  12.6 5.3 %collective-permute-start.1 = (bf16[3,16,512]{2,1,0:T(8,128)(2,1)S(1)}, bf16[3,16,512]{2,1,0:T(8,128)(2,1)S(1)}, u32[]{:S(2)}, u32[]{:S(2)}) collective-permute-start(bf16[3,16,512]{2,1,0:T(8,128)(2,1)S(1)} %hold_kernel.2), channel_id=1, source_target_pairs={{0,1},{1,2},{2,3},{3,4},{4,5},{5,6},{6,7},{7,0},{8,15},{9,8},{10,9... | collective-permute-start | bytes 147464 | tf_op jit(solution)/shard_map/ppermute | solution.py:353
  12.6 6.1 %collective-permute-start.4 = (bf16[3,16,512]{2,1,0:T(8,128)(2,1)S(1)}, bf16[3,16,512]{2,1,0:T(8,128)(2,1)S(1)}, u32[]{:S(2)}, u32[]{:S(2)}) collective-permute-start(bf16[3,16,512]{2,1,0:T(8,128)(2,1)S(1)} %get-tuple-element.31), channel_id=1, source_target_pairs={{0,6},{1,7},{2,0},{3,1},{4,2},{5,3},{6,4},{7,5},{8,10},{9,11},{10,... | collective-permute-start | bytes 147464 | tf_op jit(solution)/shard_map/ppermute | solution.py:353
  14.9 7.4 %collective-permute-start.3 = (bf16[3,16,512]{2,1,0:T(8,128)(2,1)S(1)}, bf16[3,16,512]{2,1,0:T(8,128)(2,1)S(1)}, u32[]{:S(2)}, u32[]{:S(2)}) collective-permute-start(bf16[3,16,512]{2,1,0:T(8,128)(2,1)S(1)} %get-tuple-element.32), channel_id=1, source_target_pairs={{0,2},{1,3},{2,4},{3,5},{4,6},{5,7},{6,0},{7,1},{8,14},{9,15},{10,... | collective-permute-start | bytes 147464 | tf_op jit(solution)/shard_map/ppermute | solution.py:353
  15.8 2.2 %copy-start = (f32[16,512]{1,0:T(8,128)S(1)}, f32[16,512]{1,0:T(8,128)}, u32[]{:S(2)}) copy-start(f32[16,512]{1,0:T(8,128)} %rates_ref.9) | copy-start | bytes 98308
  15.8 2.2 %copy-start.2 = (f32[16,512]{1,0:T(8,128)S(1)}, f32[16,512]{1,0:T(8,128)}, u32[]{:S(2)}) copy-start(f32[16,512]{1,0:T(8,128)} %residues_ref.3) | copy-start | bytes 98308
  15.8 6.6 %collective-permute-start.2 = (bf16[3,16,512]{2,1,0:T(8,128)(2,1)S(1)}, bf16[3,16,512]{2,1,0:T(8,128)(2,1)S(1)}, u32[]{:S(2)}, u32[]{:S(2)}) collective-permute-start(bf16[3,16,512]{2,1,0:T(8,128)(2,1)S(1)} %hold_kernel.3), channel_id=1, source_target_pairs={{0,7},{1,0},{2,1},{3,2},{4,3},{5,4},{6,5},{7,6},{8,9},{9,10},{10,1... | collective-permute-start | bytes 147464 | tf_op jit(solution)/shard_map/ppermute | solution.py:353
  17.9 0.7 %copy-start.3 = (f32[512]{0:T(512)S(1)}, f32[512]{0:T(512)}, u32[]{:S(2)}) copy-start(f32[512]{0:T(512)} %param.9) | copy-start | bytes 6148
  17.9 4.6 %collective-permute-start.7 = (bf16[3,16,512]{2,1,0:T(8,128)(2,1)S(1)}, bf16[3,16,512]{2,1,0:T(8,128)(2,1)S(1)}, u32[]{:S(2)}, u32[]{:S(2)}) collective-permute-start(bf16[3,16,512]{2,1,0:T(8,128)(2,1)S(1)} %back_kernel.1), channel_id=1, source_target_pairs={{0,8},{8,0},{16,24},{24,16},{32,40},{40,32},{48,56},{56,48},{64,72... | collective-permute-start | bytes 147464 | tf_op jit(solution)/shard_map/ppermute | solution.py:362
  18.6 3.9 %copy-start.1 = (f32[3,3,512]{2,1,0:T(4,128)S(1)}, f32[3,3,512]{2,1,0:T(4,128)}, u32[]{:S(2)}) copy-start(f32[3,3,512]{2,1,0:T(4,128)} %taps_ref.7) | copy-start | bytes 55300
  23.1 1.3 %collective-permute-start.8 = (f32[32,512]{1,0:T(8,128)S(1)}, f32[32,512]{1,0:T(8,128)S(1)}, u32[]{:S(2)}, u32[]{:S(2)}) collective-permute-start(f32[32,512]{1,0:T(8,128)S(1)} %get-tuple-element.19.kept_ref.summary_ref), channel_id=1, source_target_pairs={{0,8},{8,0},{16,24},{24,16},{32,40},{40,32},{48,56},{56,48},{64,72... | collective-permute-start | bytes 196616 | tf_op jit(solution)/shard_map/ppermute | solution.py:370
  24.5 5.7 %collective-permute-start.11 = (bf16[48,512]{1,0:T(8,128)(2,1)S(1)}, bf16[48,512]{1,0:T(8,128)(2,1)S(1)}, u32[]{:S(2)}, u32[]{:S(2)}) collective-permute-start(bf16[48,512]{1,0:T(8,128)(2,1)S(1)} %get-tuple-element.20.own_ref), channel_id=1, source_target_pairs={{0,32},{8,40},{16,48},{24,56},{32,0},{40,8},{48,16},{56,24},{64,96... | collective-permute-start | bytes 147464 | tf_op jit(solution)/shard_map/ppermute | solution.py:377
  27.6 4.1 %collective-permute-start.10 = (bf16[48,512]{1,0:T(8,128)(2,1)S(1)}, bf16[48,512]{1,0:T(8,128)(2,1)S(1)}, u32[]{:S(2)}, u32[]{:S(2)}) collective-permute-start(bf16[48,512]{1,0:T(8,128)(2,1)S(1)} %get-tuple-element.20.own_ref), channel_id=1, source_target_pairs={{0,48},{8,56},{16,0},{24,8},{32,16},{40,24},{48,32},{56,40},{64,11... | collective-permute-start | bytes 147464 | tf_op jit(solution)/shard_map/ppermute | solution.py:377
  28.7 5.3 %collective-permute-start.9 = (bf16[48,512]{1,0:T(8,128)(2,1)S(1)}, bf16[48,512]{1,0:T(8,128)(2,1)S(1)}, u32[]{:S(2)}, u32[]{:S(2)}) collective-permute-start(bf16[48,512]{1,0:T(8,128)(2,1)S(1)} %get-tuple-element.20.own_ref), channel_id=1, source_target_pairs={{0,16},{8,24},{16,32},{24,40},{32,48},{40,56},{48,0},{56,8},{64,80... | collective-permute-start | bytes 147464 | tf_op jit(solution)/shard_map/ppermute | solution.py:377
  34.2 6.2 %collective-permute-start.14 = (bf16[48,512]{1,0:T(8,128)(2,1)S(1)}, bf16[48,512]{1,0:T(8,128)(2,1)S(1)}, u32[]{:S(2)}, u32[]{:S(2)}) collective-permute-start(bf16[48,512]{1,0:T(8,128)(2,1)S(1)} %get-tuple-element.21.own_ref), channel_id=1, source_target_pairs={{0,128},{8,136},{16,144},{24,152},{32,160},{40,168},{48,176},{56,1... | collective-permute-start | bytes 147464 | tf_op jit(solution)/shard_map/ppermute | solution.py:377
  37.4 4.1 %collective-permute-start.13 = (bf16[48,512]{1,0:T(8,128)(2,1)S(1)}, bf16[48,512]{1,0:T(8,128)(2,1)S(1)}, u32[]{:S(2)}, u32[]{:S(2)}) collective-permute-start(bf16[48,512]{1,0:T(8,128)(2,1)S(1)} %get-tuple-element.21.own_ref), channel_id=1, source_target_pairs={{0,192},{8,200},{16,208},{24,216},{32,224},{40,232},{48,240},{56,2... | collective-permute-start | bytes 147464 | tf_op jit(solution)/shard_map/ppermute | solution.py:377
  38.5 5.3 %collective-permute-start.12 = (bf16[48,512]{1,0:T(8,128)(2,1)S(1)}, bf16[48,512]{1,0:T(8,128)(2,1)S(1)}, u32[]{:S(2)}, u32[]{:S(2)}) collective-permute-start(bf16[48,512]{1,0:T(8,128)(2,1)S(1)} %get-tuple-element.21.own_ref), channel_id=1, source_target_pairs={{0,64},{8,72},{16,80},{24,88},{32,96},{40,104},{48,112},{56,120},{... | collective-permute-start | bytes 147464 | tf_op jit(solution)/shard_map/ppermute | solution.py:377

commit v10 on v7

--- a/solution.py
+++ b/solution.py
@@ -31,19 +31,18 @@
             scratch[group, pl.ds(at, SUB), :] = block[stream, :, lanes].astype(jnp.float32)
 
 
-def join_kernel(at, own_ref, passed_ref, *refs):
-    out_ref = refs[-1]
+def join_kernel(at, own_ref, passed_ref, out_ref):
     out_ref[0] = own_ref[...]
     out_ref[1] = passed_ref[at]
 
 
-def back_kernel(third_ref, second_ref, first_ref, out_ref):
+def back_kernel(first_ref, second_ref, third_ref, _, out_ref):
     for at, ref in enumerate((first_ref, second_ref, third_ref)):
         out_ref[at] = ref[1]
 
 
 def with_sources(refs):
-    far, third, second, first, back, own = refs
+    first, second, third, back, far, own = refs
     me = lax.axis_index("tp")
     turn = 1 - 2 * core_index()
     places = [(own, 0), (far, 4), (first.at[0], 1), (second.at[0], 2), (third.at[0], 3)]
@@ -358,13 +357,12 @@
     two = jax.ShapeDtypeStruct((2, 3, SUB, channels), streams.dtype)
     three = jax.ShapeDtypeStruct((3, 3, SUB, channels), streams.dtype)
 
-    def both(shift, *after):
-        return kernel(functools.partial(join_kernel, shift - 1), two, (block_for(shift), passed, *after), name="join")
-
-    third, second = (along(both(k), k) for k in (3, 2))
-    first = along(both(1, far), 1)
-    back = lax.ppermute(kernel(back_kernel, three, (third, second, first)), "ctx", swap)
-    blocks = [far, third, second, first, back, block_for(0)]
+    def both(shift):
+        return kernel(functools.partial(join_kernel, shift - 1), two, (block_for(shift), passed), name="join")
+
+    first, second, third = (along(both(k), k) for k in (1, 2, 3))
+    back = lax.ppermute(kernel(back_kernel, three, (first, second, third, far)), "ctx", swap)
+    blocks = [first, second, third, back, far, block_for(0)]
     summary, ends, signal = kernel(
         state_kernel,
         (packed, spans, wide),

time: 43.2 us -> 44.2 us (1.023)
  starting transfers between devices: 19.8 us -> 20.8 us
    ppermute x4, waiting for transfers between devices: 8.91 us -> 7.31 us  [along(): return lax.ppermute(value, ('ctx', 'tp'), route)]
    ppermute x1, waiting for transfers between devices: 0.01 us -> 1.36 us  [body(): lax.ppermute(jnp.stack([block_for(-k) for k in (1, 2, 3)]), 'ctx', swap)]
    ppermute x4, starting transfers between devices: 8.89 us -> 9.99 us  [along(): return lax.ppermute(value, ('ctx', 'tp'), route)]
  transfers between devices with their start and end apart: 13 -> 13, of which waited for: 10 -> 9; matrix products, arithmetic and copies ran while one was open for 0% -> 0% of each run, Pallas kernels for 2% -> 2%
where the time goes in v10:
time: 44.2 us; the launch traced here: 43.8 us
  starting transfers between devices  20.8 us (47%)
  waiting for transfers between devices  18.4 us (42%)
  Pallas kernels  2.96 us (7%)
  local copies, waits for them, and re-layouts  1.54 us (3%)
    ppermute x6, starting transfers between devices, around(): parts[by] = lax.ppermute(value, 'ctx', route)  10.4 us
    ppermute x4, starting transfers between devices, along(): return lax.ppermute(value, ('ctx', 'tp'), route)  9.99 us
    ppermute x6, waiting for transfers between devices, around(): parts[by] = lax.ppermute(value, 'ctx', route)  7.87 us
    ppermute x4, waiting for transfers between devices, along(): return lax.ppermute(value, ('ctx', 'tp'), route)  7.31 us
    pallas_call x11, Pallas kernels, kernel(): pl.pallas_call(function, out_shape=out_shape, in_specs=[VMEM] * len(opera...  2.96 us
    ppermute x1, waiting for transfers between devices, body(): lax.ppermute(jnp.stack([block_for(-k) for k in (1, 2, 3)]), 'ctx', swap)  1.36 us
    ppermute x1, waiting for transfers between devices, body(): got = lax.ppermute(summary, 'ctx', swap)  1.11 us
    dynamic_slice x1, local copies, waits for them, and re-layouts, block_for(): return lax.dynamic_slice(by_stream, (0, 0, at), (3, SUB, channels))  0.99 us
  transfers between devices with their start and end apart: 13, of which 9 were waited for; matrix products, arithmetic and copies ran while one was open for 0% of the time, Pallas kernels for 2%

profile of v10, /device:TPU:32, one launch (start us, length us, event | category | flops | bytes accessed | tf_op | source)
XLA Modules:
  0.0 43.8 jit_solution(6445752260078554939)
XLA Ops:
  0.0 1.0 %dynamic-slice_bitcast_fusion = (bf16[3,16,512]{2,1,0:T(8,128)(2,1)S(1)}, bf16[3,16,512]{2,1,0:T(8,128)(2,1)S(1)}, bf16[3,16,512]{2,1,0:T(8,128)(2,1)S(1)}, bf16...) fusion(bf16[16,3,4096]{2,0,1:T(8,128)(2,1)} %param.5, ...), kind=kLoop, calls=%fused_computation.1 | loop fusion | bytes 786464 | tf_op jit(solution)/shard_map/dynamic_slice | solution.py:346
  1.0 0.1 collective-permute-start
  1.1 1.4 %collective-permute-done.passed_ref = bf16[3,3,16,512]{3,2,1,0:T(8,128)(2,1)S(1)} collective-permute-done((bf16[3,3,16,512]{3,2,1,0:T(8,128)(2,1)S(1)}, bf16[3,3,16,512]{3,2,1,0:T(8,128)(2,1)S(1)}, u32[]{:S(2)}, u32[]{:S(2)}) %collective-permute-start) | collective-permute-done | bytes 147488 | tf_op jit(solution)/shard_map/ppermute | solution.py:355
  2.5 2.0 %collective-permute-start.1 = (bf16[2,3,16,512]{3,2,1,0:T(8,128)(2,1)S(1)}, bf16[2,3,16,512]{3,2,1,0:T(8,128)(2,1)S(1)}, u32[]{:S(2)}, u32[]{:S(2)}) collective-permute-start(bf16[2,3,16,512]{3,2,1,0:T(8,128)(2,1)S(1)} %join.3), channel_id=1, source_target_pairs={{0,1},{1,2},{2,3},{3,4},{4,5},{5,6},{6,7},{7,0},{8,15},{9,8},{10,9... | collective-permute-start | bytes 294920 | tf_op jit(solution)/shard_map/ppermute | solution.py:353
  4.5 4.6 %collective-permute-start.2 = (bf16[2,3,16,512]{3,2,1,0:T(8,128)(2,1)S(1)}, bf16[2,3,16,512]{3,2,1,0:T(8,128)(2,1)S(1)}, u32[]{:S(2)}, u32[]{:S(2)}) collective-permute-start(bf16[2,3,16,512]{3,2,1,0:T(8,128)(2,1)S(1)} %join.4), channel_id=1, source_target_pairs={{0,2},{1,3},{2,4},{3,5},{4,6},{5,7},{6,0},{7,1},{8,14},{9,15},{10,... | collective-permute-start | bytes 294920 | tf_op jit(solution)/shard_map/ppermute | solution.py:353
  9.1 2.0 %collective-permute-start.3 = (bf16[2,3,16,512]{3,2,1,0:T(8,128)(2,1)S(1)}, bf16[2,3,16,512]{3,2,1,0:T(8,128)(2,1)S(1)}, u32[]{:S(2)}, u32[]{:S(2)}) collective-permute-start(bf16[2,3,16,512]{3,2,1,0:T(8,128)(2,1)S(1)} %join.5), channel_id=1, source_target_pairs={{0,3},{1,4},{2,5},{3,6},{4,7},{5,0},{6,1},{7,2},{8,13},{9,14},{10,... | collective-permute-start | bytes 294920 | tf_op jit(solution)/shard_map/ppermute | solution.py:353
  11.1 0.0 copy-start
  11.1 0.0 copy-start.2
  11.1 1.4 %collective-permute-start.4 = (bf16[3,16,512]{2,1,0:T(8,128)(2,1)S(1)}, bf16[3,16,512]{2,1,0:T(8,128)(2,1)S(1)}, u32[]{:S(2)}, u32[]{:S(2)}) collective-permute-start(bf16[3,16,512]{2,1,0:T(8,128)(2,1)S(1)} %get-tuple-element.36), channel_id=1, source_target_pairs={{0,4},{1,5},{2,6},{3,7},{4,0},{5,1},{6,2},{7,3},{8,12},{9,13},{10,... | collective-permute-start | bytes 147464 | tf_op jit(solution)/shard_map/ppermute | solution.py:353
  12.5 7.3 %collective-permute-done.4._.refs_4_ = bf16[3,16,512]{2,1,0:T(8,128)(2,1)S(1)} collective-permute-done((bf16[3,16,512]{2,1,0:T(8,128)(2,1)S(1)}, bf16[3,16,512]{2,1,0:T(8,128)(2,1)S(1)}, u32[]{:S(2)}, u32[]{:S(2)}) %collective-permute-start.4) | collective-permute-done | bytes 49184 | tf_op jit(solution)/shard_map/ppermute | solution.py:353
  19.8 0.0 collective-permute-done.1.first_ref.refs_0_
  19.8 0.0 collective-permute-done.2.second_ref.refs_1_
  19.8 0.0 collective-permute-done.3.third_ref.refs_2_
  19.8 0.0 copy-start.3
  19.9 0.1 collective-permute-start.5
  20.0 0.0 copy-done
  20.0 0.0 copy-done.2
  20.0 0.5 %copy-done.3 = f32[512]{0:T(512)S(1)} copy-done((f32[512]{0:T(512)S(1)}, f32[512]{0:T(512)}, u32[]{:S(2)}) %copy-start.3) | copy-done | bytes 2072
  20.5 0.0 copy-start.1
  20.5 0.1 weights_kernel.1
  20.6 0.7 %collective-permute-done.5.refs_3_ = bf16[3,3,16,512]{3,2,1,0:T(8,128)(2,1)S(1)} collective-permute-done((bf16[3,3,16,512]{3,2,1,0:T(8,128)(2,1)S(1)}, bf16[3,3,16,512]{3,2,1,0:T(8,128)(2,1)S(1)}, u32[]{:S(2)}, u32[]{:S(2)}) %collective-permute-start.5) | collective-permute-done | bytes 147488 | tf_op jit(solution)/shard_map/ppermute | solution.py:364
  21.3 0.0 copy-done.1
  21.3 0.6 %state_kernel.1 = (f32[32,512]{1,0:T(8,128)S(1)}, f32[16,8,512]{2,1,0:T(8,128)S(1)}, f32[16,8,512]{2,1,0:T(8,128)S(1)}) custom-call(bf16[2,3,16,512]{3,2,1,0:T(8,128)(2,1)S(1)} %collective-permute-done.1.first_ref.refs_0_, bf16[2,3,16,512]{3,2,1,0:T(8,128)(2,1)S(1)} %collective-permute-done.2.second_ref.refs_1_, ...), custom_call_target="tpu_custom_call" | custom-call | tf_op jit(solution)/shard_map/state_kernel/pallas_call | solution.py:324
  21.9 0.2 collective-permute-start.6
  22.2 1.1 %collective-permute-done.6.got_ref = f32[32,512]{1,0:T(8,128)S(1)} collective-permute-done((f32[32,512]{1,0:T(8,128)S(1)}, f32[32,512]{1,0:T(8,128)S(1)}, u32[]{:S(2)}, u32[]{:S(2)}) %collective-permute-start.6) | collective-permute-done | bytes 65568 | tf_op jit(solution)/shard_map/ppermute | solution.py:372
  23.3 3.1 %collective-permute-start.9 = (bf16[48,512]{1,0:T(8,128)(2,1)S(1)}, bf16[48,512]{1,0:T(8,128)(2,1)S(1)}, u32[]{:S(2)}, u32[]{:S(2)}) collective-permute-start(bf16[48,512]{1,0:T(8,128)(2,1)S(1)} %get-tuple-element.20.own_ref), channel_id=1, source_target_pairs={{0,32},{8,40},{16,48},{24,56},{32,0},{40,8},{48,16},{56,24},{64,96... | collective-permute-start | bytes 147464 | tf_op jit(solution)/shard_map/ppermute | solution.py:379
  26.4 1.1 %collective-permute-start.8 = (bf16[48,512]{1,0:T(8,128)(2,1)S(1)}, bf16[48,512]{1,0:T(8,128)(2,1)S(1)}, u32[]{:S(2)}, u32[]{:S(2)}) collective-permute-start(bf16[48,512]{1,0:T(8,128)(2,1)S(1)} %get-tuple-element.20.own_ref), channel_id=1, source_target_pairs={{0,48},{8,56},{16,0},{24,8},{32,16},{40,24},{48,32},{56,40},{64,11... | collective-permute-start | bytes 147464 | tf_op jit(solution)/shard_map/ppermute | solution.py:379
  27.6 0.9 %collective-permute-start.7 = (bf16[48,512]{1,0:T(8,128)(2,1)S(1)}, bf16[48,512]{1,0:T(8,128)(2,1)S(1)}, u32[]{:S(2)}, u32[]{:S(2)}) collective-permute-start(bf16[48,512]{1,0:T(8,128)(2,1)S(1)} %get-tuple-element.20.own_ref), channel_id=1, source_target_pairs={{0,16},{8,24},{16,32},{24,40},{32,48},{40,56},{48,0},{56,8},{64,80... | collective-permute-start | bytes 147464 | tf_op jit(solution)/shard_map/ppermute | solution.py:379
  28.4 0.5 %collective-permute-done.9.two_ref = bf16[48,512]{1,0:T(8,128)(2,1)S(1)} collective-permute-done((bf16[48,512]{1,0:T(8,128)(2,1)S(1)}, bf16[48,512]{1,0:T(8,128)(2,1)S(1)}, u32[]{:S(2)}, u32[]{:S(2)}) %collective-permute-start.9) | collective-permute-done | bytes 49184 | tf_op jit(solution)/shard_map/ppermute | solution.py:379
  29.0 1.5 %collective-permute-done.8.three_ref = bf16[48,512]{1,0:T(8,128)(2,1)S(1)} collective-permute-done((bf16[48,512]{1,0:T(8,128)(2,1)S(1)}, bf16[48,512]{1,0:T(8,128)(2,1)S(1)}, u32[]{:S(2)}, u32[]{:S(2)}) %collective-permute-start.8) | collective-permute-done | bytes 49184 | tf_op jit(solution)/shard_map/ppermute | solution.py:379
  30.5 2.4 %collective-permute-done.7.one_ref = bf16[48,512]{1,0:T(8,128)(2,1)S(1)} collective-permute-done((bf16[48,512]{1,0:T(8,128)(2,1)S(1)}, bf16[48,512]{1,0:T(8,128)(2,1)S(1)}, u32[]{:S(2)}, u32[]{:S(2)}) %collective-permute-start.7) | collective-permute-done | bytes 49184 | tf_op jit(solution)/shard_map/ppermute | solution.py:379
  32.9 0.1 row_kernel.1
  33.0 3.3 %collective-permute-start.12 = (bf16[48,512]{1,0:T(8,128)(2,1)S(1)}, bf16[48,512]{1,0:T(8,128)(2,1)S(1)}, u32[]{:S(2)}, u32[]{:S(2)}) collective-permute-start(bf16[48,512]{1,0:T(8,128)(2,1)S(1)} %get-tuple-element.21.own_ref), channel_id=1, source_target_pairs={{0,128},{8,136},{16,144},{24,152},{32,160},{40,168},{48,176},{56,1... | collective-permute-start | bytes 147464 | tf_op jit(solution)/shard_map/ppermute | solution.py:379
  36.3 1.1 %collective-permute-start.11 = (bf16[48,512]{1,0:T(8,128)(2,1)S(1)}, bf16[48,512]{1,0:T(8,128)(2,1)S(1)}, u32[]{:S(2)}, u32[]{:S(2)}) collective-permute-start(bf16[48,512]{1,0:T(8,128)(2,1)S(1)} %get-tuple-element.21.own_ref), channel_id=1, source_target_pairs={{0,192},{8,200},{16,208},{24,216},{32,224},{40,232},{48,240},{56,2... | collective-permute-start | bytes 147464 | tf_op jit(solution)/shard_map/ppermute | solution.py:379
  37.3 1.0 %collective-permute-start.10 = (bf16[48,512]{1,0:T(8,128)(2,1)S(1)}, bf16[48,512]{1,0:T(8,128)(2,1)S(1)}, u32[]{:S(2)}, u32[]{:S(2)}) collective-permute-start(bf16[48,512]{1,0:T(8,128)(2,1)S(1)} %get-tuple-element.21.own_ref), channel_id=1, source_target_pairs={{0,64},{8,72},{16,80},{24,88},{32,96},{40,104},{48,112},{56,120},{... | collective-permute-start | bytes 147464 | tf_op jit(solution)/shard_map/ppermute | solution.py:379
  38.3 0.9 %local_kernel.1 = (f32[16,8,512]{2,1,0:T(8,128)S(1)}, f32[16,8,512]{2,1,0:T(8,128)S(1)}) custom-call(bf16[2,3,16,512]{3,2,1,0:T(8,128)(2,1)S(1)} %collective-permute-done.1.first_ref.refs_0_, bf16[2,3,16,512]{3,2,1,0:T(8,128)(2,1)S(1)} %collective-permute-done.2.second_ref.refs_1_, bf16[2,3,16,512]{3,2,1,0:T(8,128)(2,1)S(1)} %collective-permute-done.3.third_ref.refs_2_, ...), custom_call_target="tpu_custom_call" | custom-call | flops 8388608 | bytes 2097152 | tf_op jit(solution)/shard_map/local_kernel/pallas_call | solution.py:324
  39.2 0.0 collective-permute-done.12.two_ref
  39.2 1.2 %collective-permute-done.11.three_ref = bf16[48,512]{1,0:T(8,128)(2,1)S(1)} collective-permute-done((bf16[48,512]{1,0:T(8,128)(2,1)S(1)}, bf16[48,512]{1,0:T(8,128)(2,1)S(1)}, u32[]{:S(2)}, u32[]{:S(2)}) %collective-permute-start.11) | collective-permute-done | bytes 49184 | tf_op jit(solution)/shard_map/ppermute | solution.py:379
  40.4 2.3 %collective-permute-done.10.one_ref = bf16[48,512]{1,0:T(8,128)(2,1)S(1)} collective-permute-done((bf16[48,512]{1,0:T(8,128)(2,1)S(1)}, bf16[48,512]{1,0:T(8,128)(2,1)S(1)}, u32[]{:S(2)}, u32[]{:S(2)}) %collective-permute-start.10) | collective-permute-done | bytes 49184 | tf_op jit(solution)/shard_map/ppermute | solution.py:379
  42.6 0.1 merge_kernel.1.carry_ref
  42.8 1.1 %final_kernel.1 = bf16[128,512]{1,0:T(8,128)(2,1)} custom-call(f32[24,512]{1,0:T(8,128)S(1)} %merge_kernel.1.carry_ref, f32[32,512]{1,0:T(8,128)S(1)} %get-tuple-element.19.kept_ref.summary_ref, f32[3,3,512]{2,1,0:T(4,128)S(1)} %copy-done.1, f32[16,512]{1,0:T(8,128)S(1)} %copy-done, f32[16,512]{1,0:T(8,128)S(1)} %copy-done.2, f32[1,512]{1,0:T(1,128)S(1)} %bitcast.25, ...), custom_call_target="tpu_custom_call" | custom-call | tf_op jit(solution)/shard_map/final_kernel/pallas_call | solution.py:324
  (6 shorter events, 0.1 us)
Async XLA Ops:
  1.0 1.5 %collective-permute-start = (bf16[3,3,16,512]{3,2,1,0:T(8,128)(2,1)S(1)}, bf16[3,3,16,512]{3,2,1,0:T(8,128)(2,1)S(1)}, u32[]{:S(2)}, u32[]{:S(2)}) collective-permute-start(bf16[3,3,16,512]{3,2,1,0:T(8,128)(2,1)S(1)} %pad_maximum_fusion), channel_id=1, source_target_pairs={{0,8},{8,0},{16,24},{24,16},{32,40},{40,32},{48,56},{56,48},{64,72... | collective-permute-start | bytes 442376 | tf_op jit(solution)/shard_map/ppermute | solution.py:355
  2.5 17.3 %collective-permute-start.1 = (bf16[2,3,16,512]{3,2,1,0:T(8,128)(2,1)S(1)}, bf16[2,3,16,512]{3,2,1,0:T(8,128)(2,1)S(1)}, u32[]{:S(2)}, u32[]{:S(2)}) collective-permute-start(bf16[2,3,16,512]{3,2,1,0:T(8,128)(2,1)S(1)} %join.3), channel_id=1, source_target_pairs={{0,1},{1,2},{2,3},{3,4},{4,5},{5,6},{6,7},{7,0},{8,15},{9,8},{10,9... | collective-permute-start | bytes 294920 | tf_op jit(solution)/shard_map/ppermute | solution.py:353
  4.5 15.3 %collective-permute-start.2 = (bf16[2,3,16,512]{3,2,1,0:T(8,128)(2,1)S(1)}, bf16[2,3,16,512]{3,2,1,0:T(8,128)(2,1)S(1)}, u32[]{:S(2)}, u32[]{:S(2)}) collective-permute-start(bf16[2,3,16,512]{3,2,1,0:T(8,128)(2,1)S(1)} %join.4), channel_id=1, source_target_pairs={{0,2},{1,3},{2,4},{3,5},{4,6},{5,7},{6,0},{7,1},{8,14},{9,15},{10,... | collective-permute-start | bytes 294920 | tf_op jit(solution)/shard_map/ppermute | solution.py:353
  9.1 10.8 %collective-permute-start.3 = (bf16[2,3,16,512]{3,2,1,0:T(8,128)(2,1)S(1)}, bf16[2,3,16,512]{3,2,1,0:T(8,128)(2,1)S(1)}, u32[]{:S(2)}, u32[]{:S(2)}) collective-permute-start(bf16[2,3,16,512]{3,2,1,0:T(8,128)(2,1)S(1)} %join.5), channel_id=1, source_target_pairs={{0,3},{1,4},{2,5},{3,6},{4,7},{5,0},{6,1},{7,2},{8,13},{9,14},{10,... | collective-permute-start | bytes 294920 | tf_op jit(solution)/shard_map/ppermute | solution.py:353
  11.1 8.9 %copy-start = (f32[16,512]{1,0:T(8,128)S(1)}, f32[16,512]{1,0:T(8,128)}, u32[]{:S(2)}) copy-start(f32[16,512]{1,0:T(8,128)} %rates_ref.9) | copy-start | bytes 98308
  11.1 8.9 %copy-start.2 = (f32[16,512]{1,0:T(8,128)S(1)}, f32[16,512]{1,0:T(8,128)}, u32[]{:S(2)}) copy-start(f32[16,512]{1,0:T(8,128)} %residues_ref.3) | copy-start | bytes 98308
  11.1 8.7 %collective-permute-start.4 = (bf16[3,16,512]{2,1,0:T(8,128)(2,1)S(1)}, bf16[3,16,512]{2,1,0:T(8,128)(2,1)S(1)}, u32[]{:S(2)}, u32[]{:S(2)}) collective-permute-start(bf16[3,16,512]{2,1,0:T(8,128)(2,1)S(1)} %get-tuple-element.36), channel_id=1, source_target_pairs={{0,4},{1,5},{2,6},{3,7},{4,0},{5,1},{6,2},{7,3},{8,12},{9,13},{10,... | collective-permute-start | bytes 147464 | tf_op jit(solution)/shard_map/ppermute | solution.py:353
  19.8 0.7 %copy-start.3 = (f32[512]{0:T(512)S(1)}, f32[512]{0:T(512)}, u32[]{:S(2)}) copy-start(f32[512]{0:T(512)} %param.9) | copy-start | bytes 6148
  19.9 1.5 %collective-permute-start.5 = (bf16[3,3,16,512]{3,2,1,0:T(8,128)(2,1)S(1)}, bf16[3,3,16,512]{3,2,1,0:T(8,128)(2,1)S(1)}, u32[]{:S(2)}, u32[]{:S(2)}) collective-permute-start(bf16[3,3,16,512]{3,2,1,0:T(8,128)(2,1)S(1)} %back_kernel.1), channel_id=1, source_target_pairs={{0,8},{8,0},{16,24},{24,16},{32,40},{40,32},{48,56},{56,48},{64,72... | collective-permute-start | bytes 442376 | tf_op jit(solution)/shard_map/ppermute | solution.py:364
  20.5 0.8 %copy-start.1 = (f32[3,3,512]{2,1,0:T(4,128)S(1)}, f32[3,3,512]{2,1,0:T(4,128)}, u32[]{:S(2)}) copy-start(f32[3,3,512]{2,1,0:T(4,128)} %taps_ref.7) | copy-start | bytes 55300
  21.9 1.3 %collective-permute-start.6 = (f32[32,512]{1,0:T(8,128)S(1)}, f32[32,512]{1,0:T(8,128)S(1)}, u32[]{:S(2)}, u32[]{:S(2)}) collective-permute-start(f32[32,512]{1,0:T(8,128)S(1)} %get-tuple-element.19.kept_ref.summary_ref), channel_id=1, source_target_pairs={{0,8},{8,0},{16,24},{24,16},{32,40},{40,32},{48,56},{56,48},{64,72... | collective-permute-start | bytes 196616 | tf_op jit(solution)/shard_map/ppermute | solution.py:372
  23.3 5.7 %collective-permute-start.9 = (bf16[48,512]{1,0:T(8,128)(2,1)S(1)}, bf16[48,512]{1,0:T(8,128)(2,1)S(1)}, u32[]{:S(2)}, u32[]{:S(2)}) collective-permute-start(bf16[48,512]{1,0:T(8,128)(2,1)S(1)} %get-tuple-element.20.own_ref), channel_id=1, source_target_pairs={{0,32},{8,40},{16,48},{24,56},{32,0},{40,8},{48,16},{56,24},{64,96... | collective-permute-start | bytes 147464 | tf_op jit(solution)/shard_map/ppermute | solution.py:379
  26.4 4.1 %collective-permute-start.8 = (bf16[48,512]{1,0:T(8,128)(2,1)S(1)}, bf16[48,512]{1,0:T(8,128)(2,1)S(1)}, u32[]{:S(2)}, u32[]{:S(2)}) collective-permute-start(bf16[48,512]{1,0:T(8,128)(2,1)S(1)} %get-tuple-element.20.own_ref), channel_id=1, source_target_pairs={{0,48},{8,56},{16,0},{24,8},{32,16},{40,24},{48,32},{56,40},{64,11... | collective-permute-start | bytes 147464 | tf_op jit(solution)/shard_map/ppermute | solution.py:379
  27.6 5.3 %collective-permute-start.7 = (bf16[48,512]{1,0:T(8,128)(2,1)S(1)}, bf16[48,512]{1,0:T(8,128)(2,1)S(1)}, u32[]{:S(2)}, u32[]{:S(2)}) collective-permute-start(bf16[48,512]{1,0:T(8,128)(2,1)S(1)} %get-tuple-element.20.own_ref), channel_id=1, source_target_pairs={{0,16},{8,24},{16,32},{24,40},{32,48},{40,56},{48,0},{56,8},{64,80... | collective-permute-start | bytes 147464 | tf_op jit(solution)/shard_map/ppermute | solution.py:379
  33.0 6.2 %collective-permute-start.12 = (bf16[48,512]{1,0:T(8,128)(2,1)S(1)}, bf16[48,512]{1,0:T(8,128)(2,1)S(1)}, u32[]{:S(2)}, u32[]{:S(2)}) collective-permute-start(bf16[48,512]{1,0:T(8,128)(2,1)S(1)} %get-tuple-element.21.own_ref), channel_id=1, source_target_pairs={{0,128},{8,136},{16,144},{24,152},{32,160},{40,168},{48,176},{56,1... | collective-permute-start | bytes 147464 | tf_op jit(solution)/shard_map/ppermute | solution.py:379
  36.3 4.1 %collective-permute-start.11 = (bf16[48,512]{1,0:T(8,128)(2,1)S(1)}, bf16[48,512]{1,0:T(8,128)(2,1)S(1)}, u32[]{:S(2)}, u32[]{:S(2)}) collective-permute-start(bf16[48,512]{1,0:T(8,128)(2,1)S(1)} %get-tuple-element.21.own_ref), channel_id=1, source_target_pairs={{0,192},{8,200},{16,208},{24,216},{32,224},{40,232},{48,240},{56,2... | collective-permute-start | bytes 147464 | tf_op jit(solution)/shard_map/ppermute | solution.py:379
  37.3 5.3 %collective-permute-start.10 = (bf16[48,512]{1,0:T(8,128)(2,1)S(1)}, bf16[48,512]{1,0:T(8,128)(2,1)S(1)}, u32[]{:S(2)}, u32[]{:S(2)}) collective-permute-start(bf16[48,512]{1,0:T(8,128)(2,1)S(1)} %get-tuple-element.21.own_ref), channel_id=1, source_target_pairs={{0,64},{8,72},{16,80},{24,88},{32,96},{40,104},{48,112},{56,120},{... | collective-permute-start | bytes 147464 | tf_op jit(solution)/shard_map/ppermute | solution.py:379

commit v11 on v7

--- a/solution.py
+++ b/solution.py
@@ -342,9 +342,9 @@
     turn = 1 - 2 * core_index()
     swap = [(i, i ^ 1) for i in range(ctx)]
 
-    def block_for(shift):
+    def block_for(shift, source):
         at = ((lax.axis_index("tp") + turn * shift) % parts) * channels
-        return lax.dynamic_slice(by_stream, (0, 0, at), (3, SUB, channels))
+        return lax.dynamic_slice(source, (0, 0, at), (3, SUB, channels))
 
     def along(value, shift):
         route = []
@@ -353,18 +353,20 @@
             route += [(c * parts + z, c * parts + (z + step) % parts) for z in range(parts)]
         return lax.ppermute(value, ("ctx", "tp"), route)
 
-    passed = lax.ppermute(jnp.stack([block_for(-k) for k in (1, 2, 3)]), "ctx", swap)
-    far = along(block_for(4), 4)
+    away = jnp.stack([block_for(-k, by_stream) for k in (1, 2, 3)])
+    passed = lax.ppermute(away, "ctx", swap)
+    far = along(block_for(4, by_stream), 4)
+    later, _ = lax.optimization_barrier((by_stream, away))
     two = jax.ShapeDtypeStruct((2, 3, SUB, channels), streams.dtype)
     three = jax.ShapeDtypeStruct((3, 3, SUB, channels), streams.dtype)
 
     def both(shift, *after):
-        return kernel(functools.partial(join_kernel, shift - 1), two, (block_for(shift), passed, *after), name="join")
+        return kernel(functools.partial(join_kernel, shift - 1), two, (block_for(shift, later), passed, *after), name="join")
 
     third, second = (along(both(k), k) for k in (3, 2))
     first = along(both(1, far), 1)
     back = lax.ppermute(kernel(back_kernel, three, (third, second, first)), "ctx", swap)
-    blocks = [far, third, second, first, back, block_for(0)]
+    blocks = [far, third, second, first, back, block_for(0, later)]
     summary, ends, signal = kernel(
         state_kernel,
         (packed, spans, wide),

time: 43.2 us -> 43.1 us (level)
    dynamic_slice x1, local copies, waits for them, and re-layouts: 0.99 us -> 0.01 us  [block_for(): return lax.dynamic_slice(source, (0, 0, at), (3, SUB, channels))]
    another operation x0 -> x1, local copies, waits for them, and re-layouts: none -> 0.94 us  [body(): away = jnp.stack([block_for(-k, by_stream) for k in (1, 2, 3)])]
where the time goes in v11:
time: 43.1 us; the launch traced here: 43 us
  starting transfers between devices  19.7 us (46%)
  waiting for transfers between devices  18.6 us (43%)
  Pallas kernels  2.96 us (7%)
  local copies, waits for them, and re-layouts  1.51 us (4%)
    ppermute x6, starting transfers between devices, around(): parts[by] = lax.ppermute(value, 'ctx', route)  10.4 us
    ppermute x4, waiting for transfers between devices, along(): return lax.ppermute(value, ('ctx', 'tp'), route)  8.94 us
    ppermute x4, starting transfers between devices, along(): return lax.ppermute(value, ('ctx', 'tp'), route)  8.86 us
    ppermute x6, waiting for transfers between devices, around(): parts[by] = lax.ppermute(value, 'ctx', route)  7.87 us
    pallas_call x11, Pallas kernels, kernel(): pl.pallas_call(function, out_shape=out_shape, in_specs=[VMEM] * len(opera...  2.96 us
    ppermute x1, waiting for transfers between devices, body(): got = lax.ppermute(summary, 'ctx', swap)  1.11 us
    another operation x1, local copies, waits for them, and re-layouts, body(): away = jnp.stack([block_for(-k, by_stream) for k in (1, 2, 3)])  0.94 us
  transfers between devices with their start and end apart: 13, of which 10 were waited for; matrix products, arithmetic and copies ran while one was open for 0% of the time, Pallas kernels for 2%

profile of v11, /device:TPU:32, one launch (start us, length us, event | category | flops | bytes accessed | tf_op | source)
XLA Modules:
  0.0 43.0 jit_solution(17185646793949171586)
XLA Ops:
  0.0 0.0 copy-start.4
  0.0 0.9 %dynamic-slice_bitcast_fusion.2 = (bf16[1,3,16,512]{3,2,1,0:T(8,128)(2,1)S(1)}, bf16[3,16,512]{2,1,0:T(8,128)(2,1)S(1)}, bf16[1,3,16,512]{3,2,1,0:T(8,128)(2,1)S(1)}, bf16[1,3,16,512]{3,2,1,0:T(8,128)(2,1)S(1)}) fusion(bf16[16,3,4096]{2,0,1:T(8,128)(2,1)} %param.5, s32[]{:T(128)S(6)} %select_n.62, s32[]{:T(128)S(6)} %select_n.60, s32[]{:T(128)S(6)} %select_n.66, ...), kind=kLoop, calls=%fused_computation.3 | loop fusion | bytes 393232 | tf_op jit(solution)/shard_map/stack | solution.py:356
  1.0 0.1 collective-permute-start.1
  1.1 6.4 %collective-permute-start = (bf16[3,16,512]{2,1,0:T(8,128)(2,1)S(1)}, bf16[3,16,512]{2,1,0:T(8,128)(2,1)S(1)}, u32[]{:S(2)}, u32[]{:S(2)}) collective-permute-start(bf16[3,16,512]{2,1,0:T(8,128)(2,1)S(1)} %get-tuple-element.36), channel_id=1, source_target_pairs={{0,4},{1,5},{2,6},{3,7},{4,0},{5,1},{6,2},{7,3},{8,12},{9,13},{10,... | collective-permute-start | bytes 147464 | tf_op jit(solution)/shard_map/ppermute | solution.py:354
  7.4 0.0 copy-done.4
  7.5 0.0 collective-permute-done.1.passed_ref
  7.5 0.9 %collective-permute-start.2 = (bf16[2,3,16,512]{3,2,1,0:T(8,128)(2,1)S(1)}, bf16[2,3,16,512]{3,2,1,0:T(8,128)(2,1)S(1)}, u32[]{:S(2)}, u32[]{:S(2)}) collective-permute-start(bf16[2,3,16,512]{3,2,1,0:T(8,128)(2,1)S(1)} %join.3), channel_id=1, source_target_pairs={{0,3},{1,4},{2,5},{3,6},{4,7},{5,0},{6,1},{7,2},{8,13},{9,14},{10,... | collective-permute-start | bytes 294920 | tf_op jit(solution)/shard_map/ppermute | solution.py:354
  8.4 1.5 %collective-permute-start.3 = (bf16[2,3,16,512]{3,2,1,0:T(8,128)(2,1)S(1)}, bf16[2,3,16,512]{3,2,1,0:T(8,128)(2,1)S(1)}, u32[]{:S(2)}, u32[]{:S(2)}) collective-permute-start(bf16[2,3,16,512]{3,2,1,0:T(8,128)(2,1)S(1)} %join.4), channel_id=1, source_target_pairs={{0,2},{1,3},{2,4},{3,5},{4,6},{5,7},{6,0},{7,1},{8,14},{9,15},{10,... | collective-permute-start | bytes 294920 | tf_op jit(solution)/shard_map/ppermute | solution.py:354
  9.9 2.4 %collective-permute-done.refs_0_ = bf16[3,16,512]{2,1,0:T(8,128)(2,1)S(1)} collective-permute-done((bf16[3,16,512]{2,1,0:T(8,128)(2,1)S(1)}, bf16[3,16,512]{2,1,0:T(8,128)(2,1)S(1)}, u32[]{:S(2)}, u32[]{:S(2)}) %collective-permute-start) | collective-permute-done | bytes 49184 | tf_op jit(solution)/shard_map/ppermute | solution.py:354
  12.3 0.0 copy-start
  12.3 0.0 copy-start.2
  12.3 0.1 collective-permute-start.4
  12.4 5.1 %collective-permute-done.2.third_ref.refs_1_ = bf16[2,3,16,512]{3,2,1,0:T(8,128)(2,1)S(1)} collective-permute-done((bf16[2,3,16,512]{3,2,1,0:T(8,128)(2,1)S(1)}, bf16[2,3,16,512]{3,2,1,0:T(8,128)(2,1)S(1)}, u32[]{:S(2)}, u32[]{:S(2)}) %collective-permute-start.2) | collective-permute-done | bytes 98336 | tf_op jit(solution)/shard_map/ppermute | solution.py:354
  17.5 1.5 %collective-permute-done.3.second_ref.refs_2_ = bf16[2,3,16,512]{3,2,1,0:T(8,128)(2,1)S(1)} collective-permute-done((bf16[2,3,16,512]{3,2,1,0:T(8,128)(2,1)S(1)}, bf16[2,3,16,512]{3,2,1,0:T(8,128)(2,1)S(1)}, u32[]{:S(2)}, u32[]{:S(2)}) %collective-permute-start.3) | collective-permute-done | bytes 98336 | tf_op jit(solution)/shard_map/ppermute | solution.py:354
  19.0 0.0 collective-permute-done.4.first_ref.refs_3_
  19.0 0.0 copy-start.3
  19.0 0.1 collective-permute-start.5
  19.1 0.0 copy-done
  19.1 0.0 copy-done.2
  19.1 0.5 %copy-done.3 = f32[512]{0:T(512)S(1)} copy-done((f32[512]{0:T(512)S(1)}, f32[512]{0:T(512)}, u32[]{:S(2)}) %copy-start.3) | copy-done | bytes 2072
  19.7 0.0 copy-start.1
  19.7 0.1 weights_kernel.1
  19.7 0.7 %collective-permute-done.5.refs_4_ = bf16[3,3,16,512]{3,2,1,0:T(8,128)(2,1)S(1)} collective-permute-done((bf16[3,3,16,512]{3,2,1,0:T(8,128)(2,1)S(1)}, bf16[3,3,16,512]{3,2,1,0:T(8,128)(2,1)S(1)}, u32[]{:S(2)}, u32[]{:S(2)}) %collective-permute-start.5) | collective-permute-done | bytes 147488 | tf_op jit(solution)/shard_map/ppermute | solution.py:368
  20.4 0.0 copy-done.1
  20.4 0.6 %state_kernel.1 = (f32[32,512]{1,0:T(8,128)S(1)}, f32[16,8,512]{2,1,0:T(8,128)S(1)}, f32[16,8,512]{2,1,0:T(8,128)S(1)}) custom-call(bf16[3,16,512]{2,1,0:T(8,128)(2,1)S(1)} %collective-permute-done.refs_0_, bf16[2,3,16,512]{3,2,1,0:T(8,128)(2,1)S(1)} %collective-permute-done.2.third_ref.refs_1_, ...), custom_call_target="tpu_custom_call" | custom-call | tf_op jit(solution)/shard_map/state_kernel/pallas_call | solution.py:325
  21.1 0.2 collective-permute-start.6
  21.3 1.1 %collective-permute-done.6.got_ref = f32[32,512]{1,0:T(8,128)S(1)} collective-permute-done((f32[32,512]{1,0:T(8,128)S(1)}, f32[32,512]{1,0:T(8,128)S(1)}, u32[]{:S(2)}, u32[]{:S(2)}) %collective-permute-start.6) | collective-permute-done | bytes 65568 | tf_op jit(solution)/shard_map/ppermute | solution.py:376
  22.4 3.1 %collective-permute-start.9 = (bf16[48,512]{1,0:T(8,128)(2,1)S(1)}, bf16[48,512]{1,0:T(8,128)(2,1)S(1)}, u32[]{:S(2)}, u32[]{:S(2)}) collective-permute-start(bf16[48,512]{1,0:T(8,128)(2,1)S(1)} %get-tuple-element.22.own_ref), channel_id=1, source_target_pairs={{0,32},{8,40},{16,48},{24,56},{32,0},{40,8},{48,16},{56,24},{64,96... | collective-permute-start | bytes 147464 | tf_op jit(solution)/shard_map/ppermute | solution.py:383
  25.6 1.1 %collective-permute-start.8 = (bf16[48,512]{1,0:T(8,128)(2,1)S(1)}, bf16[48,512]{1,0:T(8,128)(2,1)S(1)}, u32[]{:S(2)}, u32[]{:S(2)}) collective-permute-start(bf16[48,512]{1,0:T(8,128)(2,1)S(1)} %get-tuple-element.22.own_ref), channel_id=1, source_target_pairs={{0,48},{8,56},{16,0},{24,8},{32,16},{40,24},{48,32},{56,40},{64,11... | collective-permute-start | bytes 147464 | tf_op jit(solution)/shard_map/ppermute | solution.py:383
  26.7 0.9 %collective-permute-start.7 = (bf16[48,512]{1,0:T(8,128)(2,1)S(1)}, bf16[48,512]{1,0:T(8,128)(2,1)S(1)}, u32[]{:S(2)}, u32[]{:S(2)}) collective-permute-start(bf16[48,512]{1,0:T(8,128)(2,1)S(1)} %get-tuple-element.22.own_ref), channel_id=1, source_target_pairs={{0,16},{8,24},{16,32},{24,40},{32,48},{40,56},{48,0},{56,8},{64,80... | collective-permute-start | bytes 147464 | tf_op jit(solution)/shard_map/ppermute | solution.py:383
  27.6 0.5 %collective-permute-done.9.two_ref = bf16[48,512]{1,0:T(8,128)(2,1)S(1)} collective-permute-done((bf16[48,512]{1,0:T(8,128)(2,1)S(1)}, bf16[48,512]{1,0:T(8,128)(2,1)S(1)}, u32[]{:S(2)}, u32[]{:S(2)}) %collective-permute-start.9) | collective-permute-done | bytes 49184 | tf_op jit(solution)/shard_map/ppermute | solution.py:383
  28.1 1.5 %collective-permute-done.8.three_ref = bf16[48,512]{1,0:T(8,128)(2,1)S(1)} collective-permute-done((bf16[48,512]{1,0:T(8,128)(2,1)S(1)}, bf16[48,512]{1,0:T(8,128)(2,1)S(1)}, u32[]{:S(2)}, u32[]{:S(2)}) %collective-permute-start.8) | collective-permute-done | bytes 49184 | tf_op jit(solution)/shard_map/ppermute | solution.py:383
  29.6 2.4 %collective-permute-done.7.one_ref = bf16[48,512]{1,0:T(8,128)(2,1)S(1)} collective-permute-done((bf16[48,512]{1,0:T(8,128)(2,1)S(1)}, bf16[48,512]{1,0:T(8,128)(2,1)S(1)}, u32[]{:S(2)}, u32[]{:S(2)}) %collective-permute-start.7) | collective-permute-done | bytes 49184 | tf_op jit(solution)/shard_map/ppermute | solution.py:383
  32.0 0.1 row_kernel.1
  32.1 3.3 %collective-permute-start.12 = (bf16[48,512]{1,0:T(8,128)(2,1)S(1)}, bf16[48,512]{1,0:T(8,128)(2,1)S(1)}, u32[]{:S(2)}, u32[]{:S(2)}) collective-permute-start(bf16[48,512]{1,0:T(8,128)(2,1)S(1)} %get-tuple-element.23.own_ref), channel_id=1, source_target_pairs={{0,128},{8,136},{16,144},{24,152},{32,160},{40,168},{48,176},{56,1... | collective-permute-start | bytes 147464 | tf_op jit(solution)/shard_map/ppermute | solution.py:383
  35.4 1.1 %collective-permute-start.11 = (bf16[48,512]{1,0:T(8,128)(2,1)S(1)}, bf16[48,512]{1,0:T(8,128)(2,1)S(1)}, u32[]{:S(2)}, u32[]{:S(2)}) collective-permute-start(bf16[48,512]{1,0:T(8,128)(2,1)S(1)} %get-tuple-element.23.own_ref), channel_id=1, source_target_pairs={{0,192},{8,200},{16,208},{24,216},{32,224},{40,232},{48,240},{56,2... | collective-permute-start | bytes 147464 | tf_op jit(solution)/shard_map/ppermute | solution.py:383
  36.5 1.0 %collective-permute-start.10 = (bf16[48,512]{1,0:T(8,128)(2,1)S(1)}, bf16[48,512]{1,0:T(8,128)(2,1)S(1)}, u32[]{:S(2)}, u32[]{:S(2)}) collective-permute-start(bf16[48,512]{1,0:T(8,128)(2,1)S(1)} %get-tuple-element.23.own_ref), channel_id=1, source_target_pairs={{0,64},{8,72},{16,80},{24,88},{32,96},{40,104},{48,112},{56,120},{... | collective-permute-start | bytes 147464 | tf_op jit(solution)/shard_map/ppermute | solution.py:383
  37.4 0.9 %local_kernel.1 = (f32[16,8,512]{2,1,0:T(8,128)S(1)}, f32[16,8,512]{2,1,0:T(8,128)S(1)}) custom-call(bf16[3,16,512]{2,1,0:T(8,128)(2,1)S(1)} %collective-permute-done.refs_0_, bf16[2,3,16,512]{3,2,1,0:T(8,128)(2,1)S(1)} %collective-permute-done.2.third_ref.refs_1_, bf16[2,3,16,512]{3,2,1,0:T(8,128)(2,1)S(1)} %collective-permute-done.3.second_ref.refs_2_, ...), custom_call_target="tpu_custom_call" | custom-call | flops 8388608 | bytes 2097152 | tf_op jit(solution)/shard_map/local_kernel/pallas_call | solution.py:325
  38.3 0.0 collective-permute-done.12.two_ref
  38.3 1.2 %collective-permute-done.11.three_ref = bf16[48,512]{1,0:T(8,128)(2,1)S(1)} collective-permute-done((bf16[48,512]{1,0:T(8,128)(2,1)S(1)}, bf16[48,512]{1,0:T(8,128)(2,1)S(1)}, u32[]{:S(2)}, u32[]{:S(2)}) %collective-permute-start.11) | collective-permute-done | bytes 49184 | tf_op jit(solution)/shard_map/ppermute | solution.py:383
  39.5 2.3 %collective-permute-done.10.one_ref = bf16[48,512]{1,0:T(8,128)(2,1)S(1)} collective-permute-done((bf16[48,512]{1,0:T(8,128)(2,1)S(1)}, bf16[48,512]{1,0:T(8,128)(2,1)S(1)}, u32[]{:S(2)}, u32[]{:S(2)}) %collective-permute-start.10) | collective-permute-done | bytes 49184 | tf_op jit(solution)/shard_map/ppermute | solution.py:383
  41.8 0.1 merge_kernel.1.carry_ref
  41.9 1.1 %final_kernel.1 = bf16[128,512]{1,0:T(8,128)(2,1)} custom-call(f32[24,512]{1,0:T(8,128)S(1)} %merge_kernel.1.carry_ref, f32[32,512]{1,0:T(8,128)S(1)} %get-tuple-element.21.kept_ref.summary_ref, f32[3,3,512]{2,1,0:T(4,128)S(1)} %copy-done.1, f32[16,512]{1,0:T(8,128)S(1)} %copy-done, f32[16,512]{1,0:T(8,128)S(1)} %copy-done.2, f32[1,512]{1,0:T(1,128)S(1)} %bitcast.18, ...), custom_call_target="tpu_custom_call" | custom-call | tf_op jit(solution)/shard_map/final_kernel/pallas_call | solution.py:325
  (7 shorter events, 0.1 us)
Async XLA Ops:
  0.0 7.4 %copy-start.4 = (bf16[16,3,4096]{2,0,1:T(8,128)(2,1)S(1)}, bf16[16,3,4096]{2,0,1:T(8,128)(2,1)}, u32[]{:S(2)}) copy-start(bf16[16,3,4096]{2,0,1:T(8,128)(2,1)} %param.5) | copy-start | bytes 1179652
  1.0 6.5 %collective-permute-start.1 = (bf16[3,3,16,512]{3,2,1,0:T(8,128)(2,1)S(1)}, bf16[3,3,16,512]{3,2,1,0:T(8,128)(2,1)S(1)}, u32[]{:S(2)}, u32[]{:S(2)}) collective-permute-start(bf16[3,3,16,512]{3,2,1,0:T(8,128)(2,1)S(1)} %pad_maximum_fusion), channel_id=1, source_target_pairs={{0,8},{8,0},{16,24},{24,16},{32,40},{40,32},{48,56},{56,48},{64,72... | collective-permute-start | bytes 442376 | tf_op jit(solution)/shard_map/ppermute | solution.py:357
  1.1 11.2 %collective-permute-start = (bf16[3,16,512]{2,1,0:T(8,128)(2,1)S(1)}, bf16[3,16,512]{2,1,0:T(8,128)(2,1)S(1)}, u32[]{:S(2)}, u32[]{:S(2)}) collective-permute-start(bf16[3,16,512]{2,1,0:T(8,128)(2,1)S(1)} %get-tuple-element.36), channel_id=1, source_target_pairs={{0,4},{1,5},{2,6},{3,7},{4,0},{5,1},{6,2},{7,3},{8,12},{9,13},{10,... | collective-permute-start | bytes 147464 | tf_op jit(solution)/shard_map/ppermute | solution.py:354
  7.5 10.0 %collective-permute-start.2 = (bf16[2,3,16,512]{3,2,1,0:T(8,128)(2,1)S(1)}, bf16[2,3,16,512]{3,2,1,0:T(8,128)(2,1)S(1)}, u32[]{:S(2)}, u32[]{:S(2)}) collective-permute-start(bf16[2,3,16,512]{3,2,1,0:T(8,128)(2,1)S(1)} %join.3), channel_id=1, source_target_pairs={{0,3},{1,4},{2,5},{3,6},{4,7},{5,0},{6,1},{7,2},{8,13},{9,14},{10,... | collective-permute-start | bytes 294920 | tf_op jit(solution)/shard_map/ppermute | solution.py:354
  8.4 10.6 %collective-permute-start.3 = (bf16[2,3,16,512]{3,2,1,0:T(8,128)(2,1)S(1)}, bf16[2,3,16,512]{3,2,1,0:T(8,128)(2,1)S(1)}, u32[]{:S(2)}, u32[]{:S(2)}) collective-permute-start(bf16[2,3,16,512]{3,2,1,0:T(8,128)(2,1)S(1)} %join.4), channel_id=1, source_target_pairs={{0,2},{1,3},{2,4},{3,5},{4,6},{5,7},{6,0},{7,1},{8,14},{9,15},{10,... | collective-permute-start | bytes 294920 | tf_op jit(solution)/shard_map/ppermute | solution.py:354
  12.3 6.8 %copy-start = (f32[16,512]{1,0:T(8,128)S(1)}, f32[16,512]{1,0:T(8,128)}, u32[]{:S(2)}) copy-start(f32[16,512]{1,0:T(8,128)} %rates_ref.9) | copy-start | bytes 98308
  12.3 6.8 %copy-start.2 = (f32[16,512]{1,0:T(8,128)S(1)}, f32[16,512]{1,0:T(8,128)}, u32[]{:S(2)}) copy-start(f32[16,512]{1,0:T(8,128)} %residues_ref.3) | copy-start | bytes 98308
  12.3 6.7 %collective-permute-start.4 = (bf16[2,3,16,512]{3,2,1,0:T(8,128)(2,1)S(1)}, bf16[2,3,16,512]{3,2,1,0:T(8,128)(2,1)S(1)}, u32[]{:S(2)}, u32[]{:S(2)}) collective-permute-start(bf16[2,3,16,512]{3,2,1,0:T(8,128)(2,1)S(1)} %join.5), channel_id=1, source_target_pairs={{0,1},{1,2},{2,3},{3,4},{4,5},{5,6},{6,7},{7,0},{8,15},{9,8},{10,9... | collective-permute-start | bytes 294920 | tf_op jit(solution)/shard_map/ppermute | solution.py:354
  19.0 0.7 %copy-start.3 = (f32[512]{0:T(512)S(1)}, f32[512]{0:T(512)}, u32[]{:S(2)}) copy-start(f32[512]{0:T(512)} %param.9) | copy-start | bytes 6148
  19.0 1.5 %collective-permute-start.5 = (bf16[3,3,16,512]{3,2,1,0:T(8,128)(2,1)S(1)}, bf16[3,3,16,512]{3,2,1,0:T(8,128)(2,1)S(1)}, u32[]{:S(2)}, u32[]{:S(2)}) collective-permute-start(bf16[3,3,16,512]{3,2,1,0:T(8,128)(2,1)S(1)} %back_kernel.1), channel_id=1, source_target_pairs={{0,8},{8,0},{16,24},{24,16},{32,40},{40,32},{48,56},{56,48},{64,72... | collective-permute-start | bytes 442376 | tf_op jit(solution)/shard_map/ppermute | solution.py:368
  19.7 0.8 %copy-start.1 = (f32[3,3,512]{2,1,0:T(4,128)S(1)}, f32[3,3,512]{2,1,0:T(4,128)}, u32[]{:S(2)}) copy-start(f32[3,3,512]{2,1,0:T(4,128)} %taps_ref.7) | copy-start | bytes 55300
  21.1 1.3 %collective-permute-start.6 = (f32[32,512]{1,0:T(8,128)S(1)}, f32[32,512]{1,0:T(8,128)S(1)}, u32[]{:S(2)}, u32[]{:S(2)}) collective-permute-start(f32[32,512]{1,0:T(8,128)S(1)} %get-tuple-element.21.kept_ref.summary_ref), channel_id=1, source_target_pairs={{0,8},{8,0},{16,24},{24,16},{32,40},{40,32},{48,56},{56,48},{64,72... | collective-permute-start | bytes 196616 | tf_op jit(solution)/shard_map/ppermute | solution.py:376
  22.4 5.7 %collective-permute-start.9 = (bf16[48,512]{1,0:T(8,128)(2,1)S(1)}, bf16[48,512]{1,0:T(8,128)(2,1)S(1)}, u32[]{:S(2)}, u32[]{:S(2)}) collective-permute-start(bf16[48,512]{1,0:T(8,128)(2,1)S(1)} %get-tuple-element.22.own_ref), channel_id=1, source_target_pairs={{0,32},{8,40},{16,48},{24,56},{32,0},{40,8},{48,16},{56,24},{64,96... | collective-permute-start | bytes 147464 | tf_op jit(solution)/shard_map/ppermute | solution.py:383
  25.6 4.1 %collective-permute-start.8 = (bf16[48,512]{1,0:T(8,128)(2,1)S(1)}, bf16[48,512]{1,0:T(8,128)(2,1)S(1)}, u32[]{:S(2)}, u32[]{:S(2)}) collective-permute-start(bf16[48,512]{1,0:T(8,128)(2,1)S(1)} %get-tuple-element.22.own_ref), channel_id=1, source_target_pairs={{0,48},{8,56},{16,0},{24,8},{32,16},{40,24},{48,32},{56,40},{64,11... | collective-permute-start | bytes 147464 | tf_op jit(solution)/shard_map/ppermute | solution.py:383
  26.7 5.3 %collective-permute-start.7 = (bf16[48,512]{1,0:T(8,128)(2,1)S(1)}, bf16[48,512]{1,0:T(8,128)(2,1)S(1)}, u32[]{:S(2)}, u32[]{:S(2)}) collective-permute-start(bf16[48,512]{1,0:T(8,128)(2,1)S(1)} %get-tuple-element.22.own_ref), channel_id=1, source_target_pairs={{0,16},{8,24},{16,32},{24,40},{32,48},{40,56},{48,0},{56,8},{64,80... | collective-permute-start | bytes 147464 | tf_op jit(solution)/shard_map/ppermute | solution.py:383
  32.1 6.2 %collective-permute-start.12 = (bf16[48,512]{1,0:T(8,128)(2,1)S(1)}, bf16[48,512]{1,0:T(8,128)(2,1)S(1)}, u32[]{:S(2)}, u32[]{:S(2)}) collective-permute-start(bf16[48,512]{1,0:T(8,128)(2,1)S(1)} %get-tuple-element.23.own_ref), channel_id=1, source_target_pairs={{0,128},{8,136},{16,144},{24,152},{32,160},{40,168},{48,176},{56,1... | collective-permute-start | bytes 147464 | tf_op jit(solution)/shard_map/ppermute | solution.py:383
  35.4 4.1 %collective-permute-start.11 = (bf16[48,512]{1,0:T(8,128)(2,1)S(1)}, bf16[48,512]{1,0:T(8,128)(2,1)S(1)}, u32[]{:S(2)}, u32[]{:S(2)}) collective-permute-start(bf16[48,512]{1,0:T(8,128)(2,1)S(1)} %get-tuple-element.23.own_ref), channel_id=1, source_target_pairs={{0,192},{8,200},{16,208},{24,216},{32,224},{40,232},{48,240},{56,2... | collective-permute-start | bytes 147464 | tf_op jit(solution)/shard_map/ppermute | solution.py:383
  36.5 5.3 %collective-permute-start.10 = (bf16[48,512]{1,0:T(8,128)(2,1)S(1)}, bf16[48,512]{1,0:T(8,128)(2,1)S(1)}, u32[]{:S(2)}, u32[]{:S(2)}) collective-permute-start(bf16[48,512]{1,0:T(8,128)(2,1)S(1)} %get-tuple-element.23.own_ref), channel_id=1, source_target_pairs={{0,64},{8,72},{16,80},{24,88},{32,96},{40,104},{48,112},{56,120},{... | collective-permute-start | bytes 147464 | tf_op jit(solution)/shard_map/ppermute | solution.py:383

commit v12 on v7

--- a/solution.py
+++ b/solution.py
@@ -272,10 +272,11 @@
 
 
 def final_kernel(
-    carry_ref, summary_ref, taps_ref, rates_ref, residues_ref, bias_ref, decay_ref, weight_ref, local_ref, front_ref, out_ref, natural
+    carry_ref, summary_ref, taps_ref, rates_ref, residues_ref, bias_ref, decay_ref, weight_ref, local_ref, front_ref, out_ref, natural, rounded, sems
 ):
     modes, channels = rates_ref.shape
     rows = row_iota()
+    copies = []
 
     def at_first(row):
         return jnp.where(rows == 0, spread(row), 0.0)
@@ -305,7 +306,12 @@
                 total[i] = total[i] + carried
         for i in range(SUB):
             natural[start // LANES, pl.ds(i, 8, stride=SUB), :] = front[i] * total[i]
-        out_ref[:, lanes] = natural[start // LANES].astype(out_ref.dtype)
+        group = start // LANES
+        rounded[group] = natural[group].astype(out_ref.dtype)
+        copies.append(pltpu.make_async_copy(rounded.at[group], out_ref.at[:, lanes], sems.at[group]))
+        copies[-1].start()
+    for copy in copies:
+        copy.wait()
 
 
 def body(streams, short_taps, residues, rates, bias):
@@ -320,13 +326,13 @@
     plane = pltpu.VMEM((channels // LANES, tokens, LANES), f32)
     bias = bias[None]
 
-    def kernel(function, out_shape, operands, scratch=(), cost=None, name=None):
+    def kernel(function, out_shape, operands, scratch=(), cost=None, name=None, out_specs=VMEM):
         several = isinstance(out_shape, tuple)
         return pl.pallas_call(
             function,
             out_shape=out_shape,
             in_specs=[VMEM] * len(operands),
-            out_specs=(VMEM,) * len(out_shape) if several else VMEM,
+            out_specs=(VMEM,) * len(out_shape) if several else out_specs,
             scratch_shapes=list(scratch),
             compiler_params=pltpu.CompilerParams(vmem_limit_bytes=24 << 20),
             cost_estimate=cost,
@@ -399,7 +405,12 @@
         final_kernel,
         jax.ShapeDtypeStruct((tokens, channels), jnp.bfloat16),
         (carry, summary, short_taps, rates, residues, bias, decay, carry_weight, local, front),
-        [plane],
+        [
+            plane,
+            pltpu.VMEM((channels // LANES, tokens, LANES), jnp.bfloat16),
+            pltpu.SemaphoreType.DMA((channels // LANES,)),
+        ],
+        out_specs=pl.BlockSpec(memory_space=pl.ANY),
     )
 
 

time: 43.2 us -> 43.2 us (level)
  no operation moved by 1% of the time
where the time goes in v12:
time: 43.2 us; the launch traced here: 43 us
  starting transfers between devices  19.8 us (46%)
  waiting for transfers between devices  18.6 us (43%)
  Pallas kernels  2.94 us (7%)
  local copies, waits for them, and re-layouts  1.55 us (4%)
    ppermute x6, starting transfers between devices, around(): parts[by] = lax.ppermute(value, 'ctx', route)  10.4 us
    ppermute x4, waiting for transfers between devices, along(): return lax.ppermute(value, ('ctx', 'tp'), route)  8.91 us
    ppermute x4, starting transfers between devices, along(): return lax.ppermute(value, ('ctx', 'tp'), route)  8.89 us
    ppermute x6, waiting for transfers between devices, around(): parts[by] = lax.ppermute(value, 'ctx', route)  7.87 us
    pallas_call x11, Pallas kernels, kernel(): pl.pallas_call(function, out_shape=out_shape, in_specs=[VMEM] * len(opera...  2.94 us
    ppermute x1, waiting for transfers between devices, body(): got = lax.ppermute(summary, 'ctx', swap)  1.11 us
    dynamic_slice x1, local copies, waits for them, and re-layouts, block_for(): return lax.dynamic_slice(by_stream, (0, 0, at), (3, SUB, channels))  0.99 us
  transfers between devices with their start and end apart: 13, of which 10 were waited for; matrix products, arithmetic and copies ran while one was open for 0% of the time, Pallas kernels for 2%

profile of v12, /device:TPU:32, one launch (start us, length us, event | category | flops | bytes accessed | tf_op | source)
XLA Modules:
  0.0 43.0 jit_solution(14548499162684820827)
XLA Ops:
  0.0 1.0 %dynamic-slice_bitcast_fusion = (bf16[3,16,512]{2,1,0:T(8,128)(2,1)S(1)}, bf16[3,16,512]{2,1,0:T(8,128)(2,1)S(1)}, bf16[1,3,16,512]{3,2,1,0:T(8,128)(2,1)S(1)}, ...) fusion(bf16[16,3,4096]{2,0,1:T(8,128)(2,1)} %param.5, ...), kind=kLoop, calls=%fused_computation.1 | loop fusion | bytes 786464 | tf_op jit(solution)/shard_map/dynamic_slice | solution.py:353
  1.0 0.1 collective-permute-start.1
  1.1 6.4 %collective-permute-start = (bf16[3,16,512]{2,1,0:T(8,128)(2,1)S(1)}, bf16[3,16,512]{2,1,0:T(8,128)(2,1)S(1)}, u32[]{:S(2)}, u32[]{:S(2)}) collective-permute-start(bf16[3,16,512]{2,1,0:T(8,128)(2,1)S(1)} %get-tuple-element.35), channel_id=1, source_target_pairs={{0,4},{1,5},{2,6},{3,7},{4,0},{5,1},{6,2},{7,3},{8,12},{9,13},{10,... | collective-permute-start | bytes 147464 | tf_op jit(solution)/shard_map/ppermute | solution.py:360
  7.5 0.0 collective-permute-done.1.passed_ref
  7.5 0.9 %collective-permute-start.2 = (bf16[2,3,16,512]{3,2,1,0:T(8,128)(2,1)S(1)}, bf16[2,3,16,512]{3,2,1,0:T(8,128)(2,1)S(1)}, u32[]{:S(2)}, u32[]{:S(2)}) collective-permute-start(bf16[2,3,16,512]{3,2,1,0:T(8,128)(2,1)S(1)} %join.3), channel_id=1, source_target_pairs={{0,3},{1,4},{2,5},{3,6},{4,7},{5,0},{6,1},{7,2},{8,13},{9,14},{10,... | collective-permute-start | bytes 294920 | tf_op jit(solution)/shard_map/ppermute | solution.py:360
  8.4 1.5 %collective-permute-start.3 = (bf16[2,3,16,512]{3,2,1,0:T(8,128)(2,1)S(1)}, bf16[2,3,16,512]{3,2,1,0:T(8,128)(2,1)S(1)}, u32[]{:S(2)}, u32[]{:S(2)}) collective-permute-start(bf16[2,3,16,512]{3,2,1,0:T(8,128)(2,1)S(1)} %join.4), channel_id=1, source_target_pairs={{0,2},{1,3},{2,4},{3,5},{4,6},{5,7},{6,0},{7,1},{8,14},{9,15},{10,... | collective-permute-start | bytes 294920 | tf_op jit(solution)/shard_map/ppermute | solution.py:360
  10.0 2.3 %collective-permute-done.refs_0_ = bf16[3,16,512]{2,1,0:T(8,128)(2,1)S(1)} collective-permute-done((bf16[3,16,512]{2,1,0:T(8,128)(2,1)S(1)}, bf16[3,16,512]{2,1,0:T(8,128)(2,1)S(1)}, u32[]{:S(2)}, u32[]{:S(2)}) %collective-permute-start) | collective-permute-done | bytes 49184 | tf_op jit(solution)/shard_map/ppermute | solution.py:360
  12.3 0.0 copy-start
  12.3 0.0 copy-start.2
  12.3 0.1 collective-permute-start.4
  12.4 5.0 %collective-permute-done.2.third_ref.refs_1_ = bf16[2,3,16,512]{3,2,1,0:T(8,128)(2,1)S(1)} collective-permute-done((bf16[2,3,16,512]{3,2,1,0:T(8,128)(2,1)S(1)}, bf16[2,3,16,512]{3,2,1,0:T(8,128)(2,1)S(1)}, u32[]{:S(2)}, u32[]{:S(2)}) %collective-permute-start.2) | collective-permute-done | bytes 98336 | tf_op jit(solution)/shard_map/ppermute | solution.py:360
  17.5 1.5 %collective-permute-done.3.second_ref.refs_2_ = bf16[2,3,16,512]{3,2,1,0:T(8,128)(2,1)S(1)} collective-permute-done((bf16[2,3,16,512]{3,2,1,0:T(8,128)(2,1)S(1)}, bf16[2,3,16,512]{3,2,1,0:T(8,128)(2,1)S(1)}, u32[]{:S(2)}, u32[]{:S(2)}) %collective-permute-start.3) | collective-permute-done | bytes 98336 | tf_op jit(solution)/shard_map/ppermute | solution.py:360
  19.0 0.0 collective-permute-done.4.first_ref.refs_3_
  19.0 0.0 copy-start.3
  19.0 0.1 collective-permute-start.5
  19.1 0.0 copy-done
  19.1 0.0 copy-done.2
  19.1 0.5 %copy-done.3 = f32[512]{0:T(512)S(1)} copy-done((f32[512]{0:T(512)S(1)}, f32[512]{0:T(512)}, u32[]{:S(2)}) %copy-start.3) | copy-done | bytes 2072
  19.7 0.0 copy-start.1
  19.7 0.1 weights_kernel.1
  19.8 0.7 %collective-permute-done.5.refs_4_ = bf16[3,3,16,512]{3,2,1,0:T(8,128)(2,1)S(1)} collective-permute-done((bf16[3,3,16,512]{3,2,1,0:T(8,128)(2,1)S(1)}, bf16[3,3,16,512]{3,2,1,0:T(8,128)(2,1)S(1)}, u32[]{:S(2)}, u32[]{:S(2)}) %collective-permute-start.5) | collective-permute-done | bytes 147488 | tf_op jit(solution)/shard_map/ppermute | solution.py:372
  20.5 0.0 copy-done.1
  20.5 0.6 %state_kernel.1 = (f32[32,512]{1,0:T(8,128)S(1)}, f32[16,8,512]{2,1,0:T(8,128)S(1)}, f32[16,8,512]{2,1,0:T(8,128)S(1)}) custom-call(bf16[3,16,512]{2,1,0:T(8,128)(2,1)S(1)} %collective-permute-done.refs_0_, bf16[2,3,16,512]{3,2,1,0:T(8,128)(2,1)S(1)} %collective-permute-done.2.third_ref.refs_1_, ...), custom_call_target="tpu_custom_call" | custom-call | tf_op jit(solution)/shard_map/state_kernel/pallas_call | solution.py:331
  21.1 0.2 collective-permute-start.6
  21.3 1.1 %collective-permute-done.6.got_ref = f32[32,512]{1,0:T(8,128)S(1)} collective-permute-done((f32[32,512]{1,0:T(8,128)S(1)}, f32[32,512]{1,0:T(8,128)S(1)}, u32[]{:S(2)}, u32[]{:S(2)}) %collective-permute-start.6) | collective-permute-done | bytes 65568 | tf_op jit(solution)/shard_map/ppermute | solution.py:380
  22.5 3.1 %collective-permute-start.9 = (bf16[48,512]{1,0:T(8,128)(2,1)S(1)}, bf16[48,512]{1,0:T(8,128)(2,1)S(1)}, u32[]{:S(2)}, u32[]{:S(2)}) collective-permute-start(bf16[48,512]{1,0:T(8,128)(2,1)S(1)} %get-tuple-element.20.own_ref), channel_id=1, source_target_pairs={{0,32},{8,40},{16,48},{24,56},{32,0},{40,8},{48,16},{56,24},{64,96... | collective-permute-start | bytes 147464 | tf_op jit(solution)/shard_map/ppermute | solution.py:387
  25.6 1.1 %collective-permute-start.8 = (bf16[48,512]{1,0:T(8,128)(2,1)S(1)}, bf16[48,512]{1,0:T(8,128)(2,1)S(1)}, u32[]{:S(2)}, u32[]{:S(2)}) collective-permute-start(bf16[48,512]{1,0:T(8,128)(2,1)S(1)} %get-tuple-element.20.own_ref), channel_id=1, source_target_pairs={{0,48},{8,56},{16,0},{24,8},{32,16},{40,24},{48,32},{56,40},{64,11... | collective-permute-start | bytes 147464 | tf_op jit(solution)/shard_map/ppermute | solution.py:387
  26.7 0.9 %collective-permute-start.7 = (bf16[48,512]{1,0:T(8,128)(2,1)S(1)}, bf16[48,512]{1,0:T(8,128)(2,1)S(1)}, u32[]{:S(2)}, u32[]{:S(2)}) collective-permute-start(bf16[48,512]{1,0:T(8,128)(2,1)S(1)} %get-tuple-element.20.own_ref), channel_id=1, source_target_pairs={{0,16},{8,24},{16,32},{24,40},{32,48},{40,56},{48,0},{56,8},{64,80... | collective-permute-start | bytes 147464 | tf_op jit(solution)/shard_map/ppermute | solution.py:387
  27.6 0.5 %collective-permute-done.9.two_ref = bf16[48,512]{1,0:T(8,128)(2,1)S(1)} collective-permute-done((bf16[48,512]{1,0:T(8,128)(2,1)S(1)}, bf16[48,512]{1,0:T(8,128)(2,1)S(1)}, u32[]{:S(2)}, u32[]{:S(2)}) %collective-permute-start.9) | collective-permute-done | bytes 49184 | tf_op jit(solution)/shard_map/ppermute | solution.py:387
  28.1 1.5 %collective-permute-done.8.three_ref = bf16[48,512]{1,0:T(8,128)(2,1)S(1)} collective-permute-done((bf16[48,512]{1,0:T(8,128)(2,1)S(1)}, bf16[48,512]{1,0:T(8,128)(2,1)S(1)}, u32[]{:S(2)}, u32[]{:S(2)}) %collective-permute-start.8) | collective-permute-done | bytes 49184 | tf_op jit(solution)/shard_map/ppermute | solution.py:387
  29.7 2.4 %collective-permute-done.7.one_ref = bf16[48,512]{1,0:T(8,128)(2,1)S(1)} collective-permute-done((bf16[48,512]{1,0:T(8,128)(2,1)S(1)}, bf16[48,512]{1,0:T(8,128)(2,1)S(1)}, u32[]{:S(2)}, u32[]{:S(2)}) %collective-permute-start.7) | collective-permute-done | bytes 49184 | tf_op jit(solution)/shard_map/ppermute | solution.py:387
  32.0 0.1 row_kernel.1
  32.1 3.3 %collective-permute-start.12 = (bf16[48,512]{1,0:T(8,128)(2,1)S(1)}, bf16[48,512]{1,0:T(8,128)(2,1)S(1)}, u32[]{:S(2)}, u32[]{:S(2)}) collective-permute-start(bf16[48,512]{1,0:T(8,128)(2,1)S(1)} %get-tuple-element.21.own_ref), channel_id=1, source_target_pairs={{0,128},{8,136},{16,144},{24,152},{32,160},{40,168},{48,176},{56,1... | collective-permute-start | bytes 147464 | tf_op jit(solution)/shard_map/ppermute | solution.py:387
  35.4 1.1 %collective-permute-start.11 = (bf16[48,512]{1,0:T(8,128)(2,1)S(1)}, bf16[48,512]{1,0:T(8,128)(2,1)S(1)}, u32[]{:S(2)}, u32[]{:S(2)}) collective-permute-start(bf16[48,512]{1,0:T(8,128)(2,1)S(1)} %get-tuple-element.21.own_ref), channel_id=1, source_target_pairs={{0,192},{8,200},{16,208},{24,216},{32,224},{40,232},{48,240},{56,2... | collective-permute-start | bytes 147464 | tf_op jit(solution)/shard_map/ppermute | solution.py:387
  36.5 1.0 %collective-permute-start.10 = (bf16[48,512]{1,0:T(8,128)(2,1)S(1)}, bf16[48,512]{1,0:T(8,128)(2,1)S(1)}, u32[]{:S(2)}, u32[]{:S(2)}) collective-permute-start(bf16[48,512]{1,0:T(8,128)(2,1)S(1)} %get-tuple-element.21.own_ref), channel_id=1, source_target_pairs={{0,64},{8,72},{16,80},{24,88},{32,96},{40,104},{48,112},{56,120},{... | collective-permute-start | bytes 147464 | tf_op jit(solution)/shard_map/ppermute | solution.py:387
  37.5 0.9 %local_kernel.1 = (f32[16,8,512]{2,1,0:T(8,128)S(1)}, f32[16,8,512]{2,1,0:T(8,128)S(1)}) custom-call(bf16[3,16,512]{2,1,0:T(8,128)(2,1)S(1)} %collective-permute-done.refs_0_, bf16[2,3,16,512]{3,2,1,0:T(8,128)(2,1)S(1)} %collective-permute-done.2.third_ref.refs_1_, bf16[2,3,16,512]{3,2,1,0:T(8,128)(2,1)S(1)} %collective-permute-done.3.second_ref.refs_2_, ...), custom_call_target="tpu_custom_call" | custom-call | flops 8388608 | bytes 2097152 | tf_op jit(solution)/shard_map/local_kernel/pallas_call | solution.py:331
  38.3 0.0 collective-permute-done.12.two_ref
  38.3 1.2 %collective-permute-done.11.three_ref = bf16[48,512]{1,0:T(8,128)(2,1)S(1)} collective-permute-done((bf16[48,512]{1,0:T(8,128)(2,1)S(1)}, bf16[48,512]{1,0:T(8,128)(2,1)S(1)}, u32[]{:S(2)}, u32[]{:S(2)}) %collective-permute-start.11) | collective-permute-done | bytes 49184 | tf_op jit(solution)/shard_map/ppermute | solution.py:387
  39.5 2.3 %collective-permute-done.10.one_ref = bf16[48,512]{1,0:T(8,128)(2,1)S(1)} collective-permute-done((bf16[48,512]{1,0:T(8,128)(2,1)S(1)}, bf16[48,512]{1,0:T(8,128)(2,1)S(1)}, u32[]{:S(2)}, u32[]{:S(2)}) %collective-permute-start.10) | collective-permute-done | bytes 49184 | tf_op jit(solution)/shard_map/ppermute | solution.py:387
  41.8 0.1 merge_kernel.1.carry_ref
  41.9 1.0 %final_kernel.1 = bf16[128,512]{1,0:T(8,128)(2,1)} custom-call(f32[24,512]{1,0:T(8,128)S(1)} %merge_kernel.1.carry_ref, f32[32,512]{1,0:T(8,128)S(1)} %get-tuple-element.19.kept_ref.summary_ref, f32[3,3,512]{2,1,0:T(4,128)S(1)} %copy-done.1, f32[16,512]{1,0:T(8,128)S(1)} %copy-done, f32[16,512]{1,0:T(8,128)S(1)} %copy-done.2, f32[1,512]{1,0:T(1,128)S(1)} %bitcast.25, ...), custom_call_target="tpu_custom_call" | custom-call | tf_op jit(solution)/shard_map/final_kernel/pallas_call | solution.py:331
  (6 shorter events, 0.1 us)
Async XLA Ops:
  1.0 6.5 %collective-permute-start.1 = (bf16[3,3,16,512]{3,2,1,0:T(8,128)(2,1)S(1)}, bf16[3,3,16,512]{3,2,1,0:T(8,128)(2,1)S(1)}, u32[]{:S(2)}, u32[]{:S(2)}) collective-permute-start(bf16[3,3,16,512]{3,2,1,0:T(8,128)(2,1)S(1)} %pad_maximum_fusion), channel_id=1, source_target_pairs={{0,8},{8,0},{16,24},{24,16},{32,40},{40,32},{48,56},{56,48},{64,72... | collective-permute-start | bytes 442376 | tf_op jit(solution)/shard_map/ppermute | solution.py:362
  1.1 11.2 %collective-permute-start = (bf16[3,16,512]{2,1,0:T(8,128)(2,1)S(1)}, bf16[3,16,512]{2,1,0:T(8,128)(2,1)S(1)}, u32[]{:S(2)}, u32[]{:S(2)}) collective-permute-start(bf16[3,16,512]{2,1,0:T(8,128)(2,1)S(1)} %get-tuple-element.35), channel_id=1, source_target_pairs={{0,4},{1,5},{2,6},{3,7},{4,0},{5,1},{6,2},{7,3},{8,12},{9,13},{10,... | collective-permute-start | bytes 147464 | tf_op jit(solution)/shard_map/ppermute | solution.py:360
  7.5 9.9 %collective-permute-start.2 = (bf16[2,3,16,512]{3,2,1,0:T(8,128)(2,1)S(1)}, bf16[2,3,16,512]{3,2,1,0:T(8,128)(2,1)S(1)}, u32[]{:S(2)}, u32[]{:S(2)}) collective-permute-start(bf16[2,3,16,512]{3,2,1,0:T(8,128)(2,1)S(1)} %join.3), channel_id=1, source_target_pairs={{0,3},{1,4},{2,5},{3,6},{4,7},{5,0},{6,1},{7,2},{8,13},{9,14},{10,... | collective-permute-start | bytes 294920 | tf_op jit(solution)/shard_map/ppermute | solution.py:360
  8.4 10.6 %collective-permute-start.3 = (bf16[2,3,16,512]{3,2,1,0:T(8,128)(2,1)S(1)}, bf16[2,3,16,512]{3,2,1,0:T(8,128)(2,1)S(1)}, u32[]{:S(2)}, u32[]{:S(2)}) collective-permute-start(bf16[2,3,16,512]{3,2,1,0:T(8,128)(2,1)S(1)} %join.4), channel_id=1, source_target_pairs={{0,2},{1,3},{2,4},{3,5},{4,6},{5,7},{6,0},{7,1},{8,14},{9,15},{10,... | collective-permute-start | bytes 294920 | tf_op jit(solution)/shard_map/ppermute | solution.py:360
  12.3 6.8 %copy-start = (f32[16,512]{1,0:T(8,128)S(1)}, f32[16,512]{1,0:T(8,128)}, u32[]{:S(2)}) copy-start(f32[16,512]{1,0:T(8,128)} %rates_ref.9) | copy-start | bytes 98308
  12.3 6.8 %copy-start.2 = (f32[16,512]{1,0:T(8,128)S(1)}, f32[16,512]{1,0:T(8,128)}, u32[]{:S(2)}) copy-start(f32[16,512]{1,0:T(8,128)} %residues_ref.3) | copy-start | bytes 98308
  12.3 6.7 %collective-permute-start.4 = (bf16[2,3,16,512]{3,2,1,0:T(8,128)(2,1)S(1)}, bf16[2,3,16,512]{3,2,1,0:T(8,128)(2,1)S(1)}, u32[]{:S(2)}, u32[]{:S(2)}) collective-permute-start(bf16[2,3,16,512]{3,2,1,0:T(8,128)(2,1)S(1)} %join.5), channel_id=1, source_target_pairs={{0,1},{1,2},{2,3},{3,4},{4,5},{5,6},{6,7},{7,0},{8,15},{9,8},{10,9... | collective-permute-start | bytes 294920 | tf_op jit(solution)/shard_map/ppermute | solution.py:360
  19.0 0.7 %copy-start.3 = (f32[512]{0:T(512)S(1)}, f32[512]{0:T(512)}, u32[]{:S(2)}) copy-start(f32[512]{0:T(512)} %param.9) | copy-start | bytes 6148
  19.0 1.5 %collective-permute-start.5 = (bf16[3,3,16,512]{3,2,1,0:T(8,128)(2,1)S(1)}, bf16[3,3,16,512]{3,2,1,0:T(8,128)(2,1)S(1)}, u32[]{:S(2)}, u32[]{:S(2)}) collective-permute-start(bf16[3,3,16,512]{3,2,1,0:T(8,128)(2,1)S(1)} %back_kernel.1), channel_id=1, source_target_pairs={{0,8},{8,0},{16,24},{24,16},{32,40},{40,32},{48,56},{56,48},{64,72... | collective-permute-start | bytes 442376 | tf_op jit(solution)/shard_map/ppermute | solution.py:372
  19.7 0.8 %copy-start.1 = (f32[3,3,512]{2,1,0:T(4,128)S(1)}, f32[3,3,512]{2,1,0:T(4,128)}, u32[]{:S(2)}) copy-start(f32[3,3,512]{2,1,0:T(4,128)} %taps_ref.7) | copy-start | bytes 55300
  21.1 1.3 %collective-permute-start.6 = (f32[32,512]{1,0:T(8,128)S(1)}, f32[32,512]{1,0:T(8,128)S(1)}, u32[]{:S(2)}, u32[]{:S(2)}) collective-permute-start(f32[32,512]{1,0:T(8,128)S(1)} %get-tuple-element.19.kept_ref.summary_ref), channel_id=1, source_target_pairs={{0,8},{8,0},{16,24},{24,16},{32,40},{40,32},{48,56},{56,48},{64,72... | collective-permute-start | bytes 196616 | tf_op jit(solution)/shard_map/ppermute | solution.py:380
  22.5 5.7 %collective-permute-start.9 = (bf16[48,512]{1,0:T(8,128)(2,1)S(1)}, bf16[48,512]{1,0:T(8,128)(2,1)S(1)}, u32[]{:S(2)}, u32[]{:S(2)}) collective-permute-start(bf16[48,512]{1,0:T(8,128)(2,1)S(1)} %get-tuple-element.20.own_ref), channel_id=1, source_target_pairs={{0,32},{8,40},{16,48},{24,56},{32,0},{40,8},{48,16},{56,24},{64,96... | collective-permute-start | bytes 147464 | tf_op jit(solution)/shard_map/ppermute | solution.py:387
  25.6 4.1 %collective-permute-start.8 = (bf16[48,512]{1,0:T(8,128)(2,1)S(1)}, bf16[48,512]{1,0:T(8,128)(2,1)S(1)}, u32[]{:S(2)}, u32[]{:S(2)}) collective-permute-start(bf16[48,512]{1,0:T(8,128)(2,1)S(1)} %get-tuple-element.20.own_ref), channel_id=1, source_target_pairs={{0,48},{8,56},{16,0},{24,8},{32,16},{40,24},{48,32},{56,40},{64,11... | collective-permute-start | bytes 147464 | tf_op jit(solution)/shard_map/ppermute | solution.py:387
  26.7 5.3 %collective-permute-start.7 = (bf16[48,512]{1,0:T(8,128)(2,1)S(1)}, bf16[48,512]{1,0:T(8,128)(2,1)S(1)}, u32[]{:S(2)}, u32[]{:S(2)}) collective-permute-start(bf16[48,512]{1,0:T(8,128)(2,1)S(1)} %get-tuple-element.20.own_ref), channel_id=1, source_target_pairs={{0,16},{8,24},{16,32},{24,40},{32,48},{40,56},{48,0},{56,8},{64,80... | collective-permute-start | bytes 147464 | tf_op jit(solution)/shard_map/ppermute | solution.py:387
  32.1 6.2 %collective-permute-start.12 = (bf16[48,512]{1,0:T(8,128)(2,1)S(1)}, bf16[48,512]{1,0:T(8,128)(2,1)S(1)}, u32[]{:S(2)}, u32[]{:S(2)}) collective-permute-start(bf16[48,512]{1,0:T(8,128)(2,1)S(1)} %get-tuple-element.21.own_ref), channel_id=1, source_target_pairs={{0,128},{8,136},{16,144},{24,152},{32,160},{40,168},{48,176},{56,1... | collective-permute-start | bytes 147464 | tf_op jit(solution)/shard_map/ppermute | solution.py:387
  35.4 4.1 %collective-permute-start.11 = (bf16[48,512]{1,0:T(8,128)(2,1)S(1)}, bf16[48,512]{1,0:T(8,128)(2,1)S(1)}, u32[]{:S(2)}, u32[]{:S(2)}) collective-permute-start(bf16[48,512]{1,0:T(8,128)(2,1)S(1)} %get-tuple-element.21.own_ref), channel_id=1, source_target_pairs={{0,192},{8,200},{16,208},{24,216},{32,224},{40,232},{48,240},{56,2... | collective-permute-start | bytes 147464 | tf_op jit(solution)/shard_map/ppermute | solution.py:387
  36.5 5.3 %collective-permute-start.10 = (bf16[48,512]{1,0:T(8,128)(2,1)S(1)}, bf16[48,512]{1,0:T(8,128)(2,1)S(1)}, u32[]{:S(2)}, u32[]{:S(2)}) collective-permute-start(bf16[48,512]{1,0:T(8,128)(2,1)S(1)} %get-tuple-element.21.own_ref), channel_id=1, source_target_pairs={{0,64},{8,72},{16,80},{24,88},{32,96},{40,104},{48,112},{56,120},{... | collective-permute-start | bytes 147464 | tf_op jit(solution)/shard_map/ppermute | solution.py:387

commit v13 on v7

--- a/solution.py
+++ b/solution.py
@@ -9,7 +9,7 @@
 
 LENGTH = 4096
 SUB = 16
-PIECES = 6
+PIECES = 7
 LANES = 128
 BLOCK = 128
 VMEM = pl.BlockSpec(memory_space=pltpu.VMEM)
@@ -37,17 +37,17 @@
     out_ref[1] = passed_ref[at]
 
 
-def back_kernel(third_ref, second_ref, first_ref, out_ref):
-    for at, ref in enumerate((first_ref, second_ref, third_ref)):
-        out_ref[at] = ref[1]
+def back_kernel(*refs):
+    for at, ref in enumerate(refs[:-1]):
+        refs[-1][at] = ref[1]
 
 
 def with_sources(refs):
-    far, third, second, first, back, own = refs
+    far, third, second, first, back, last, own = refs
     me = lax.axis_index("tp")
     turn = 1 - 2 * core_index()
     places = [(own, 0), (far, 4), (first.at[0], 1), (second.at[0], 2), (third.at[0], 3)]
-    places += [(back.at[k - 1], -k) for k in (1, 2, 3)]
+    places += [(last.at[0], -1), (back.at[1], -2), (back.at[0], -3)]
     return [(ref, lax.rem(me - turn * shift + 8, 8)) for ref, shift in places]
 
 
@@ -356,15 +356,16 @@
     passed = lax.ppermute(jnp.stack([block_for(-k) for k in (1, 2, 3)]), "ctx", swap)
     far = along(block_for(4), 4)
     two = jax.ShapeDtypeStruct((2, 3, SUB, channels), streams.dtype)
-    three = jax.ShapeDtypeStruct((3, 3, SUB, channels), streams.dtype)
+    one = jax.ShapeDtypeStruct((1, 3, SUB, channels), streams.dtype)
 
     def both(shift, *after):
         return kernel(functools.partial(join_kernel, shift - 1), two, (block_for(shift), passed, *after), name="join")
 
     third, second = (along(both(k), k) for k in (3, 2))
     first = along(both(1, far), 1)
-    back = lax.ppermute(kernel(back_kernel, three, (third, second, first)), "ctx", swap)
-    blocks = [far, third, second, first, back, block_for(0)]
+    back = lax.ppermute(kernel(back_kernel, two, (third, second)), "ctx", swap)
+    last = lax.ppermute(kernel(back_kernel, one, (first,)), "ctx", swap)
+    blocks = [far, third, second, first, back, last, block_for(0)]
     summary, ends, signal = kernel(
         state_kernel,
         (packed, spans, wide),

time: 43.2 us -> 43.4 us (level)
  starting transfers between devices: 19.8 us -> 20.6 us
    ppermute x1 -> x2, starting transfers between devices: 0.09 us -> 0.65 us  [the longest x1 0.56 us: body(): last = lax.ppermute(kernel(back_kernel, one, (first,)), 'ctx', swap)]
    unnamed x8, local copies, waits for them, and re-layouts: 0.56 us -> 0.12 us
    pallas_call x11 -> x12, Pallas kernels: 2.96 us -> 2.96 us  [kernel(): pl.pallas_call(function, out_shape=out_shape, in_specs=[VMEM] * len(opera...]
  transfers between devices with their start and end apart: 13 -> 14, of which waited for: 10 -> 10; matrix products, arithmetic and copies ran while one was open for 0% -> 0% of each run, Pallas kernels for 2% -> 2%
where the time goes in v13:
time: 43.4 us; the launch traced here: 43.2 us
  starting transfers between devices  20.6 us (47%)
  waiting for transfers between devices  18.4 us (42%)
  Pallas kernels  2.96 us (7%)
  local copies, waits for them, and re-layouts  1.12 us (3%)
    ppermute x6, starting transfers between devices, around(): parts[by] = lax.ppermute(value, 'ctx', route)  10.4 us
    ppermute x4, waiting for transfers between devices, along(): return lax.ppermute(value, ('ctx', 'tp'), route)  8.97 us
    ppermute x4, starting transfers between devices, along(): return lax.ppermute(value, ('ctx', 'tp'), route)  8.86 us
    ppermute x6, waiting for transfers between devices, around(): parts[by] = lax.ppermute(value, 'ctx', route)  7.87 us
    pallas_call x12, Pallas kernels, kernel(): pl.pallas_call(function, out_shape=out_shape, in_specs=[VMEM] * len(opera...  2.96 us
    dynamic_slice x1, local copies, waits for them, and re-layouts, block_for(): return lax.dynamic_slice(by_stream, (0, 0, at), (3, SUB, channels))  0.99 us
    ppermute x1, waiting for transfers between devices, body(): got = lax.ppermute(summary, 'ctx', swap)  0.9 us
  transfers between devices with their start and end apart: 14, of which 10 were waited for; matrix products, arithmetic and copies ran while one was open for 0% of the time, Pallas kernels for 2%

profile of v13, /device:TPU:32, one launch (start us, length us, event | category | flops | bytes accessed | tf_op | source)
XLA Modules:
  0.0 43.2 jit_solution(10040694518946422016)
XLA Ops:
  0.0 1.0 %dynamic-slice_bitcast_fusion = (bf16[3,16,512]{2,1,0:T(8,128)(2,1)S(1)}, bf16[3,16,512]{2,1,0:T(8,128)(2,1)S(1)}, bf16[1,3,16,512]{3,2,1,0:T(8,128)(2,1)S(1)}, ...) fusion(bf16[16,3,4096]{2,0,1:T(8,128)(2,1)} %param.5, ...), kind=kLoop, calls=%fused_computation.1 | loop fusion | bytes 786464 | tf_op jit(solution)/shard_map/dynamic_slice | solution.py:347
  1.0 0.1 collective-permute-start.1
  1.1 6.4 %collective-permute-start = (bf16[3,16,512]{2,1,0:T(8,128)(2,1)S(1)}, bf16[3,16,512]{2,1,0:T(8,128)(2,1)S(1)}, u32[]{:S(2)}, u32[]{:S(2)}) collective-permute-start(bf16[3,16,512]{2,1,0:T(8,128)(2,1)S(1)} %get-tuple-element.35), channel_id=1, source_target_pairs={{0,4},{1,5},{2,6},{3,7},{4,0},{5,1},{6,2},{7,3},{8,12},{9,13},{10,... | collective-permute-start | bytes 147464 | tf_op jit(solution)/shard_map/ppermute | solution.py:354
  7.5 0.0 collective-permute-done.1.passed_ref
  7.5 0.9 %collective-permute-start.2 = (bf16[2,3,16,512]{3,2,1,0:T(8,128)(2,1)S(1)}, bf16[2,3,16,512]{3,2,1,0:T(8,128)(2,1)S(1)}, u32[]{:S(2)}, u32[]{:S(2)}) collective-permute-start(bf16[2,3,16,512]{3,2,1,0:T(8,128)(2,1)S(1)} %join.3), channel_id=1, source_target_pairs={{0,3},{1,4},{2,5},{3,6},{4,7},{5,0},{6,1},{7,2},{8,13},{9,14},{10,... | collective-permute-start | bytes 294920 | tf_op jit(solution)/shard_map/ppermute | solution.py:354
  8.4 1.5 %collective-permute-start.3 = (bf16[2,3,16,512]{3,2,1,0:T(8,128)(2,1)S(1)}, bf16[2,3,16,512]{3,2,1,0:T(8,128)(2,1)S(1)}, u32[]{:S(2)}, u32[]{:S(2)}) collective-permute-start(bf16[2,3,16,512]{3,2,1,0:T(8,128)(2,1)S(1)} %join.4), channel_id=1, source_target_pairs={{0,2},{1,3},{2,4},{3,5},{4,6},{5,7},{6,0},{7,1},{8,14},{9,15},{10,... | collective-permute-start | bytes 294920 | tf_op jit(solution)/shard_map/ppermute | solution.py:354
  10.0 2.3 %collective-permute-done.refs_0_ = bf16[3,16,512]{2,1,0:T(8,128)(2,1)S(1)} collective-permute-done((bf16[3,16,512]{2,1,0:T(8,128)(2,1)S(1)}, bf16[3,16,512]{2,1,0:T(8,128)(2,1)S(1)}, u32[]{:S(2)}, u32[]{:S(2)}) %collective-permute-start) | collective-permute-done | bytes 49184 | tf_op jit(solution)/shard_map/ppermute | solution.py:354
  12.3 0.0 collective-permute-start.4
  12.4 5.1 %collective-permute-done.2.refs_0_.refs_1_ = bf16[2,3,16,512]{3,2,1,0:T(8,128)(2,1)S(1)} collective-permute-done((bf16[2,3,16,512]{3,2,1,0:T(8,128)(2,1)S(1)}, bf16[2,3,16,512]{3,2,1,0:T(8,128)(2,1)S(1)}, u32[]{:S(2)}, u32[]{:S(2)}) %collective-permute-start.2) | collective-permute-done | bytes 98336 | tf_op jit(solution)/shard_map/ppermute | solution.py:354
  17.5 1.5 %collective-permute-done.3.refs_1_.refs_2_ = bf16[2,3,16,512]{3,2,1,0:T(8,128)(2,1)S(1)} collective-permute-done((bf16[2,3,16,512]{3,2,1,0:T(8,128)(2,1)S(1)}, bf16[2,3,16,512]{3,2,1,0:T(8,128)(2,1)S(1)}, u32[]{:S(2)}, u32[]{:S(2)}) %collective-permute-start.3) | collective-permute-done | bytes 98336 | tf_op jit(solution)/shard_map/ppermute | solution.py:354
  19.0 0.0 copy-start
  19.0 0.0 copy-start.2
  19.0 0.1 collective-permute-start.5
  19.1 0.0 collective-permute-done.4.refs_0_.refs_3_
  19.1 0.0 copy-start.3
  19.2 0.6 %collective-permute-start.6 = (bf16[1,3,16,512]{3,2,1,0:T(8,128)(2,1)S(1)}, bf16[1,3,16,512]{3,2,1,0:T(8,128)(2,1)S(1)}, u32[]{:S(2)}, u32[]{:S(2)}) collective-permute-start(bf16[1,3,16,512]{3,2,1,0:T(8,128)(2,1)S(1)} %back_kernel.3), channel_id=1, source_target_pairs={{0,8},{8,0},{16,24},{24,16},{32,40},{40,32},{48,56},{56,48},{64,72... | collective-permute-start | bytes 147464 | tf_op jit(solution)/shard_map/ppermute | solution.py:367
  19.7 0.0 copy-done
  19.8 0.0 copy-done.2
  19.8 0.0 copy-done.3
  19.8 0.0 copy-start.1
  19.8 0.1 weights_kernel.1
  19.9 0.7 %collective-permute-done.6.refs_5_ = bf16[1,3,16,512]{3,2,1,0:T(8,128)(2,1)S(1)} collective-permute-done((bf16[1,3,16,512]{3,2,1,0:T(8,128)(2,1)S(1)}, bf16[1,3,16,512]{3,2,1,0:T(8,128)(2,1)S(1)}, u32[]{:S(2)}, u32[]{:S(2)}) %collective-permute-start.6) | collective-permute-done | bytes 49184 | tf_op jit(solution)/shard_map/ppermute | solution.py:367
  20.6 0.0 collective-permute-done.5.refs_4_
  20.6 0.0 copy-done.1
  20.6 0.6 %state_kernel.1 = (f32[32,512]{1,0:T(8,128)S(1)}, f32[16,8,512]{2,1,0:T(8,128)S(1)}, f32[16,8,512]{2,1,0:T(8,128)S(1)}) custom-call(bf16[3,16,512]{2,1,0:T(8,128)(2,1)S(1)} %collective-permute-done.refs_0_, bf16[2,3,16,512]{3,2,1,0:T(8,128)(2,1)S(1)} %collective-permute-done.2.refs_0_.refs_1_, ...), custom_call_target="tpu_custom_call" | custom-call | tf_op jit(solution)/shard_map/state_kernel/pallas_call | solution.py:325
  21.2 0.5 %collective-permute-start.7 = (f32[32,512]{1,0:T(8,128)S(1)}, f32[32,512]{1,0:T(8,128)S(1)}, u32[]{:S(2)}, u32[]{:S(2)}) collective-permute-start(f32[32,512]{1,0:T(8,128)S(1)} %get-tuple-element.19.kept_ref.summary_ref), channel_id=1, source_target_pairs={{0,8},{8,0},{16,24},{24,16},{32,40},{40,32},{48,56},{56,48},{64,72... | collective-permute-start | bytes 196616 | tf_op jit(solution)/shard_map/ppermute | solution.py:375
  21.7 0.9 %collective-permute-done.7.got_ref = f32[32,512]{1,0:T(8,128)S(1)} collective-permute-done((f32[32,512]{1,0:T(8,128)S(1)}, f32[32,512]{1,0:T(8,128)S(1)}, u32[]{:S(2)}, u32[]{:S(2)}) %collective-permute-start.7) | collective-permute-done | bytes 65568 | tf_op jit(solution)/shard_map/ppermute | solution.py:375
  22.7 3.1 %collective-permute-start.10 = (bf16[48,512]{1,0:T(8,128)(2,1)S(1)}, bf16[48,512]{1,0:T(8,128)(2,1)S(1)}, u32[]{:S(2)}, u32[]{:S(2)}) collective-permute-start(bf16[48,512]{1,0:T(8,128)(2,1)S(1)} %get-tuple-element.20.own_ref), channel_id=1, source_target_pairs={{0,32},{8,40},{16,48},{24,56},{32,0},{40,8},{48,16},{56,24},{64,96... | collective-permute-start | bytes 147464 | tf_op jit(solution)/shard_map/ppermute | solution.py:382
  25.8 1.1 %collective-permute-start.9 = (bf16[48,512]{1,0:T(8,128)(2,1)S(1)}, bf16[48,512]{1,0:T(8,128)(2,1)S(1)}, u32[]{:S(2)}, u32[]{:S(2)}) collective-permute-start(bf16[48,512]{1,0:T(8,128)(2,1)S(1)} %get-tuple-element.20.own_ref), channel_id=1, source_target_pairs={{0,48},{8,56},{16,0},{24,8},{32,16},{40,24},{48,32},{56,40},{64,11... | collective-permute-start | bytes 147464 | tf_op jit(solution)/shard_map/ppermute | solution.py:382
  26.9 0.9 %collective-permute-start.8 = (bf16[48,512]{1,0:T(8,128)(2,1)S(1)}, bf16[48,512]{1,0:T(8,128)(2,1)S(1)}, u32[]{:S(2)}, u32[]{:S(2)}) collective-permute-start(bf16[48,512]{1,0:T(8,128)(2,1)S(1)} %get-tuple-element.20.own_ref), channel_id=1, source_target_pairs={{0,16},{8,24},{16,32},{24,40},{32,48},{40,56},{48,0},{56,8},{64,80... | collective-permute-start | bytes 147464 | tf_op jit(solution)/shard_map/ppermute | solution.py:382
  27.8 0.5 %collective-permute-done.10.two_ref = bf16[48,512]{1,0:T(8,128)(2,1)S(1)} collective-permute-done((bf16[48,512]{1,0:T(8,128)(2,1)S(1)}, bf16[48,512]{1,0:T(8,128)(2,1)S(1)}, u32[]{:S(2)}, u32[]{:S(2)}) %collective-permute-start.10) | collective-permute-done | bytes 49184 | tf_op jit(solution)/shard_map/ppermute | solution.py:382
  28.4 1.5 %collective-permute-done.9.three_ref = bf16[48,512]{1,0:T(8,128)(2,1)S(1)} collective-permute-done((bf16[48,512]{1,0:T(8,128)(2,1)S(1)}, bf16[48,512]{1,0:T(8,128)(2,1)S(1)}, u32[]{:S(2)}, u32[]{:S(2)}) %collective-permute-start.9) | collective-permute-done | bytes 49184 | tf_op jit(solution)/shard_map/ppermute | solution.py:382
  29.9 2.4 %collective-permute-done.8.one_ref = bf16[48,512]{1,0:T(8,128)(2,1)S(1)} collective-permute-done((bf16[48,512]{1,0:T(8,128)(2,1)S(1)}, bf16[48,512]{1,0:T(8,128)(2,1)S(1)}, u32[]{:S(2)}, u32[]{:S(2)}) %collective-permute-start.8) | collective-permute-done | bytes 49184 | tf_op jit(solution)/shard_map/ppermute | solution.py:382
  32.2 0.1 row_kernel.1
  32.4 3.3 %collective-permute-start.13 = (bf16[48,512]{1,0:T(8,128)(2,1)S(1)}, bf16[48,512]{1,0:T(8,128)(2,1)S(1)}, u32[]{:S(2)}, u32[]{:S(2)}) collective-permute-start(bf16[48,512]{1,0:T(8,128)(2,1)S(1)} %get-tuple-element.21.own_ref), channel_id=1, source_target_pairs={{0,128},{8,136},{16,144},{24,152},{32,160},{40,168},{48,176},{56,1... | collective-permute-start | bytes 147464 | tf_op jit(solution)/shard_map/ppermute | solution.py:382
  35.6 1.1 %collective-permute-start.12 = (bf16[48,512]{1,0:T(8,128)(2,1)S(1)}, bf16[48,512]{1,0:T(8,128)(2,1)S(1)}, u32[]{:S(2)}, u32[]{:S(2)}) collective-permute-start(bf16[48,512]{1,0:T(8,128)(2,1)S(1)} %get-tuple-element.21.own_ref), channel_id=1, source_target_pairs={{0,192},{8,200},{16,208},{24,216},{32,224},{40,232},{48,240},{56,2... | collective-permute-start | bytes 147464 | tf_op jit(solution)/shard_map/ppermute | solution.py:382
  36.7 1.0 %collective-permute-start.11 = (bf16[48,512]{1,0:T(8,128)(2,1)S(1)}, bf16[48,512]{1,0:T(8,128)(2,1)S(1)}, u32[]{:S(2)}, u32[]{:S(2)}) collective-permute-start(bf16[48,512]{1,0:T(8,128)(2,1)S(1)} %get-tuple-element.21.own_ref), channel_id=1, source_target_pairs={{0,64},{8,72},{16,80},{24,88},{32,96},{40,104},{48,112},{56,120},{... | collective-permute-start | bytes 147464 | tf_op jit(solution)/shard_map/ppermute | solution.py:382
  37.7 0.9 %local_kernel.1 = (f32[16,8,512]{2,1,0:T(8,128)S(1)}, f32[16,8,512]{2,1,0:T(8,128)S(1)}) custom-call(bf16[3,16,512]{2,1,0:T(8,128)(2,1)S(1)} %collective-permute-done.refs_0_, bf16[2,3,16,512]{3,2,1,0:T(8,128)(2,1)S(1)} %collective-permute-done.2.refs_0_.refs_1_, bf16[2,3,16,512]{3,2,1,0:T(8,128)(2,1)S(1)} %collective-permute-done.3.refs_1_.refs_2_, ...), custom_call_target="tpu_custom_call" | custom-call | flops 8388608 | bytes 2097152 | tf_op jit(solution)/shard_map/local_kernel/pallas_call | solution.py:325
  38.5 0.0 collective-permute-done.13.two_ref
  38.5 1.2 %collective-permute-done.12.three_ref = bf16[48,512]{1,0:T(8,128)(2,1)S(1)} collective-permute-done((bf16[48,512]{1,0:T(8,128)(2,1)S(1)}, bf16[48,512]{1,0:T(8,128)(2,1)S(1)}, u32[]{:S(2)}, u32[]{:S(2)}) %collective-permute-start.12) | collective-permute-done | bytes 49184 | tf_op jit(solution)/shard_map/ppermute | solution.py:382
  39.7 2.3 %collective-permute-done.11.one_ref = bf16[48,512]{1,0:T(8,128)(2,1)S(1)} collective-permute-done((bf16[48,512]{1,0:T(8,128)(2,1)S(1)}, bf16[48,512]{1,0:T(8,128)(2,1)S(1)}, u32[]{:S(2)}, u32[]{:S(2)}) %collective-permute-start.11) | collective-permute-done | bytes 49184 | tf_op jit(solution)/shard_map/ppermute | solution.py:382
  42.0 0.1 merge_kernel.1.carry_ref
  42.2 1.1 %final_kernel.1 = bf16[128,512]{1,0:T(8,128)(2,1)} custom-call(f32[24,512]{1,0:T(8,128)S(1)} %merge_kernel.1.carry_ref, f32[32,512]{1,0:T(8,128)S(1)} %get-tuple-element.19.kept_ref.summary_ref, f32[3,3,512]{2,1,0:T(4,128)S(1)} %copy-done.1, f32[16,512]{1,0:T(8,128)S(1)} %copy-done, f32[16,512]{1,0:T(8,128)S(1)} %copy-done.2, f32[1,512]{1,0:T(1,128)S(1)} %bitcast.25, ...), custom_call_target="tpu_custom_call" | custom-call | tf_op jit(solution)/shard_map/final_kernel/pallas_call | solution.py:325
  (7 shorter events, 0.1 us)
Async XLA Ops:
  1.0 6.5 %collective-permute-start.1 = (bf16[3,3,16,512]{3,2,1,0:T(8,128)(2,1)S(1)}, bf16[3,3,16,512]{3,2,1,0:T(8,128)(2,1)S(1)}, u32[]{:S(2)}, u32[]{:S(2)}) collective-permute-start(bf16[3,3,16,512]{3,2,1,0:T(8,128)(2,1)S(1)} %pad_maximum_fusion), channel_id=1, source_target_pairs={{0,8},{8,0},{16,24},{24,16},{32,40},{40,32},{48,56},{56,48},{64,72... | collective-permute-start | bytes 442376 | tf_op jit(solution)/shard_map/ppermute | solution.py:356
  1.1 11.2 %collective-permute-start = (bf16[3,16,512]{2,1,0:T(8,128)(2,1)S(1)}, bf16[3,16,512]{2,1,0:T(8,128)(2,1)S(1)}, u32[]{:S(2)}, u32[]{:S(2)}) collective-permute-start(bf16[3,16,512]{2,1,0:T(8,128)(2,1)S(1)} %get-tuple-element.35), channel_id=1, source_target_pairs={{0,4},{1,5},{2,6},{3,7},{4,0},{5,1},{6,2},{7,3},{8,12},{9,13},{10,... | collective-permute-start | bytes 147464 | tf_op jit(solution)/shard_map/ppermute | solution.py:354
  7.5 9.9 %collective-permute-start.2 = (bf16[2,3,16,512]{3,2,1,0:T(8,128)(2,1)S(1)}, bf16[2,3,16,512]{3,2,1,0:T(8,128)(2,1)S(1)}, u32[]{:S(2)}, u32[]{:S(2)}) collective-permute-start(bf16[2,3,16,512]{3,2,1,0:T(8,128)(2,1)S(1)} %join.3), channel_id=1, source_target_pairs={{0,3},{1,4},{2,5},{3,6},{4,7},{5,0},{6,1},{7,2},{8,13},{9,14},{10,... | collective-permute-start | bytes 294920 | tf_op jit(solution)/shard_map/ppermute | solution.py:354
  8.4 10.6 %collective-permute-start.3 = (bf16[2,3,16,512]{3,2,1,0:T(8,128)(2,1)S(1)}, bf16[2,3,16,512]{3,2,1,0:T(8,128)(2,1)S(1)}, u32[]{:S(2)}, u32[]{:S(2)}) collective-permute-start(bf16[2,3,16,512]{3,2,1,0:T(8,128)(2,1)S(1)} %join.4), channel_id=1, source_target_pairs={{0,2},{1,3},{2,4},{3,5},{4,6},{5,7},{6,0},{7,1},{8,14},{9,15},{10,... | collective-permute-start | bytes 294920 | tf_op jit(solution)/shard_map/ppermute | solution.py:354
  12.3 6.8 %collective-permute-start.4 = (bf16[2,3,16,512]{3,2,1,0:T(8,128)(2,1)S(1)}, bf16[2,3,16,512]{3,2,1,0:T(8,128)(2,1)S(1)}, u32[]{:S(2)}, u32[]{:S(2)}) collective-permute-start(bf16[2,3,16,512]{3,2,1,0:T(8,128)(2,1)S(1)} %join.5), channel_id=1, source_target_pairs={{0,1},{1,2},{2,3},{3,4},{4,5},{5,6},{6,7},{7,0},{8,15},{9,8},{10,9... | collective-permute-start | bytes 294920 | tf_op jit(solution)/shard_map/ppermute | solution.py:354
  19.0 0.8 %copy-start = (f32[16,512]{1,0:T(8,128)S(1)}, f32[16,512]{1,0:T(8,128)}, u32[]{:S(2)}) copy-start(f32[16,512]{1,0:T(8,128)} %rates_ref.9) | copy-start | bytes 98308
  19.0 0.8 %copy-start.2 = (f32[16,512]{1,0:T(8,128)S(1)}, f32[16,512]{1,0:T(8,128)}, u32[]{:S(2)}) copy-start(f32[16,512]{1,0:T(8,128)} %residues_ref.3) | copy-start | bytes 98308
  19.0 1.6 %collective-permute-start.5 = (bf16[2,3,16,512]{3,2,1,0:T(8,128)(2,1)S(1)}, bf16[2,3,16,512]{3,2,1,0:T(8,128)(2,1)S(1)}, u32[]{:S(2)}, u32[]{:S(2)}) collective-permute-start(bf16[2,3,16,512]{3,2,1,0:T(8,128)(2,1)S(1)} %back_kernel.2), channel_id=1, source_target_pairs={{0,8},{8,0},{16,24},{24,16},{32,40},{40,32},{48,56},{56,48},{64,72... | collective-permute-start | bytes 294920 | tf_op jit(solution)/shard_map/ppermute | solution.py:366
  19.1 0.7 %copy-start.3 = (f32[512]{0:T(512)S(1)}, f32[512]{0:T(512)}, u32[]{:S(2)}) copy-start(f32[512]{0:T(512)} %param.9) | copy-start | bytes 6148
  19.2 1.4 %collective-permute-start.6 = (bf16[1,3,16,512]{3,2,1,0:T(8,128)(2,1)S(1)}, bf16[1,3,16,512]{3,2,1,0:T(8,128)(2,1)S(1)}, u32[]{:S(2)}, u32[]{:S(2)}) collective-permute-start(bf16[1,3,16,512]{3,2,1,0:T(8,128)(2,1)S(1)} %back_kernel.3), channel_id=1, source_target_pairs={{0,8},{8,0},{16,24},{24,16},{32,40},{40,32},{48,56},{56,48},{64,72... | collective-permute-start | bytes 147464 | tf_op jit(solution)/shard_map/ppermute | solution.py:367
  19.8 0.8 %copy-start.1 = (f32[3,3,512]{2,1,0:T(4,128)S(1)}, f32[3,3,512]{2,1,0:T(4,128)}, u32[]{:S(2)}) copy-start(f32[3,3,512]{2,1,0:T(4,128)} %taps_ref.7) | copy-start | bytes 55300
  21.2 1.4 %collective-permute-start.7 = (f32[32,512]{1,0:T(8,128)S(1)}, f32[32,512]{1,0:T(8,128)S(1)}, u32[]{:S(2)}, u32[]{:S(2)}) collective-permute-start(f32[32,512]{1,0:T(8,128)S(1)} %get-tuple-element.19.kept_ref.summary_ref), channel_id=1, source_target_pairs={{0,8},{8,0},{16,24},{24,16},{32,40},{40,32},{48,56},{56,48},{64,72... | collective-permute-start | bytes 196616 | tf_op jit(solution)/shard_map/ppermute | solution.py:375
  22.7 5.7 %collective-permute-start.10 = (bf16[48,512]{1,0:T(8,128)(2,1)S(1)}, bf16[48,512]{1,0:T(8,128)(2,1)S(1)}, u32[]{:S(2)}, u32[]{:S(2)}) collective-permute-start(bf16[48,512]{1,0:T(8,128)(2,1)S(1)} %get-tuple-element.20.own_ref), channel_id=1, source_target_pairs={{0,32},{8,40},{16,48},{24,56},{32,0},{40,8},{48,16},{56,24},{64,96... | collective-permute-start | bytes 147464 | tf_op jit(solution)/shard_map/ppermute | solution.py:382
  25.8 4.1 %collective-permute-start.9 = (bf16[48,512]{1,0:T(8,128)(2,1)S(1)}, bf16[48,512]{1,0:T(8,128)(2,1)S(1)}, u32[]{:S(2)}, u32[]{:S(2)}) collective-permute-start(bf16[48,512]{1,0:T(8,128)(2,1)S(1)} %get-tuple-element.20.own_ref), channel_id=1, source_target_pairs={{0,48},{8,56},{16,0},{24,8},{32,16},{40,24},{48,32},{56,40},{64,11... | collective-permute-start | bytes 147464 | tf_op jit(solution)/shard_map/ppermute | solution.py:382
  26.9 5.3 %collective-permute-start.8 = (bf16[48,512]{1,0:T(8,128)(2,1)S(1)}, bf16[48,512]{1,0:T(8,128)(2,1)S(1)}, u32[]{:S(2)}, u32[]{:S(2)}) collective-permute-start(bf16[48,512]{1,0:T(8,128)(2,1)S(1)} %get-tuple-element.20.own_ref), channel_id=1, source_target_pairs={{0,16},{8,24},{16,32},{24,40},{32,48},{40,56},{48,0},{56,8},{64,80... | collective-permute-start | bytes 147464 | tf_op jit(solution)/shard_map/ppermute | solution.py:382
  32.4 6.2 %collective-permute-start.13 = (bf16[48,512]{1,0:T(8,128)(2,1)S(1)}, bf16[48,512]{1,0:T(8,128)(2,1)S(1)}, u32[]{:S(2)}, u32[]{:S(2)}) collective-permute-start(bf16[48,512]{1,0:T(8,128)(2,1)S(1)} %get-tuple-element.21.own_ref), channel_id=1, source_target_pairs={{0,128},{8,136},{16,144},{24,152},{32,160},{40,168},{48,176},{56,1... | collective-permute-start | bytes 147464 | tf_op jit(solution)/shard_map/ppermute | solution.py:382
  35.6 4.1 %collective-permute-start.12 = (bf16[48,512]{1,0:T(8,128)(2,1)S(1)}, bf16[48,512]{1,0:T(8,128)(2,1)S(1)}, u32[]{:S(2)}, u32[]{:S(2)}) collective-permute-start(bf16[48,512]{1,0:T(8,128)(2,1)S(1)} %get-tuple-element.21.own_ref), channel_id=1, source_target_pairs={{0,192},{8,200},{16,208},{24,216},{32,224},{40,232},{48,240},{56,2... | collective-permute-start | bytes 147464 | tf_op jit(solution)/shard_map/ppermute | solution.py:382
  36.7 5.3 %collective-permute-start.11 = (bf16[48,512]{1,0:T(8,128)(2,1)S(1)}, bf16[48,512]{1,0:T(8,128)(2,1)S(1)}, u32[]{:S(2)}, u32[]{:S(2)}) collective-permute-start(bf16[48,512]{1,0:T(8,128)(2,1)S(1)} %get-tuple-element.21.own_ref), channel_id=1, source_target_pairs={{0,64},{8,72},{16,80},{24,88},{32,96},{40,104},{48,112},{56,120},{... | collective-permute-start | bytes 147464 | tf_op jit(solution)/shard_map/ppermute | solution.py:382
